TPU v7x, 32 devices: a whole 2x2x4 slice. The times are simulated.
32 devices in a mesh: groups: 2 (over y), panel: 4 (over z), rhs: 2 (over x), coef: 2 (over core).
Axes of the slice: x: 2, y: 2, z: 4, core: 2. Of those that a mesh axis runs over, the one named last changes fastest.
Arguments:
- couplings: bfloat16 [4, 9, 2, 1024, 2, 2, 512], P('panel', None, 'coef', None, None, 'rhs'), may hold values from -1 to 66, as said below
- observations: bfloat16 [1024, 4, 2, 1024], P(('groups', 'rhs'), 'panel', 'coef'), parts along dimension 0, may hold values from -1 to 1
- replicate_mask: int32 [1024, 128], P(('groups', 'rhs')), parts along dimension 0, may hold values 0 or 1
Outputs:
- solution: float32 [8, 2, 1024, 128], P(('groups', 'panel'), 'coef', 'rhs'), parts along dimension 0
- residual: float32 [8, 2, 1024, 128], P(('groups', 'panel'), 'coef', 'rhs'), parts along dimension 0
There are 2 independent parts, one for each index of `groups`. A program takes and returns all parts, laid end to end along the dimension named above; an argument that names none is the same for every part. Nothing has to cross between parts.
Inputs may be any that keep to these rules, and one draw needn't show every extreme that they name: `couplings`: K[p, m] equals the transpose of K[(p + m - 4) mod 4, 8 - m], and the operator A is positive definite.
All inputs are finite; a program needn't handle non-finite values. No bound on the sum of `replicate_mask` on one device may be relied on, other than what follows from the above.
Results may differ from a plain program's by a relative error of at most 0.0075.
The roundings to bfloat16 on the way count: a program that leaves them out, or rounds other values in their place, can miss the bound.
Values may be sent and summed in bfloat16 or wider, within the bound.
No kernel may reach another device: no remote copies, remote signals or barrier semaphores. Data moves between devices by JAX's collectives and lax.ppermute only.
A program may use at most 128 MiB of HBM per device.

v0:
```python
import functools

import jax
import jax.numpy as jnp
from jax import lax
from jax.experimental import pallas as pl
from jax.experimental.pallas import tpu as pltpu
from jax.sharding import PartitionSpec as P

ITERS = 3
LANES = 128
SUB = 8
VMEM_LIMIT = 14 * 2**20
F32 = jnp.float32
BF16 = jnp.bfloat16
VMEM = pl.BlockSpec(memory_space=pltpu.VMEM)
ANY = pl.BlockSpec(memory_space=pl.ANY)
HBM = pl.BlockSpec(memory_space=pltpu.HBM)


def mm(a, b, dims=(1, 0)):
    return lax.dot_general(
        a,
        b,
        (((dims[0],), (dims[1],)), ((), ())),
        precision=lax.Precision.HIGHEST,
        preferred_element_type=F32,
    )


def call(body, outs, *args, scratch=(), after=(), any_args=0, any_outs=False):
    inputs, outputs, waits = len(args), len(outs), len(after)

    def ordered(*refs):
        token = refs[inputs + waits + outputs]
        token[...] = jnp.zeros_like(token)
        body(
            *refs[:inputs],
            *refs[inputs + waits : inputs + waits + outputs],
            *refs[inputs + waits + outputs + 1 :],
        )

    return pl.pallas_call(
        ordered,
        out_shape=list(outs) + [shape(SUB)],
        in_specs=[HBM] * any_args + [VMEM] * (inputs - any_args) + [ANY] * waits,
        out_specs=[ANY if any_outs else VMEM] * outputs + [VMEM],
        scratch_shapes=list(scratch),
        cost_estimate=pl.CostEstimate(flops=1, bytes_accessed=1, transcendentals=0),
        compiler_params=pltpu.CompilerParams(vmem_limit_bytes=VMEM_LIMIT),
    )(*args, *after)


def shape(rows, cols=LANES, dtype=F32):
    return jax.ShapeDtypeStruct((rows, cols), dtype)


def permute(value, axis, pairs):
    return lax.ppermute(value, axis, pairs)


def shifted(value, axis, by):
    n = lax.axis_size(axis)
    return permute(value, axis, [((i + by) % n, i) for i in range(n)])


def mate(i, s, n):
    return i ^ s if n & (n - 1) == 0 else (s - i) % n


def swapped(value, axis, s, n):
    return permute(value, axis, [(mate(i, s, n), i) for i in range(n)])


def sum_near(value):
    axes = ("panel", "rhs")
    count = lax.axis_size(axes)
    one, two, three = (swapped(value, axes, s, count) for s in (1, 2, 3))
    return (value + one) + (two + three)


def from_far(value):
    axes = ("panel", "rhs")
    return swapped(value, axes, 4, lax.axis_size(axes))


def sum_far(value, meanwhile=None):
    other = from_far(value)
    if meanwhile is not None:
        other, _ = lax.optimization_barrier((other, meanwhile))
    return value + other


def by_stages():
    return lax.axis_size("panel") == 4 and lax.axis_size("rhs") == 2


def reduce_one(value):
    value = value + swapped(value, "coef", 1, 2)
    if not by_stages():
        value = lax.psum(value, ("panel", "rhs"))
        return value, value
    near = sum_near(value)
    return sum_far(near), near


def reduce_both(mine, mates, square):
    value = mine + swapped(mates, "coef", 1, 2)
    whole = square + swapped(square, "coef", 1, 2)
    if by_stages():
        rows = value.shape[0]
        value = sum_far(value, meanwhile=square)
        both = sum_near(jnp.concatenate([value, whole], axis=0))
        value, whole = both[:rows], both[rows:]
        terms = [whole, from_far(whole)]
    else:
        value, whole = lax.psum((value, whole), ("panel", "rhs"))
        terms = [whole]
    return [value, swapped(value, "coef", 1, 2)], terms


def right_side_parts(obs, mask, n, strip):
    def body(obs_hbm, mask_hbm, *refs):
        *outs, obs_ref, mask_ref, sems = refs
        copies = [
            pltpu.make_async_copy(mask_hbm, mask_ref, sems.at[0]),
            pltpu.make_async_copy(obs_hbm, obs_ref, sems.at[1]),
        ]
        for copy in copies:
            copy.start()
        for copy in copies:
            copy.wait()
        signs = (2 * mask_ref[...] - 1).astype(BF16)
        me = lax.axis_index("rhs")
        for s in range(n):
            place = pl.multiple_of(mate(me, s, n) * strip, strip)
            outs[s][...] = lax.dot_general(
                obs_ref[:, pl.ds(place, strip)],
                signs,
                (((0,), (0,)), ((), ())),
                preferred_element_type=F32,
            )

    *parts, token = call(
        body,
        [shape(strip)] * n,
        pltpu.with_memory_space_constraint(obs, pltpu.HBM),
        pltpu.with_memory_space_constraint(mask, pltpu.HBM),
        scratch=[
            pltpu.VMEM(obs.shape, BF16),
            pltpu.VMEM(mask.shape, mask.dtype),
            pltpu.SemaphoreType.DMA((2,)),
        ],
        any_args=2,
    )
    return parts, token


def sum_and_round(parts, token):
    strip = parts[0].shape[0]

    def body(*refs):
        *ins, out, low = refs
        total = ins[0][...]
        for ref in ins[1:]:
            total = total + ref[...]
        out[...] = total
        low[...] = total.astype(BF16)

    return call(
        body, [shape(strip), shape(strip, dtype=BF16)], *parts, after=[token]
    )


def retiled(blocks, links, count, token):
    rows, strip = blocks.shape[1], blocks.shape[3]
    tiles = strip // LANES

    def body(k_ref, out, sems):
        copies = []
        for i, link in enumerate(links()):
            for t in range(tiles):
                copy = pltpu.make_async_copy(
                    k_ref.at[link, :, :, pl.ds(t * LANES, LANES)], out.at[i, t], sems.at[i, t]
                )
                copy.start()
                copies.append(copy)
        for copy in copies:
            copy.wait()

    packed, token = call(
        body,
        [pltpu.VMEM((count, tiles, rows, 2, LANES), BF16)],
        blocks,
        scratch=[pltpu.SemaphoreType.DMA((count, tiles))],
        after=[token],
        any_args=1,
        any_outs=True,
    )
    return packed, token


def link_products(packed, pieces, acc, n, last, after=()):
    count, tiles, rows = packed.shape[:3]
    packed = packed.reshape(count, tiles, 2 * rows, LANES)
    packed = pltpu.with_memory_space_constraint(packed, pltpu.VMEM)
    strip = tiles * LANES
    block = min(512, 2 * rows)

    def body(*refs):
        k_ref, own_ref, other_ref = refs[:3]
        acc_ref = refs[3] if acc is not None else None
        outs = refs[3 + (acc is not None) : -3]
        weights, even_acc, odd_acc = refs[-3:]
        half = lax.axis_index("coef")
        weights[:, pl.ds(pl.multiple_of(half * LANES, LANES), LANES)] = own_ref[...]
        weights[:, pl.ds(pl.multiple_of((1 - half) * LANES, LANES), LANES)] = other_ref[...]
        for start in range(0, 2 * rows, block):
            here = slice(start, start + block)
            left = jnp.concatenate(
                [k_ref[i, t, here, :] for i in range(count) for t in range(tiles)], axis=1
            )
            right = jnp.concatenate([weights[...]] * count, axis=0)
            product = jnp.dot(left, right, preferred_element_type=F32)
            even_acc[here, :] = product[:, :LANES]
            odd_acc[here, :] = product[:, LANES:]
        me = lax.axis_index("rhs")
        size = rows // len(outs)
        for s in range(len(outs)):
            start = mate(me, s, n) * size if last else 0
            even = even_acc[pl.ds(2 * start, size, stride=2), :]
            odd = odd_acc[pl.ds(2 * start + 1, size, stride=2), :]
            total = even + odd
            if acc_ref is not None:
                total = total + acc_ref[pl.ds(start, size), :]
            outs[s][...] = total

    args = [packed, *pieces] + ([acc] if acc is not None else [])
    *result, token = call(
        body,
        [shape(rows // n)] * n if last else [shape(rows)],
        *args,
        scratch=[
            pltpu.VMEM((strip, 2 * LANES), BF16),
            pltpu.VMEM((2 * rows, LANES), F32),
            pltpu.VMEM((2 * rows, LANES), F32),
        ],
        after=after,
    )
    return (result if last else result[0]), token


def link_groups(links):
    reach = (links - 1) // 2
    panels = lax.axis_size("panel")
    groups = []
    if links == 2 * panels + 1 and panels & (panels - 1) == 0:
        for s in range(panels):

            def numbers(s=s):
                me = lax.axis_index("panel")
                start = lax.rem((me ^ s) - me + reach + panels, panels)
                return [start + panels * i for i in range(3 if s == 0 else 2)]

            bring = functools.partial(swapped, axis="panel", s=s, n=panels)
            groups.append((bring, numbers, 3 if s == 0 else 2))
        return groups
    offsets = {}
    for link in range(links):
        offsets.setdefault((link - reach) % panels, []).append(link)
    for o in sorted(offsets, key=lambda o: min(o, panels - o)):
        bring = functools.partial(shifted, axis="panel", by=o)
        groups.append((bring, functools.partial(list, offsets[o]), len(offsets[o])))
    return groups


def operate(packed, groups, low, direction, between):
    n = lax.axis_size("rhs")
    last = len(groups) - 1
    arrived = [low] + [bring(low) for bring, _, _ in groups[:0:-1]][::-1]
    directions = [direction] + [swapped(direction, "rhs", s, n) for s in range(1, n)]
    acc, after, tokens = None, (), []
    for place in range(last + 1):
        piece = arrived[place]
        if place:
            piece, held = lax.optimization_barrier((piece, tokens[0 if place < last else -1]))
            after = (*after, *held)
        pair = [piece, swapped(piece, "coef", 1, 2)]
        if place == 1:
            after = (*after, *directions[1:])
        acc, token = link_products(packed[place], pair, acc, n, place == last, after)
        after = ()
        if place == 0:
            after = (between(token),)
            tokens.append((token, *after))
        else:
            tokens.append((token,))
    return acc, directions


PACKED = LANES // 2 + SUB


def corner():
    row = lax.broadcasted_iota(jnp.int32, (LANES // 2, LANES), 0)
    lane = lax.broadcasted_iota(jnp.int32, (LANES // 2, LANES), 1)
    return row, lane, lane < LANES // 2


def packed_symmetric(matrix):
    half = LANES // 2
    row, lane, left = corner()
    top = matrix[:half]
    last = pltpu.roll(matrix[half:], half, 1)
    body = jnp.where(left & (lane > row), last, top)
    diagonal = jnp.sum(jnp.where(lane == row, last, 0.0), axis=0, keepdims=True)
    return jnp.concatenate([body, jnp.broadcast_to(diagonal, (SUB, LANES))], axis=0)


def unpacked_symmetric(rows):
    half = LANES // 2
    row, lane, left = corner()
    body, diagonal = rows[:half], rows[half : half + 1]
    top = jnp.where(left & (lane >= row), 0.0, body)
    last = jnp.where(left & (lane > row), body, 0.0)
    sides = jnp.concatenate([top, pltpu.roll(last, half, 1)], axis=0)
    top = jnp.where(lane == row, body, 0.0)
    last = jnp.where(lane == row, jnp.broadcast_to(diagonal, body.shape), 0.0)
    return sides + sides.T + jnp.concatenate([top, pltpu.roll(last, half, 1)], axis=0)


def symmetric(raw):
    return 0.5 * (raw + raw.T)


JOINT = PACKED + SUB + LANES


def linear_grams(parts, directions, before, beta, first, final):
    strip = parts[0].shape[0]
    n = len(parts)
    extra = [] if first or final else [*before, beta]
    rows = PACKED if final else JOINT // 2

    def body(*refs):
        images, ds = refs[:n], refs[n : 2 * n]
        rest = refs[2 * n : 2 * n + len(extra)]
        outs = refs[2 * n + len(extra) :]
        curve = cross = None
        for s in range(n):
            image, d = images[s][...], ds[s][...]
            term = mm(d, image, (0, 0))
            curve = term if s == 0 else curve + term
            if extra:
                r = d - mm(rest[s][...], rest[n][...])
                term = mm(r, image, (0, 0))
                cross = term if s == 0 else cross + term
        if final:
            outs[0][...] = packed_symmetric(symmetric(curve))
            return
        mine, mates, stacked = outs
        if first:
            r = ds[0][...]
            sym, whole = mm(r, r, (0, 0)), curve
        else:
            sym, whole = symmetric(curve), cross
        stacked[:PACKED] = packed_symmetric(sym)
        stacked[PACKED : PACKED + SUB] = jnp.zeros((SUB, LANES), F32)
        stacked[PACKED + SUB :] = whole
        half = lax.axis_index("coef")
        mine[...] = stacked[pl.ds(pl.multiple_of(half * rows, SUB), rows), :]
        mates[...] = stacked[pl.ds(pl.multiple_of((1 - half) * rows, SUB), rows), :]

    *pieces, _ = call(
        body,
        [shape(rows)] * (1 if final else 2),
        *parts,
        *directions,
        *extra,
        scratch=[] if final else [pltpu.VMEM((2 * rows, LANES), F32)],
    )
    return pieces


def square_gram(image_parts):
    strip = image_parts[0].shape[0]
    parts = len(image_parts)

    def body(*refs):
        ins, image_out, out = refs[:parts], refs[parts], refs[parts + 1]
        image = ins[0][...]
        for ref in ins[1:]:
            image = image + ref[...]
        image_out[...] = image
        out[...] = packed_symmetric(mm(image, image, (0, 0)))

    image, square, _ = call(
        body,
        [shape(strip), shape(PACKED)],
        *image_parts,
    )
    return image, square


def inverted(matrices, lane):
    strips = matrices[0].shape[0] // SUB
    many = len(matrices)
    place = lax.broadcasted_iota(jnp.int32, (SUB, LANES), 0)

    def lanes_of(value, at):
        return jnp.broadcast_to(value[:, at : at + 1], (SUB, LANES))

    def rows_of(value):
        return [jnp.broadcast_to(value[i : i + 1], (SUB, LANES)) for i in range(SUB)]

    def updated(row, rows):
        factors = [lanes_of(row, i) for i in range(SUB)]
        for factor, other in zip(factors, rows):
            row = row - factor * other
        return row

    def step(_, carry):
        held = [list(carry[m * strips : (m + 1) * strips]) for m in range(many)]
        rows = [rows_of(value) for value in carry[many * strips :]]
        now = []
        for a, last in zip(held, rows):
            a[1] = updated(a[1], last)
            now.append([a[1], *(lanes_of(a[1], SUB + i) for i in range(SUB))])
        for i in range(SUB):
            here = place == i
            for index, values in enumerate(now):
                column = values[1 + i]
                inverse = 1.0 / column[i : i + 1]

                def pivot(value):
                    row = value[i : i + 1] * inverse
                    return jnp.where(here, row, value - column * row)

                now[index] = [
                    pivot(value) if at < 1 or at > 1 + i else value
                    for at, value in enumerate(values)
                ]
            if 2 + i < strips:
                for a, last in zip(held, rows):
                    a[2 + i] = updated(a[2 + i], last)
        turned = []
        for a, values in zip(held, now):
            a[1] = values[0]
            turned.append([pltpu.roll(row, LANES - SUB, 1) for row in a[1:] + a[:1]])
        return tuple([row for a in turned for row in a] + [a[0] for a in turned])

    start = []
    for value in matrices:
        value = pltpu.roll(value, (SUB - lane) % LANES, 1)
        a = [value[SUB * k : SUB * (k + 1)] for k in range(strips)]
        start += a[-1:] + a[:-1]
    start += [jnp.zeros((SUB, LANES), F32)] * many
    carry = lax.fori_loop(0, strips, step, tuple(start))
    found = []
    for m in range(many):
        a = list(carry[m * strips : (m + 1) * strips])
        rows = rows_of(carry[many * strips + m])
        a = [updated(row, rows) for row in a[1:]] + a[:1]
        found.append(pltpu.roll(jnp.concatenate(a, axis=0), LANES - SUB, 1))
    return found


def eliminated(*systems):
    half = LANES // 2
    row = lax.broadcasted_iota(jnp.int32, (half, LANES), 0)
    lane = lax.broadcasted_iota(jnp.int32, (half, LANES), 1)
    left = lane < half
    first = inverted(
        [
            jnp.where(left, matrix[:half], (lane - half == row).astype(F32))
            for matrix, _ in systems
        ],
        0,
    )
    tops, lasts = [], []
    for (matrix, sides), value in zip(systems, first):
        top = mm(value[:, :half], jnp.concatenate([matrix[:half], sides[:half]], axis=1))
        low = jnp.concatenate([matrix[half:], sides[half:]], axis=1)
        tops.append(top)
        lasts.append(low - mm(matrix[half:, :half], top))
    second = inverted(
        [jnp.where(left, (lane == row).astype(F32), last[:, :LANES]) for last in lasts], half
    )
    found = []
    for top, last, value in zip(tops, lasts, second):
        low = mm(value[:, :half], last[:, LANES:])
        high = top[:, LANES:] - mm(
            top[:, :LANES], jnp.concatenate([jnp.zeros_like(low), low], axis=0)
        )
        found.append(jnp.concatenate([high, low], axis=0))
    return found


def identity():
    return (
        lax.broadcasted_iota(jnp.int32, (LANES, LANES), 0)
        == lax.broadcasted_iota(jnp.int32, (LANES, LANES), 1)
    ).astype(F32)


def stepped(solution, direction, alpha, token):
    fields = [direction, alpha] + ([] if solution is None else [solution])

    def body(d, a, *refs):
        change = mm(d[...], a[...])
        refs[-1][...] = change if solution is None else refs[0][...] + change

    return call(body, [shape(direction.shape[0])], *fields, after=[token])


def last_alpha(small, gram):
    def body(small, g, out):
        out[...] = eliminated((unpacked_symmetric(small[...]), g[...]))[0]

    return call(body, [shape(LANES)], small, gram)[0]


def finish(alpha, residual, direction, solution, image):
    strip = residual.shape[0]

    def body(a, r, d, s, *refs):
        *images, out, new_r = refs
        image = images[0][...]
        for ref in images[1:]:
            image = image + ref[...]
        out[...] = s[...] + mm(d[...], a[...])
        new_r[...] = r[...] - mm(image, a[...])

    return call(
        body,
        [shape(strip), shape(strip)],
        alpha,
        residual,
        direction,
        solution,
        *image,
    )[:-1]


def advance(pieces, gram, residual, image):
    strip = residual.shape[0]
    rows = pieces[0].shape[0]
    first = gram is None
    fields = [*pieces, residual, image] + ([] if first else [gram])

    def body(*refs):
        mine, mates, r, image, *refs = refs
        *refs, raw = refs
        half = lax.axis_index("coef")
        raw[pl.ds(pl.multiple_of(half * rows, SUB), rows), :] = mine[...]
        raw[pl.ds(pl.multiple_of((1 - half) * rows, SUB), rows), :] = mates[...]
        sym, whole = unpacked_symmetric(raw[:PACKED, :]), raw[PACKED + SUB :, :]
        *refs, new_r, alpha_out, partial, inverse_out = refs
        g = sym if first else refs[0][...]
        curvature = symmetric(whole) if first else sym
        alpha, inverse_out[...] = eliminated((curvature, g), (g, identity()))
        new_r[...] = r[...] - mm(image[...], alpha)
        shared = mm(whole, alpha)
        alpha_out[...] = alpha
        partial[...] = g - (shared + shared.T)

    return call(
        body,
        [shape(strip)] + [shape(LANES)] * 3,
        *fields,
        scratch=[pltpu.VMEM((2 * rows, LANES), F32)],
    )[:-1]


def turn(square, alpha, partial, inverse, residual, direction):
    strip = residual.shape[0]

    def body(alpha, partial, inverse, r, d, *refs):
        *terms, new_d, low, beta_out, gram_out = refs
        square = terms[0][...]
        for ref in terms[1:]:
            square = square + ref[...]
        a = alpha[...]
        following = partial[...] + mm(a, mm(unpacked_symmetric(square), a), (0, 0))
        beta = mm(inverse[...], following)
        value = r[...] + mm(d[...], beta)
        low[...] = value.astype(BF16)
        new_d[...] = value
        beta_out[...] = beta
        gram_out[...] = following

    return call(
        body,
        [shape(strip), shape(strip, dtype=BF16), shape(LANES), shape(LANES)],
        alpha,
        partial,
        inverse,
        residual,
        direction,
        *square,
    )[:-1]


def shards(couplings, observations, replicate_mask):
    links, rows = couplings.shape[1], couplings.shape[3]
    strip = couplings.shape[6]
    blocks = couplings.reshape(links, rows, couplings.shape[4], strip)
    blocks = pltpu.with_memory_space_constraint(blocks, pltpu.HBM)
    n = lax.axis_size("rhs")
    obs_matrix = observations.reshape(observations.shape[0], rows)
    parts, token = right_side_parts(obs_matrix, replicate_mask, n, strip)
    own = [parts[0]] + [swapped(parts[s], "rhs", s, n) for s in range(1, n)]
    groups = link_groups(links)
    packed = []
    for _, numbers, count in groups[:2]:
        value, token = retiled(blocks, numbers, count, token)
        packed.append(value)
    residual, low, token = sum_and_round(own, token)
    for _, numbers, count in groups[2:]:
        value, token = retiled(blocks, numbers, count, token)
        packed.append(value)
    retile_token = token
    direction = residual
    solution = gram = beta = before = alpha = None
    for step in range(ITERS):
        first, final = step == 0, step + 1 == ITERS
        state = [solution]

        def between(token):
            if first:
                return retile_token
            state[0], token = stepped(solution, before[0], alpha, token)
            return token

        parts, directions = operate(packed, groups, low, direction, between)
        (solution,) = state
        linear = linear_grams(parts, directions, before, beta, first, final)
        if final:
            small, near = reduce_one(*linear)
            parts[1:], _ = lax.optimization_barrier((parts[1:], near))
        image_parts = [parts[0]] + [swapped(parts[s], "rhs", s, n) for s in range(1, n)]
        if final:
            alpha = last_alpha(small, gram)
            solution, residual = finish(alpha, residual, direction, solution, image_parts)
            break
        image, square = square_gram(image_parts)
        linear, square = reduce_both(*linear, square)
        residual, alpha, partial, inverse = advance(linear, gram, residual, image)
        square[1:], alpha = lax.optimization_barrier((square[1:], alpha))
        before = directions
        direction, low, beta, gram = turn(
            square, alpha, partial, inverse, residual, direction
        )
    shape_out = (1, 1, strip, LANES)
    return (solution.reshape(shape_out), residual.reshape(shape_out))


def solution(mesh):
    placed = (
        P("panel", None, "coef", None, None, "rhs", None),
        P(("groups", "rhs"), "panel", "coef", None),
        P(("groups", "rhs"), None),
    )
    return jax.shard_map(
        shards,
        mesh=mesh,
        in_specs=placed,
        out_specs=(
            P(("groups", "panel"), "coef", "rhs", None),
            P(("groups", "panel"), "coef", "rhs", None),
        ),
        check_vma=False,
    )
```

profile of v0, /device:TPU:0, one launch (start us, length us, event | category | flops | bytes accessed | tf_op | source)
XLA Modules:
  0.0 161.7 jit_solution(10596207043072312622)
XLA Ops:
  2.1 3.0 %collective-permute-start = (f32[512,128]{1,0:T(8,128)S(1)}, f32[512,128]{1,0:T(8,128)S(1)}, u32[]{:S(2)}, u32[]{:S(2)}) collective-permute-start(f32[512,128]{1,0:T(8,128)S(1)} %get-tuple-element.100), channel_id=1, source_target_pairs={{2,0},{0,2},{3,1},{1,3},{6,4},{4,6},{7,5},{5,7},{10,8},{8,10},{11,... | collective-permute-start | bytes 786440 | tf_op jit(solution)/shard_map/ppermute | solution.py:59
  5.1 2.9 %shard_map.51 = (bf16[3,4,1024,2,128]{4,3,2,1,0:T(2,128)(2,1)S(1)}, f32[8,128]{1,0:T(8,128)S(1)}) custom-call(bf16[9,1024,2,512]{3,2,1,0:T(2,128)(2,1)} %bitcast.20, f32[8,128]{1,0:T(8,128)S(1)} %get-tuple-element.101.refs_1_), custom_call_target="tpu_custom_call" | custom-call | flops 1 | bytes 1 | tf_op jit(solution)/shard_map/pallas_call | solution.py:43
  8.0 2.2 %shard_map.52 = (bf16[2,4,1024,2,128]{4,3,2,1,0:T(2,128)(2,1)S(1)}, f32[8,128]{1,0:T(8,128)S(1)}) custom-call(bf16[9,1024,2,512]{3,2,1,0:T(2,128)(2,1)} %bitcast.21, f32[8,128]{1,0:T(8,128)S(1)} %get-tuple-element.102.refs_1_), custom_call_target="tpu_custom_call" | custom-call | flops 1 | bytes 1 | tf_op jit(solution)/shard_map/pallas_call | solution.py:43
  15.0 2.6 %collective-permute-start.2 = (bf16[512,128]{1,0:T(8,128)(2,1)S(1)}, bf16[512,128]{1,0:T(8,128)(2,1)S(1)}, u32[]{:S(2)}, u32[]{:S(2)}) collective-permute-start(bf16[512,128]{1,0:T(8,128)(2,1)S(1)} %get-tuple-element.107.refs_1_), channel_id=1, source_target_pairs={{8,0},{12,4},{0,8},{4,12},{9,1},{13,5},{1,9},{5,13},{10,2},{14,6},... | collective-permute-start | bytes 393224 | tf_op jit(solution)/shard_map/ppermute | solution.py:59
  17.6 2.2 %shard_map.54 = (bf16[2,4,1024,2,128]{4,3,2,1,0:T(2,128)(2,1)S(1)}, f32[8,128]{1,0:T(8,128)S(1)}) custom-call(bf16[9,1024,2,512]{3,2,1,0:T(2,128)(2,1)} %bitcast.22, f32[8,128]{1,0:T(8,128)S(1)} %get-tuple-element.104.refs_1_), custom_call_target="tpu_custom_call" | custom-call | flops 1 | bytes 1 | tf_op jit(solution)/shard_map/pallas_call | solution.py:43
  19.8 2.2 %shard_map.55 = (bf16[2,4,1024,2,128]{4,3,2,1,0:T(2,128)(2,1)S(1)}, f32[8,128]{1,0:T(8,128)S(1)}) custom-call(bf16[9,1024,2,512]{3,2,1,0:T(2,128)(2,1)} %bitcast.23, f32[8,128]{1,0:T(8,128)S(1)} %get-tuple-element.105.refs_1_), custom_call_target="tpu_custom_call" | custom-call | flops 1 | bytes 1 | tf_op jit(solution)/shard_map/pallas_call | solution.py:43
  22.0 2.0 %shard_map.56 = (f32[1024,128]{1,0:T(8,128)S(1)}, f32[8,128]{1,0:T(8,128)S(1)}) custom-call(bf16[3,4,2048,128]{3,2,1,0:T(8,128)(2,1)S(1)} %bitcast.8, bf16[512,128]{1,0:T(8,128)(2,1)S(1)} %get-tuple-element.107.refs_1_, bf16[512,128]{1,0:T(8,128)(2,1)S(1)} %collective-permute-done.3.refs_2_), custom_call_target="tpu_custom_call" | custom-call | flops 1 | bytes 1 | tf_op jit(solution)/shard_map/pallas_call | solution.py:43
  24.6 1.9 %collective-permute-start.1 = (bf16[512,128]{1,0:T(8,128)(2,1)S(1)}, bf16[512,128]{1,0:T(8,128)(2,1)S(1)}, u32[]{:S(2)}, u32[]{:S(2)}) collective-permute-start(bf16[512,128]{1,0:T(8,128)(2,1)S(1)} %get-tuple-element.107.refs_1_), channel_id=1, source_target_pairs={{12,0},{8,4},{4,8},{0,12},{13,1},{9,5},{5,9},{1,13},{14,2},{10,6},... | collective-permute-start | bytes 393224 | tf_op jit(solution)/shard_map/ppermute | solution.py:59
  26.5 1.9 %shard_map.57 = (f32[1024,128]{1,0:T(8,128)S(1)}, f32[8,128]{1,0:T(8,128)}) custom-call(bf16[2,4,2048,128]{3,2,1,0:T(8,128)(2,1)S(1)} %bitcast.14, bf16[512,128]{1,0:T(8,128)(2,1)S(1)} %collective-permute-done.5.refs_1_, bf16[512,128]{1,0:T(8,128)(2,1)S(1)} %collective-permute-done.6.refs_2_, f32[1024,128]{1,0:T(8,128)S(1)} %get-tuple-element.115.refs_3_, ...), custom_call_target="tpu_custom_call" | custom-call | flops 1 | bytes 1 | tf_op jit(solution)/shard_map/pallas_call | solution.py:43
  29.8 2.1 %collective-permute-done.1.refs_1_ = bf16[512,128]{1,0:T(8,128)(2,1)S(1)} collective-permute-done((bf16[512,128]{1,0:T(8,128)(2,1)S(1)}, bf16[512,128]{1,0:T(8,128)(2,1)S(1)}, u32[]{:S(2)}, u32[]{:S(2)}) %collective-permute-start.1) | collective-permute-done | bytes 131104 | tf_op jit(solution)/shard_map/ppermute | solution.py:59
  38.6 4.9 %collective-permute-done.11.refs_1_ = f32[512,128]{1,0:T(8,128)S(1)} collective-permute-done((f32[512,128]{1,0:T(8,128)S(1)}, f32[512,128]{1,0:T(8,128)S(1)}, u32[]{:S(2)}, u32[]{:S(2)}) %collective-permute-start.11) | collective-permute-done | bytes 262176 | tf_op jit(solution)/shard_map/ppermute | solution.py:59
  51.1 2.7 %collective-permute-done.15 = f32[176,128]{1,0:T(8,128)S(1)} collective-permute-done((f32[176,128]{1,0:T(8,128)S(1)}, f32[176,128]{1,0:T(8,128)S(1)}, u32[]{:S(2)}, u32[]{:S(2)}) %collective-permute-start.15) | collective-permute-done | bytes 90144 | tf_op jit(solution)/shard_map/ppermute | solution.py:59
  55.1 8.4 %shard_map.62 = (f32[512,128]{1,0:T(8,128)S(1)}, f32[128,128]{1,0:T(8,128)S(1)}, f32[128,128]{1,0:T(8,128)S(1)}, f32[128,128]{1,0:T(8,128)S(1)}, f32[8,128]{1,0:T(8,128)}) custom-call(f32[104,128]{1,0:T(8,128)S(1)} %slice.17.refs_0_, f32[104,128]{1,0:T(8,128)S(1)} %collective-permute-done.17.refs_1_, ...), custom_call_target="tpu_custom_call" | custom-call | flops 1 | bytes 1 | tf_op jit(solution)/shard_map/pallas_call | solution.py:43
  69.0 2.0 %shard_map.64 = (f32[1024,128]{1,0:T(8,128)S(1)}, f32[8,128]{1,0:T(8,128)S(1)}) custom-call(bf16[3,4,2048,128]{3,2,1,0:T(8,128)(2,1)S(1)} %bitcast.9, bf16[512,128]{1,0:T(8,128)(2,1)S(1)} %get-tuple-element.139.refs_1_, bf16[512,128]{1,0:T(8,128)(2,1)S(1)} %collective-permute-done.20.refs_2_), custom_call_target="tpu_custom_call" | custom-call | flops 1 | bytes 1 | tf_op jit(solution)/shard_map/pallas_call | solution.py:43
  72.3 4.0 %collective-permute-done.19.refs_1_ = bf16[512,128]{1,0:T(8,128)(2,1)S(1)} collective-permute-done((bf16[512,128]{1,0:T(8,128)(2,1)S(1)}, bf16[512,128]{1,0:T(8,128)(2,1)S(1)}, u32[]{:S(2)}, u32[]{:S(2)}) %collective-permute-start.19) | collective-permute-done | bytes 131104 | tf_op jit(solution)/shard_map/ppermute | solution.py:59
  76.4 2.0 %collective-permute-start.18 = (bf16[512,128]{1,0:T(8,128)(2,1)S(1)}, bf16[512,128]{1,0:T(8,128)(2,1)S(1)}, u32[]{:S(2)}, u32[]{:S(2)}) collective-permute-start(bf16[512,128]{1,0:T(8,128)(2,1)S(1)} %get-tuple-element.139.refs_1_), channel_id=1, source_target_pairs={{12,0},{8,4},{4,8},{0,12},{13,1},{9,5},{5,9},{1,13},{14,2},{10,6},... | collective-permute-start | bytes 393224 | tf_op jit(solution)/shard_map/ppermute | solution.py:59
  78.4 1.9 %shard_map.66 = (f32[1024,128]{1,0:T(8,128)S(1)}, f32[8,128]{1,0:T(8,128)}) custom-call(bf16[2,4,2048,128]{3,2,1,0:T(8,128)(2,1)S(1)} %bitcast.15, bf16[512,128]{1,0:T(8,128)(2,1)S(1)} %collective-permute-done.22.refs_1_, bf16[512,128]{1,0:T(8,128)(2,1)S(1)} %collective-permute-done.23.refs_2_, f32[1024,128]{1,0:T(8,128)S(1)} %get-tuple-element.144.refs_3_, ...), custom_call_target="tpu_custom_call" | custom-call | flops 1 | bytes 1 | tf_op jit(solution)/shard_map/pallas_call | solution.py:43
  81.7 2.3 %collective-permute-done.18.refs_1_ = bf16[512,128]{1,0:T(8,128)(2,1)S(1)} collective-permute-done((bf16[512,128]{1,0:T(8,128)(2,1)S(1)}, bf16[512,128]{1,0:T(8,128)(2,1)S(1)}, u32[]{:S(2)}, u32[]{:S(2)}) %collective-permute-start.18) | collective-permute-done | bytes 131104 | tf_op jit(solution)/shard_map/ppermute | solution.py:59
  88.7 2.5 %shard_map.69 = (f32[104,128]{1,0:T(8,128)S(1)}, f32[104,128]{1,0:T(8,128)S(1)}, f32[8,128]{1,0:T(8,128)}) custom-call(f32[512,128]{1,0:T(8,128)S(1)} %get-tuple-element.155.refs_0_, f32[512,128]{1,0:T(8,128)S(1)} %get-tuple-element.156.refs_1_, f32[512,128]{1,0:T(8,128)S(1)} %get-tuple-element.147.refs_2_.refs_4_.refs_0_, ...), custom_call_target="tpu_custom_call" | custom-call | flops 1 | bytes 1 | tf_op jit(solution)/shard_map/pallas_call | solution.py:43
  92.5 3.1 %collective-permute-done.28.refs_1_ = f32[512,128]{1,0:T(8,128)S(1)} collective-permute-done((f32[512,128]{1,0:T(8,128)S(1)}, f32[512,128]{1,0:T(8,128)S(1)}, u32[]{:S(2)}, u32[]{:S(2)}) %collective-permute-start.28) | collective-permute-done | bytes 262176 | tf_op jit(solution)/shard_map/ppermute | solution.py:59
  99.4 2.0 %collective-permute-start.32 = (f32[176,128]{1,0:T(8,128)S(1)}, f32[176,128]{1,0:T(8,128)S(1)}, u32[]{:S(2)}, u32[]{:S(2)}) collective-permute-start(f32[176,128]{1,0:T(8,128)S(1)} %pad_maximum_fusion.1), channel_id=1, source_target_pairs={{6,0},{4,2},{2,4},{0,6},{14,8},{12,10},{10,12},{8,14},{7,1},{5,3},... | collective-permute-start | bytes 270344 | tf_op jit(solution)/shard_map/ppermute | solution.py:59
  102.6 2.1 %collective-permute-done.31 = f32[176,128]{1,0:T(8,128)S(1)} collective-permute-done((f32[176,128]{1,0:T(8,128)S(1)}, f32[176,128]{1,0:T(8,128)S(1)}, u32[]{:S(2)}, u32[]{:S(2)}) %collective-permute-start.31) | collective-permute-done | bytes 90144 | tf_op jit(solution)/shard_map/ppermute | solution.py:59
  107.3 8.4 %shard_map.71 = (f32[512,128]{1,0:T(8,128)S(1)}, f32[128,128]{1,0:T(8,128)S(1)}, f32[128,128]{1,0:T(8,128)S(1)}, f32[128,128]{1,0:T(8,128)S(1)}, f32[8,128]{1,0:T(8,128)}) custom-call(f32[104,128]{1,0:T(8,128)S(1)} %slice.19.refs_0_, f32[104,128]{1,0:T(8,128)S(1)} %collective-permute-done.34.refs_1_, f32[512,128]{1,0:T(8,128)S(1)} %get-tuple-element.137.refs_3_.refs_2_, ...), custom_call_target="tpu_custom_call" | custom-call | flops 1 | bytes 1 | tf_op jit(solution)/shard_map/pallas_call | solution.py:43
  121.0 2.0 %shard_map.73 = (f32[1024,128]{1,0:T(8,128)S(1)}, f32[8,128]{1,0:T(8,128)S(1)}) custom-call(bf16[3,4,2048,128]{3,2,1,0:T(8,128)(2,1)S(1)} %bitcast.10, bf16[512,128]{1,0:T(8,128)(2,1)S(1)} %get-tuple-element.170.refs_1_, bf16[512,128]{1,0:T(8,128)(2,1)S(1)} %collective-permute-done.37.refs_2_), custom_call_target="tpu_custom_call" | custom-call | flops 1 | bytes 1 | tf_op jit(solution)/shard_map/pallas_call | solution.py:43
  123.4 5.3 %collective-permute-done.36.refs_1_ = bf16[512,128]{1,0:T(8,128)(2,1)S(1)} collective-permute-done((bf16[512,128]{1,0:T(8,128)(2,1)S(1)}, bf16[512,128]{1,0:T(8,128)(2,1)S(1)}, u32[]{:S(2)}, u32[]{:S(2)}) %collective-permute-start.36) | collective-permute-done | bytes 131104 | tf_op jit(solution)/shard_map/ppermute | solution.py:59
  128.8 2.1 %collective-permute-start.35 = (bf16[512,128]{1,0:T(8,128)(2,1)S(1)}, bf16[512,128]{1,0:T(8,128)(2,1)S(1)}, u32[]{:S(2)}, u32[]{:S(2)}) collective-permute-start(bf16[512,128]{1,0:T(8,128)(2,1)S(1)} %get-tuple-element.170.refs_1_), channel_id=1, source_target_pairs={{12,0},{8,4},{4,8},{0,12},{13,1},{9,5},{5,9},{1,13},{14,2},{10,6},... | collective-permute-start | bytes 393224 | tf_op jit(solution)/shard_map/ppermute | solution.py:59
  130.9 1.9 %shard_map.75 = (f32[1024,128]{1,0:T(8,128)S(1)}, f32[8,128]{1,0:T(8,128)}) custom-call(bf16[2,4,2048,128]{3,2,1,0:T(8,128)(2,1)S(1)} %bitcast.16, bf16[512,128]{1,0:T(8,128)(2,1)S(1)} %collective-permute-done.39.refs_1_, bf16[512,128]{1,0:T(8,128)(2,1)S(1)} %collective-permute-done.40.refs_2_, f32[1024,128]{1,0:T(8,128)S(1)} %get-tuple-element.176.refs_3_, ...), custom_call_target="tpu_custom_call" | custom-call | flops 1 | bytes 1 | tf_op jit(solution)/shard_map/pallas_call | solution.py:43
  134.2 2.2 %collective-permute-done.35.refs_1_ = bf16[512,128]{1,0:T(8,128)(2,1)S(1)} collective-permute-done((bf16[512,128]{1,0:T(8,128)(2,1)S(1)}, bf16[512,128]{1,0:T(8,128)(2,1)S(1)}, u32[]{:S(2)}, u32[]{:S(2)}) %collective-permute-start.35) | collective-permute-done | bytes 131104 | tf_op jit(solution)/shard_map/ppermute | solution.py:59
  143.1 2.5 %collective-permute-start.46 = (f32[72,128]{1,0:T(8,128)S(1)}, f32[72,128]{1,0:T(8,128)S(1)}, u32[]{:S(2)}, u32[]{:S(2)}) collective-permute-start(f32[72,128]{1,0:T(8,128)S(1)} %add.63), channel_id=1, source_target_pairs={{6,0},{4,2},{2,4},{0,6},{14,8},{12,10},{10,12},{8,14},{7,1},{5,3},... | collective-permute-start | bytes 110600 | tf_op jit(solution)/shard_map/ppermute | solution.py:59
  149.1 2.7 %collective-permute-start.47 = (f32[72,128]{1,0:T(8,128)S(1)}, f32[72,128]{1,0:T(8,128)S(1)}, u32[]{:S(2)}, u32[]{:S(2)}) collective-permute-start(f32[72,128]{1,0:T(8,128)S(1)} %add_add_fusion.2), channel_id=1, source_target_pairs={{8,0},{10,2},{12,4},{14,6},{0,8},{2,10},{4,12},{6,14},{9,1},{11,3}... | collective-permute-start | bytes 110600 | tf_op jit(solution)/shard_map/ppermute | solution.py:59
  151.8 2.2 %collective-permute-done.47 = f32[72,128]{1,0:T(8,128)S(1)} collective-permute-done((f32[72,128]{1,0:T(8,128)S(1)}, f32[72,128]{1,0:T(8,128)S(1)}, u32[]{:S(2)}, u32[]{:S(2)}) %collective-permute-start.47) | collective-permute-done | bytes 36896 | tf_op jit(solution)/shard_map/ppermute | solution.py:59
  154.0 6.4 %shard_map.79 = (f32[128,128]{1,0:T(8,128)S(1)}, f32[8,128]{1,0:T(8,128)}) custom-call(f32[72,128]{1,0:T(8,128)S(1)} %add.67.refs_0_, f32[128,128]{1,0:T(8,128)S(1)} %get-tuple-element.190.refs_1_), custom_call_target="tpu_custom_call" | custom-call | flops 1 | bytes 1 | tf_op jit(solution)/shard_map/pallas_call | solution.py:43
  (114 shorter events, 64.1 us)
Async XLA Ops:
  2.1 9.3 %collective-permute-start = (f32[512,128]{1,0:T(8,128)S(1)}, f32[512,128]{1,0:T(8,128)S(1)}, u32[]{:S(2)}, u32[]{:S(2)}) collective-permute-start(f32[512,128]{1,0:T(8,128)S(1)} %get-tuple-element.100), channel_id=1, source_target_pairs={{2,0},{0,2},{3,1},{1,3},{6,4},{4,6},{7,5},{5,7},{10,8},{8,10},{11,... | collective-permute-start | bytes 786440 | tf_op jit(solution)/shard_map/ppermute | solution.py:59
  11.5 10.5 %collective-permute-start.3 = (bf16[512,128]{1,0:T(8,128)(2,1)S(1)}, bf16[512,128]{1,0:T(8,128)(2,1)S(1)}, u32[]{:S(2)}, u32[]{:S(2)}) collective-permute-start(bf16[512,128]{1,0:T(8,128)(2,1)S(1)} %get-tuple-element.107.refs_1_), channel_id=1, source_target_pairs={{1,0},{0,1},{3,2},{2,3},{5,4},{4,5},{7,6},{6,7},{9,8},{8,9},{11,10... | collective-permute-start | bytes 393224 | tf_op jit(solution)/shard_map/ppermute | solution.py:59
  11.6 12.4 %collective-permute-start.5 = (bf16[512,128]{1,0:T(8,128)(2,1)S(1)}, bf16[512,128]{1,0:T(8,128)(2,1)S(1)}, u32[]{:S(2)}, u32[]{:S(2)}) collective-permute-start(bf16[512,128]{1,0:T(8,128)(2,1)S(1)} %get-tuple-element.107.refs_1_), channel_id=1, source_target_pairs={{4,0},{0,4},{12,8},{8,12},{5,1},{1,5},{13,9},{9,13},{6,2},{2,6},{1... | collective-permute-start | bytes 393224 | tf_op jit(solution)/shard_map/ppermute | solution.py:59
  13.5 13.0 %collective-permute-start.7 = (f32[512,128]{1,0:T(8,128)S(1)}, f32[512,128]{1,0:T(8,128)S(1)}, u32[]{:S(2)}, u32[]{:S(2)}) collective-permute-start(f32[512,128]{1,0:T(8,128)S(1)} %get-tuple-element.118.refs_2_.refs_4_.refs_0_), channel_id=1, source_target_pairs={{2,0},{0,2},{3,1},{1,3},{6,4},{4,6},{7,5},{5,7},{10,8},{8,10},{11,... | collective-permute-start | bytes 786440 | tf_op jit(solution)/shard_map/ppermute | solution.py:59
  15.0 9.1 %collective-permute-start.2 = (bf16[512,128]{1,0:T(8,128)(2,1)S(1)}, bf16[512,128]{1,0:T(8,128)(2,1)S(1)}, u32[]{:S(2)}, u32[]{:S(2)}) collective-permute-start(bf16[512,128]{1,0:T(8,128)(2,1)S(1)} %get-tuple-element.107.refs_1_), channel_id=1, source_target_pairs={{8,0},{12,4},{0,8},{4,12},{9,1},{13,5},{1,9},{5,13},{10,2},{14,6},... | collective-permute-start | bytes 393224 | tf_op jit(solution)/shard_map/ppermute | solution.py:59
  24.1 4.3 %collective-permute-start.4 = (bf16[512,128]{1,0:T(8,128)(2,1)S(1)}, bf16[512,128]{1,0:T(8,128)(2,1)S(1)}, u32[]{:S(2)}, u32[]{:S(2)}) collective-permute-start(bf16[512,128]{1,0:T(8,128)(2,1)S(1)} %collective-permute-done.2.refs_1_), channel_id=1, source_target_pairs={{1,0},{0,1},{3,2},{2,3},{5,4},{4,5},{7,6},{6,7},{9,8},{8,9},{11,10... | collective-permute-start | bytes 393224 | tf_op jit(solution)/shard_map/ppermute | solution.py:59
  24.6 7.4 %collective-permute-start.1 = (bf16[512,128]{1,0:T(8,128)(2,1)S(1)}, bf16[512,128]{1,0:T(8,128)(2,1)S(1)}, u32[]{:S(2)}, u32[]{:S(2)}) collective-permute-start(bf16[512,128]{1,0:T(8,128)(2,1)S(1)} %get-tuple-element.107.refs_1_), channel_id=1, source_target_pairs={{12,0},{8,4},{4,8},{0,12},{13,1},{9,5},{5,9},{1,13},{14,2},{10,6},... | collective-permute-start | bytes 393224 | tf_op jit(solution)/shard_map/ppermute | solution.py:59
  35.2 8.4 %collective-permute-start.11 = (f32[512,128]{1,0:T(8,128)S(1)}, f32[512,128]{1,0:T(8,128)S(1)}, u32[]{:S(2)}, u32[]{:S(2)}) collective-permute-start(f32[512,128]{1,0:T(8,128)S(1)} %get-tuple-element.127.refs_1_), channel_id=1, source_target_pairs={{2,0},{0,2},{3,1},{1,3},{6,4},{4,6},{7,5},{5,7},{10,8},{8,10},{11,... | collective-permute-start | bytes 786440 | tf_op jit(solution)/shard_map/ppermute | solution.py:59
  38.2 6.3 %collective-permute-start.10 = (f32[104,128]{1,0:T(8,128)S(1)}, f32[104,128]{1,0:T(8,128)S(1)}, u32[]{:S(2)}, u32[]{:S(2)}) collective-permute-start(f32[104,128]{1,0:T(8,128)S(1)} %add.51), channel_id=1, source_target_pairs={{8,0},{10,2},{12,4},{14,6},{0,8},{2,10},{4,12},{6,14},{9,1},{11,3}... | collective-permute-start | bytes 159752 | tf_op jit(solution)/shard_map/ppermute | solution.py:59
  45.8 4.8 %collective-permute-start.13 = (f32[176,128]{1,0:T(8,128)S(1)}, f32[176,128]{1,0:T(8,128)S(1)}, u32[]{:S(2)}, u32[]{:S(2)}) collective-permute-start(f32[176,128]{1,0:T(8,128)S(1)} %pad_maximum_fusion), channel_id=1, source_target_pairs={{2,0},{0,2},{6,4},{4,6},{10,8},{8,10},{14,12},{12,14},{3,1},{1,3},... | collective-permute-start | bytes 270344 | tf_op jit(solution)/shard_map/ppermute | solution.py:59
  46.4 4.6 %collective-permute-start.14 = (f32[176,128]{1,0:T(8,128)S(1)}, f32[176,128]{1,0:T(8,128)S(1)}, u32[]{:S(2)}, u32[]{:S(2)}) collective-permute-start(f32[176,128]{1,0:T(8,128)S(1)} %pad_maximum_fusion), channel_id=1, source_target_pairs={{4,0},{6,2},{0,4},{2,6},{12,8},{14,10},{8,12},{10,14},{5,1},{7,3},... | collective-permute-start | bytes 270344 | tf_op jit(solution)/shard_map/ppermute | solution.py:59
  47.8 6.0 %collective-permute-start.15 = (f32[176,128]{1,0:T(8,128)S(1)}, f32[176,128]{1,0:T(8,128)S(1)}, u32[]{:S(2)}, u32[]{:S(2)}) collective-permute-start(f32[176,128]{1,0:T(8,128)S(1)} %pad_maximum_fusion), channel_id=1, source_target_pairs={{6,0},{4,2},{2,4},{0,6},{14,8},{12,10},{10,12},{8,14},{7,1},{5,3},... | collective-permute-start | bytes 270344 | tf_op jit(solution)/shard_map/ppermute | solution.py:59
  53.9 9.6 %collective-permute-start.16 = (f32[72,128]{1,0:T(8,128)S(1)}, f32[72,128]{1,0:T(8,128)S(1)}, u32[]{:S(2)}, u32[]{:S(2)}) collective-permute-start(f32[72,128]{1,0:T(8,128)S(1)} %slice.16.refs_5_), channel_id=1, source_target_pairs={{8,0},{10,2},{12,4},{14,6},{0,8},{2,10},{4,12},{6,14},{9,1},{11,3}... | collective-permute-start | bytes 110600 | tf_op jit(solution)/shard_map/ppermute | solution.py:59
  65.3 7.0 %collective-permute-start.22 = (bf16[512,128]{1,0:T(8,128)(2,1)S(1)}, bf16[512,128]{1,0:T(8,128)(2,1)S(1)}, u32[]{:S(2)}, u32[]{:S(2)}) collective-permute-start(bf16[512,128]{1,0:T(8,128)(2,1)S(1)} %get-tuple-element.139.refs_1_), channel_id=1, source_target_pairs={{4,0},{0,4},{12,8},{8,12},{5,1},{1,5},{13,9},{9,13},{6,2},{2,6},{1... | collective-permute-start | bytes 393224 | tf_op jit(solution)/shard_map/ppermute | solution.py:59
  66.8 11.6 %collective-permute-start.24 = (f32[512,128]{1,0:T(8,128)S(1)}, f32[512,128]{1,0:T(8,128)S(1)}, u32[]{:S(2)}, u32[]{:S(2)}) collective-permute-start(f32[512,128]{1,0:T(8,128)S(1)} %get-tuple-element.147.refs_2_.refs_4_.refs_0_), channel_id=1, source_target_pairs={{2,0},{0,2},{3,1},{1,3},{6,4},{4,6},{7,5},{5,7},{10,8},{8,10},{11,... | collective-permute-start | bytes 786440 | tf_op jit(solution)/shard_map/ppermute | solution.py:59
  67.4 8.9 %collective-permute-start.19 = (bf16[512,128]{1,0:T(8,128)(2,1)S(1)}, bf16[512,128]{1,0:T(8,128)(2,1)S(1)}, u32[]{:S(2)}, u32[]{:S(2)}) collective-permute-start(bf16[512,128]{1,0:T(8,128)(2,1)S(1)} %get-tuple-element.139.refs_1_), channel_id=1, source_target_pairs={{8,0},{12,4},{0,8},{4,12},{9,1},{13,5},{1,9},{5,13},{10,2},{14,6},... | collective-permute-start | bytes 393224 | tf_op jit(solution)/shard_map/ppermute | solution.py:59
  72.3 6.1 %collective-permute-start.23 = (bf16[512,128]{1,0:T(8,128)(2,1)S(1)}, bf16[512,128]{1,0:T(8,128)(2,1)S(1)}, u32[]{:S(2)}, u32[]{:S(2)}) collective-permute-start(bf16[512,128]{1,0:T(8,128)(2,1)S(1)} %collective-permute-done.22.refs_1_), channel_id=1, source_target_pairs={{1,0},{0,1},{3,2},{2,3},{5,4},{4,5},{7,6},{6,7},{9,8},{8,9},{11,10... | collective-permute-start | bytes 393224 | tf_op jit(solution)/shard_map/ppermute | solution.py:59
  76.4 7.7 %collective-permute-start.18 = (bf16[512,128]{1,0:T(8,128)(2,1)S(1)}, bf16[512,128]{1,0:T(8,128)(2,1)S(1)}, u32[]{:S(2)}, u32[]{:S(2)}) collective-permute-start(bf16[512,128]{1,0:T(8,128)(2,1)S(1)} %get-tuple-element.139.refs_1_), channel_id=1, source_target_pairs={{12,0},{8,4},{4,8},{0,12},{13,1},{9,5},{5,9},{1,13},{14,2},{10,6},... | collective-permute-start | bytes 393224 | tf_op jit(solution)/shard_map/ppermute | solution.py:59
  87.3 8.4 %collective-permute-start.28 = (f32[512,128]{1,0:T(8,128)S(1)}, f32[512,128]{1,0:T(8,128)S(1)}, u32[]{:S(2)}, u32[]{:S(2)}) collective-permute-start(f32[512,128]{1,0:T(8,128)S(1)} %get-tuple-element.156.refs_1_), channel_id=1, source_target_pairs={{2,0},{0,2},{3,1},{1,3},{6,4},{4,6},{7,5},{5,7},{10,8},{8,10},{11,... | collective-permute-start | bytes 786440 | tf_op jit(solution)/shard_map/ppermute | solution.py:59
  92.4 5.1 %collective-permute-start.27 = (f32[104,128]{1,0:T(8,128)S(1)}, f32[104,128]{1,0:T(8,128)S(1)}, u32[]{:S(2)}, u32[]{:S(2)}) collective-permute-start(f32[104,128]{1,0:T(8,128)S(1)} %add.57), channel_id=1, source_target_pairs={{8,0},{10,2},{12,4},{14,6},{0,8},{2,10},{4,12},{6,14},{9,1},{11,3}... | collective-permute-start | bytes 159752 | tf_op jit(solution)/shard_map/ppermute | solution.py:59
  97.9 4.8 %collective-permute-start.30 = (f32[176,128]{1,0:T(8,128)S(1)}, f32[176,128]{1,0:T(8,128)S(1)}, u32[]{:S(2)}, u32[]{:S(2)}) collective-permute-start(f32[176,128]{1,0:T(8,128)S(1)} %pad_maximum_fusion.1), channel_id=1, source_target_pairs={{2,0},{0,2},{6,4},{4,6},{10,8},{8,10},{14,12},{12,14},{3,1},{1,3},... | collective-permute-start | bytes 270344 | tf_op jit(solution)/shard_map/ppermute | solution.py:59
  99.4 5.4 %collective-permute-start.31 = (f32[176,128]{1,0:T(8,128)S(1)}, f32[176,128]{1,0:T(8,128)S(1)}, u32[]{:S(2)}, u32[]{:S(2)}) collective-permute-start(f32[176,128]{1,0:T(8,128)S(1)} %pad_maximum_fusion.1), channel_id=1, source_target_pairs={{4,0},{6,2},{0,4},{2,6},{12,8},{14,10},{8,12},{10,14},{5,1},{7,3},... | collective-permute-start | bytes 270344 | tf_op jit(solution)/shard_map/ppermute | solution.py:59
  99.4 6.4 %collective-permute-start.32 = (f32[176,128]{1,0:T(8,128)S(1)}, f32[176,128]{1,0:T(8,128)S(1)}, u32[]{:S(2)}, u32[]{:S(2)}) collective-permute-start(f32[176,128]{1,0:T(8,128)S(1)} %pad_maximum_fusion.1), channel_id=1, source_target_pairs={{6,0},{4,2},{2,4},{0,6},{14,8},{12,10},{10,12},{8,14},{7,1},{5,3},... | collective-permute-start | bytes 270344 | tf_op jit(solution)/shard_map/ppermute | solution.py:59
  105.9 9.8 %collective-permute-start.33 = (f32[72,128]{1,0:T(8,128)S(1)}, f32[72,128]{1,0:T(8,128)S(1)}, u32[]{:S(2)}, u32[]{:S(2)}) collective-permute-start(f32[72,128]{1,0:T(8,128)S(1)} %slice.18.refs_5_), channel_id=1, source_target_pairs={{8,0},{10,2},{12,4},{14,6},{0,8},{2,10},{4,12},{6,14},{9,1},{11,3}... | collective-permute-start | bytes 110600 | tf_op jit(solution)/shard_map/ppermute | solution.py:59
  117.5 5.9 %collective-permute-start.39 = (bf16[512,128]{1,0:T(8,128)(2,1)S(1)}, bf16[512,128]{1,0:T(8,128)(2,1)S(1)}, u32[]{:S(2)}, u32[]{:S(2)}) collective-permute-start(bf16[512,128]{1,0:T(8,128)(2,1)S(1)} %get-tuple-element.170.refs_1_), channel_id=1, source_target_pairs={{4,0},{0,4},{12,8},{8,12},{5,1},{1,5},{13,9},{9,13},{6,2},{2,6},{1... | collective-permute-start | bytes 393224 | tf_op jit(solution)/shard_map/ppermute | solution.py:59
  118.7 12.1 %collective-permute-start.41 = (f32[512,128]{1,0:T(8,128)S(1)}, f32[512,128]{1,0:T(8,128)S(1)}, u32[]{:S(2)}, u32[]{:S(2)}) collective-permute-start(f32[512,128]{1,0:T(8,128)S(1)} %get-tuple-element.179.refs_2_), channel_id=1, source_target_pairs={{2,0},{0,2},{3,1},{1,3},{6,4},{4,6},{7,5},{5,7},{10,8},{8,10},{11,... | collective-permute-start | bytes 786440 | tf_op jit(solution)/shard_map/ppermute | solution.py:59
  119.9 8.9 %collective-permute-start.36 = (bf16[512,128]{1,0:T(8,128)(2,1)S(1)}, bf16[512,128]{1,0:T(8,128)(2,1)S(1)}, u32[]{:S(2)}, u32[]{:S(2)}) collective-permute-start(bf16[512,128]{1,0:T(8,128)(2,1)S(1)} %get-tuple-element.170.refs_1_), channel_id=1, source_target_pairs={{8,0},{12,4},{0,8},{4,12},{9,1},{13,5},{1,9},{5,13},{10,2},{14,6},... | collective-permute-start | bytes 393224 | tf_op jit(solution)/shard_map/ppermute | solution.py:59
  123.4 7.5 %collective-permute-start.40 = (bf16[512,128]{1,0:T(8,128)(2,1)S(1)}, bf16[512,128]{1,0:T(8,128)(2,1)S(1)}, u32[]{:S(2)}, u32[]{:S(2)}) collective-permute-start(bf16[512,128]{1,0:T(8,128)(2,1)S(1)} %collective-permute-done.39.refs_1_), channel_id=1, source_target_pairs={{1,0},{0,1},{3,2},{2,3},{5,4},{4,5},{7,6},{6,7},{9,8},{8,9},{11,10... | collective-permute-start | bytes 393224 | tf_op jit(solution)/shard_map/ppermute | solution.py:59
  128.8 7.7 %collective-permute-start.35 = (bf16[512,128]{1,0:T(8,128)(2,1)S(1)}, bf16[512,128]{1,0:T(8,128)(2,1)S(1)}, u32[]{:S(2)}, u32[]{:S(2)}) collective-permute-start(bf16[512,128]{1,0:T(8,128)(2,1)S(1)} %get-tuple-element.170.refs_1_), channel_id=1, source_target_pairs={{12,0},{8,4},{4,8},{0,12},{13,1},{9,5},{5,9},{1,13},{14,2},{10,6},... | collective-permute-start | bytes 393224 | tf_op jit(solution)/shard_map/ppermute | solution.py:59
  143.1 4.9 %collective-permute-start.46 = (f32[72,128]{1,0:T(8,128)S(1)}, f32[72,128]{1,0:T(8,128)S(1)}, u32[]{:S(2)}, u32[]{:S(2)}) collective-permute-start(f32[72,128]{1,0:T(8,128)S(1)} %add.63), channel_id=1, source_target_pairs={{6,0},{4,2},{2,4},{0,6},{14,8},{12,10},{10,12},{8,14},{7,1},{5,3},... | collective-permute-start | bytes 110600 | tf_op jit(solution)/shard_map/ppermute | solution.py:59
  148.0 12.4 %collective-permute-start.48 = (f32[512,128]{1,0:T(8,128)S(1)}, f32[512,128]{1,0:T(8,128)S(1)}, u32[]{:S(2)}, u32[]{:S(2)}) collective-permute-start(f32[512,128]{1,0:T(8,128)S(1)} %get-tuple-element.193.refs_1_), channel_id=1, source_target_pairs={{2,0},{0,2},{3,1},{1,3},{6,4},{4,6},{7,5},{5,7},{10,8},{8,10},{11,... | collective-permute-start | bytes 786440 | tf_op jit(solution)/shard_map/ppermute | solution.py:59
  149.1 4.9 %collective-permute-start.47 = (f32[72,128]{1,0:T(8,128)S(1)}, f32[72,128]{1,0:T(8,128)S(1)}, u32[]{:S(2)}, u32[]{:S(2)}) collective-permute-start(f32[72,128]{1,0:T(8,128)S(1)} %add_add_fusion.2), channel_id=1, source_target_pairs={{8,0},{10,2},{12,4},{14,6},{0,8},{2,10},{4,12},{6,14},{9,1},{11,3}... | collective-permute-start | bytes 110600 | tf_op jit(solution)/shard_map/ppermute | solution.py:59
  (17 other events, 38.9 us)
where the time goes:
time: 162 us
  Pallas kernels  68 us (42%)
  waiting for transfers between devices  49.7 us (31%)
  starting transfers between devices  42.9 us (26%)
    pallas_call x31, Pallas kernels, call(): pl.pallas_call(ordered, out_shape=list(outs) + [shape(SUB)], in_specs=[HB...  68 us
    ppermute x49, waiting for transfers between devices, permute(): return lax.ppermute(value, axis, pairs)  49.7 us
    ppermute x49, starting transfers between devices, permute(): return lax.ppermute(value, axis, pairs)  42.9 us
  transfers between devices with their start and end apart: 49, of which 29 were waited for; matrix products, arithmetic and copies ran while one was open for 0% of the time, Pallas kernels for 34%

commit v1 on v0

--- a/solution.py
+++ b/solution.py
@@ -201,27 +201,44 @@
 
 
 def link_products(packed, pieces, acc, n, last, after=()):
-    count, tiles, rows = packed.shape[:3]
-    packed = packed.reshape(count, tiles, 2 * rows, LANES)
-    packed = pltpu.with_memory_space_constraint(packed, pltpu.VMEM)
+    tiles, rows = packed[0].shape[1:3]
+    counts = [value.shape[0] for value in packed]
+    many = len(packed)
+    packed = [
+        pltpu.with_memory_space_constraint(
+            value.reshape(value.shape[0], tiles, 2 * rows, LANES), pltpu.VMEM
+        )
+        for value in packed
+    ]
     strip = tiles * LANES
     block = min(512, 2 * rows)
 
     def body(*refs):
-        k_ref, own_ref, other_ref = refs[:3]
-        acc_ref = refs[3] if acc is not None else None
-        outs = refs[3 + (acc is not None) : -3]
+        k_refs, piece_refs = refs[:many], refs[many : 3 * many]
+        acc_ref = refs[3 * many] if acc is not None else None
+        outs = refs[3 * many + (acc is not None) : -3]
         weights, even_acc, odd_acc = refs[-3:]
         half = lax.axis_index("coef")
-        weights[:, pl.ds(pl.multiple_of(half * LANES, LANES), LANES)] = own_ref[...]
-        weights[:, pl.ds(pl.multiple_of((1 - half) * LANES, LANES), LANES)] = other_ref[...]
+        own = pl.ds(pl.multiple_of(half * LANES, LANES), LANES)
+        other = pl.ds(pl.multiple_of((1 - half) * LANES, LANES), LANES)
+        at = 0
+        for g in range(many):
+            for _ in range(counts[g]):
+                weights[at : at + strip, own] = piece_refs[2 * g][...]
+                weights[at : at + strip, other] = piece_refs[2 * g + 1][...]
+                at += strip
         for start in range(0, 2 * rows, block):
             here = slice(start, start + block)
             left = jnp.concatenate(
-                [k_ref[i, t, here, :] for i in range(count) for t in range(tiles)], axis=1
+                [
+                    k_refs[g][i, t, here, :]
+                    for g in range(many)
+                    for i in range(counts[g])
+                    for t in range(tiles)
+                ],
+                axis=1,
             )
-            right = jnp.concatenate([weights[...]] * count, axis=0)
-            product = jnp.dot(left, right, preferred_element_type=F32)
+            product = jnp.dot(left, weights[...], preferred_element_type=F32)
             even_acc[here, :] = product[:, :LANES]
             odd_acc[here, :] = product[:, LANES:]
         me = lax.axis_index("rhs")
@@ -235,13 +252,14 @@
                 total = total + acc_ref[pl.ds(start, size), :]
             outs[s][...] = total
 
-    args = [packed, *pieces] + ([acc] if acc is not None else [])
+    args = [*packed, *(value for pair in pieces for value in pair)]
+    args += [acc] if acc is not None else []
     *result, token = call(
         body,
         [shape(rows // n)] * n if last else [shape(rows)],
         *args,
         scratch=[
-            pltpu.VMEM((strip, 2 * LANES), BF16),
+            pltpu.VMEM((sum(counts) * strip, 2 * LANES), BF16),
             pltpu.VMEM((2 * rows, LANES), F32),
             pltpu.VMEM((2 * rows, LANES), F32),
         ],
@@ -279,22 +297,17 @@
     last = len(groups) - 1
     arrived = [low] + [bring(low) for bring, _, _ in groups[:0:-1]][::-1]
     directions = [direction] + [swapped(direction, "rhs", s, n) for s in range(1, n)]
-    acc, after, tokens = None, (), []
-    for place in range(last + 1):
-        piece = arrived[place]
-        if place:
-            piece, held = lax.optimization_barrier((piece, tokens[0 if place < last else -1]))
-            after = (*after, *held)
-        pair = [piece, swapped(piece, "coef", 1, 2)]
-        if place == 1:
-            after = (*after, *directions[1:])
-        acc, token = link_products(packed[place], pair, acc, n, place == last, after)
-        after = ()
-        if place == 0:
-            after = (between(token),)
-            tokens.append((token, *after))
-        else:
-            tokens.append((token,))
+    pairs = [[low, swapped(low, "coef", 1, 2)]]
+    acc, token = link_products(packed[:1], pairs, None, n, last == 0)
+    after = (token, between(token))
+    for piece in arrived[1:]:
+        piece, _ = lax.optimization_barrier((piece, after))
+        pairs.append([piece, swapped(piece, "coef", 1, 2)])
+    after = (*after, *directions[1:])
+    if last > 1:
+        acc, _ = link_products(packed[1:last], pairs[1:last], acc, n, False, after)
+    if last:
+        acc, _ = link_products(packed[last:], pairs[last:], acc, n, True, after)
     return acc, directions
 
 
@@ -404,8 +417,8 @@
 
 def inverted(matrices, lane):
     strips = matrices[0].shape[0] // SUB
-    many = len(matrices)
     place = lax.broadcasted_iota(jnp.int32, (SUB, LANES), 0)
+    held = [[value[SUB * k : SUB * (k + 1)] for k in range(strips)] for value in matrices]
 
     def lanes_of(value, at):
         return jnp.broadcast_to(value[:, at : at + 1], (SUB, LANES))
@@ -413,56 +426,43 @@
     def rows_of(value):
         return [jnp.broadcast_to(value[i : i + 1], (SUB, LANES)) for i in range(SUB)]
 
-    def updated(row, rows):
-        factors = [lanes_of(row, i) for i in range(SUB)]
-        for factor, other in zip(factors, rows):
-            row = row - factor * other
-        return row
-
-    def step(_, carry):
-        held = [list(carry[m * strips : (m + 1) * strips]) for m in range(many)]
-        rows = [rows_of(value) for value in carry[many * strips :]]
-        now = []
-        for a, last in zip(held, rows):
-            a[1] = updated(a[1], last)
-            now.append([a[1], *(lanes_of(a[1], SUB + i) for i in range(SUB))])
+    def update(k, j, spread):
+        for a, rows in zip(held, spread):
+            row = a[k]
+            for i in range(SUB):
+                row = row - lanes_of(a[k], lane + SUB * j + i) * rows[i]
+            a[k] = row
+
+    for j in range(strips):
+        if j:
+            spread = [rows_of(a[j - 1]) for a in held]
+            update(j, j - 1, spread)
+        waiting = [k for k in range(strips) if j and k not in (j, j - 1)]
+        now = [
+            [a[j], *(lanes_of(a[j], lane + SUB * j + i) for i in range(SUB))] for a in held
+        ]
         for i in range(SUB):
             here = place == i
             for index, values in enumerate(now):
                 column = values[1 + i]
                 inverse = 1.0 / column[i : i + 1]
 
-                def pivot(value):
+                def step(value):
                     row = value[i : i + 1] * inverse
                     return jnp.where(here, row, value - column * row)
 
                 now[index] = [
-                    pivot(value) if at < 1 or at > 1 + i else value
+                    step(value) if at < 1 or at > 1 + i else value
                     for at, value in enumerate(values)
                 ]
-            if 2 + i < strips:
-                for a, last in zip(held, rows):
-                    a[2 + i] = updated(a[2 + i], last)
-        turned = []
+            for k in waiting[i : i + 1]:
+                update(k, j - 1, spread)
         for a, values in zip(held, now):
-            a[1] = values[0]
-            turned.append([pltpu.roll(row, LANES - SUB, 1) for row in a[1:] + a[:1]])
-        return tuple([row for a in turned for row in a] + [a[0] for a in turned])
-
-    start = []
-    for value in matrices:
-        value = pltpu.roll(value, (SUB - lane) % LANES, 1)
-        a = [value[SUB * k : SUB * (k + 1)] for k in range(strips)]
-        start += a[-1:] + a[:-1]
-    start += [jnp.zeros((SUB, LANES), F32)] * many
-    carry = lax.fori_loop(0, strips, step, tuple(start))
-    found = []
-    for m in range(many):
-        a = list(carry[m * strips : (m + 1) * strips])
-        rows = rows_of(carry[many * strips + m])
-        a = [updated(row, rows) for row in a[1:]] + a[:1]
-        found.append(pltpu.roll(jnp.concatenate(a, axis=0), LANES - SUB, 1))
-    return found
+            a[j] = values[0]
+    spread = [rows_of(a[-1]) for a in held]
+    for k in range(strips - 1):
+        update(k, strips - 1, spread)
+    return [jnp.concatenate(a, axis=0) for a in held]
 
 
 def eliminated(*systems):
@@ -479,7 +479,8 @@
     )
     tops, lasts = [], []
     for (matrix, sides), value in zip(systems, first):
-        top = mm(value[:, :half], jnp.concatenate([matrix[:half], sides[:half]], axis=1))
+        value = pltpu.roll(value, half, 1)[:, :half]
+        top = mm(value, jnp.concatenate([matrix[:half], sides[:half]], axis=1))
         low = jnp.concatenate([matrix[half:], sides[half:]], axis=1)
         tops.append(top)
         lasts.append(low - mm(matrix[half:, :half], top))
@@ -496,6 +497,63 @@
     return found
 
 
+def eliminated_alone(matrix, sides):
+    n = matrix.shape[0]
+    strips = n // SUB
+    place = lax.broadcasted_iota(jnp.int32, (SUB, LANES), 0)
+
+    def cut(value):
+        return [value[SUB * k : SUB * (k + 1)] for k in range(strips)]
+
+    def lanes_of(value, lane):
+        return jnp.broadcast_to(value[:, lane : lane + 1], (SUB, LANES))
+
+    held = [(cut(matrix), cut(sides))]
+
+    def rows_of(value):
+        return [jnp.broadcast_to(value[i : i + 1], (SUB, LANES)) for i in range(SUB)]
+
+    def update(k, j, spread):
+        for (a, b), (rows_a, rows_b) in zip(held, spread):
+            row_a, row_b = a[k], b[k]
+            for i in range(SUB):
+                factor = lanes_of(a[k], SUB * j + i)
+                row_a = row_a - factor * rows_a[i]
+                row_b = row_b - factor * rows_b[i]
+            a[k], b[k] = row_a, row_b
+
+    for j in range(strips):
+        if j:
+            spread = [(rows_of(a[j - 1]), rows_of(b[j - 1])) for a, b in held]
+            update(j, j - 1, spread)
+        waiting = [k for k in range(strips) if j and k not in (j, j - 1)]
+        now = [
+            [a[j], b[j], *(lanes_of(a[j], SUB * j + i) for i in range(SUB))] for a, b in held
+        ]
+        for i in range(SUB):
+            here = place == i
+            for index, values in enumerate(now):
+                column = values[2 + i]
+                inverse = 1.0 / column[i : i + 1]
+
+                def step(value):
+                    row = value[i : i + 1] * inverse
+                    return jnp.where(here, row, value - column * row)
+
+                now[index] = [
+                    step(value) if place_of < 2 or place_of > 2 + i else value
+                    for place_of, value in enumerate(values)
+                ]
+            for k in waiting[2 * i : 2 * i + 2]:
+                update(k, j - 1, spread)
+        for (a, b), values in zip(held, now):
+            a[j], b[j] = values[:2]
+    spread = [(rows_of(a[-1]), rows_of(b[-1])) for a, b in held]
+    for k in range(strips - 1):
+        update(k, strips - 1, spread)
+    return jnp.concatenate(held[0][1], axis=0)
+
+
 def identity():
     return (
         lax.broadcasted_iota(jnp.int32, (LANES, LANES), 0)
@@ -513,28 +571,23 @@
     return call(body, [shape(direction.shape[0])], *fields, after=[token])
 
 
-def last_alpha(small, gram):
-    def body(small, g, out):
-        out[...] = eliminated((unpacked_symmetric(small[...]), g[...]))[0]
-
-    return call(body, [shape(LANES)], small, gram)[0]
-
-
-def finish(alpha, residual, direction, solution, image):
+def finish(small, gram, residual, direction, solution, image):
     strip = residual.shape[0]
 
-    def body(a, r, d, s, *refs):
+    def body(small, g, r, d, s, *refs):
         *images, out, new_r = refs
+        alpha = eliminated_alone(unpacked_symmetric(small[...]), g[...])
         image = images[0][...]
         for ref in images[1:]:
             image = image + ref[...]
-        out[...] = s[...] + mm(d[...], a[...])
-        new_r[...] = r[...] - mm(image, a[...])
+        out[...] = s[...] + mm(d[...], alpha)
+        new_r[...] = r[...] - mm(image, alpha)
 
     return call(
         body,
         [shape(strip), shape(strip)],
-        alpha,
+        small,
+        gram,
         residual,
         direction,
         solution,
@@ -640,8 +693,9 @@
             parts[1:], _ = lax.optimization_barrier((parts[1:], near))
         image_parts = [parts[0]] + [swapped(parts[s], "rhs", s, n) for s in range(1, n)]
         if final:
-            alpha = last_alpha(small, gram)
-            solution, residual = finish(alpha, residual, direction, solution, image_parts)
+            solution, residual = finish(
+                small, gram, residual, direction, solution, image_parts
+            )
             break
         image, square = square_gram(image_parts)
         linear, square = reduce_both(*linear, square)

time: 162 us -> 151 us (0.932)
  waiting for transfers between devices: 49.7 us -> 38.4 us
  starting transfers between devices: 42.9 us -> 50.5 us
  Pallas kernels: 68 us -> 60.5 us
    ppermute x49, waiting for transfers between devices: 49.7 us -> 38.4 us  [permute(): return lax.ppermute(value, axis, pairs)]
    ppermute x49, starting transfers between devices: 42.9 us -> 50.5 us  [permute(): return lax.ppermute(value, axis, pairs)]
    pallas_call x31 -> x27, Pallas kernels: 68 us -> 60.5 us  [call(): pl.pallas_call(ordered, out_shape=list(outs) + [shape(SUB)], in_specs=[HB...]
  transfers between devices with their start and end apart: 49 -> 49, of which waited for: 29 -> 25; matrix products, arithmetic and copies ran while one was open for 0% -> 0% of each run, Pallas kernels for 34% -> 29%
where the time goes in v1:
time: 151 us
  Pallas kernels  60.5 us (40%)
  starting transfers between devices  50.5 us (33%)
  waiting for transfers between devices  38.4 us (25%)
    pallas_call x27, Pallas kernels, call(): pl.pallas_call(ordered, out_shape=list(outs) + [shape(SUB)], in_specs=[HB...  60.5 us
    ppermute x49, starting transfers between devices, permute(): return lax.ppermute(value, axis, pairs)  50.5 us
    ppermute x49, waiting for transfers between devices, permute(): return lax.ppermute(value, axis, pairs)  38.4 us
  transfers between devices with their start and end apart: 49, of which 25 were waited for; matrix products, arithmetic and copies ran while one was open for 0% of the time, Pallas kernels for 29%

profile of v1, /device:TPU:0, one launch (start us, length us, event | category | flops | bytes accessed | tf_op | source)
XLA Modules:
  0.0 150.6 jit_solution(2537355990939049732)
XLA Ops:
  2.1 3.0 %collective-permute-start = (f32[512,128]{1,0:T(8,128)S(1)}, f32[512,128]{1,0:T(8,128)S(1)}, u32[]{:S(2)}, u32[]{:S(2)}) collective-permute-start(f32[512,128]{1,0:T(8,128)S(1)} %get-tuple-element.78), channel_id=1, source_target_pairs={{2,0},{0,2},{3,1},{1,3},{6,4},{4,6},{7,5},{5,7},{10,8},{8,10},{11,... | collective-permute-start | bytes 786440 | tf_op jit(solution)/shard_map/ppermute | solution.py:59
  5.1 2.9 %shard_map.51 = (bf16[3,4,1024,2,128]{4,3,2,1,0:T(2,128)(2,1)S(1)}, f32[8,128]{1,0:T(8,128)S(1)}) custom-call(bf16[9,1024,2,512]{3,2,1,0:T(2,128)(2,1)} %bitcast.20, f32[8,128]{1,0:T(8,128)S(1)} %get-tuple-element.79.refs_1_), custom_call_target="tpu_custom_call" | custom-call | flops 1 | bytes 1 | tf_op jit(solution)/shard_map/pallas_call | solution.py:43
  8.0 2.2 %shard_map.52 = (bf16[2,4,1024,2,128]{4,3,2,1,0:T(2,128)(2,1)S(1)}, f32[8,128]{1,0:T(8,128)S(1)}) custom-call(bf16[9,1024,2,512]{3,2,1,0:T(2,128)(2,1)} %bitcast.21, f32[8,128]{1,0:T(8,128)S(1)} %get-tuple-element.80.refs_1_), custom_call_target="tpu_custom_call" | custom-call | flops 1 | bytes 1 | tf_op jit(solution)/shard_map/pallas_call | solution.py:43
  11.6 2.9 %collective-permute-start.6 = (bf16[512,128]{1,0:T(8,128)(2,1)S(1)}, bf16[512,128]{1,0:T(8,128)(2,1)S(1)}, u32[]{:S(2)}, u32[]{:S(2)}) collective-permute-start(bf16[512,128]{1,0:T(8,128)(2,1)S(1)} %get-tuple-element.85.refs_1_), channel_id=1, source_target_pairs={{8,0},{12,4},{0,8},{4,12},{9,1},{13,5},{1,9},{5,13},{10,2},{14,6},... | collective-permute-start | bytes 393224 | tf_op jit(solution)/shard_map/ppermute | solution.py:59
  17.8 2.2 %shard_map.54 = (bf16[2,4,1024,2,128]{4,3,2,1,0:T(2,128)(2,1)S(1)}, f32[8,128]{1,0:T(8,128)S(1)}) custom-call(bf16[9,1024,2,512]{3,2,1,0:T(2,128)(2,1)} %bitcast.22, f32[8,128]{1,0:T(8,128)S(1)} %get-tuple-element.82.refs_1_), custom_call_target="tpu_custom_call" | custom-call | flops 1 | bytes 1 | tf_op jit(solution)/shard_map/pallas_call | solution.py:43
  20.0 2.2 %shard_map.55 = (bf16[2,4,1024,2,128]{4,3,2,1,0:T(2,128)(2,1)S(1)}, f32[8,128]{1,0:T(8,128)S(1)}) custom-call(bf16[9,1024,2,512]{3,2,1,0:T(2,128)(2,1)} %bitcast.23, f32[8,128]{1,0:T(8,128)S(1)} %get-tuple-element.83.refs_1_), custom_call_target="tpu_custom_call" | custom-call | flops 1 | bytes 1 | tf_op jit(solution)/shard_map/pallas_call | solution.py:43
  22.3 2.0 %shard_map.56 = (f32[1024,128]{1,0:T(8,128)S(1)}, f32[8,128]{1,0:T(8,128)S(1)}) custom-call(bf16[3,4,2048,128]{3,2,1,0:T(8,128)(2,1)S(1)} %bitcast.8, bf16[512,128]{1,0:T(8,128)(2,1)S(1)} %get-tuple-element.85.refs_1_, bf16[512,128]{1,0:T(8,128)(2,1)S(1)} %collective-permute-done.2.refs_2_), custom_call_target="tpu_custom_call" | custom-call | flops 1 | bytes 1 | tf_op jit(solution)/shard_map/pallas_call | solution.py:43
  25.9 3.0 %shard_map.57 = (f32[1024,128]{1,0:T(8,128)S(1)}, f32[8,128]{1,0:T(8,128)}) custom-call(bf16[2,4,2048,128]{3,2,1,0:T(8,128)(2,1)S(1)} %bitcast.14, bf16[2,4,2048,128]{3,2,1,0:T(8,128)(2,1)S(1)} %bitcast.17, bf16[512,128]{1,0:T(8,128)(2,1)S(1)} %collective-permute-done.4.refs_2_, bf16[512,128]{1,0:T(8,128)(2,1)S(1)} %collective-permute-done.5.refs_3_, ...), custom_call_target="tpu_custom_call" | custom-call | flops 1 | bytes 1 | tf_op jit(solution)/shard_map/pallas_call | solution.py:43
  28.9 1.9 %shard_map.58 = (f32[512,128]{1,0:T(8,128)S(1)}, f32[512,128]{1,0:T(8,128)S(1)}, f32[8,128]{1,0:T(8,128)}) custom-call(bf16[2,4,2048,128]{3,2,1,0:T(8,128)(2,1)S(1)} %bitcast.11, bf16[512,128]{1,0:T(8,128)(2,1)S(1)} %collective-permute-done.1.refs_1_, bf16[512,128]{1,0:T(8,128)(2,1)S(1)} %collective-permute-done.3.refs_2_, ...), custom_call_target="tpu_custom_call" | custom-call | flops 1 | bytes 1 | tf_op jit(solution)/shard_map/pallas_call | solution.py:43
  34.4 4.4 %collective-permute-start.10 = (f32[104,128]{1,0:T(8,128)S(1)}, f32[104,128]{1,0:T(8,128)S(1)}, u32[]{:S(2)}, u32[]{:S(2)}) collective-permute-start(f32[104,128]{1,0:T(8,128)S(1)} %add.51), channel_id=1, source_target_pairs={{8,0},{10,2},{12,4},{14,6},{0,8},{2,10},{4,12},{6,14},{9,1},{11,3}... | collective-permute-start | bytes 159752 | tf_op jit(solution)/shard_map/ppermute | solution.py:59
  42.9 2.3 %collective-permute-start.14 = (f32[176,128]{1,0:T(8,128)S(1)}, f32[176,128]{1,0:T(8,128)S(1)}, u32[]{:S(2)}, u32[]{:S(2)}) collective-permute-start(f32[176,128]{1,0:T(8,128)S(1)} %pad_maximum_fusion), channel_id=1, source_target_pairs={{4,0},{6,2},{0,4},{2,6},{12,8},{14,10},{8,12},{10,14},{5,1},{7,3},... | collective-permute-start | bytes 270344 | tf_op jit(solution)/shard_map/ppermute | solution.py:59
  48.5 2.2 %collective-permute-done.15 = f32[176,128]{1,0:T(8,128)S(1)} collective-permute-done((f32[176,128]{1,0:T(8,128)S(1)}, f32[176,128]{1,0:T(8,128)S(1)}, u32[]{:S(2)}, u32[]{:S(2)}) %collective-permute-start.15) | collective-permute-done | bytes 90144 | tf_op jit(solution)/shard_map/ppermute | solution.py:59
  50.8 2.8 %collective-permute-start.16 = (f32[72,128]{1,0:T(8,128)S(1)}, f32[72,128]{1,0:T(8,128)S(1)}, u32[]{:S(2)}, u32[]{:S(2)}) collective-permute-start(f32[72,128]{1,0:T(8,128)S(1)} %slice.16.refs_5_), channel_id=1, source_target_pairs={{8,0},{10,2},{12,4},{14,6},{0,8},{2,10},{4,12},{6,14},{9,1},{11,3}... | collective-permute-start | bytes 110600 | tf_op jit(solution)/shard_map/ppermute | solution.py:59
  53.6 5.8 %shard_map.61 = (f32[512,128]{1,0:T(8,128)S(1)}, f32[128,128]{1,0:T(8,128)S(1)}, f32[128,128]{1,0:T(8,128)S(1)}, f32[128,128]{1,0:T(8,128)S(1)}, f32[8,128]{1,0:T(8,128)}) custom-call(f32[104,128]{1,0:T(8,128)S(1)} %slice.17.refs_0_, f32[104,128]{1,0:T(8,128)S(1)} %collective-permute-done.17.refs_1_, ...), custom_call_target="tpu_custom_call" | custom-call | flops 1 | bytes 1 | tf_op jit(solution)/shard_map/pallas_call | solution.py:43
  63.8 2.1 %collective-permute-start.18 = (bf16[512,128]{1,0:T(8,128)(2,1)S(1)}, bf16[512,128]{1,0:T(8,128)(2,1)S(1)}, u32[]{:S(2)}, u32[]{:S(2)}) collective-permute-start(bf16[512,128]{1,0:T(8,128)(2,1)S(1)} %get-tuple-element.110.refs_1_), channel_id=1, source_target_pairs={{12,0},{8,4},{4,8},{0,12},{13,1},{9,5},{5,9},{1,13},{14,2},{10,6},... | collective-permute-start | bytes 393224 | tf_op jit(solution)/shard_map/ppermute | solution.py:59
  67.4 2.0 %shard_map.63 = (f32[1024,128]{1,0:T(8,128)S(1)}, f32[8,128]{1,0:T(8,128)S(1)}) custom-call(bf16[3,4,2048,128]{3,2,1,0:T(8,128)(2,1)S(1)} %bitcast.9, bf16[512,128]{1,0:T(8,128)(2,1)S(1)} %get-tuple-element.110.refs_1_, bf16[512,128]{1,0:T(8,128)(2,1)S(1)} %collective-permute-done.19.refs_2_), custom_call_target="tpu_custom_call" | custom-call | flops 1 | bytes 1 | tf_op jit(solution)/shard_map/pallas_call | solution.py:43
  69.8 2.2 %collective-permute-done.23.refs_4_ = bf16[512,128]{1,0:T(8,128)(2,1)S(1)} collective-permute-done((bf16[512,128]{1,0:T(8,128)(2,1)S(1)}, bf16[512,128]{1,0:T(8,128)(2,1)S(1)}, u32[]{:S(2)}, u32[]{:S(2)}) %collective-permute-start.23) | collective-permute-done | bytes 131104 | tf_op jit(solution)/shard_map/ppermute | solution.py:59
  72.5 2.0 %collective-permute-done.18.refs_1_ = bf16[512,128]{1,0:T(8,128)(2,1)S(1)} collective-permute-done((bf16[512,128]{1,0:T(8,128)(2,1)S(1)}, bf16[512,128]{1,0:T(8,128)(2,1)S(1)}, u32[]{:S(2)}, u32[]{:S(2)}) %collective-permute-start.18) | collective-permute-done | bytes 131104 | tf_op jit(solution)/shard_map/ppermute | solution.py:59
  74.6 3.0 %shard_map.65 = (f32[1024,128]{1,0:T(8,128)S(1)}, f32[8,128]{1,0:T(8,128)}) custom-call(bf16[2,4,2048,128]{3,2,1,0:T(8,128)(2,1)S(1)} %bitcast.15, bf16[2,4,2048,128]{3,2,1,0:T(8,128)(2,1)S(1)} %bitcast.18, bf16[512,128]{1,0:T(8,128)(2,1)S(1)} %collective-permute-done.21.refs_2_, bf16[512,128]{1,0:T(8,128)(2,1)S(1)} %collective-permute-done.22.refs_3_, ...), custom_call_target="tpu_custom_call" | custom-call | flops 1 | bytes 1 | tf_op jit(solution)/shard_map/pallas_call | solution.py:43
  79.5 2.1 %collective-permute-start.28 = (f32[512,128]{1,0:T(8,128)S(1)}, f32[512,128]{1,0:T(8,128)S(1)}, u32[]{:S(2)}, u32[]{:S(2)}) collective-permute-start(f32[512,128]{1,0:T(8,128)S(1)} %get-tuple-element.120.refs_1_), channel_id=1, source_target_pairs={{2,0},{0,2},{3,1},{1,3},{6,4},{4,6},{7,5},{5,7},{10,8},{8,10},{11,... | collective-permute-start | bytes 786440 | tf_op jit(solution)/shard_map/ppermute | solution.py:59
  81.6 2.5 %shard_map.67 = (f32[104,128]{1,0:T(8,128)S(1)}, f32[104,128]{1,0:T(8,128)S(1)}, f32[8,128]{1,0:T(8,128)}) custom-call(f32[512,128]{1,0:T(8,128)S(1)} %get-tuple-element.119.refs_0_, f32[512,128]{1,0:T(8,128)S(1)} %get-tuple-element.120.refs_1_, f32[512,128]{1,0:T(8,128)S(1)} %get-tuple-element.117.refs_2_.refs_4_.refs_0_, ...), custom_call_target="tpu_custom_call" | custom-call | flops 1 | bytes 1 | tf_op jit(solution)/shard_map/pallas_call | solution.py:43
  92.2 2.2 %collective-permute-start.31 = (f32[176,128]{1,0:T(8,128)S(1)}, f32[176,128]{1,0:T(8,128)S(1)}, u32[]{:S(2)}, u32[]{:S(2)}) collective-permute-start(f32[176,128]{1,0:T(8,128)S(1)} %pad_maximum_fusion.1), channel_id=1, source_target_pairs={{4,0},{6,2},{0,4},{2,6},{12,8},{14,10},{8,12},{10,14},{5,1},{7,3},... | collective-permute-start | bytes 270344 | tf_op jit(solution)/shard_map/ppermute | solution.py:59
  95.2 2.3 %collective-permute-done.31 = f32[176,128]{1,0:T(8,128)S(1)} collective-permute-done((f32[176,128]{1,0:T(8,128)S(1)}, f32[176,128]{1,0:T(8,128)S(1)}, u32[]{:S(2)}, u32[]{:S(2)}) %collective-permute-start.31) | collective-permute-done | bytes 90144 | tf_op jit(solution)/shard_map/ppermute | solution.py:59
  97.5 2.4 %collective-permute-done.32 = f32[176,128]{1,0:T(8,128)S(1)} collective-permute-done((f32[176,128]{1,0:T(8,128)S(1)}, f32[176,128]{1,0:T(8,128)S(1)}, u32[]{:S(2)}, u32[]{:S(2)}) %collective-permute-start.32) | collective-permute-done | bytes 90144 | tf_op jit(solution)/shard_map/ppermute | solution.py:59
  101.4 6.0 %shard_map.69 = (f32[512,128]{1,0:T(8,128)S(1)}, f32[128,128]{1,0:T(8,128)S(1)}, f32[128,128]{1,0:T(8,128)S(1)}, f32[128,128]{1,0:T(8,128)S(1)}, f32[8,128]{1,0:T(8,128)}) custom-call(f32[104,128]{1,0:T(8,128)S(1)} %slice.19.refs_0_, f32[104,128]{1,0:T(8,128)S(1)} %collective-permute-done.34.refs_1_, f32[512,128]{1,0:T(8,128)S(1)} %get-tuple-element.108.refs_3_.refs_2_, ...), custom_call_target="tpu_custom_call" | custom-call | flops 1 | bytes 1 | tf_op jit(solution)/shard_map/pallas_call | solution.py:43
  114.3 2.0 %shard_map.71 = (f32[1024,128]{1,0:T(8,128)S(1)}, f32[8,128]{1,0:T(8,128)S(1)}) custom-call(bf16[3,4,2048,128]{3,2,1,0:T(8,128)(2,1)S(1)} %bitcast.10, bf16[512,128]{1,0:T(8,128)(2,1)S(1)} %get-tuple-element.134.refs_1_, bf16[512,128]{1,0:T(8,128)(2,1)S(1)} %collective-permute-done.36.refs_2_), custom_call_target="tpu_custom_call" | custom-call | flops 1 | bytes 1 | tf_op jit(solution)/shard_map/pallas_call | solution.py:43
  116.7 2.9 %collective-permute-done.40.refs_4_ = bf16[512,128]{1,0:T(8,128)(2,1)S(1)} collective-permute-done((bf16[512,128]{1,0:T(8,128)(2,1)S(1)}, bf16[512,128]{1,0:T(8,128)(2,1)S(1)}, u32[]{:S(2)}, u32[]{:S(2)}) %collective-permute-start.40) | collective-permute-done | bytes 131104 | tf_op jit(solution)/shard_map/ppermute | solution.py:59
  122.0 3.1 %shard_map.73 = (f32[1024,128]{1,0:T(8,128)S(1)}, f32[8,128]{1,0:T(8,128)}) custom-call(bf16[2,4,2048,128]{3,2,1,0:T(8,128)(2,1)S(1)} %bitcast.16, bf16[2,4,2048,128]{3,2,1,0:T(8,128)(2,1)S(1)} %bitcast.19, bf16[512,128]{1,0:T(8,128)(2,1)S(1)} %collective-permute-done.38.refs_2_, bf16[512,128]{1,0:T(8,128)(2,1)S(1)} %collective-permute-done.39.refs_3_, ...), custom_call_target="tpu_custom_call" | custom-call | flops 1 | bytes 1 | tf_op jit(solution)/shard_map/pallas_call | solution.py:43
  130.9 2.3 %collective-permute-start.45 = (f32[72,128]{1,0:T(8,128)S(1)}, f32[72,128]{1,0:T(8,128)S(1)}, u32[]{:S(2)}, u32[]{:S(2)}) collective-permute-start(f32[72,128]{1,0:T(8,128)S(1)} %add.63), channel_id=1, source_target_pairs={{4,0},{6,2},{0,4},{2,6},{12,8},{14,10},{8,12},{10,14},{5,1},{7,3},... | collective-permute-start | bytes 110600 | tf_op jit(solution)/shard_map/ppermute | solution.py:59
  135.1 2.9 %collective-permute-done.46 = f32[72,128]{1,0:T(8,128)S(1)} collective-permute-done((f32[72,128]{1,0:T(8,128)S(1)}, f32[72,128]{1,0:T(8,128)S(1)}, u32[]{:S(2)}, u32[]{:S(2)}) %collective-permute-start.46) | collective-permute-done | bytes 36896 | tf_op jit(solution)/shard_map/ppermute | solution.py:59
  140.2 4.2 %collective-permute-done.47 = f32[72,128]{1,0:T(8,128)S(1)} collective-permute-done((f32[72,128]{1,0:T(8,128)S(1)}, f32[72,128]{1,0:T(8,128)S(1)}, u32[]{:S(2)}, u32[]{:S(2)}) %collective-permute-start.47) | collective-permute-done | bytes 36896 | tf_op jit(solution)/shard_map/ppermute | solution.py:59
  145.0 5.6 %shard_map.76 = (f32[512,128]{1,0:T(8,128)}, f32[512,128]{1,0:T(8,128)}, f32[8,128]{1,0:T(8,128)}) custom-call(f32[72,128]{1,0:T(8,128)S(1)} %add.67.refs_0_, f32[128,128]{1,0:T(8,128)S(1)} %get-tuple-element.147.refs_1_, f32[512,128]{1,0:T(8,128)S(1)} %get-tuple-element.132.refs_3_.refs_2_, f32[512,128]{1,0:T(8,128)S(1)} %get-tuple-element.142.refs_2_.refs_3_, ...), custom_call_target="tpu_custom_call" | custom-call | flops 1 | bytes 1 | tf_op jit(solution)/shard_map/pallas_call | solution.py:43
  (110 shorter events, 58.0 us)
Async XLA Ops:
  2.1 9.3 %collective-permute-start = (f32[512,128]{1,0:T(8,128)S(1)}, f32[512,128]{1,0:T(8,128)S(1)}, u32[]{:S(2)}, u32[]{:S(2)}) collective-permute-start(f32[512,128]{1,0:T(8,128)S(1)} %get-tuple-element.78), channel_id=1, source_target_pairs={{2,0},{0,2},{3,1},{1,3},{6,4},{4,6},{7,5},{5,7},{10,8},{8,10},{11,... | collective-permute-start | bytes 786440 | tf_op jit(solution)/shard_map/ppermute | solution.py:59
  11.5 10.7 %collective-permute-start.2 = (bf16[512,128]{1,0:T(8,128)(2,1)S(1)}, bf16[512,128]{1,0:T(8,128)(2,1)S(1)}, u32[]{:S(2)}, u32[]{:S(2)}) collective-permute-start(bf16[512,128]{1,0:T(8,128)(2,1)S(1)} %get-tuple-element.85.refs_1_), channel_id=1, source_target_pairs={{1,0},{0,1},{3,2},{2,3},{5,4},{4,5},{7,6},{6,7},{9,8},{8,9},{11,10... | collective-permute-start | bytes 393224 | tf_op jit(solution)/shard_map/ppermute | solution.py:59
  11.6 12.7 %collective-permute-start.6 = (bf16[512,128]{1,0:T(8,128)(2,1)S(1)}, bf16[512,128]{1,0:T(8,128)(2,1)S(1)}, u32[]{:S(2)}, u32[]{:S(2)}) collective-permute-start(bf16[512,128]{1,0:T(8,128)(2,1)S(1)} %get-tuple-element.85.refs_1_), channel_id=1, source_target_pairs={{8,0},{12,4},{0,8},{4,12},{9,1},{13,5},{1,9},{5,13},{10,2},{14,6},... | collective-permute-start | bytes 393224 | tf_op jit(solution)/shard_map/ppermute | solution.py:59
  14.5 9.8 %collective-permute-start.4 = (bf16[512,128]{1,0:T(8,128)(2,1)S(1)}, bf16[512,128]{1,0:T(8,128)(2,1)S(1)}, u32[]{:S(2)}, u32[]{:S(2)}) collective-permute-start(bf16[512,128]{1,0:T(8,128)(2,1)S(1)} %get-tuple-element.85.refs_1_), channel_id=1, source_target_pairs={{4,0},{0,4},{12,8},{8,12},{5,1},{1,5},{13,9},{9,13},{6,2},{2,6},{1... | collective-permute-start | bytes 393224 | tf_op jit(solution)/shard_map/ppermute | solution.py:59
  16.1 9.8 %collective-permute-start.8 = (f32[512,128]{1,0:T(8,128)S(1)}, f32[512,128]{1,0:T(8,128)S(1)}, u32[]{:S(2)}, u32[]{:S(2)}) collective-permute-start(f32[512,128]{1,0:T(8,128)S(1)} %get-tuple-element.95.refs_2_.refs_4_.refs_0_), channel_id=1, source_target_pairs={{2,0},{0,2},{3,1},{1,3},{6,4},{4,6},{7,5},{5,7},{10,8},{8,10},{11,... | collective-permute-start | bytes 786440 | tf_op jit(solution)/shard_map/ppermute | solution.py:59
  17.6 7.9 %collective-permute-start.1 = (bf16[512,128]{1,0:T(8,128)(2,1)S(1)}, bf16[512,128]{1,0:T(8,128)(2,1)S(1)}, u32[]{:S(2)}, u32[]{:S(2)}) collective-permute-start(bf16[512,128]{1,0:T(8,128)(2,1)S(1)} %get-tuple-element.85.refs_1_), channel_id=1, source_target_pairs={{12,0},{8,4},{4,8},{0,12},{13,1},{9,5},{5,9},{1,13},{14,2},{10,6},... | collective-permute-start | bytes 393224 | tf_op jit(solution)/shard_map/ppermute | solution.py:59
  30.8 8.5 %collective-permute-start.11 = (f32[512,128]{1,0:T(8,128)S(1)}, f32[512,128]{1,0:T(8,128)S(1)}, u32[]{:S(2)}, u32[]{:S(2)}) collective-permute-start(f32[512,128]{1,0:T(8,128)S(1)} %get-tuple-element.98.refs_1_), channel_id=1, source_target_pairs={{2,0},{0,2},{3,1},{1,3},{6,4},{4,6},{7,5},{5,7},{10,8},{8,10},{11,... | collective-permute-start | bytes 786440 | tf_op jit(solution)/shard_map/ppermute | solution.py:59
  34.4 7.7 %collective-permute-start.10 = (f32[104,128]{1,0:T(8,128)S(1)}, f32[104,128]{1,0:T(8,128)S(1)}, u32[]{:S(2)}, u32[]{:S(2)}) collective-permute-start(f32[104,128]{1,0:T(8,128)S(1)} %add.51), channel_id=1, source_target_pairs={{8,0},{10,2},{12,4},{14,6},{0,8},{2,10},{4,12},{6,14},{9,1},{11,3}... | collective-permute-start | bytes 159752 | tf_op jit(solution)/shard_map/ppermute | solution.py:59
  42.1 4.6 %collective-permute-start.13 = (f32[176,128]{1,0:T(8,128)S(1)}, f32[176,128]{1,0:T(8,128)S(1)}, u32[]{:S(2)}, u32[]{:S(2)}) collective-permute-start(f32[176,128]{1,0:T(8,128)S(1)} %pad_maximum_fusion), channel_id=1, source_target_pairs={{2,0},{0,2},{6,4},{4,6},{10,8},{8,10},{14,12},{12,14},{3,1},{1,3},... | collective-permute-start | bytes 270344 | tf_op jit(solution)/shard_map/ppermute | solution.py:59
  42.9 5.6 %collective-permute-start.14 = (f32[176,128]{1,0:T(8,128)S(1)}, f32[176,128]{1,0:T(8,128)S(1)}, u32[]{:S(2)}, u32[]{:S(2)}) collective-permute-start(f32[176,128]{1,0:T(8,128)S(1)} %pad_maximum_fusion), channel_id=1, source_target_pairs={{4,0},{6,2},{0,4},{2,6},{12,8},{14,10},{8,12},{10,14},{5,1},{7,3},... | collective-permute-start | bytes 270344 | tf_op jit(solution)/shard_map/ppermute | solution.py:59
  45.3 5.4 %collective-permute-start.15 = (f32[176,128]{1,0:T(8,128)S(1)}, f32[176,128]{1,0:T(8,128)S(1)}, u32[]{:S(2)}, u32[]{:S(2)}) collective-permute-start(f32[176,128]{1,0:T(8,128)S(1)} %pad_maximum_fusion), channel_id=1, source_target_pairs={{6,0},{4,2},{2,4},{0,6},{14,8},{12,10},{10,12},{8,14},{7,1},{5,3},... | collective-permute-start | bytes 270344 | tf_op jit(solution)/shard_map/ppermute | solution.py:59
  50.8 8.7 %collective-permute-start.16 = (f32[72,128]{1,0:T(8,128)S(1)}, f32[72,128]{1,0:T(8,128)S(1)}, u32[]{:S(2)}, u32[]{:S(2)}) collective-permute-start(f32[72,128]{1,0:T(8,128)S(1)} %slice.16.refs_5_), channel_id=1, source_target_pairs={{8,0},{10,2},{12,4},{14,6},{0,8},{2,10},{4,12},{6,14},{9,1},{11,3}... | collective-permute-start | bytes 110600 | tf_op jit(solution)/shard_map/ppermute | solution.py:59
  61.3 6.1 %collective-permute-start.19 = (bf16[512,128]{1,0:T(8,128)(2,1)S(1)}, bf16[512,128]{1,0:T(8,128)(2,1)S(1)}, u32[]{:S(2)}, u32[]{:S(2)}) collective-permute-start(bf16[512,128]{1,0:T(8,128)(2,1)S(1)} %get-tuple-element.110.refs_1_), channel_id=1, source_target_pairs={{1,0},{0,1},{3,2},{2,3},{5,4},{4,5},{7,6},{6,7},{9,8},{8,9},{11,10... | collective-permute-start | bytes 393224 | tf_op jit(solution)/shard_map/ppermute | solution.py:59
  61.5 10.5 %collective-permute-start.23 = (bf16[512,128]{1,0:T(8,128)(2,1)S(1)}, bf16[512,128]{1,0:T(8,128)(2,1)S(1)}, u32[]{:S(2)}, u32[]{:S(2)}) collective-permute-start(bf16[512,128]{1,0:T(8,128)(2,1)S(1)} %get-tuple-element.110.refs_1_), channel_id=1, source_target_pairs={{8,0},{12,4},{0,8},{4,12},{9,1},{13,5},{1,9},{5,13},{10,2},{14,6},... | collective-permute-start | bytes 393224 | tf_op jit(solution)/shard_map/ppermute | solution.py:59
  62.6 9.3 %collective-permute-start.21 = (bf16[512,128]{1,0:T(8,128)(2,1)S(1)}, bf16[512,128]{1,0:T(8,128)(2,1)S(1)}, u32[]{:S(2)}, u32[]{:S(2)}) collective-permute-start(bf16[512,128]{1,0:T(8,128)(2,1)S(1)} %get-tuple-element.110.refs_1_), channel_id=1, source_target_pairs={{4,0},{0,4},{12,8},{8,12},{5,1},{1,5},{13,9},{9,13},{6,2},{2,6},{1... | collective-permute-start | bytes 393224 | tf_op jit(solution)/shard_map/ppermute | solution.py:59
  63.8 10.7 %collective-permute-start.18 = (bf16[512,128]{1,0:T(8,128)(2,1)S(1)}, bf16[512,128]{1,0:T(8,128)(2,1)S(1)}, u32[]{:S(2)}, u32[]{:S(2)}) collective-permute-start(bf16[512,128]{1,0:T(8,128)(2,1)S(1)} %get-tuple-element.110.refs_1_), channel_id=1, source_target_pairs={{12,0},{8,4},{4,8},{0,12},{13,1},{9,5},{5,9},{1,13},{14,2},{10,6},... | collective-permute-start | bytes 393224 | tf_op jit(solution)/shard_map/ppermute | solution.py:59
  65.9 8.7 %collective-permute-start.25 = (f32[512,128]{1,0:T(8,128)S(1)}, f32[512,128]{1,0:T(8,128)S(1)}, u32[]{:S(2)}, u32[]{:S(2)}) collective-permute-start(f32[512,128]{1,0:T(8,128)S(1)} %get-tuple-element.117.refs_2_.refs_4_.refs_0_), channel_id=1, source_target_pairs={{2,0},{0,2},{3,1},{1,3},{6,4},{4,6},{7,5},{5,7},{10,8},{8,10},{11,... | collective-permute-start | bytes 786440 | tf_op jit(solution)/shard_map/ppermute | solution.py:59
  79.5 8.7 %collective-permute-start.28 = (f32[512,128]{1,0:T(8,128)S(1)}, f32[512,128]{1,0:T(8,128)S(1)}, u32[]{:S(2)}, u32[]{:S(2)}) collective-permute-start(f32[512,128]{1,0:T(8,128)S(1)} %get-tuple-element.120.refs_1_), channel_id=1, source_target_pairs={{2,0},{0,2},{3,1},{1,3},{6,4},{4,6},{7,5},{5,7},{10,8},{8,10},{11,... | collective-permute-start | bytes 786440 | tf_op jit(solution)/shard_map/ppermute | solution.py:59
  85.3 5.1 %collective-permute-start.27 = (f32[104,128]{1,0:T(8,128)S(1)}, f32[104,128]{1,0:T(8,128)S(1)}, u32[]{:S(2)}, u32[]{:S(2)}) collective-permute-start(f32[104,128]{1,0:T(8,128)S(1)} %add.57), channel_id=1, source_target_pairs={{8,0},{10,2},{12,4},{14,6},{0,8},{2,10},{4,12},{6,14},{9,1},{11,3}... | collective-permute-start | bytes 159752 | tf_op jit(solution)/shard_map/ppermute | solution.py:59
  90.5 4.7 %collective-permute-start.30 = (f32[176,128]{1,0:T(8,128)S(1)}, f32[176,128]{1,0:T(8,128)S(1)}, u32[]{:S(2)}, u32[]{:S(2)}) collective-permute-start(f32[176,128]{1,0:T(8,128)S(1)} %pad_maximum_fusion.1), channel_id=1, source_target_pairs={{2,0},{0,2},{6,4},{4,6},{10,8},{8,10},{14,12},{12,14},{3,1},{1,3},... | collective-permute-start | bytes 270344 | tf_op jit(solution)/shard_map/ppermute | solution.py:59
  92.2 5.2 %collective-permute-start.31 = (f32[176,128]{1,0:T(8,128)S(1)}, f32[176,128]{1,0:T(8,128)S(1)}, u32[]{:S(2)}, u32[]{:S(2)}) collective-permute-start(f32[176,128]{1,0:T(8,128)S(1)} %pad_maximum_fusion.1), channel_id=1, source_target_pairs={{4,0},{6,2},{0,4},{2,6},{12,8},{14,10},{8,12},{10,14},{5,1},{7,3},... | collective-permute-start | bytes 270344 | tf_op jit(solution)/shard_map/ppermute | solution.py:59
  94.4 5.4 %collective-permute-start.32 = (f32[176,128]{1,0:T(8,128)S(1)}, f32[176,128]{1,0:T(8,128)S(1)}, u32[]{:S(2)}, u32[]{:S(2)}) collective-permute-start(f32[176,128]{1,0:T(8,128)S(1)} %pad_maximum_fusion.1), channel_id=1, source_target_pairs={{6,0},{4,2},{2,4},{0,6},{14,8},{12,10},{10,12},{8,14},{7,1},{5,3},... | collective-permute-start | bytes 270344 | tf_op jit(solution)/shard_map/ppermute | solution.py:59
  100.0 7.5 %collective-permute-start.33 = (f32[72,128]{1,0:T(8,128)S(1)}, f32[72,128]{1,0:T(8,128)S(1)}, u32[]{:S(2)}, u32[]{:S(2)}) collective-permute-start(f32[72,128]{1,0:T(8,128)S(1)} %slice.18.refs_5_), channel_id=1, source_target_pairs={{8,0},{10,2},{12,4},{14,6},{0,8},{2,10},{4,12},{6,14},{9,1},{11,3}... | collective-permute-start | bytes 110600 | tf_op jit(solution)/shard_map/ppermute | solution.py:59
  109.1 5.2 %collective-permute-start.36 = (bf16[512,128]{1,0:T(8,128)(2,1)S(1)}, bf16[512,128]{1,0:T(8,128)(2,1)S(1)}, u32[]{:S(2)}, u32[]{:S(2)}) collective-permute-start(bf16[512,128]{1,0:T(8,128)(2,1)S(1)} %get-tuple-element.134.refs_1_), channel_id=1, source_target_pairs={{1,0},{0,1},{3,2},{2,3},{5,4},{4,5},{7,6},{6,7},{9,8},{8,9},{11,10... | collective-permute-start | bytes 393224 | tf_op jit(solution)/shard_map/ppermute | solution.py:59
  109.3 10.3 %collective-permute-start.40 = (bf16[512,128]{1,0:T(8,128)(2,1)S(1)}, bf16[512,128]{1,0:T(8,128)(2,1)S(1)}, u32[]{:S(2)}, u32[]{:S(2)}) collective-permute-start(bf16[512,128]{1,0:T(8,128)(2,1)S(1)} %get-tuple-element.134.refs_1_), channel_id=1, source_target_pairs={{8,0},{12,4},{0,8},{4,12},{9,1},{13,5},{1,9},{5,13},{10,2},{14,6},... | collective-permute-start | bytes 393224 | tf_op jit(solution)/shard_map/ppermute | solution.py:59
  110.8 8.8 %collective-permute-start.38 = (bf16[512,128]{1,0:T(8,128)(2,1)S(1)}, bf16[512,128]{1,0:T(8,128)(2,1)S(1)}, u32[]{:S(2)}, u32[]{:S(2)}) collective-permute-start(bf16[512,128]{1,0:T(8,128)(2,1)S(1)} %get-tuple-element.134.refs_1_), channel_id=1, source_target_pairs={{4,0},{0,4},{12,8},{8,12},{5,1},{1,5},{13,9},{9,13},{6,2},{2,6},{1... | collective-permute-start | bytes 393224 | tf_op jit(solution)/shard_map/ppermute | solution.py:59
  111.9 10.1 %collective-permute-start.42 = (f32[512,128]{1,0:T(8,128)S(1)}, f32[512,128]{1,0:T(8,128)S(1)}, u32[]{:S(2)}, u32[]{:S(2)}) collective-permute-start(f32[512,128]{1,0:T(8,128)S(1)} %get-tuple-element.142.refs_2_.refs_3_), channel_id=1, source_target_pairs={{2,0},{0,2},{3,1},{1,3},{6,4},{4,6},{7,5},{5,7},{10,8},{8,10},{11,... | collective-permute-start | bytes 786440 | tf_op jit(solution)/shard_map/ppermute | solution.py:59
  113.2 8.7 %collective-permute-start.35 = (bf16[512,128]{1,0:T(8,128)(2,1)S(1)}, bf16[512,128]{1,0:T(8,128)(2,1)S(1)}, u32[]{:S(2)}, u32[]{:S(2)}) collective-permute-start(bf16[512,128]{1,0:T(8,128)(2,1)S(1)} %get-tuple-element.134.refs_1_), channel_id=1, source_target_pairs={{12,0},{8,4},{4,8},{0,12},{13,1},{9,5},{5,9},{1,13},{14,2},{10,6},... | collective-permute-start | bytes 393224 | tf_op jit(solution)/shard_map/ppermute | solution.py:59
  129.5 4.4 %collective-permute-start.44 = (f32[72,128]{1,0:T(8,128)S(1)}, f32[72,128]{1,0:T(8,128)S(1)}, u32[]{:S(2)}, u32[]{:S(2)}) collective-permute-start(f32[72,128]{1,0:T(8,128)S(1)} %add.63), channel_id=1, source_target_pairs={{2,0},{0,2},{6,4},{4,6},{10,8},{8,10},{14,12},{12,14},{3,1},{1,3},... | collective-permute-start | bytes 110600 | tf_op jit(solution)/shard_map/ppermute | solution.py:59
  133.2 4.9 %collective-permute-start.46 = (f32[72,128]{1,0:T(8,128)S(1)}, f32[72,128]{1,0:T(8,128)S(1)}, u32[]{:S(2)}, u32[]{:S(2)}) collective-permute-start(f32[72,128]{1,0:T(8,128)S(1)} %add.63), channel_id=1, source_target_pairs={{6,0},{4,2},{2,4},{0,6},{14,8},{12,10},{10,12},{8,14},{7,1},{5,3},... | collective-permute-start | bytes 110600 | tf_op jit(solution)/shard_map/ppermute | solution.py:59
  138.0 6.9 %collective-permute-start.48 = (f32[512,128]{1,0:T(8,128)S(1)}, f32[512,128]{1,0:T(8,128)S(1)}, u32[]{:S(2)}, u32[]{:S(2)}) collective-permute-start(f32[512,128]{1,0:T(8,128)S(1)} %get-tuple-element.149.refs_1_), channel_id=1, source_target_pairs={{2,0},{0,2},{3,1},{1,3},{6,4},{4,6},{7,5},{5,7},{10,8},{8,10},{11,... | collective-permute-start | bytes 786440 | tf_op jit(solution)/shard_map/ppermute | solution.py:59
  139.5 4.9 %collective-permute-start.47 = (f32[72,128]{1,0:T(8,128)S(1)}, f32[72,128]{1,0:T(8,128)S(1)}, u32[]{:S(2)}, u32[]{:S(2)}) collective-permute-start(f32[72,128]{1,0:T(8,128)S(1)} %add_add_fusion.2), channel_id=1, source_target_pairs={{8,0},{10,2},{12,4},{14,6},{0,8},{2,10},{4,12},{6,14},{9,1},{11,3}... | collective-permute-start | bytes 110600 | tf_op jit(solution)/shard_map/ppermute | solution.py:59
  (17 other events, 37.9 us)

commit v2 on v1

--- a/solution.py
+++ b/solution.py
@@ -98,10 +98,8 @@
 def reduce_one(value):
     value = value + swapped(value, "coef", 1, 2)
     if not by_stages():
-        value = lax.psum(value, ("panel", "rhs"))
-        return value, value
-    near = sum_near(value)
-    return sum_far(near), near
+        return lax.psum(value, ("panel", "rhs"))
+    return sum_far(sum_near(value))
 
 
 def reduce_both(mine, mates, square):
@@ -200,7 +198,7 @@
     return packed, token
 
 
-def link_products(packed, pieces, acc, n, last, after=()):
+def link_products(packed, pieces, acc, n, slots, after=()):
     tiles, rows = packed[0].shape[1:3]
     counts = [value.shape[0] for value in packed]
     many = len(packed)
@@ -211,7 +209,8 @@
         for value in packed
     ]
     strip = tiles * LANES
-    block = min(512, 2 * rows)
+    size = rows if slots is None else rows // n
+    block = min(512, 2 * size)
 
     def body(*refs):
         k_refs, piece_refs = refs[:many], refs[many : 3 * many]
@@ -227,45 +226,44 @@
                 weights[at : at + strip, own] = piece_refs[2 * g][...]
                 weights[at : at + strip, other] = piece_refs[2 * g + 1][...]
                 at += strip
-        for start in range(0, 2 * rows, block):
-            here = slice(start, start + block)
-            left = jnp.concatenate(
-                [
-                    k_refs[g][i, t, here, :]
-                    for g in range(many)
-                    for i in range(counts[g])
-                    for t in range(tiles)
-                ],
-                axis=1,
-            )
-            product = jnp.dot(left, weights[...], preferred_element_type=F32)
-            even_acc[here, :] = product[:, :LANES]
-            odd_acc[here, :] = product[:, LANES:]
         me = lax.axis_index("rhs")
-        size = rows // len(outs)
-        for s in range(len(outs)):
-            start = mate(me, s, n) * size if last else 0
-            even = even_acc[pl.ds(2 * start, size, stride=2), :]
-            odd = odd_acc[pl.ds(2 * start + 1, size, stride=2), :]
+        for out, s in zip(outs, [None] if slots is None else slots):
+            first = 0 if s is None else pl.multiple_of(mate(me, s, n) * size, size)
+            for start in range(0, 2 * size, block):
+                here = slice(start, start + block)
+                left = jnp.concatenate(
+                    [
+                        k_refs[g][i, t, pl.ds(2 * first + start, block), :]
+                        for g in range(many)
+                        for i in range(counts[g])
+                        for t in range(tiles)
+                    ],
+                    axis=1,
+                )
+                product = jnp.dot(left, weights[...], preferred_element_type=F32)
+                even_acc[here, :] = product[:, :LANES]
+                odd_acc[here, :] = product[:, LANES:]
+            even = even_acc[pl.ds(0, size, stride=2), :]
+            odd = odd_acc[pl.ds(1, size, stride=2), :]
             total = even + odd
             if acc_ref is not None:
-                total = total + acc_ref[pl.ds(start, size), :]
-            outs[s][...] = total
+                total = total + acc_ref[pl.ds(first, size), :]
+            out[...] = total
 
     args = [*packed, *(value for pair in pieces for value in pair)]
     args += [acc] if acc is not None else []
     *result, token = call(
         body,
-        [shape(rows // n)] * n if last else [shape(rows)],
+        [shape(size)] * (1 if slots is None else len(slots)),
         *args,
         scratch=[
             pltpu.VMEM((sum(counts) * strip, 2 * LANES), BF16),
-            pltpu.VMEM((2 * rows, LANES), F32),
-            pltpu.VMEM((2 * rows, LANES), F32),
+            pltpu.VMEM((2 * size, LANES), F32),
+            pltpu.VMEM((2 * size, LANES), F32),
         ],
         after=after,
     )
-    return (result if last else result[0]), token
+    return result, token
 
 
 def link_groups(links):
@@ -294,21 +292,20 @@
 
 def operate(packed, groups, low, direction, between):
     n = lax.axis_size("rhs")
-    last = len(groups) - 1
     arrived = [low] + [bring(low) for bring, _, _ in groups[:0:-1]][::-1]
     directions = [direction] + [swapped(direction, "rhs", s, n) for s in range(1, n)]
     pairs = [[low, swapped(low, "coef", 1, 2)]]
-    acc, token = link_products(packed[:1], pairs, None, n, last == 0)
+    (acc,), token = link_products(packed[:1], pairs, None, n, None)
     after = (token, between(token))
-    for piece in arrived[1:]:
+    for place, piece in enumerate(arrived[1:]):
         piece, _ = lax.optimization_barrier((piece, after))
+        if place > 1:
+            piece, pairs[place - 1][1] = lax.optimization_barrier((piece, pairs[place - 1][1]))
         pairs.append([piece, swapped(piece, "coef", 1, 2)])
     after = (*after, *directions[1:])
-    if last > 1:
-        acc, _ = link_products(packed[1:last], pairs[1:last], acc, n, False, after)
-    if last:
-        acc, _ = link_products(packed[last:], pairs[last:], acc, n, True, after)
-    return acc, directions
+    mates, token = link_products(packed[1:], pairs[1:], acc, n, range(1, n), after)
+    own, _ = link_products(packed[1:], pairs[1:], acc, n, [0], (token,))
+    return own + mates, directions
 
 
 PACKED = LANES // 2 + SUB
@@ -349,10 +346,10 @@
 JOINT = PACKED + SUB + LANES
 
 
-def linear_grams(parts, directions, before, beta, first, final):
+def linear_grams(parts, directions, residual, turns, first, final):
     strip = parts[0].shape[0]
     n = len(parts)
-    extra = [] if first or final else [*before, beta]
+    extra = [] if first or final else [residual, *turns]
     rows = PACKED if final else JOINT // 2
 
     def body(*refs):
@@ -365,7 +362,7 @@
             term = mm(d, image, (0, 0))
             curve = term if s == 0 else curve + term
             if extra:
-                r = d - mm(rest[s][...], rest[n][...])
+                r = rest[0][...] if s == 0 else d - rest[s][...]
                 term = mm(r, image, (0, 0))
                 cross = term if s == 0 else cross + term
         if final:
@@ -415,6 +412,18 @@
     return image, square
 
 
+def reciprocal(value):
+    near = pl.reciprocal(value, approx=True)
+    for _ in range(2):
+        near = near * (2.0 - value * near)
+    return near
+
+
+def next_pivot(column, following, i, inverse):
+    product = column[i + 1 : i + 2] * following[i : i + 1]
+    return following[i + 1 : i + 2] - product * inverse
+
+
 def inverted(matrices, lane):
     strips = matrices[0].shape[0] // SUB
     place = lax.broadcasted_iota(jnp.int32, (SUB, LANES), 0)
@@ -441,11 +450,14 @@
         now = [
             [a[j], *(lanes_of(a[j], lane + SUB * j + i) for i in range(SUB))] for a in held
         ]
+        pivots = [values[1][:1] for values in now]
         for i in range(SUB):
             here = place == i
             for index, values in enumerate(now):
                 column = values[1 + i]
-                inverse = 1.0 / column[i : i + 1]
+                inverse = reciprocal(pivots[index])
+                if i + 1 < SUB:
+                    pivots[index] = next_pivot(column, values[2 + i], i, inverse)
 
                 def step(value):
                     row = value[i : i + 1] * inverse
@@ -530,11 +542,14 @@
         now = [
             [a[j], b[j], *(lanes_of(a[j], SUB * j + i) for i in range(SUB))] for a, b in held
         ]
+        pivots = [values[2][:1] for values in now]
         for i in range(SUB):
             here = place == i
             for index, values in enumerate(now):
                 column = values[2 + i]
-                inverse = 1.0 / column[i : i + 1]
+                inverse = reciprocal(pivots[index])
+                if i + 1 < SUB:
+                    pivots[index] = next_pivot(column, values[3 + i], i, inverse)
 
                 def step(value):
                     row = value[i : i + 1] * inverse
@@ -561,14 +576,21 @@
     ).astype(F32)
 
 
-def stepped(solution, direction, alpha, token):
-    fields = [direction, alpha] + ([] if solution is None else [solution])
-
-    def body(d, a, *refs):
-        change = mm(d[...], a[...])
-        refs[-1][...] = change if solution is None else refs[0][...] + change
-
-    return call(body, [shape(direction.shape[0])], *fields, after=[token])
+def stepped(solution, before, alpha, beta, token):
+    fields = [*before, alpha, beta] + ([] if solution is None else [solution])
+    n = len(before)
+
+    def body(*refs):
+        ds, a, b, refs = refs[:n], refs[n], refs[n + 1], refs[n + 2 :]
+        change = mm(ds[0][...], a[...])
+        refs[-n][...] = change if solution is None else refs[0][...] + change
+        for s in range(1, n):
+            refs[s - n][...] = mm(ds[s][...], b[...])
+
+    solution, *turns, token = call(
+        body, [shape(before[0].shape[0])] * n, *fields, after=[token]
+    )
+    return solution, turns, token
 
 
 def finish(small, gram, residual, direction, solution, image):
@@ -677,22 +699,20 @@
     solution = gram = beta = before = alpha = None
     for step in range(ITERS):
         first, final = step == 0, step + 1 == ITERS
-        state = [solution]
+        state = [solution, None]
 
         def between(token):
             if first:
                 return retile_token
-            state[0], token = stepped(solution, before[0], alpha, token)
+            *state[:], token = stepped(solution, before, alpha, beta, token)
             return token
 
         parts, directions = operate(packed, groups, low, direction, between)
-        (solution,) = state
-        linear = linear_grams(parts, directions, before, beta, first, final)
+        solution, turns = state
+        image_parts = [parts[0]] + [swapped(parts[s], "rhs", s, n) for s in range(1, n)]
+        linear = linear_grams(parts, directions, residual, turns, first, final)
         if final:
-            small, near = reduce_one(*linear)
-            parts[1:], _ = lax.optimization_barrier((parts[1:], near))
-        image_parts = [parts[0]] + [swapped(parts[s], "rhs", s, n) for s in range(1, n)]
-        if final:
+            small = reduce_one(*linear)
             solution, residual = finish(
                 small, gram, residual, direction, solution, image_parts
             )

time: 151 us -> 155 us (1.026)
  waiting for transfers between devices: 38.4 us -> 44.5 us
  starting transfers between devices: 50.5 us -> 47.8 us
    ppermute x49, waiting for transfers between devices: 38.4 us -> 44.5 us  [permute(): return lax.ppermute(value, axis, pairs)]
    ppermute x49, starting transfers between devices: 50.5 us -> 47.8 us  [permute(): return lax.ppermute(value, axis, pairs)]
  transfers between devices with their start and end apart: 49 -> 49, of which waited for: 25 -> 23; matrix products, arithmetic and copies ran while one was open for 0% -> 0% of each run, Pallas kernels for 29% -> 27%
where the time goes in v2:
time: 155 us
  Pallas kernels  61 us (39%)
  starting transfers between devices  47.8 us (31%)
  waiting for transfers between devices  44.5 us (29%)
    pallas_call x27, Pallas kernels, call(): pl.pallas_call(ordered, out_shape=list(outs) + [shape(SUB)], in_specs=[HB...  61 us
    ppermute x49, starting transfers between devices, permute(): return lax.ppermute(value, axis, pairs)  47.8 us
    ppermute x49, waiting for transfers between devices, permute(): return lax.ppermute(value, axis, pairs)  44.5 us
  transfers between devices with their start and end apart: 49, of which 23 were waited for; matrix products, arithmetic and copies ran while one was open for 0% of the time, Pallas kernels for 27%

profile of v2, /device:TPU:0, one launch (start us, length us, event | category | flops | bytes accessed | tf_op | source)
XLA Modules:
  0.0 154.5 jit_solution(2183415483019847382)
XLA Ops:
  2.1 3.0 %collective-permute-start = (f32[512,128]{1,0:T(8,128)S(1)}, f32[512,128]{1,0:T(8,128)S(1)}, u32[]{:S(2)}, u32[]{:S(2)}) collective-permute-start(f32[512,128]{1,0:T(8,128)S(1)} %get-tuple-element.88), channel_id=1, source_target_pairs={{2,0},{0,2},{3,1},{1,3},{6,4},{4,6},{7,5},{5,7},{10,8},{8,10},{11,... | collective-permute-start | bytes 786440 | tf_op jit(solution)/shard_map/ppermute | solution.py:59
  5.1 2.9 %shard_map.51 = (bf16[3,4,1024,2,128]{4,3,2,1,0:T(2,128)(2,1)S(1)}, f32[8,128]{1,0:T(8,128)S(1)}) custom-call(bf16[9,1024,2,512]{3,2,1,0:T(2,128)(2,1)} %bitcast.29, f32[8,128]{1,0:T(8,128)S(1)} %get-tuple-element.84.refs_1_), custom_call_target="tpu_custom_call" | custom-call | flops 1 | bytes 1 | tf_op jit(solution)/shard_map/pallas_call | solution.py:43
  8.0 2.2 %shard_map.52 = (bf16[2,4,1024,2,128]{4,3,2,1,0:T(2,128)(2,1)S(1)}, f32[8,128]{1,0:T(8,128)S(1)}) custom-call(bf16[9,1024,2,512]{3,2,1,0:T(2,128)(2,1)} %bitcast.30, f32[8,128]{1,0:T(8,128)S(1)} %get-tuple-element.85.refs_1_), custom_call_target="tpu_custom_call" | custom-call | flops 1 | bytes 1 | tf_op jit(solution)/shard_map/pallas_call | solution.py:43
  11.6 1.9 %collective-permute-start.1 = (bf16[512,128]{1,0:T(8,128)(2,1)S(1)}, bf16[512,128]{1,0:T(8,128)(2,1)S(1)}, u32[]{:S(2)}, u32[]{:S(2)}) collective-permute-start(bf16[512,128]{1,0:T(8,128)(2,1)S(1)} %get-tuple-element.94.refs_1_), channel_id=1, source_target_pairs={{4,0},{0,4},{12,8},{8,12},{5,1},{1,5},{13,9},{9,13},{6,2},{2,6},{1... | collective-permute-start | bytes 393224 | tf_op jit(solution)/shard_map/ppermute | solution.py:59
  13.5 2.6 %collective-permute-start.5 = (bf16[512,128]{1,0:T(8,128)(2,1)S(1)}, bf16[512,128]{1,0:T(8,128)(2,1)S(1)}, u32[]{:S(2)}, u32[]{:S(2)}) collective-permute-start(bf16[512,128]{1,0:T(8,128)(2,1)S(1)} %get-tuple-element.94.refs_1_), channel_id=1, source_target_pairs={{8,0},{12,4},{0,8},{4,12},{9,1},{13,5},{1,9},{5,13},{10,2},{14,6},... | collective-permute-start | bytes 393224 | tf_op jit(solution)/shard_map/ppermute | solution.py:59
  16.1 2.2 %shard_map.54 = (bf16[2,4,1024,2,128]{4,3,2,1,0:T(2,128)(2,1)S(1)}, f32[8,128]{1,0:T(8,128)S(1)}) custom-call(bf16[9,1024,2,512]{3,2,1,0:T(2,128)(2,1)} %bitcast.31, f32[8,128]{1,0:T(8,128)S(1)} %get-tuple-element.90.refs_1_), custom_call_target="tpu_custom_call" | custom-call | flops 1 | bytes 1 | tf_op jit(solution)/shard_map/pallas_call | solution.py:43
  18.3 2.2 %shard_map.55 = (bf16[2,4,1024,2,128]{4,3,2,1,0:T(2,128)(2,1)S(1)}, f32[8,128]{1,0:T(8,128)S(1)}) custom-call(bf16[9,1024,2,512]{3,2,1,0:T(2,128)(2,1)} %bitcast.32, f32[8,128]{1,0:T(8,128)S(1)} %get-tuple-element.92.refs_1_), custom_call_target="tpu_custom_call" | custom-call | flops 1 | bytes 1 | tf_op jit(solution)/shard_map/pallas_call | solution.py:43
  20.5 2.0 %shard_map.56 = (f32[1024,128]{1,0:T(8,128)S(1)}, f32[8,128]{1,0:T(8,128)S(1)}) custom-call(bf16[3,4,2048,128]{3,2,1,0:T(8,128)(2,1)S(1)} %bitcast.26, bf16[512,128]{1,0:T(8,128)(2,1)S(1)} %get-tuple-element.94.refs_1_, bf16[512,128]{1,0:T(8,128)(2,1)S(1)} %collective-permute-done.2.refs_2_), custom_call_target="tpu_custom_call" | custom-call | flops 1 | bytes 1 | tf_op jit(solution)/shard_map/pallas_call | solution.py:43
  24.4 2.0 %collective-permute-done.5.refs_5_ = bf16[512,128]{1,0:T(8,128)(2,1)S(1)} collective-permute-done((bf16[512,128]{1,0:T(8,128)(2,1)S(1)}, bf16[512,128]{1,0:T(8,128)(2,1)S(1)}, u32[]{:S(2)}, u32[]{:S(2)}) %collective-permute-start.5) | collective-permute-done | bytes 131104 | tf_op jit(solution)/shard_map/ppermute | solution.py:59
  26.9 4.5 %collective-permute-done.8.refs_12_.refs_3_.refs_1_ = f32[512,128]{1,0:T(8,128)S(1)} collective-permute-done((f32[512,128]{1,0:T(8,128)S(1)}, f32[512,128]{1,0:T(8,128)S(1)}, u32[]{:S(2)}, u32[]{:S(2)}) %collective-permute-start.8) | collective-permute-done | bytes 262176 | tf_op jit(solution)/shard_map/ppermute | solution.py:59
  31.4 2.0 %shard_map.57 = (f32[512,128]{1,0:T(8,128)S(1)}, f32[8,128]{1,0:T(8,128)S(1)}) custom-call(bf16[2,4,2048,128]{3,2,1,0:T(8,128)(2,1)S(1)} %bitcast.8, bf16[2,4,2048,128]{3,2,1,0:T(8,128)(2,1)S(1)} %bitcast.14, bf16[2,4,2048,128]{3,2,1,0:T(8,128)(2,1)S(1)} %bitcast.20, bf16[512,128]{1,0:T(8,128)(2,1)S(1)} %collective-permute-done.1.refs_3_, ...), custom_call_target="tpu_custom_call" | custom-call | flops 1 | bytes 1 | tf_op jit(solution)/shard_map/pallas_call | solution.py:43
  35.1 2.5 %shard_map.58 = (f32[512,128]{1,0:T(8,128)S(1)}, f32[8,128]{1,0:T(8,128)}) custom-call(bf16[2,4,2048,128]{3,2,1,0:T(8,128)(2,1)S(1)} %bitcast.9, bf16[2,4,2048,128]{3,2,1,0:T(8,128)(2,1)S(1)} %bitcast.15, bf16[2,4,2048,128]{3,2,1,0:T(8,128)(2,1)S(1)} %bitcast.21, bf16[512,128]{1,0:T(8,128)(2,1)S(1)} %collective-permute-done.1.refs_3_, ...), custom_call_target="tpu_custom_call" | custom-call | flops 1 | bytes 1 | tf_op jit(solution)/shard_map/pallas_call | solution.py:43
  42.9 3.5 %collective-permute-done.10 = f32[104,128]{1,0:T(8,128)S(1)} collective-permute-done((f32[104,128]{1,0:T(8,128)S(1)}, f32[104,128]{1,0:T(8,128)S(1)}, u32[]{:S(2)}, u32[]{:S(2)}) %collective-permute-start.10) | collective-permute-done | bytes 53280 | tf_op jit(solution)/shard_map/ppermute | solution.py:59
  53.7 2.0 %collective-permute-start.16 = (f32[72,128]{1,0:T(8,128)S(1)}, f32[72,128]{1,0:T(8,128)S(1)}, u32[]{:S(2)}, u32[]{:S(2)}) collective-permute-start(f32[72,128]{1,0:T(8,128)S(1)} %slice.16.refs_5_), channel_id=1, source_target_pairs={{8,0},{10,2},{12,4},{14,6},{0,8},{2,10},{4,12},{6,14},{9,1},{11,3}... | collective-permute-start | bytes 110600 | tf_op jit(solution)/shard_map/ppermute | solution.py:59
  55.7 6.9 %shard_map.61 = (f32[512,128]{1,0:T(8,128)S(1)}, f32[128,128]{1,0:T(8,128)S(1)}, f32[128,128]{1,0:T(8,128)S(1)}, f32[128,128]{1,0:T(8,128)S(1)}, f32[8,128]{1,0:T(8,128)}) custom-call(f32[104,128]{1,0:T(8,128)S(1)} %slice.17.refs_0_, f32[104,128]{1,0:T(8,128)S(1)} %collective-permute-done.17.refs_1_, ...), custom_call_target="tpu_custom_call" | custom-call | flops 1 | bytes 1 | tf_op jit(solution)/shard_map/pallas_call | solution.py:43
  66.9 2.0 %collective-permute-start.20 = (bf16[512,128]{1,0:T(8,128)(2,1)S(1)}, bf16[512,128]{1,0:T(8,128)(2,1)S(1)}, u32[]{:S(2)}, u32[]{:S(2)}) collective-permute-start(bf16[512,128]{1,0:T(8,128)(2,1)S(1)} %get-tuple-element.119.refs_1_), channel_id=1, source_target_pairs={{12,0},{8,4},{4,8},{0,12},{13,1},{9,5},{5,9},{1,13},{14,2},{10,6},... | collective-permute-start | bytes 393224 | tf_op jit(solution)/shard_map/ppermute | solution.py:59
  68.9 2.0 %shard_map.63 = (f32[1024,128]{1,0:T(8,128)S(1)}, f32[8,128]{1,0:T(8,128)S(1)}) custom-call(bf16[3,4,2048,128]{3,2,1,0:T(8,128)(2,1)S(1)} %bitcast.27, bf16[512,128]{1,0:T(8,128)(2,1)S(1)} %get-tuple-element.119.refs_1_, bf16[512,128]{1,0:T(8,128)(2,1)S(1)} %collective-permute-done.19.refs_2_), custom_call_target="tpu_custom_call" | custom-call | flops 1 | bytes 1 | tf_op jit(solution)/shard_map/pallas_call | solution.py:43
  73.2 5.5 %collective-permute-done.22.refs_5_ = bf16[512,128]{1,0:T(8,128)(2,1)S(1)} collective-permute-done((bf16[512,128]{1,0:T(8,128)(2,1)S(1)}, bf16[512,128]{1,0:T(8,128)(2,1)S(1)}, u32[]{:S(2)}, u32[]{:S(2)}) %collective-permute-start.22) | collective-permute-done | bytes 131104 | tf_op jit(solution)/shard_map/ppermute | solution.py:59
  80.5 2.0 %shard_map.65 = (f32[512,128]{1,0:T(8,128)S(1)}, f32[8,128]{1,0:T(8,128)S(1)}) custom-call(bf16[2,4,2048,128]{3,2,1,0:T(8,128)(2,1)S(1)} %bitcast.10, bf16[2,4,2048,128]{3,2,1,0:T(8,128)(2,1)S(1)} %bitcast.16, bf16[2,4,2048,128]{3,2,1,0:T(8,128)(2,1)S(1)} %bitcast.22, bf16[512,128]{1,0:T(8,128)(2,1)S(1)} %collective-permute-done.18.refs_3_, ...), custom_call_target="tpu_custom_call" | custom-call | flops 1 | bytes 1 | tf_op jit(solution)/shard_map/pallas_call | solution.py:43
  84.0 2.5 %shard_map.66 = (f32[512,128]{1,0:T(8,128)S(1)}, f32[8,128]{1,0:T(8,128)}) custom-call(bf16[2,4,2048,128]{3,2,1,0:T(8,128)(2,1)S(1)} %bitcast.11, bf16[2,4,2048,128]{3,2,1,0:T(8,128)(2,1)S(1)} %bitcast.17, bf16[2,4,2048,128]{3,2,1,0:T(8,128)(2,1)S(1)} %bitcast.23, bf16[512,128]{1,0:T(8,128)(2,1)S(1)} %collective-permute-done.18.refs_3_, ...), custom_call_target="tpu_custom_call" | custom-call | flops 1 | bytes 1 | tf_op jit(solution)/shard_map/pallas_call | solution.py:43
  89.3 2.1 %collective-permute-start.27 = (f32[104,128]{1,0:T(8,128)S(1)}, f32[104,128]{1,0:T(8,128)S(1)}, u32[]{:S(2)}, u32[]{:S(2)}) collective-permute-start(f32[104,128]{1,0:T(8,128)S(1)} %add.57), channel_id=1, source_target_pairs={{8,0},{10,2},{12,4},{14,6},{0,8},{2,10},{4,12},{6,14},{9,1},{11,3}... | collective-permute-start | bytes 159752 | tf_op jit(solution)/shard_map/ppermute | solution.py:59
  92.4 2.0 %collective-permute-done.27 = f32[104,128]{1,0:T(8,128)S(1)} collective-permute-done((f32[104,128]{1,0:T(8,128)S(1)}, f32[104,128]{1,0:T(8,128)S(1)}, u32[]{:S(2)}, u32[]{:S(2)}) %collective-permute-start.27) | collective-permute-done | bytes 53280 | tf_op jit(solution)/shard_map/ppermute | solution.py:59
  94.4 2.3 %collective-permute-start.31 = (f32[176,128]{1,0:T(8,128)S(1)}, f32[176,128]{1,0:T(8,128)S(1)}, u32[]{:S(2)}, u32[]{:S(2)}) collective-permute-start(f32[176,128]{1,0:T(8,128)S(1)} %pad_maximum_fusion.1), channel_id=1, source_target_pairs={{4,0},{6,2},{0,4},{2,6},{12,8},{14,10},{8,12},{10,14},{5,1},{7,3},... | collective-permute-start | bytes 270344 | tf_op jit(solution)/shard_map/ppermute | solution.py:59
  99.5 2.7 %collective-permute-done.32 = f32[176,128]{1,0:T(8,128)S(1)} collective-permute-done((f32[176,128]{1,0:T(8,128)S(1)}, f32[176,128]{1,0:T(8,128)S(1)}, u32[]{:S(2)}, u32[]{:S(2)}) %collective-permute-start.32) | collective-permute-done | bytes 90144 | tf_op jit(solution)/shard_map/ppermute | solution.py:59
  104.8 7.2 %shard_map.69 = (f32[512,128]{1,0:T(8,128)S(1)}, f32[128,128]{1,0:T(8,128)S(1)}, f32[128,128]{1,0:T(8,128)S(1)}, f32[128,128]{1,0:T(8,128)S(1)}, f32[8,128]{1,0:T(8,128)}) custom-call(f32[104,128]{1,0:T(8,128)S(1)} %slice.19.refs_0_, f32[104,128]{1,0:T(8,128)S(1)} %collective-permute-done.34.refs_1_, ...), custom_call_target="tpu_custom_call" | custom-call | flops 1 | bytes 1 | tf_op jit(solution)/shard_map/pallas_call | solution.py:43
  118.2 2.0 %shard_map.71 = (f32[1024,128]{1,0:T(8,128)S(1)}, f32[8,128]{1,0:T(8,128)S(1)}) custom-call(bf16[3,4,2048,128]{3,2,1,0:T(8,128)(2,1)S(1)} %bitcast.28, bf16[512,128]{1,0:T(8,128)(2,1)S(1)} %get-tuple-element.146.refs_1_, bf16[512,128]{1,0:T(8,128)(2,1)S(1)} %collective-permute-done.36.refs_2_), custom_call_target="tpu_custom_call" | custom-call | flops 1 | bytes 1 | tf_op jit(solution)/shard_map/pallas_call | solution.py:43
  122.9 5.1 %collective-permute-done.39.refs_5_ = bf16[512,128]{1,0:T(8,128)(2,1)S(1)} collective-permute-done((bf16[512,128]{1,0:T(8,128)(2,1)S(1)}, bf16[512,128]{1,0:T(8,128)(2,1)S(1)}, u32[]{:S(2)}, u32[]{:S(2)}) %collective-permute-start.39) | collective-permute-done | bytes 131104 | tf_op jit(solution)/shard_map/ppermute | solution.py:59
  130.2 2.0 %shard_map.73 = (f32[512,128]{1,0:T(8,128)S(1)}, f32[8,128]{1,0:T(8,128)S(1)}) custom-call(bf16[2,4,2048,128]{3,2,1,0:T(8,128)(2,1)S(1)} %bitcast.12, bf16[2,4,2048,128]{3,2,1,0:T(8,128)(2,1)S(1)} %bitcast.18, bf16[2,4,2048,128]{3,2,1,0:T(8,128)(2,1)S(1)} %bitcast.24, bf16[512,128]{1,0:T(8,128)(2,1)S(1)} %collective-permute-done.35.refs_3_, ...), custom_call_target="tpu_custom_call" | custom-call | flops 1 | bytes 1 | tf_op jit(solution)/shard_map/pallas_call | solution.py:43
  132.2 2.5 %shard_map.74 = (f32[512,128]{1,0:T(8,128)S(1)}, f32[8,128]{1,0:T(8,128)}) custom-call(bf16[2,4,2048,128]{3,2,1,0:T(8,128)(2,1)S(1)} %bitcast.13, bf16[2,4,2048,128]{3,2,1,0:T(8,128)(2,1)S(1)} %bitcast.19, bf16[2,4,2048,128]{3,2,1,0:T(8,128)(2,1)S(1)} %bitcast.25, bf16[512,128]{1,0:T(8,128)(2,1)S(1)} %collective-permute-done.35.refs_3_, ...), custom_call_target="tpu_custom_call" | custom-call | flops 1 | bytes 1 | tf_op jit(solution)/shard_map/pallas_call | solution.py:43
  137.1 2.7 %collective-permute-start.46 = (f32[72,128]{1,0:T(8,128)S(1)}, f32[72,128]{1,0:T(8,128)S(1)}, u32[]{:S(2)}, u32[]{:S(2)}) collective-permute-start(f32[72,128]{1,0:T(8,128)S(1)} %add.63), channel_id=1, source_target_pairs={{6,0},{4,2},{2,4},{0,6},{14,8},{12,10},{10,12},{8,14},{7,1},{5,3},... | collective-permute-start | bytes 110600 | tf_op jit(solution)/shard_map/ppermute | solution.py:59
  146.1 3.2 %collective-permute-done.47 = f32[72,128]{1,0:T(8,128)S(1)} collective-permute-done((f32[72,128]{1,0:T(8,128)S(1)}, f32[72,128]{1,0:T(8,128)S(1)}, u32[]{:S(2)}, u32[]{:S(2)}) %collective-permute-start.47) | collective-permute-done | bytes 36896 | tf_op jit(solution)/shard_map/ppermute | solution.py:59
  149.3 5.2 %shard_map.76 = (f32[512,128]{1,0:T(8,128)}, f32[512,128]{1,0:T(8,128)}, f32[8,128]{1,0:T(8,128)}) custom-call(f32[72,128]{1,0:T(8,128)S(1)} %add.67.refs_0_, f32[128,128]{1,0:T(8,128)S(1)} %get-tuple-element.162.refs_1_, f32[512,128]{1,0:T(8,128)S(1)} %get-tuple-element.144.refs_3_.refs_2_, f32[512,128]{1,0:T(8,128)S(1)} %get-tuple-element.157.refs_2_.refs_3_, ...), custom_call_target="tpu_custom_call" | custom-call | flops 1 | bytes 1 | tf_op jit(solution)/shard_map/pallas_call | solution.py:43
  (110 shorter events, 58.6 us)
Async XLA Ops:
  2.1 9.3 %collective-permute-start = (f32[512,128]{1,0:T(8,128)S(1)}, f32[512,128]{1,0:T(8,128)S(1)}, u32[]{:S(2)}, u32[]{:S(2)}) collective-permute-start(f32[512,128]{1,0:T(8,128)S(1)} %get-tuple-element.88), channel_id=1, source_target_pairs={{2,0},{0,2},{3,1},{1,3},{6,4},{4,6},{7,5},{5,7},{10,8},{8,10},{11,... | collective-permute-start | bytes 786440 | tf_op jit(solution)/shard_map/ppermute | solution.py:59
  11.5 9.0 %collective-permute-start.2 = (bf16[512,128]{1,0:T(8,128)(2,1)S(1)}, bf16[512,128]{1,0:T(8,128)(2,1)S(1)}, u32[]{:S(2)}, u32[]{:S(2)}) collective-permute-start(bf16[512,128]{1,0:T(8,128)(2,1)S(1)} %get-tuple-element.94.refs_1_), channel_id=1, source_target_pairs={{1,0},{0,1},{3,2},{2,3},{5,4},{4,5},{7,6},{6,7},{9,8},{8,9},{11,10... | collective-permute-start | bytes 393224 | tf_op jit(solution)/shard_map/ppermute | solution.py:59
  11.6 11.0 %collective-permute-start.1 = (bf16[512,128]{1,0:T(8,128)(2,1)S(1)}, bf16[512,128]{1,0:T(8,128)(2,1)S(1)}, u32[]{:S(2)}, u32[]{:S(2)}) collective-permute-start(bf16[512,128]{1,0:T(8,128)(2,1)S(1)} %get-tuple-element.94.refs_1_), channel_id=1, source_target_pairs={{4,0},{0,4},{12,8},{8,12},{5,1},{1,5},{13,9},{9,13},{6,2},{2,6},{1... | collective-permute-start | bytes 393224 | tf_op jit(solution)/shard_map/ppermute | solution.py:59
  13.5 12.9 %collective-permute-start.5 = (bf16[512,128]{1,0:T(8,128)(2,1)S(1)}, bf16[512,128]{1,0:T(8,128)(2,1)S(1)}, u32[]{:S(2)}, u32[]{:S(2)}) collective-permute-start(bf16[512,128]{1,0:T(8,128)(2,1)S(1)} %get-tuple-element.94.refs_1_), channel_id=1, source_target_pairs={{8,0},{12,4},{0,8},{4,12},{9,1},{13,5},{1,9},{5,13},{10,2},{14,6},... | collective-permute-start | bytes 393224 | tf_op jit(solution)/shard_map/ppermute | solution.py:59
  16.1 10.3 %collective-permute-start.3 = (bf16[512,128]{1,0:T(8,128)(2,1)S(1)}, bf16[512,128]{1,0:T(8,128)(2,1)S(1)}, u32[]{:S(2)}, u32[]{:S(2)}) collective-permute-start(bf16[512,128]{1,0:T(8,128)(2,1)S(1)} %get-tuple-element.94.refs_1_), channel_id=1, source_target_pairs={{12,0},{8,4},{4,8},{0,12},{13,1},{9,5},{5,9},{1,13},{14,2},{10,6},... | collective-permute-start | bytes 393224 | tf_op jit(solution)/shard_map/ppermute | solution.py:59
  22.6 8.7 %collective-permute-start.8 = (f32[512,128]{1,0:T(8,128)S(1)}, f32[512,128]{1,0:T(8,128)S(1)}, u32[]{:S(2)}, u32[]{:S(2)}) collective-permute-start(f32[512,128]{1,0:T(8,128)S(1)} %get-tuple-element.104.refs_2_.refs_4_.refs_0_), channel_id=1, source_target_pairs={{2,0},{0,2},{3,1},{1,3},{6,4},{4,6},{7,5},{5,7},{10,8},{8,10},{11,... | collective-permute-start | bytes 786440 | tf_op jit(solution)/shard_map/ppermute | solution.py:59
  26.4 5.0 %collective-permute-start.6 = (bf16[512,128]{1,0:T(8,128)(2,1)S(1)}, bf16[512,128]{1,0:T(8,128)(2,1)S(1)}, u32[]{:S(2)}, u32[]{:S(2)}) collective-permute-start(bf16[512,128]{1,0:T(8,128)(2,1)S(1)} %collective-permute-done.5.refs_5_), channel_id=1, source_target_pairs={{1,0},{0,1},{3,2},{2,3},{5,4},{4,5},{7,6},{6,7},{9,8},{8,9},{11,10... | collective-permute-start | bytes 393224 | tf_op jit(solution)/shard_map/ppermute | solution.py:59
  26.4 5.0 %collective-permute-start.7 = (bf16[512,128]{1,0:T(8,128)(2,1)S(1)}, bf16[512,128]{1,0:T(8,128)(2,1)S(1)}, u32[]{:S(2)}, u32[]{:S(2)}) collective-permute-start(bf16[512,128]{1,0:T(8,128)(2,1)S(1)} %collective-permute-done.3.refs_7_), channel_id=1, source_target_pairs={{1,0},{0,1},{3,2},{2,3},{5,4},{4,5},{7,6},{6,7},{9,8},{8,9},{11,10... | collective-permute-start | bytes 393224 | tf_op jit(solution)/shard_map/ppermute | solution.py:59
  33.4 8.5 %collective-permute-start.11 = (f32[512,128]{1,0:T(8,128)S(1)}, f32[512,128]{1,0:T(8,128)S(1)}, u32[]{:S(2)}, u32[]{:S(2)}) collective-permute-start(f32[512,128]{1,0:T(8,128)S(1)} %get-tuple-element.107.refs_1_), channel_id=1, source_target_pairs={{2,0},{0,2},{3,1},{1,3},{6,4},{4,6},{7,5},{5,7},{10,8},{8,10},{11,... | collective-permute-start | bytes 786440 | tf_op jit(solution)/shard_map/ppermute | solution.py:59
  40.1 6.2 %collective-permute-start.10 = (f32[104,128]{1,0:T(8,128)S(1)}, f32[104,128]{1,0:T(8,128)S(1)}, u32[]{:S(2)}, u32[]{:S(2)}) collective-permute-start(f32[104,128]{1,0:T(8,128)S(1)} %add.51), channel_id=1, source_target_pairs={{8,0},{10,2},{12,4},{14,6},{0,8},{2,10},{4,12},{6,14},{9,1},{11,3}... | collective-permute-start | bytes 159752 | tf_op jit(solution)/shard_map/ppermute | solution.py:59
  46.6 6.1 %collective-permute-start.15 = (f32[176,128]{1,0:T(8,128)S(1)}, f32[176,128]{1,0:T(8,128)S(1)}, u32[]{:S(2)}, u32[]{:S(2)}) collective-permute-start(f32[176,128]{1,0:T(8,128)S(1)} %pad_maximum_fusion), channel_id=1, source_target_pairs={{6,0},{4,2},{2,4},{0,6},{14,8},{12,10},{10,12},{8,14},{7,1},{5,3},... | collective-permute-start | bytes 270344 | tf_op jit(solution)/shard_map/ppermute | solution.py:59
  48.2 5.4 %collective-permute-start.13 = (f32[176,128]{1,0:T(8,128)S(1)}, f32[176,128]{1,0:T(8,128)S(1)}, u32[]{:S(2)}, u32[]{:S(2)}) collective-permute-start(f32[176,128]{1,0:T(8,128)S(1)} %pad_maximum_fusion), channel_id=1, source_target_pairs={{2,0},{0,2},{6,4},{4,6},{10,8},{8,10},{14,12},{12,14},{3,1},{1,3},... | collective-permute-start | bytes 270344 | tf_op jit(solution)/shard_map/ppermute | solution.py:59
  53.7 8.9 %collective-permute-start.16 = (f32[72,128]{1,0:T(8,128)S(1)}, f32[72,128]{1,0:T(8,128)S(1)}, u32[]{:S(2)}, u32[]{:S(2)}) collective-permute-start(f32[72,128]{1,0:T(8,128)S(1)} %slice.16.refs_5_), channel_id=1, source_target_pairs={{8,0},{10,2},{12,4},{14,6},{0,8},{2,10},{4,12},{6,14},{9,1},{11,3}... | collective-permute-start | bytes 110600 | tf_op jit(solution)/shard_map/ppermute | solution.py:59
  64.5 7.3 %collective-permute-start.18 = (bf16[512,128]{1,0:T(8,128)(2,1)S(1)}, bf16[512,128]{1,0:T(8,128)(2,1)S(1)}, u32[]{:S(2)}, u32[]{:S(2)}) collective-permute-start(bf16[512,128]{1,0:T(8,128)(2,1)S(1)} %get-tuple-element.119.refs_1_), channel_id=1, source_target_pairs={{4,0},{0,4},{12,8},{8,12},{5,1},{1,5},{13,9},{9,13},{6,2},{2,6},{1... | collective-permute-start | bytes 393224 | tf_op jit(solution)/shard_map/ppermute | solution.py:59
  65.8 12.9 %collective-permute-start.22 = (bf16[512,128]{1,0:T(8,128)(2,1)S(1)}, bf16[512,128]{1,0:T(8,128)(2,1)S(1)}, u32[]{:S(2)}, u32[]{:S(2)}) collective-permute-start(bf16[512,128]{1,0:T(8,128)(2,1)S(1)} %get-tuple-element.119.refs_1_), channel_id=1, source_target_pairs={{8,0},{12,4},{0,8},{4,12},{9,1},{13,5},{1,9},{5,13},{10,2},{14,6},... | collective-permute-start | bytes 393224 | tf_op jit(solution)/shard_map/ppermute | solution.py:59
  66.9 11.7 %collective-permute-start.20 = (bf16[512,128]{1,0:T(8,128)(2,1)S(1)}, bf16[512,128]{1,0:T(8,128)(2,1)S(1)}, u32[]{:S(2)}, u32[]{:S(2)}) collective-permute-start(bf16[512,128]{1,0:T(8,128)(2,1)S(1)} %get-tuple-element.119.refs_1_), channel_id=1, source_target_pairs={{12,0},{8,4},{4,8},{0,12},{13,1},{9,5},{5,9},{1,13},{14,2},{10,6},... | collective-permute-start | bytes 393224 | tf_op jit(solution)/shard_map/ppermute | solution.py:59
  71.8 6.8 %collective-permute-start.21 = (bf16[512,128]{1,0:T(8,128)(2,1)S(1)}, bf16[512,128]{1,0:T(8,128)(2,1)S(1)}, u32[]{:S(2)}, u32[]{:S(2)}) collective-permute-start(bf16[512,128]{1,0:T(8,128)(2,1)S(1)} %collective-permute-done.18.refs_3_), channel_id=1, source_target_pairs={{1,0},{0,1},{3,2},{2,3},{5,4},{4,5},{7,6},{6,7},{9,8},{8,9},{11,10... | collective-permute-start | bytes 393224 | tf_op jit(solution)/shard_map/ppermute | solution.py:59
  71.8 8.7 %collective-permute-start.25 = (f32[512,128]{1,0:T(8,128)S(1)}, f32[512,128]{1,0:T(8,128)S(1)}, u32[]{:S(2)}, u32[]{:S(2)}) collective-permute-start(f32[512,128]{1,0:T(8,128)S(1)} %get-tuple-element.129.refs_2_.refs_4_.refs_0_), channel_id=1, source_target_pairs={{2,0},{0,2},{3,1},{1,3},{6,4},{4,6},{7,5},{5,7},{10,8},{8,10},{11,... | collective-permute-start | bytes 786440 | tf_op jit(solution)/shard_map/ppermute | solution.py:59
  82.5 8.9 %collective-permute-start.28 = (f32[512,128]{1,0:T(8,128)S(1)}, f32[512,128]{1,0:T(8,128)S(1)}, u32[]{:S(2)}, u32[]{:S(2)}) collective-permute-start(f32[512,128]{1,0:T(8,128)S(1)} %get-tuple-element.132.refs_1_), channel_id=1, source_target_pairs={{2,0},{0,2},{3,1},{1,3},{6,4},{4,6},{7,5},{5,7},{10,8},{8,10},{11,... | collective-permute-start | bytes 786440 | tf_op jit(solution)/shard_map/ppermute | solution.py:59
  89.3 5.1 %collective-permute-start.27 = (f32[104,128]{1,0:T(8,128)S(1)}, f32[104,128]{1,0:T(8,128)S(1)}, u32[]{:S(2)}, u32[]{:S(2)}) collective-permute-start(f32[104,128]{1,0:T(8,128)S(1)} %add.57), channel_id=1, source_target_pairs={{8,0},{10,2},{12,4},{14,6},{0,8},{2,10},{4,12},{6,14},{9,1},{11,3}... | collective-permute-start | bytes 159752 | tf_op jit(solution)/shard_map/ppermute | solution.py:59
  94.4 5.1 %collective-permute-start.31 = (f32[176,128]{1,0:T(8,128)S(1)}, f32[176,128]{1,0:T(8,128)S(1)}, u32[]{:S(2)}, u32[]{:S(2)}) collective-permute-start(f32[176,128]{1,0:T(8,128)S(1)} %pad_maximum_fusion.1), channel_id=1, source_target_pairs={{4,0},{6,2},{0,4},{2,6},{12,8},{14,10},{8,12},{10,14},{5,1},{7,3},... | collective-permute-start | bytes 270344 | tf_op jit(solution)/shard_map/ppermute | solution.py:59
  96.7 5.5 %collective-permute-start.32 = (f32[176,128]{1,0:T(8,128)S(1)}, f32[176,128]{1,0:T(8,128)S(1)}, u32[]{:S(2)}, u32[]{:S(2)}) collective-permute-start(f32[176,128]{1,0:T(8,128)S(1)} %pad_maximum_fusion.1), channel_id=1, source_target_pairs={{6,0},{4,2},{2,4},{0,6},{14,8},{12,10},{10,12},{8,14},{7,1},{5,3},... | collective-permute-start | bytes 270344 | tf_op jit(solution)/shard_map/ppermute | solution.py:59
  96.8 6.0 %collective-permute-start.30 = (f32[176,128]{1,0:T(8,128)S(1)}, f32[176,128]{1,0:T(8,128)S(1)}, u32[]{:S(2)}, u32[]{:S(2)}) collective-permute-start(f32[176,128]{1,0:T(8,128)S(1)} %pad_maximum_fusion.1), channel_id=1, source_target_pairs={{2,0},{0,2},{6,4},{4,6},{10,8},{8,10},{14,12},{12,14},{3,1},{1,3},... | collective-permute-start | bytes 270344 | tf_op jit(solution)/shard_map/ppermute | solution.py:59
  102.9 9.0 %collective-permute-start.33 = (f32[72,128]{1,0:T(8,128)S(1)}, f32[72,128]{1,0:T(8,128)S(1)}, u32[]{:S(2)}, u32[]{:S(2)}) collective-permute-start(f32[72,128]{1,0:T(8,128)S(1)} %slice.18.refs_5_), channel_id=1, source_target_pairs={{8,0},{10,2},{12,4},{14,6},{0,8},{2,10},{4,12},{6,14},{9,1},{11,3}... | collective-permute-start | bytes 110600 | tf_op jit(solution)/shard_map/ppermute | solution.py:59
  113.8 7.7 %collective-permute-start.35 = (bf16[512,128]{1,0:T(8,128)(2,1)S(1)}, bf16[512,128]{1,0:T(8,128)(2,1)S(1)}, u32[]{:S(2)}, u32[]{:S(2)}) collective-permute-start(bf16[512,128]{1,0:T(8,128)(2,1)S(1)} %get-tuple-element.146.refs_1_), channel_id=1, source_target_pairs={{4,0},{0,4},{12,8},{8,12},{5,1},{1,5},{13,9},{9,13},{6,2},{2,6},{1... | collective-permute-start | bytes 393224 | tf_op jit(solution)/shard_map/ppermute | solution.py:59
  115.1 12.9 %collective-permute-start.39 = (bf16[512,128]{1,0:T(8,128)(2,1)S(1)}, bf16[512,128]{1,0:T(8,128)(2,1)S(1)}, u32[]{:S(2)}, u32[]{:S(2)}) collective-permute-start(bf16[512,128]{1,0:T(8,128)(2,1)S(1)} %get-tuple-element.146.refs_1_), channel_id=1, source_target_pairs={{8,0},{12,4},{0,8},{4,12},{9,1},{13,5},{1,9},{5,13},{10,2},{14,6},... | collective-permute-start | bytes 393224 | tf_op jit(solution)/shard_map/ppermute | solution.py:59
  116.3 11.7 %collective-permute-start.37 = (bf16[512,128]{1,0:T(8,128)(2,1)S(1)}, bf16[512,128]{1,0:T(8,128)(2,1)S(1)}, u32[]{:S(2)}, u32[]{:S(2)}) collective-permute-start(bf16[512,128]{1,0:T(8,128)(2,1)S(1)} %get-tuple-element.146.refs_1_), channel_id=1, source_target_pairs={{12,0},{8,4},{4,8},{0,12},{13,1},{9,5},{5,9},{1,13},{14,2},{10,6},... | collective-permute-start | bytes 393224 | tf_op jit(solution)/shard_map/ppermute | solution.py:59
  121.5 6.5 %collective-permute-start.38 = (bf16[512,128]{1,0:T(8,128)(2,1)S(1)}, bf16[512,128]{1,0:T(8,128)(2,1)S(1)}, u32[]{:S(2)}, u32[]{:S(2)}) collective-permute-start(bf16[512,128]{1,0:T(8,128)(2,1)S(1)} %collective-permute-done.35.refs_3_), channel_id=1, source_target_pairs={{1,0},{0,1},{3,2},{2,3},{5,4},{4,5},{7,6},{6,7},{9,8},{8,9},{11,10... | collective-permute-start | bytes 393224 | tf_op jit(solution)/shard_map/ppermute | solution.py:59
  121.5 8.7 %collective-permute-start.42 = (f32[512,128]{1,0:T(8,128)S(1)}, f32[512,128]{1,0:T(8,128)S(1)}, u32[]{:S(2)}, u32[]{:S(2)}) collective-permute-start(f32[512,128]{1,0:T(8,128)S(1)} %get-tuple-element.157.refs_2_.refs_3_), channel_id=1, source_target_pairs={{2,0},{0,2},{3,1},{1,3},{6,4},{4,6},{7,5},{5,7},{10,8},{8,10},{11,... | collective-permute-start | bytes 786440 | tf_op jit(solution)/shard_map/ppermute | solution.py:59
  137.1 4.9 %collective-permute-start.46 = (f32[72,128]{1,0:T(8,128)S(1)}, f32[72,128]{1,0:T(8,128)S(1)}, u32[]{:S(2)}, u32[]{:S(2)}) collective-permute-start(f32[72,128]{1,0:T(8,128)S(1)} %add.63), channel_id=1, source_target_pairs={{6,0},{4,2},{2,4},{0,6},{14,8},{12,10},{10,12},{8,14},{7,1},{5,3},... | collective-permute-start | bytes 110600 | tf_op jit(solution)/shard_map/ppermute | solution.py:59
  140.6 8.7 %collective-permute-start.48 = (f32[512,128]{1,0:T(8,128)S(1)}, f32[512,128]{1,0:T(8,128)S(1)}, u32[]{:S(2)}, u32[]{:S(2)}) collective-permute-start(f32[512,128]{1,0:T(8,128)S(1)} %get-tuple-element.160.refs_1_), channel_id=1, source_target_pairs={{2,0},{0,2},{3,1},{1,3},{6,4},{4,6},{7,5},{5,7},{10,8},{8,10},{11,... | collective-permute-start | bytes 786440 | tf_op jit(solution)/shard_map/ppermute | solution.py:59
  144.4 4.9 %collective-permute-start.47 = (f32[72,128]{1,0:T(8,128)S(1)}, f32[72,128]{1,0:T(8,128)S(1)}, u32[]{:S(2)}, u32[]{:S(2)}) collective-permute-start(f32[72,128]{1,0:T(8,128)S(1)} %add_add_fusion.2), channel_id=1, source_target_pairs={{8,0},{10,2},{12,4},{14,6},{0,8},{2,10},{4,12},{6,14},{9,1},{11,3}... | collective-permute-start | bytes 110600 | tf_op jit(solution)/shard_map/ppermute | solution.py:59
  (17 other events, 46.7 us)

commit v3 on v2

--- a/solution.py
+++ b/solution.py
@@ -220,27 +220,26 @@
         half = lax.axis_index("coef")
         own = pl.ds(pl.multiple_of(half * LANES, LANES), LANES)
         other = pl.ds(pl.multiple_of((1 - half) * LANES, LANES), LANES)
-        at = 0
         for g in range(many):
-            for _ in range(counts[g]):
-                weights[at : at + strip, own] = piece_refs[2 * g][...]
-                weights[at : at + strip, other] = piece_refs[2 * g + 1][...]
-                at += strip
+            weights[g, :, own] = piece_refs[2 * g][...]
+            weights[g, :, other] = piece_refs[2 * g + 1][...]
         me = lax.axis_index("rhs")
         for out, s in zip(outs, [None] if slots is None else slots):
             first = 0 if s is None else pl.multiple_of(mate(me, s, n) * size, size)
             for start in range(0, 2 * size, block):
                 here = slice(start, start + block)
-                left = jnp.concatenate(
-                    [
-                        k_refs[g][i, t, pl.ds(2 * first + start, block), :]
-                        for g in range(many)
-                        for i in range(counts[g])
-                        for t in range(tiles)
-                    ],
-                    axis=1,
-                )
-                product = jnp.dot(left, weights[...], preferred_element_type=F32)
+                product = None
+                for g in range(many):
+                    for i in range(counts[g]):
+                        left = jnp.concatenate(
+                            [
+                                k_refs[g][i, t, pl.ds(2 * first + start, block), :]
+                                for t in range(tiles)
+                            ],
+                            axis=1,
+                        )
+                        term = jnp.dot(left, weights[g], preferred_element_type=F32)
+                        product = term if product is None else product + term
                 even_acc[here, :] = product[:, :LANES]
                 odd_acc[here, :] = product[:, LANES:]
             even = even_acc[pl.ds(0, size, stride=2), :]
@@ -257,7 +256,7 @@
         [shape(size)] * (1 if slots is None else len(slots)),
         *args,
         scratch=[
-            pltpu.VMEM((sum(counts) * strip, 2 * LANES), BF16),
+            pltpu.VMEM((many, strip, 2 * LANES), BF16),
             pltpu.VMEM((2 * size, LANES), F32),
             pltpu.VMEM((2 * size, LANES), F32),
         ],
@@ -290,21 +289,24 @@
     return groups
 
 
-def operate(packed, groups, low, direction, between):
+def operate(packed, groups, low, direction, between, final):
     n = lax.axis_size("rhs")
     arrived = [low] + [bring(low) for bring, _, _ in groups[:0:-1]][::-1]
     directions = [direction] + [swapped(direction, "rhs", s, n) for s in range(1, n)]
     pairs = [[low, swapped(low, "coef", 1, 2)]]
     (acc,), token = link_products(packed[:1], pairs, None, n, None)
     after = (token, between(token))
-    for place, piece in enumerate(arrived[1:]):
+    for piece in arrived[1:]:
         piece, _ = lax.optimization_barrier((piece, after))
-        if place > 1:
-            piece, pairs[place - 1][1] = lax.optimization_barrier((piece, pairs[place - 1][1]))
         pairs.append([piece, swapped(piece, "coef", 1, 2)])
     after = (*after, *directions[1:])
-    mates, token = link_products(packed[1:], pairs[1:], acc, n, range(1, n), after)
-    own, _ = link_products(packed[1:], pairs[1:], acc, n, [0], (token,))
+    if len(groups) > 2:
+        (acc,), _ = link_products(packed[1:-1], pairs[1:-1], acc, n, None, after)
+    if final:
+        parts, _ = link_products(packed[-1:], pairs[-1:], acc, n, range(n), after)
+        return parts, directions
+    mates, token = link_products(packed[-1:], pairs[-1:], acc, n, range(1, n), after)
+    own, _ = link_products(packed[-1:], pairs[-1:], acc, n, [0], (token,))
     return own + mates, directions
 
 
@@ -450,14 +452,11 @@
         now = [
             [a[j], *(lanes_of(a[j], lane + SUB * j + i) for i in range(SUB))] for a in held
         ]
-        pivots = [values[1][:1] for values in now]
         for i in range(SUB):
             here = place == i
             for index, values in enumerate(now):
                 column = values[1 + i]
-                inverse = reciprocal(pivots[index])
-                if i + 1 < SUB:
-                    pivots[index] = next_pivot(column, values[2 + i], i, inverse)
+                inverse = 1.0 / column[i : i + 1]
 
                 def step(value):
                     row = value[i : i + 1] * inverse
@@ -707,7 +706,7 @@
             *state[:], token = stepped(solution, before, alpha, beta, token)
             return token
 
-        parts, directions = operate(packed, groups, low, direction, between)
+        parts, directions = operate(packed, groups, low, direction, between, final)
         solution, turns = state
         image_parts = [parts[0]] + [swapped(parts[s], "rhs", s, n) for s in range(1, n)]
         linear = linear_grams(parts, directions, residual, turns, first, final)

time: 155 us -> 146 us (0.942)
  waiting for transfers between devices: 44.5 us -> 35 us
  starting transfers between devices: 47.8 us -> 49.4 us
    ppermute x49, waiting for transfers between devices: 44.5 us -> 35 us  [permute(): return lax.ppermute(value, axis, pairs)]
    pallas_call x27 -> x29, Pallas kernels: 61 us -> 60.7 us  [call(): pl.pallas_call(ordered, out_shape=list(outs) + [shape(SUB)], in_specs=[HB...]
  transfers between devices with their start and end apart: 49 -> 49, of which waited for: 23 -> 23; matrix products, arithmetic and copies ran while one was open for 0% -> 0% of each run, Pallas kernels for 27% -> 31%
where the time goes in v3:
time: 146 us
  Pallas kernels  60.7 us (42%)
  starting transfers between devices  49.4 us (34%)
  waiting for transfers between devices  35 us (24%)
    pallas_call x29, Pallas kernels, call(): pl.pallas_call(ordered, out_shape=list(outs) + [shape(SUB)], in_specs=[HB...  60.7 us
    ppermute x49, starting transfers between devices, permute(): return lax.ppermute(value, axis, pairs)  49.4 us
    ppermute x49, waiting for transfers between devices, permute(): return lax.ppermute(value, axis, pairs)  35 us
  transfers between devices with their start and end apart: 49, of which 23 were waited for; matrix products, arithmetic and copies ran while one was open for 0% of the time, Pallas kernels for 31%

profile of v3, /device:TPU:0, one launch (start us, length us, event | category | flops | bytes accessed | tf_op | source)
XLA Modules:
  0.0 146.2 jit_solution(11248480600986988760)
XLA Ops:
  2.1 3.0 %collective-permute-start = (f32[512,128]{1,0:T(8,128)S(1)}, f32[512,128]{1,0:T(8,128)S(1)}, u32[]{:S(2)}, u32[]{:S(2)}) collective-permute-start(f32[512,128]{1,0:T(8,128)S(1)} %get-tuple-element.81), channel_id=1, source_target_pairs={{2,0},{0,2},{3,1},{1,3},{6,4},{4,6},{7,5},{5,7},{10,8},{8,10},{11,... | collective-permute-start | bytes 786440 | tf_op jit(solution)/shard_map/ppermute | solution.py:59
  5.1 2.9 %shard_map.51 = (bf16[3,4,1024,2,128]{4,3,2,1,0:T(2,128)(2,1)S(1)}, f32[8,128]{1,0:T(8,128)S(1)}) custom-call(bf16[9,1024,2,512]{3,2,1,0:T(2,128)(2,1)} %bitcast.22, f32[8,128]{1,0:T(8,128)S(1)} %get-tuple-element.82.refs_1_), custom_call_target="tpu_custom_call" | custom-call | flops 1 | bytes 1 | tf_op jit(solution)/shard_map/pallas_call | solution.py:43
  8.0 2.2 %shard_map.52 = (bf16[2,4,1024,2,128]{4,3,2,1,0:T(2,128)(2,1)S(1)}, f32[8,128]{1,0:T(8,128)S(1)}) custom-call(bf16[9,1024,2,512]{3,2,1,0:T(2,128)(2,1)} %bitcast.23, f32[8,128]{1,0:T(8,128)S(1)} %get-tuple-element.83.refs_1_), custom_call_target="tpu_custom_call" | custom-call | flops 1 | bytes 1 | tf_op jit(solution)/shard_map/pallas_call | solution.py:43
  11.6 2.9 %collective-permute-start.6 = (bf16[512,128]{1,0:T(8,128)(2,1)S(1)}, bf16[512,128]{1,0:T(8,128)(2,1)S(1)}, u32[]{:S(2)}, u32[]{:S(2)}) collective-permute-start(bf16[512,128]{1,0:T(8,128)(2,1)S(1)} %get-tuple-element.88.refs_1_), channel_id=1, source_target_pairs={{8,0},{12,4},{0,8},{4,12},{9,1},{13,5},{1,9},{5,13},{10,2},{14,6},... | collective-permute-start | bytes 393224 | tf_op jit(solution)/shard_map/ppermute | solution.py:59
  17.8 2.2 %shard_map.54 = (bf16[2,4,1024,2,128]{4,3,2,1,0:T(2,128)(2,1)S(1)}, f32[8,128]{1,0:T(8,128)S(1)}) custom-call(bf16[9,1024,2,512]{3,2,1,0:T(2,128)(2,1)} %bitcast.24, f32[8,128]{1,0:T(8,128)S(1)} %get-tuple-element.85.refs_1_), custom_call_target="tpu_custom_call" | custom-call | flops 1 | bytes 1 | tf_op jit(solution)/shard_map/pallas_call | solution.py:43
  20.0 2.2 %shard_map.55 = (bf16[2,4,1024,2,128]{4,3,2,1,0:T(2,128)(2,1)S(1)}, f32[8,128]{1,0:T(8,128)S(1)}) custom-call(bf16[9,1024,2,512]{3,2,1,0:T(2,128)(2,1)} %bitcast.25, f32[8,128]{1,0:T(8,128)S(1)} %get-tuple-element.86.refs_1_), custom_call_target="tpu_custom_call" | custom-call | flops 1 | bytes 1 | tf_op jit(solution)/shard_map/pallas_call | solution.py:43
  22.3 2.0 %shard_map.56 = (f32[1024,128]{1,0:T(8,128)S(1)}, f32[8,128]{1,0:T(8,128)S(1)}) custom-call(bf16[3,4,2048,128]{3,2,1,0:T(8,128)(2,1)S(1)} %bitcast.13, bf16[512,128]{1,0:T(8,128)(2,1)S(1)} %get-tuple-element.88.refs_1_, bf16[512,128]{1,0:T(8,128)(2,1)S(1)} %collective-permute-done.2.refs_2_), custom_call_target="tpu_custom_call" | custom-call | flops 1 | bytes 1 | tf_op jit(solution)/shard_map/pallas_call | solution.py:43
  25.8 3.0 %shard_map.57 = (f32[1024,128]{1,0:T(8,128)S(1)}, f32[8,128]{1,0:T(8,128)}) custom-call(bf16[2,4,2048,128]{3,2,1,0:T(8,128)(2,1)S(1)} %bitcast.16, bf16[2,4,2048,128]{3,2,1,0:T(8,128)(2,1)S(1)} %bitcast.19, bf16[512,128]{1,0:T(8,128)(2,1)S(1)} %collective-permute-done.4.refs_2_, bf16[512,128]{1,0:T(8,128)(2,1)S(1)} %collective-permute-done.5.refs_3_, ...), custom_call_target="tpu_custom_call" | custom-call | flops 1 | bytes 1 | tf_op jit(solution)/shard_map/pallas_call | solution.py:43
  34.6 4.3 %collective-permute-start.10 = (f32[104,128]{1,0:T(8,128)S(1)}, f32[104,128]{1,0:T(8,128)S(1)}, u32[]{:S(2)}, u32[]{:S(2)}) collective-permute-start(f32[104,128]{1,0:T(8,128)S(1)} %add.51), channel_id=1, source_target_pairs={{8,0},{10,2},{12,4},{14,6},{0,8},{2,10},{4,12},{6,14},{9,1},{11,3}... | collective-permute-start | bytes 159752 | tf_op jit(solution)/shard_map/ppermute | solution.py:59
  40.0 2.3 %collective-permute-done.10 = f32[104,128]{1,0:T(8,128)S(1)} collective-permute-done((f32[104,128]{1,0:T(8,128)S(1)}, f32[104,128]{1,0:T(8,128)S(1)}, u32[]{:S(2)}, u32[]{:S(2)}) %collective-permute-start.10) | collective-permute-done | bytes 53280 | tf_op jit(solution)/shard_map/ppermute | solution.py:59
  48.3 1.9 %collective-permute-done.15 = f32[176,128]{1,0:T(8,128)S(1)} collective-permute-done((f32[176,128]{1,0:T(8,128)S(1)}, f32[176,128]{1,0:T(8,128)S(1)}, u32[]{:S(2)}, u32[]{:S(2)}) %collective-permute-start.15) | collective-permute-done | bytes 90144 | tf_op jit(solution)/shard_map/ppermute | solution.py:59
  50.3 2.3 %collective-permute-start.16 = (f32[72,128]{1,0:T(8,128)S(1)}, f32[72,128]{1,0:T(8,128)S(1)}, u32[]{:S(2)}, u32[]{:S(2)}) collective-permute-start(f32[72,128]{1,0:T(8,128)S(1)} %slice.16.refs_5_), channel_id=1, source_target_pairs={{8,0},{10,2},{12,4},{14,6},{0,8},{2,10},{4,12},{6,14},{9,1},{11,3}... | collective-permute-start | bytes 110600 | tf_op jit(solution)/shard_map/ppermute | solution.py:59
  52.6 5.8 %shard_map.62 = (f32[512,128]{1,0:T(8,128)S(1)}, f32[128,128]{1,0:T(8,128)S(1)}, f32[128,128]{1,0:T(8,128)S(1)}, f32[128,128]{1,0:T(8,128)S(1)}, f32[8,128]{1,0:T(8,128)}) custom-call(f32[104,128]{1,0:T(8,128)S(1)} %slice.17.refs_0_, f32[104,128]{1,0:T(8,128)S(1)} %collective-permute-done.17.refs_1_, ...), custom_call_target="tpu_custom_call" | custom-call | flops 1 | bytes 1 | tf_op jit(solution)/shard_map/pallas_call | solution.py:43
  62.7 2.1 %collective-permute-start.18 = (bf16[512,128]{1,0:T(8,128)(2,1)S(1)}, bf16[512,128]{1,0:T(8,128)(2,1)S(1)}, u32[]{:S(2)}, u32[]{:S(2)}) collective-permute-start(bf16[512,128]{1,0:T(8,128)(2,1)S(1)} %get-tuple-element.114.refs_1_), channel_id=1, source_target_pairs={{12,0},{8,4},{4,8},{0,12},{13,1},{9,5},{5,9},{1,13},{14,2},{10,6},... | collective-permute-start | bytes 393224 | tf_op jit(solution)/shard_map/ppermute | solution.py:59
  66.3 2.0 %shard_map.64 = (f32[1024,128]{1,0:T(8,128)S(1)}, f32[8,128]{1,0:T(8,128)S(1)}) custom-call(bf16[3,4,2048,128]{3,2,1,0:T(8,128)(2,1)S(1)} %bitcast.14, bf16[512,128]{1,0:T(8,128)(2,1)S(1)} %get-tuple-element.114.refs_1_, bf16[512,128]{1,0:T(8,128)(2,1)S(1)} %collective-permute-done.19.refs_2_), custom_call_target="tpu_custom_call" | custom-call | flops 1 | bytes 1 | tf_op jit(solution)/shard_map/pallas_call | solution.py:43
  68.9 2.1 %collective-permute-done.23.refs_4_ = bf16[512,128]{1,0:T(8,128)(2,1)S(1)} collective-permute-done((bf16[512,128]{1,0:T(8,128)(2,1)S(1)}, bf16[512,128]{1,0:T(8,128)(2,1)S(1)}, u32[]{:S(2)}, u32[]{:S(2)}) %collective-permute-start.23) | collective-permute-done | bytes 131104 | tf_op jit(solution)/shard_map/ppermute | solution.py:59
  71.5 2.0 %collective-permute-done.18.refs_1_ = bf16[512,128]{1,0:T(8,128)(2,1)S(1)} collective-permute-done((bf16[512,128]{1,0:T(8,128)(2,1)S(1)}, bf16[512,128]{1,0:T(8,128)(2,1)S(1)}, u32[]{:S(2)}, u32[]{:S(2)}) %collective-permute-start.18) | collective-permute-done | bytes 131104 | tf_op jit(solution)/shard_map/ppermute | solution.py:59
  73.5 3.0 %shard_map.66 = (f32[1024,128]{1,0:T(8,128)S(1)}, f32[8,128]{1,0:T(8,128)}) custom-call(bf16[2,4,2048,128]{3,2,1,0:T(8,128)(2,1)S(1)} %bitcast.17, bf16[2,4,2048,128]{3,2,1,0:T(8,128)(2,1)S(1)} %bitcast.20, bf16[512,128]{1,0:T(8,128)(2,1)S(1)} %collective-permute-done.21.refs_2_, bf16[512,128]{1,0:T(8,128)(2,1)S(1)} %collective-permute-done.22.refs_3_, ...), custom_call_target="tpu_custom_call" | custom-call | flops 1 | bytes 1 | tf_op jit(solution)/shard_map/pallas_call | solution.py:43
  77.3 2.1 %collective-permute-start.28 = (f32[512,128]{1,0:T(8,128)S(1)}, f32[512,128]{1,0:T(8,128)S(1)}, u32[]{:S(2)}, u32[]{:S(2)}) collective-permute-start(f32[512,128]{1,0:T(8,128)S(1)} %get-tuple-element.126.refs_1_), channel_id=1, source_target_pairs={{2,0},{0,2},{3,1},{1,3},{6,4},{4,6},{7,5},{5,7},{10,8},{8,10},{11,... | collective-permute-start | bytes 786440 | tf_op jit(solution)/shard_map/ppermute | solution.py:59
  90.1 2.2 %collective-permute-start.31 = (f32[176,128]{1,0:T(8,128)S(1)}, f32[176,128]{1,0:T(8,128)S(1)}, u32[]{:S(2)}, u32[]{:S(2)}) collective-permute-start(f32[176,128]{1,0:T(8,128)S(1)} %pad_maximum_fusion.1), channel_id=1, source_target_pairs={{4,0},{6,2},{0,4},{2,6},{12,8},{14,10},{8,12},{10,14},{5,1},{7,3},... | collective-permute-start | bytes 270344 | tf_op jit(solution)/shard_map/ppermute | solution.py:59
  93.3 1.9 %collective-permute-done.31 = f32[176,128]{1,0:T(8,128)S(1)} collective-permute-done((f32[176,128]{1,0:T(8,128)S(1)}, f32[176,128]{1,0:T(8,128)S(1)}, u32[]{:S(2)}, u32[]{:S(2)}) %collective-permute-start.31) | collective-permute-done | bytes 90144 | tf_op jit(solution)/shard_map/ppermute | solution.py:59
  95.2 2.5 %collective-permute-done.32 = f32[176,128]{1,0:T(8,128)S(1)} collective-permute-done((f32[176,128]{1,0:T(8,128)S(1)}, f32[176,128]{1,0:T(8,128)S(1)}, u32[]{:S(2)}, u32[]{:S(2)}) %collective-permute-start.32) | collective-permute-done | bytes 90144 | tf_op jit(solution)/shard_map/ppermute | solution.py:59
  99.3 5.8 %shard_map.71 = (f32[512,128]{1,0:T(8,128)S(1)}, f32[128,128]{1,0:T(8,128)S(1)}, f32[128,128]{1,0:T(8,128)S(1)}, f32[128,128]{1,0:T(8,128)S(1)}, f32[8,128]{1,0:T(8,128)}) custom-call(f32[104,128]{1,0:T(8,128)S(1)} %slice.19.refs_0_, f32[104,128]{1,0:T(8,128)S(1)} %collective-permute-done.34.refs_1_, ...), custom_call_target="tpu_custom_call" | custom-call | flops 1 | bytes 1 | tf_op jit(solution)/shard_map/pallas_call | solution.py:43
  105.1 1.9 %shard_map.72 = (f32[512,128]{1,0:T(8,128)S(1)}, bf16[512,128]{1,0:T(8,128)(2,1)S(1)}, f32[128,128]{1,0:T(8,128)S(1)}, f32[128,128]{1,0:T(8,128)S(1)}, f32[8,128]{1,0:T(8,128)}) custom-call(f32[128,128]{1,0:T(8,128)S(1)} %get-tuple-element.135.refs_0_.refs_2_, f32[128,128]{1,0:T(8,128)S(1)} %get-tuple-element.136.refs_1_, ...), custom_call_target="tpu_custom_call" | custom-call | flops 1 | bytes 1 | tf_op jit(solution)/shard_map/pallas_call | solution.py:43
  112.2 2.0 %shard_map.73 = (f32[1024,128]{1,0:T(8,128)S(1)}, f32[8,128]{1,0:T(8,128)S(1)}) custom-call(bf16[3,4,2048,128]{3,2,1,0:T(8,128)(2,1)S(1)} %bitcast.15, bf16[512,128]{1,0:T(8,128)(2,1)S(1)} %get-tuple-element.140.refs_1_, bf16[512,128]{1,0:T(8,128)(2,1)S(1)} %collective-permute-done.36.refs_2_), custom_call_target="tpu_custom_call" | custom-call | flops 1 | bytes 1 | tf_op jit(solution)/shard_map/pallas_call | solution.py:43
  115.4 2.1 %collective-permute-done.40.refs_4_ = bf16[512,128]{1,0:T(8,128)(2,1)S(1)} collective-permute-done((bf16[512,128]{1,0:T(8,128)(2,1)S(1)}, bf16[512,128]{1,0:T(8,128)(2,1)S(1)}, u32[]{:S(2)}, u32[]{:S(2)}) %collective-permute-start.40) | collective-permute-done | bytes 131104 | tf_op jit(solution)/shard_map/ppermute | solution.py:59
  119.9 3.0 %shard_map.75 = (f32[1024,128]{1,0:T(8,128)S(1)}, f32[8,128]{1,0:T(8,128)}) custom-call(bf16[2,4,2048,128]{3,2,1,0:T(8,128)(2,1)S(1)} %bitcast.18, bf16[2,4,2048,128]{3,2,1,0:T(8,128)(2,1)S(1)} %bitcast.21, bf16[512,128]{1,0:T(8,128)(2,1)S(1)} %collective-permute-done.38.refs_2_, bf16[512,128]{1,0:T(8,128)(2,1)S(1)} %collective-permute-done.39.refs_3_, ...), custom_call_target="tpu_custom_call" | custom-call | flops 1 | bytes 1 | tf_op jit(solution)/shard_map/pallas_call | solution.py:43
  122.9 1.9 %shard_map.76 = (f32[512,128]{1,0:T(8,128)S(1)}, f32[512,128]{1,0:T(8,128)S(1)}, f32[8,128]{1,0:T(8,128)}) custom-call(bf16[2,4,2048,128]{3,2,1,0:T(8,128)(2,1)S(1)} %bitcast.12, bf16[512,128]{1,0:T(8,128)(2,1)S(1)} %collective-permute-done.35.refs_1_, bf16[512,128]{1,0:T(8,128)(2,1)S(1)} %collective-permute-done.37.refs_2_, ...), custom_call_target="tpu_custom_call" | custom-call | flops 1 | bytes 1 | tf_op jit(solution)/shard_map/pallas_call | solution.py:43
  128.7 2.3 %collective-permute-start.45 = (f32[72,128]{1,0:T(8,128)S(1)}, f32[72,128]{1,0:T(8,128)S(1)}, u32[]{:S(2)}, u32[]{:S(2)}) collective-permute-start(f32[72,128]{1,0:T(8,128)S(1)} %add.63), channel_id=1, source_target_pairs={{4,0},{6,2},{0,4},{2,6},{12,8},{14,10},{8,12},{10,14},{5,1},{7,3},... | collective-permute-start | bytes 110600 | tf_op jit(solution)/shard_map/ppermute | solution.py:59
  132.9 3.0 %collective-permute-done.46 = f32[72,128]{1,0:T(8,128)S(1)} collective-permute-done((f32[72,128]{1,0:T(8,128)S(1)}, f32[72,128]{1,0:T(8,128)S(1)}, u32[]{:S(2)}, u32[]{:S(2)}) %collective-permute-start.46) | collective-permute-done | bytes 36896 | tf_op jit(solution)/shard_map/ppermute | solution.py:59
  137.2 3.8 %collective-permute-done.47 = f32[72,128]{1,0:T(8,128)S(1)} collective-permute-done((f32[72,128]{1,0:T(8,128)S(1)}, f32[72,128]{1,0:T(8,128)S(1)}, u32[]{:S(2)}, u32[]{:S(2)}) %collective-permute-start.47) | collective-permute-done | bytes 36896 | tf_op jit(solution)/shard_map/ppermute | solution.py:59
  141.0 5.2 %shard_map.78 = (f32[512,128]{1,0:T(8,128)}, f32[512,128]{1,0:T(8,128)}, f32[8,128]{1,0:T(8,128)}) custom-call(f32[72,128]{1,0:T(8,128)S(1)} %add.67.refs_0_, f32[128,128]{1,0:T(8,128)S(1)} %get-tuple-element.154.refs_1_, f32[512,128]{1,0:T(8,128)S(1)} %get-tuple-element.138.refs_3_.refs_2_, f32[512,128]{1,0:T(8,128)S(1)} %get-tuple-element.149.refs_2_.refs_3_, ...), custom_call_target="tpu_custom_call" | custom-call | flops 1 | bytes 1 | tf_op jit(solution)/shard_map/pallas_call | solution.py:43
  (112 shorter events, 57.4 us)
Async XLA Ops:
  2.1 9.3 %collective-permute-start = (f32[512,128]{1,0:T(8,128)S(1)}, f32[512,128]{1,0:T(8,128)S(1)}, u32[]{:S(2)}, u32[]{:S(2)}) collective-permute-start(f32[512,128]{1,0:T(8,128)S(1)} %get-tuple-element.81), channel_id=1, source_target_pairs={{2,0},{0,2},{3,1},{1,3},{6,4},{4,6},{7,5},{5,7},{10,8},{8,10},{11,... | collective-permute-start | bytes 786440 | tf_op jit(solution)/shard_map/ppermute | solution.py:59
  11.5 10.7 %collective-permute-start.2 = (bf16[512,128]{1,0:T(8,128)(2,1)S(1)}, bf16[512,128]{1,0:T(8,128)(2,1)S(1)}, u32[]{:S(2)}, u32[]{:S(2)}) collective-permute-start(bf16[512,128]{1,0:T(8,128)(2,1)S(1)} %get-tuple-element.88.refs_1_), channel_id=1, source_target_pairs={{1,0},{0,1},{3,2},{2,3},{5,4},{4,5},{7,6},{6,7},{9,8},{8,9},{11,10... | collective-permute-start | bytes 393224 | tf_op jit(solution)/shard_map/ppermute | solution.py:59
  11.6 12.6 %collective-permute-start.6 = (bf16[512,128]{1,0:T(8,128)(2,1)S(1)}, bf16[512,128]{1,0:T(8,128)(2,1)S(1)}, u32[]{:S(2)}, u32[]{:S(2)}) collective-permute-start(bf16[512,128]{1,0:T(8,128)(2,1)S(1)} %get-tuple-element.88.refs_1_), channel_id=1, source_target_pairs={{8,0},{12,4},{0,8},{4,12},{9,1},{13,5},{1,9},{5,13},{10,2},{14,6},... | collective-permute-start | bytes 393224 | tf_op jit(solution)/shard_map/ppermute | solution.py:59
  14.5 9.8 %collective-permute-start.4 = (bf16[512,128]{1,0:T(8,128)(2,1)S(1)}, bf16[512,128]{1,0:T(8,128)(2,1)S(1)}, u32[]{:S(2)}, u32[]{:S(2)}) collective-permute-start(bf16[512,128]{1,0:T(8,128)(2,1)S(1)} %get-tuple-element.88.refs_1_), channel_id=1, source_target_pairs={{4,0},{0,4},{12,8},{8,12},{5,1},{1,5},{13,9},{9,13},{6,2},{2,6},{1... | collective-permute-start | bytes 393224 | tf_op jit(solution)/shard_map/ppermute | solution.py:59
  16.1 9.8 %collective-permute-start.8 = (f32[512,128]{1,0:T(8,128)S(1)}, f32[512,128]{1,0:T(8,128)S(1)}, u32[]{:S(2)}, u32[]{:S(2)}) collective-permute-start(f32[512,128]{1,0:T(8,128)S(1)} %get-tuple-element.98.refs_2_.refs_4_.refs_0_), channel_id=1, source_target_pairs={{2,0},{0,2},{3,1},{1,3},{6,4},{4,6},{7,5},{5,7},{10,8},{8,10},{11,... | collective-permute-start | bytes 786440 | tf_op jit(solution)/shard_map/ppermute | solution.py:59
  17.6 7.9 %collective-permute-start.1 = (bf16[512,128]{1,0:T(8,128)(2,1)S(1)}, bf16[512,128]{1,0:T(8,128)(2,1)S(1)}, u32[]{:S(2)}, u32[]{:S(2)}) collective-permute-start(bf16[512,128]{1,0:T(8,128)(2,1)S(1)} %get-tuple-element.88.refs_1_), channel_id=1, source_target_pairs={{12,0},{8,4},{4,8},{0,12},{13,1},{9,5},{5,9},{1,13},{14,2},{10,6},... | collective-permute-start | bytes 393224 | tf_op jit(solution)/shard_map/ppermute | solution.py:59
  29.7 9.3 %collective-permute-start.11 = (f32[512,128]{1,0:T(8,128)S(1)}, f32[512,128]{1,0:T(8,128)S(1)}, u32[]{:S(2)}, u32[]{:S(2)}) collective-permute-start(f32[512,128]{1,0:T(8,128)S(1)} %get-tuple-element.102.refs_1_), channel_id=1, source_target_pairs={{2,0},{0,2},{3,1},{1,3},{6,4},{4,6},{7,5},{5,7},{10,8},{8,10},{11,... | collective-permute-start | bytes 786440 | tf_op jit(solution)/shard_map/ppermute | solution.py:59
  34.6 7.6 %collective-permute-start.10 = (f32[104,128]{1,0:T(8,128)S(1)}, f32[104,128]{1,0:T(8,128)S(1)}, u32[]{:S(2)}, u32[]{:S(2)}) collective-permute-start(f32[104,128]{1,0:T(8,128)S(1)} %add.51), channel_id=1, source_target_pairs={{8,0},{10,2},{12,4},{14,6},{0,8},{2,10},{4,12},{6,14},{9,1},{11,3}... | collective-permute-start | bytes 159752 | tf_op jit(solution)/shard_map/ppermute | solution.py:59
  42.3 4.6 %collective-permute-start.13 = (f32[176,128]{1,0:T(8,128)S(1)}, f32[176,128]{1,0:T(8,128)S(1)}, u32[]{:S(2)}, u32[]{:S(2)}) collective-permute-start(f32[176,128]{1,0:T(8,128)S(1)} %pad_maximum_fusion), channel_id=1, source_target_pairs={{2,0},{0,2},{6,4},{4,6},{10,8},{8,10},{14,12},{12,14},{3,1},{1,3},... | collective-permute-start | bytes 270344 | tf_op jit(solution)/shard_map/ppermute | solution.py:59
  42.9 5.4 %collective-permute-start.14 = (f32[176,128]{1,0:T(8,128)S(1)}, f32[176,128]{1,0:T(8,128)S(1)}, u32[]{:S(2)}, u32[]{:S(2)}) collective-permute-start(f32[176,128]{1,0:T(8,128)S(1)} %pad_maximum_fusion), channel_id=1, source_target_pairs={{4,0},{6,2},{0,4},{2,6},{12,8},{14,10},{8,12},{10,14},{5,1},{7,3},... | collective-permute-start | bytes 270344 | tf_op jit(solution)/shard_map/ppermute | solution.py:59
  44.2 6.0 %collective-permute-start.15 = (f32[176,128]{1,0:T(8,128)S(1)}, f32[176,128]{1,0:T(8,128)S(1)}, u32[]{:S(2)}, u32[]{:S(2)}) collective-permute-start(f32[176,128]{1,0:T(8,128)S(1)} %pad_maximum_fusion), channel_id=1, source_target_pairs={{6,0},{4,2},{2,4},{0,6},{14,8},{12,10},{10,12},{8,14},{7,1},{5,3},... | collective-permute-start | bytes 270344 | tf_op jit(solution)/shard_map/ppermute | solution.py:59
  50.3 8.1 %collective-permute-start.16 = (f32[72,128]{1,0:T(8,128)S(1)}, f32[72,128]{1,0:T(8,128)S(1)}, u32[]{:S(2)}, u32[]{:S(2)}) collective-permute-start(f32[72,128]{1,0:T(8,128)S(1)} %slice.16.refs_5_), channel_id=1, source_target_pairs={{8,0},{10,2},{12,4},{14,6},{0,8},{2,10},{4,12},{6,14},{9,1},{11,3}... | collective-permute-start | bytes 110600 | tf_op jit(solution)/shard_map/ppermute | solution.py:59
  60.3 6.0 %collective-permute-start.19 = (bf16[512,128]{1,0:T(8,128)(2,1)S(1)}, bf16[512,128]{1,0:T(8,128)(2,1)S(1)}, u32[]{:S(2)}, u32[]{:S(2)}) collective-permute-start(bf16[512,128]{1,0:T(8,128)(2,1)S(1)} %get-tuple-element.114.refs_1_), channel_id=1, source_target_pairs={{1,0},{0,1},{3,2},{2,3},{5,4},{4,5},{7,6},{6,7},{9,8},{8,9},{11,10... | collective-permute-start | bytes 393224 | tf_op jit(solution)/shard_map/ppermute | solution.py:59
  60.5 10.5 %collective-permute-start.23 = (bf16[512,128]{1,0:T(8,128)(2,1)S(1)}, bf16[512,128]{1,0:T(8,128)(2,1)S(1)}, u32[]{:S(2)}, u32[]{:S(2)}) collective-permute-start(bf16[512,128]{1,0:T(8,128)(2,1)S(1)} %get-tuple-element.114.refs_1_), channel_id=1, source_target_pairs={{8,0},{12,4},{0,8},{4,12},{9,1},{13,5},{1,9},{5,13},{10,2},{14,6},... | collective-permute-start | bytes 393224 | tf_op jit(solution)/shard_map/ppermute | solution.py:59
  61.6 9.4 %collective-permute-start.21 = (bf16[512,128]{1,0:T(8,128)(2,1)S(1)}, bf16[512,128]{1,0:T(8,128)(2,1)S(1)}, u32[]{:S(2)}, u32[]{:S(2)}) collective-permute-start(bf16[512,128]{1,0:T(8,128)(2,1)S(1)} %get-tuple-element.114.refs_1_), channel_id=1, source_target_pairs={{4,0},{0,4},{12,8},{8,12},{5,1},{1,5},{13,9},{9,13},{6,2},{2,6},{1... | collective-permute-start | bytes 393224 | tf_op jit(solution)/shard_map/ppermute | solution.py:59
  62.7 10.7 %collective-permute-start.18 = (bf16[512,128]{1,0:T(8,128)(2,1)S(1)}, bf16[512,128]{1,0:T(8,128)(2,1)S(1)}, u32[]{:S(2)}, u32[]{:S(2)}) collective-permute-start(bf16[512,128]{1,0:T(8,128)(2,1)S(1)} %get-tuple-element.114.refs_1_), channel_id=1, source_target_pairs={{12,0},{8,4},{4,8},{0,12},{13,1},{9,5},{5,9},{1,13},{14,2},{10,6},... | collective-permute-start | bytes 393224 | tf_op jit(solution)/shard_map/ppermute | solution.py:59
  64.8 8.6 %collective-permute-start.25 = (f32[512,128]{1,0:T(8,128)S(1)}, f32[512,128]{1,0:T(8,128)S(1)}, u32[]{:S(2)}, u32[]{:S(2)}) collective-permute-start(f32[512,128]{1,0:T(8,128)S(1)} %get-tuple-element.122.refs_2_.refs_4_.refs_0_), channel_id=1, source_target_pairs={{2,0},{0,2},{3,1},{1,3},{6,4},{4,6},{7,5},{5,7},{10,8},{8,10},{11,... | collective-permute-start | bytes 786440 | tf_op jit(solution)/shard_map/ppermute | solution.py:59
  77.3 8.8 %collective-permute-start.28 = (f32[512,128]{1,0:T(8,128)S(1)}, f32[512,128]{1,0:T(8,128)S(1)}, u32[]{:S(2)}, u32[]{:S(2)}) collective-permute-start(f32[512,128]{1,0:T(8,128)S(1)} %get-tuple-element.126.refs_1_), channel_id=1, source_target_pairs={{2,0},{0,2},{3,1},{1,3},{6,4},{4,6},{7,5},{5,7},{10,8},{8,10},{11,... | collective-permute-start | bytes 786440 | tf_op jit(solution)/shard_map/ppermute | solution.py:59
  83.6 5.1 %collective-permute-start.27 = (f32[104,128]{1,0:T(8,128)S(1)}, f32[104,128]{1,0:T(8,128)S(1)}, u32[]{:S(2)}, u32[]{:S(2)}) collective-permute-start(f32[104,128]{1,0:T(8,128)S(1)} %add.57), channel_id=1, source_target_pairs={{8,0},{10,2},{12,4},{14,6},{0,8},{2,10},{4,12},{6,14},{9,1},{11,3}... | collective-permute-start | bytes 159752 | tf_op jit(solution)/shard_map/ppermute | solution.py:59
  88.7 4.6 %collective-permute-start.30 = (f32[176,128]{1,0:T(8,128)S(1)}, f32[176,128]{1,0:T(8,128)S(1)}, u32[]{:S(2)}, u32[]{:S(2)}) collective-permute-start(f32[176,128]{1,0:T(8,128)S(1)} %pad_maximum_fusion.1), channel_id=1, source_target_pairs={{2,0},{0,2},{6,4},{4,6},{10,8},{8,10},{14,12},{12,14},{3,1},{1,3},... | collective-permute-start | bytes 270344 | tf_op jit(solution)/shard_map/ppermute | solution.py:59
  90.1 5.1 %collective-permute-start.31 = (f32[176,128]{1,0:T(8,128)S(1)}, f32[176,128]{1,0:T(8,128)S(1)}, u32[]{:S(2)}, u32[]{:S(2)}) collective-permute-start(f32[176,128]{1,0:T(8,128)S(1)} %pad_maximum_fusion.1), channel_id=1, source_target_pairs={{4,0},{6,2},{0,4},{2,6},{12,8},{14,10},{8,12},{10,14},{5,1},{7,3},... | collective-permute-start | bytes 270344 | tf_op jit(solution)/shard_map/ppermute | solution.py:59
  92.3 5.4 %collective-permute-start.32 = (f32[176,128]{1,0:T(8,128)S(1)}, f32[176,128]{1,0:T(8,128)S(1)}, u32[]{:S(2)}, u32[]{:S(2)}) collective-permute-start(f32[176,128]{1,0:T(8,128)S(1)} %pad_maximum_fusion.1), channel_id=1, source_target_pairs={{6,0},{4,2},{2,4},{0,6},{14,8},{12,10},{10,12},{8,14},{7,1},{5,3},... | collective-permute-start | bytes 270344 | tf_op jit(solution)/shard_map/ppermute | solution.py:59
  97.9 7.3 %collective-permute-start.33 = (f32[72,128]{1,0:T(8,128)S(1)}, f32[72,128]{1,0:T(8,128)S(1)}, u32[]{:S(2)}, u32[]{:S(2)}) collective-permute-start(f32[72,128]{1,0:T(8,128)S(1)} %slice.18.refs_5_), channel_id=1, source_target_pairs={{8,0},{10,2},{12,4},{14,6},{0,8},{2,10},{4,12},{6,14},{9,1},{11,3}... | collective-permute-start | bytes 110600 | tf_op jit(solution)/shard_map/ppermute | solution.py:59
  107.0 5.1 %collective-permute-start.36 = (bf16[512,128]{1,0:T(8,128)(2,1)S(1)}, bf16[512,128]{1,0:T(8,128)(2,1)S(1)}, u32[]{:S(2)}, u32[]{:S(2)}) collective-permute-start(bf16[512,128]{1,0:T(8,128)(2,1)S(1)} %get-tuple-element.140.refs_1_), channel_id=1, source_target_pairs={{1,0},{0,1},{3,2},{2,3},{5,4},{4,5},{7,6},{6,7},{9,8},{8,9},{11,10... | collective-permute-start | bytes 393224 | tf_op jit(solution)/shard_map/ppermute | solution.py:59
  107.2 10.3 %collective-permute-start.40 = (bf16[512,128]{1,0:T(8,128)(2,1)S(1)}, bf16[512,128]{1,0:T(8,128)(2,1)S(1)}, u32[]{:S(2)}, u32[]{:S(2)}) collective-permute-start(bf16[512,128]{1,0:T(8,128)(2,1)S(1)} %get-tuple-element.140.refs_1_), channel_id=1, source_target_pairs={{8,0},{12,4},{0,8},{4,12},{9,1},{13,5},{1,9},{5,13},{10,2},{14,6},... | collective-permute-start | bytes 393224 | tf_op jit(solution)/shard_map/ppermute | solution.py:59
  108.7 8.8 %collective-permute-start.38 = (bf16[512,128]{1,0:T(8,128)(2,1)S(1)}, bf16[512,128]{1,0:T(8,128)(2,1)S(1)}, u32[]{:S(2)}, u32[]{:S(2)}) collective-permute-start(bf16[512,128]{1,0:T(8,128)(2,1)S(1)} %get-tuple-element.140.refs_1_), channel_id=1, source_target_pairs={{4,0},{0,4},{12,8},{8,12},{5,1},{1,5},{13,9},{9,13},{6,2},{2,6},{1... | collective-permute-start | bytes 393224 | tf_op jit(solution)/shard_map/ppermute | solution.py:59
  109.8 10.1 %collective-permute-start.42 = (f32[512,128]{1,0:T(8,128)S(1)}, f32[512,128]{1,0:T(8,128)S(1)}, u32[]{:S(2)}, u32[]{:S(2)}) collective-permute-start(f32[512,128]{1,0:T(8,128)S(1)} %get-tuple-element.149.refs_2_.refs_3_), channel_id=1, source_target_pairs={{2,0},{0,2},{3,1},{1,3},{6,4},{4,6},{7,5},{5,7},{10,8},{8,10},{11,... | collective-permute-start | bytes 786440 | tf_op jit(solution)/shard_map/ppermute | solution.py:59
  111.1 8.8 %collective-permute-start.35 = (bf16[512,128]{1,0:T(8,128)(2,1)S(1)}, bf16[512,128]{1,0:T(8,128)(2,1)S(1)}, u32[]{:S(2)}, u32[]{:S(2)}) collective-permute-start(bf16[512,128]{1,0:T(8,128)(2,1)S(1)} %get-tuple-element.140.refs_1_), channel_id=1, source_target_pairs={{12,0},{8,4},{4,8},{0,12},{13,1},{9,5},{5,9},{1,13},{14,2},{10,6},... | collective-permute-start | bytes 393224 | tf_op jit(solution)/shard_map/ppermute | solution.py:59
  127.4 5.0 %collective-permute-start.44 = (f32[72,128]{1,0:T(8,128)S(1)}, f32[72,128]{1,0:T(8,128)S(1)}, u32[]{:S(2)}, u32[]{:S(2)}) collective-permute-start(f32[72,128]{1,0:T(8,128)S(1)} %add.63), channel_id=1, source_target_pairs={{2,0},{0,2},{6,4},{4,6},{10,8},{8,10},{14,12},{12,14},{3,1},{1,3},... | collective-permute-start | bytes 110600 | tf_op jit(solution)/shard_map/ppermute | solution.py:59
  130.9 5.0 %collective-permute-start.46 = (f32[72,128]{1,0:T(8,128)S(1)}, f32[72,128]{1,0:T(8,128)S(1)}, u32[]{:S(2)}, u32[]{:S(2)}) collective-permute-start(f32[72,128]{1,0:T(8,128)S(1)} %add.63), channel_id=1, source_target_pairs={{6,0},{4,2},{2,4},{0,6},{14,8},{12,10},{10,12},{8,14},{7,1},{5,3},... | collective-permute-start | bytes 110600 | tf_op jit(solution)/shard_map/ppermute | solution.py:59
  131.8 9.1 %collective-permute-start.48 = (f32[512,128]{1,0:T(8,128)S(1)}, f32[512,128]{1,0:T(8,128)S(1)}, u32[]{:S(2)}, u32[]{:S(2)}) collective-permute-start(f32[512,128]{1,0:T(8,128)S(1)} %get-tuple-element.152.refs_1_), channel_id=1, source_target_pairs={{2,0},{0,2},{3,1},{1,3},{6,4},{4,6},{7,5},{5,7},{10,8},{8,10},{11,... | collective-permute-start | bytes 786440 | tf_op jit(solution)/shard_map/ppermute | solution.py:59
  135.9 5.0 %collective-permute-start.47 = (f32[72,128]{1,0:T(8,128)S(1)}, f32[72,128]{1,0:T(8,128)S(1)}, u32[]{:S(2)}, u32[]{:S(2)}) collective-permute-start(f32[72,128]{1,0:T(8,128)S(1)} %add_add_fusion.2), channel_id=1, source_target_pairs={{8,0},{10,2},{12,4},{14,6},{0,8},{2,10},{4,12},{6,14},{9,1},{11,3}... | collective-permute-start | bytes 110600 | tf_op jit(solution)/shard_map/ppermute | solution.py:59
  (17 other events, 38.1 us)

commit v4 on v3

--- a/solution.py
+++ b/solution.py
@@ -270,7 +270,7 @@
     panels = lax.axis_size("panel")
     groups = []
     if links == 2 * panels + 1 and panels & (panels - 1) == 0:
-        for s in range(panels):
+        for s in sorted(range(panels), key=lambda s: (s > 0, s % 2)):
 
             def numbers(s=s):
                 me = lax.axis_index("panel")
@@ -358,24 +358,23 @@
         images, ds = refs[:n], refs[n : 2 * n]
         rest = refs[2 * n : 2 * n + len(extra)]
         outs = refs[2 * n + len(extra) :]
-        curve = cross = None
+        found = None
         for s in range(n):
-            image, d = images[s][...], ds[s][...]
-            term = mm(d, image, (0, 0))
-            curve = term if s == 0 else curve + term
+            image, right = images[s][...], ds[s][...]
             if extra:
-                r = rest[0][...] if s == 0 else d - rest[s][...]
-                term = mm(r, image, (0, 0))
-                cross = term if s == 0 else cross + term
+                r = rest[0][...] if s == 0 else right - rest[s][...]
+                right = jnp.concatenate([right, r], axis=1)
+            term = mm(image, right, (0, 0))
+            found = term if s == 0 else found + term
         if final:
-            outs[0][...] = packed_symmetric(symmetric(curve))
+            outs[0][...] = packed_symmetric(symmetric(found))
             return
         mine, mates, stacked = outs
         if first:
             r = ds[0][...]
-            sym, whole = mm(r, r, (0, 0)), curve
+            sym, whole = mm(r, r, (0, 0)), found
         else:
-            sym, whole = symmetric(curve), cross
+            sym, whole = symmetric(found[:, :LANES]), found[:, LANES:]
         stacked[:PACKED] = packed_symmetric(sym)
         stacked[PACKED : PACKED + SUB] = jnp.zeros((SUB, LANES), F32)
         stacked[PACKED + SUB :] = whole
@@ -634,7 +633,7 @@
         curvature = symmetric(whole) if first else sym
         alpha, inverse_out[...] = eliminated((curvature, g), (g, identity()))
         new_r[...] = r[...] - mm(image[...], alpha)
-        shared = mm(whole, alpha)
+        shared = mm(whole, alpha, (0, 0))
         alpha_out[...] = alpha
         partial[...] = g - (shared + shared.T)
 

time: 146 us -> 149 us (1.021)
  waiting for transfers between devices: 35 us -> 41.3 us
  starting transfers between devices: 49.4 us -> 46.1 us
    ppermute x49, waiting for transfers between devices: 35 us -> 41.3 us  [permute(): return lax.ppermute(value, axis, pairs)]
    ppermute x49, starting transfers between devices: 49.4 us -> 46.1 us  [permute(): return lax.ppermute(value, axis, pairs)]
  transfers between devices with their start and end apart: 49 -> 49, of which waited for: 23 -> 23; matrix products, arithmetic and copies ran while one was open for 0% -> 0% of each run, Pallas kernels for 31% -> 30%
where the time goes in v4:
time: 149 us; the launch traced here: 148 us
  Pallas kernels  60 us (40%)
  starting transfers between devices  46.1 us (31%)
  waiting for transfers between devices  41.3 us (28%)
    pallas_call x29, Pallas kernels, call(): pl.pallas_call(ordered, out_shape=list(outs) + [shape(SUB)], in_specs=[HB...  60 us
    ppermute x49, starting transfers between devices, permute(): return lax.ppermute(value, axis, pairs)  46.1 us
    ppermute x49, waiting for transfers between devices, permute(): return lax.ppermute(value, axis, pairs)  41.3 us
  transfers between devices with their start and end apart: 49, of which 23 were waited for; matrix products, arithmetic and copies ran while one was open for 0% of the time, Pallas kernels for 30%

profile of v4, /device:TPU:0, one launch (start us, length us, event | category | flops | bytes accessed | tf_op | source)
XLA Modules:
  0.0 148.5 jit_solution(12975323124241328023)
XLA Ops:
  2.1 3.0 %collective-permute-start = (f32[512,128]{1,0:T(8,128)S(1)}, f32[512,128]{1,0:T(8,128)S(1)}, u32[]{:S(2)}, u32[]{:S(2)}) collective-permute-start(f32[512,128]{1,0:T(8,128)S(1)} %get-tuple-element.81), channel_id=1, source_target_pairs={{2,0},{0,2},{3,1},{1,3},{6,4},{4,6},{7,5},{5,7},{10,8},{8,10},{11,... | collective-permute-start | bytes 786440 | tf_op jit(solution)/shard_map/ppermute | solution.py:59
  5.1 2.9 %shard_map.51 = (bf16[3,4,1024,2,128]{4,3,2,1,0:T(2,128)(2,1)S(1)}, f32[8,128]{1,0:T(8,128)S(1)}) custom-call(bf16[9,1024,2,512]{3,2,1,0:T(2,128)(2,1)} %bitcast.22, f32[8,128]{1,0:T(8,128)S(1)} %get-tuple-element.82.refs_1_), custom_call_target="tpu_custom_call" | custom-call | flops 1 | bytes 1 | tf_op jit(solution)/shard_map/pallas_call | solution.py:43
  8.0 2.2 %shard_map.52 = (bf16[2,4,1024,2,128]{4,3,2,1,0:T(2,128)(2,1)S(1)}, f32[8,128]{1,0:T(8,128)S(1)}) custom-call(bf16[9,1024,2,512]{3,2,1,0:T(2,128)(2,1)} %bitcast.23, f32[8,128]{1,0:T(8,128)S(1)} %get-tuple-element.83.refs_1_), custom_call_target="tpu_custom_call" | custom-call | flops 1 | bytes 1 | tf_op jit(solution)/shard_map/pallas_call | solution.py:43
  11.6 1.9 %collective-permute-start.6 = (bf16[512,128]{1,0:T(8,128)(2,1)S(1)}, bf16[512,128]{1,0:T(8,128)(2,1)S(1)}, u32[]{:S(2)}, u32[]{:S(2)}) collective-permute-start(bf16[512,128]{1,0:T(8,128)(2,1)S(1)} %get-tuple-element.88.refs_1_), channel_id=1, source_target_pairs={{4,0},{0,4},{12,8},{8,12},{5,1},{1,5},{13,9},{9,13},{6,2},{2,6},{1... | collective-permute-start | bytes 393224 | tf_op jit(solution)/shard_map/ppermute | solution.py:59
  13.5 2.6 %collective-permute-start.4 = (bf16[512,128]{1,0:T(8,128)(2,1)S(1)}, bf16[512,128]{1,0:T(8,128)(2,1)S(1)}, u32[]{:S(2)}, u32[]{:S(2)}) collective-permute-start(bf16[512,128]{1,0:T(8,128)(2,1)S(1)} %get-tuple-element.88.refs_1_), channel_id=1, source_target_pairs={{8,0},{12,4},{0,8},{4,12},{9,1},{13,5},{1,9},{5,13},{10,2},{14,6},... | collective-permute-start | bytes 393224 | tf_op jit(solution)/shard_map/ppermute | solution.py:59
  17.8 2.2 %shard_map.54 = (bf16[2,4,1024,2,128]{4,3,2,1,0:T(2,128)(2,1)S(1)}, f32[8,128]{1,0:T(8,128)S(1)}) custom-call(bf16[9,1024,2,512]{3,2,1,0:T(2,128)(2,1)} %bitcast.24, f32[8,128]{1,0:T(8,128)S(1)} %get-tuple-element.85.refs_1_), custom_call_target="tpu_custom_call" | custom-call | flops 1 | bytes 1 | tf_op jit(solution)/shard_map/pallas_call | solution.py:43
  20.0 2.2 %shard_map.55 = (bf16[2,4,1024,2,128]{4,3,2,1,0:T(2,128)(2,1)S(1)}, f32[8,128]{1,0:T(8,128)S(1)}) custom-call(bf16[9,1024,2,512]{3,2,1,0:T(2,128)(2,1)} %bitcast.25, f32[8,128]{1,0:T(8,128)S(1)} %get-tuple-element.86.refs_1_), custom_call_target="tpu_custom_call" | custom-call | flops 1 | bytes 1 | tf_op jit(solution)/shard_map/pallas_call | solution.py:43
  22.3 2.0 %shard_map.56 = (f32[1024,128]{1,0:T(8,128)S(1)}, f32[8,128]{1,0:T(8,128)S(1)}) custom-call(bf16[3,4,2048,128]{3,2,1,0:T(8,128)(2,1)S(1)} %bitcast.13, bf16[512,128]{1,0:T(8,128)(2,1)S(1)} %get-tuple-element.88.refs_1_, bf16[512,128]{1,0:T(8,128)(2,1)S(1)} %collective-permute-done.2.refs_2_), custom_call_target="tpu_custom_call" | custom-call | flops 1 | bytes 1 | tf_op jit(solution)/shard_map/pallas_call | solution.py:43
  27.4 3.0 %shard_map.57 = (f32[1024,128]{1,0:T(8,128)S(1)}, f32[8,128]{1,0:T(8,128)}) custom-call(bf16[2,4,2048,128]{3,2,1,0:T(8,128)(2,1)S(1)} %bitcast.16, bf16[2,4,2048,128]{3,2,1,0:T(8,128)(2,1)S(1)} %bitcast.19, bf16[512,128]{1,0:T(8,128)(2,1)S(1)} %collective-permute-done.4.refs_2_, bf16[512,128]{1,0:T(8,128)(2,1)S(1)} %collective-permute-done.5.refs_3_, ...), custom_call_target="tpu_custom_call" | custom-call | flops 1 | bytes 1 | tf_op jit(solution)/shard_map/pallas_call | solution.py:43
  31.2 1.9 %collective-permute-start.11 = (f32[512,128]{1,0:T(8,128)S(1)}, f32[512,128]{1,0:T(8,128)S(1)}, u32[]{:S(2)}, u32[]{:S(2)}) collective-permute-start(f32[512,128]{1,0:T(8,128)S(1)} %get-tuple-element.102.refs_1_), channel_id=1, source_target_pairs={{2,0},{0,2},{3,1},{1,3},{6,4},{4,6},{7,5},{5,7},{10,8},{8,10},{11,... | collective-permute-start | bytes 786440 | tf_op jit(solution)/shard_map/ppermute | solution.py:59
  36.9 2.3 %collective-permute-start.10 = (f32[104,128]{1,0:T(8,128)S(1)}, f32[104,128]{1,0:T(8,128)S(1)}, u32[]{:S(2)}, u32[]{:S(2)}) collective-permute-start(f32[104,128]{1,0:T(8,128)S(1)} %add.51), channel_id=1, source_target_pairs={{8,0},{10,2},{12,4},{14,6},{0,8},{2,10},{4,12},{6,14},{9,1},{11,3}... | collective-permute-start | bytes 159752 | tf_op jit(solution)/shard_map/ppermute | solution.py:59
  40.8 2.3 %collective-permute-done.10 = f32[104,128]{1,0:T(8,128)S(1)} collective-permute-done((f32[104,128]{1,0:T(8,128)S(1)}, f32[104,128]{1,0:T(8,128)S(1)}, u32[]{:S(2)}, u32[]{:S(2)}) %collective-permute-start.10) | collective-permute-done | bytes 53280 | tf_op jit(solution)/shard_map/ppermute | solution.py:59
  49.1 2.0 %collective-permute-done.15 = f32[176,128]{1,0:T(8,128)S(1)} collective-permute-done((f32[176,128]{1,0:T(8,128)S(1)}, f32[176,128]{1,0:T(8,128)S(1)}, u32[]{:S(2)}, u32[]{:S(2)}) %collective-permute-start.15) | collective-permute-done | bytes 90144 | tf_op jit(solution)/shard_map/ppermute | solution.py:59
  51.2 1.8 %collective-permute-start.16 = (f32[72,128]{1,0:T(8,128)S(1)}, f32[72,128]{1,0:T(8,128)S(1)}, u32[]{:S(2)}, u32[]{:S(2)}) collective-permute-start(f32[72,128]{1,0:T(8,128)S(1)} %slice.16.refs_5_), channel_id=1, source_target_pairs={{8,0},{10,2},{12,4},{14,6},{0,8},{2,10},{4,12},{6,14},{9,1},{11,3}... | collective-permute-start | bytes 110600 | tf_op jit(solution)/shard_map/ppermute | solution.py:59
  53.0 5.8 %shard_map.62 = (f32[512,128]{1,0:T(8,128)S(1)}, f32[128,128]{1,0:T(8,128)S(1)}, f32[128,128]{1,0:T(8,128)S(1)}, f32[128,128]{1,0:T(8,128)S(1)}, f32[8,128]{1,0:T(8,128)}) custom-call(f32[104,128]{1,0:T(8,128)S(1)} %slice.17.refs_0_, f32[104,128]{1,0:T(8,128)S(1)} %collective-permute-done.17.refs_1_, ...), custom_call_target="tpu_custom_call" | custom-call | flops 1 | bytes 1 | tf_op jit(solution)/shard_map/pallas_call | solution.py:43
  58.9 1.8 %shard_map.63 = (f32[512,128]{1,0:T(8,128)S(1)}, bf16[512,128]{1,0:T(8,128)(2,1)S(1)}, f32[128,128]{1,0:T(8,128)S(1)}, f32[128,128]{1,0:T(8,128)S(1)}, f32[8,128]{1,0:T(8,128)}) custom-call(f32[128,128]{1,0:T(8,128)S(1)} %get-tuple-element.109.refs_0_.refs_2_, f32[128,128]{1,0:T(8,128)S(1)} %get-tuple-element.110.refs_1_, ...), custom_call_target="tpu_custom_call" | custom-call | flops 1 | bytes 1 | tf_op jit(solution)/shard_map/pallas_call | solution.py:43
  63.3 2.0 %collective-permute-start.18 = (bf16[512,128]{1,0:T(8,128)(2,1)S(1)}, bf16[512,128]{1,0:T(8,128)(2,1)S(1)}, u32[]{:S(2)}, u32[]{:S(2)}) collective-permute-start(bf16[512,128]{1,0:T(8,128)(2,1)S(1)} %get-tuple-element.114.refs_1_), channel_id=1, source_target_pairs={{12,0},{8,4},{4,8},{0,12},{13,1},{9,5},{5,9},{1,13},{14,2},{10,6},... | collective-permute-start | bytes 393224 | tf_op jit(solution)/shard_map/ppermute | solution.py:59
  66.7 2.0 %shard_map.64 = (f32[1024,128]{1,0:T(8,128)S(1)}, f32[8,128]{1,0:T(8,128)S(1)}) custom-call(bf16[3,4,2048,128]{3,2,1,0:T(8,128)(2,1)S(1)} %bitcast.14, bf16[512,128]{1,0:T(8,128)(2,1)S(1)} %get-tuple-element.114.refs_1_, bf16[512,128]{1,0:T(8,128)(2,1)S(1)} %collective-permute-done.19.refs_2_), custom_call_target="tpu_custom_call" | custom-call | flops 1 | bytes 1 | tf_op jit(solution)/shard_map/pallas_call | solution.py:43
  69.3 5.7 %collective-permute-done.21.refs_2_ = bf16[512,128]{1,0:T(8,128)(2,1)S(1)} collective-permute-done((bf16[512,128]{1,0:T(8,128)(2,1)S(1)}, bf16[512,128]{1,0:T(8,128)(2,1)S(1)}, u32[]{:S(2)}, u32[]{:S(2)}) %collective-permute-start.21) | collective-permute-done | bytes 131104 | tf_op jit(solution)/shard_map/ppermute | solution.py:59
  76.4 3.0 %shard_map.66 = (f32[1024,128]{1,0:T(8,128)S(1)}, f32[8,128]{1,0:T(8,128)}) custom-call(bf16[2,4,2048,128]{3,2,1,0:T(8,128)(2,1)S(1)} %bitcast.17, bf16[2,4,2048,128]{3,2,1,0:T(8,128)(2,1)S(1)} %bitcast.20, bf16[512,128]{1,0:T(8,128)(2,1)S(1)} %collective-permute-done.21.refs_2_, bf16[512,128]{1,0:T(8,128)(2,1)S(1)} %collective-permute-done.22.refs_3_, ...), custom_call_target="tpu_custom_call" | custom-call | flops 1 | bytes 1 | tf_op jit(solution)/shard_map/pallas_call | solution.py:43
  84.8 1.8 %collective-permute-start.27 = (f32[104,128]{1,0:T(8,128)S(1)}, f32[104,128]{1,0:T(8,128)S(1)}, u32[]{:S(2)}, u32[]{:S(2)}) collective-permute-start(f32[104,128]{1,0:T(8,128)S(1)} %add.57), channel_id=1, source_target_pairs={{8,0},{10,2},{12,4},{14,6},{0,8},{2,10},{4,12},{6,14},{9,1},{11,3}... | collective-permute-start | bytes 159752 | tf_op jit(solution)/shard_map/ppermute | solution.py:59
  86.6 2.0 %collective-permute-done.28.refs_1_ = f32[512,128]{1,0:T(8,128)S(1)} collective-permute-done((f32[512,128]{1,0:T(8,128)S(1)}, f32[512,128]{1,0:T(8,128)S(1)}, u32[]{:S(2)}, u32[]{:S(2)}) %collective-permute-start.28) | collective-permute-done | bytes 262176 | tf_op jit(solution)/shard_map/ppermute | solution.py:59
  95.6 1.9 %collective-permute-done.31 = f32[176,128]{1,0:T(8,128)S(1)} collective-permute-done((f32[176,128]{1,0:T(8,128)S(1)}, f32[176,128]{1,0:T(8,128)S(1)}, u32[]{:S(2)}, u32[]{:S(2)}) %collective-permute-start.31) | collective-permute-done | bytes 90144 | tf_op jit(solution)/shard_map/ppermute | solution.py:59
  100.5 5.8 %shard_map.71 = (f32[512,128]{1,0:T(8,128)S(1)}, f32[128,128]{1,0:T(8,128)S(1)}, f32[128,128]{1,0:T(8,128)S(1)}, f32[128,128]{1,0:T(8,128)S(1)}, f32[8,128]{1,0:T(8,128)}) custom-call(f32[104,128]{1,0:T(8,128)S(1)} %slice.19.refs_0_, f32[104,128]{1,0:T(8,128)S(1)} %collective-permute-done.34.refs_1_, ...), custom_call_target="tpu_custom_call" | custom-call | flops 1 | bytes 1 | tf_op jit(solution)/shard_map/pallas_call | solution.py:43
  111.8 2.0 %collective-permute-start.35 = (bf16[512,128]{1,0:T(8,128)(2,1)S(1)}, bf16[512,128]{1,0:T(8,128)(2,1)S(1)}, u32[]{:S(2)}, u32[]{:S(2)}) collective-permute-start(bf16[512,128]{1,0:T(8,128)(2,1)S(1)} %get-tuple-element.140.refs_1_), channel_id=1, source_target_pairs={{12,0},{8,4},{4,8},{0,12},{13,1},{9,5},{5,9},{1,13},{14,2},{10,6},... | collective-permute-start | bytes 393224 | tf_op jit(solution)/shard_map/ppermute | solution.py:59
  113.8 2.0 %shard_map.73 = (f32[1024,128]{1,0:T(8,128)S(1)}, f32[8,128]{1,0:T(8,128)S(1)}) custom-call(bf16[3,4,2048,128]{3,2,1,0:T(8,128)(2,1)S(1)} %bitcast.15, bf16[512,128]{1,0:T(8,128)(2,1)S(1)} %get-tuple-element.140.refs_1_, bf16[512,128]{1,0:T(8,128)(2,1)S(1)} %collective-permute-done.36.refs_2_), custom_call_target="tpu_custom_call" | custom-call | flops 1 | bytes 1 | tf_op jit(solution)/shard_map/pallas_call | solution.py:43
  117.1 5.2 %collective-permute-done.38.refs_2_ = bf16[512,128]{1,0:T(8,128)(2,1)S(1)} collective-permute-done((bf16[512,128]{1,0:T(8,128)(2,1)S(1)}, bf16[512,128]{1,0:T(8,128)(2,1)S(1)}, u32[]{:S(2)}, u32[]{:S(2)}) %collective-permute-start.38) | collective-permute-done | bytes 131104 | tf_op jit(solution)/shard_map/ppermute | solution.py:59
  123.6 3.0 %shard_map.75 = (f32[1024,128]{1,0:T(8,128)S(1)}, f32[8,128]{1,0:T(8,128)}) custom-call(bf16[2,4,2048,128]{3,2,1,0:T(8,128)(2,1)S(1)} %bitcast.18, bf16[2,4,2048,128]{3,2,1,0:T(8,128)(2,1)S(1)} %bitcast.21, bf16[512,128]{1,0:T(8,128)(2,1)S(1)} %collective-permute-done.38.refs_2_, bf16[512,128]{1,0:T(8,128)(2,1)S(1)} %collective-permute-done.39.refs_3_, ...), custom_call_target="tpu_custom_call" | custom-call | flops 1 | bytes 1 | tf_op jit(solution)/shard_map/pallas_call | solution.py:43
  126.6 1.9 %shard_map.76 = (f32[512,128]{1,0:T(8,128)S(1)}, f32[512,128]{1,0:T(8,128)S(1)}, f32[8,128]{1,0:T(8,128)}) custom-call(bf16[2,4,2048,128]{3,2,1,0:T(8,128)(2,1)S(1)} %bitcast.12, bf16[512,128]{1,0:T(8,128)(2,1)S(1)} %collective-permute-done.35.refs_1_, bf16[512,128]{1,0:T(8,128)(2,1)S(1)} %collective-permute-done.37.refs_2_, ...), custom_call_target="tpu_custom_call" | custom-call | flops 1 | bytes 1 | tf_op jit(solution)/shard_map/pallas_call | solution.py:43
  135.6 2.3 %collective-permute-done.46 = f32[72,128]{1,0:T(8,128)S(1)} collective-permute-done((f32[72,128]{1,0:T(8,128)S(1)}, f32[72,128]{1,0:T(8,128)S(1)}, u32[]{:S(2)}, u32[]{:S(2)}) %collective-permute-start.46) | collective-permute-done | bytes 36896 | tf_op jit(solution)/shard_map/ppermute | solution.py:59
  139.7 3.6 %collective-permute-done.47 = f32[72,128]{1,0:T(8,128)S(1)} collective-permute-done((f32[72,128]{1,0:T(8,128)S(1)}, f32[72,128]{1,0:T(8,128)S(1)}, u32[]{:S(2)}, u32[]{:S(2)}) %collective-permute-start.47) | collective-permute-done | bytes 36896 | tf_op jit(solution)/shard_map/ppermute | solution.py:59
  143.3 5.2 %shard_map.78 = (f32[512,128]{1,0:T(8,128)}, f32[512,128]{1,0:T(8,128)}, f32[8,128]{1,0:T(8,128)}) custom-call(f32[72,128]{1,0:T(8,128)S(1)} %add.67.refs_0_, f32[128,128]{1,0:T(8,128)S(1)} %get-tuple-element.154.refs_1_, f32[512,128]{1,0:T(8,128)S(1)} %get-tuple-element.138.refs_3_.refs_2_, f32[512,128]{1,0:T(8,128)S(1)} %get-tuple-element.149.refs_2_.refs_3_, ...), custom_call_target="tpu_custom_call" | custom-call | flops 1 | bytes 1 | tf_op jit(solution)/shard_map/pallas_call | solution.py:43
  (112 shorter events, 58.1 us)
Async XLA Ops:
  2.1 9.3 %collective-permute-start = (f32[512,128]{1,0:T(8,128)S(1)}, f32[512,128]{1,0:T(8,128)S(1)}, u32[]{:S(2)}, u32[]{:S(2)}) collective-permute-start(f32[512,128]{1,0:T(8,128)S(1)} %get-tuple-element.81), channel_id=1, source_target_pairs={{2,0},{0,2},{3,1},{1,3},{6,4},{4,6},{7,5},{5,7},{10,8},{8,10},{11,... | collective-permute-start | bytes 786440 | tf_op jit(solution)/shard_map/ppermute | solution.py:59
  11.5 10.7 %collective-permute-start.2 = (bf16[512,128]{1,0:T(8,128)(2,1)S(1)}, bf16[512,128]{1,0:T(8,128)(2,1)S(1)}, u32[]{:S(2)}, u32[]{:S(2)}) collective-permute-start(bf16[512,128]{1,0:T(8,128)(2,1)S(1)} %get-tuple-element.88.refs_1_), channel_id=1, source_target_pairs={{1,0},{0,1},{3,2},{2,3},{5,4},{4,5},{7,6},{6,7},{9,8},{8,9},{11,10... | collective-permute-start | bytes 393224 | tf_op jit(solution)/shard_map/ppermute | solution.py:59
  11.6 12.6 %collective-permute-start.6 = (bf16[512,128]{1,0:T(8,128)(2,1)S(1)}, bf16[512,128]{1,0:T(8,128)(2,1)S(1)}, u32[]{:S(2)}, u32[]{:S(2)}) collective-permute-start(bf16[512,128]{1,0:T(8,128)(2,1)S(1)} %get-tuple-element.88.refs_1_), channel_id=1, source_target_pairs={{4,0},{0,4},{12,8},{8,12},{5,1},{1,5},{13,9},{9,13},{6,2},{2,6},{1... | collective-permute-start | bytes 393224 | tf_op jit(solution)/shard_map/ppermute | solution.py:59
  13.5 12.6 %collective-permute-start.4 = (bf16[512,128]{1,0:T(8,128)(2,1)S(1)}, bf16[512,128]{1,0:T(8,128)(2,1)S(1)}, u32[]{:S(2)}, u32[]{:S(2)}) collective-permute-start(bf16[512,128]{1,0:T(8,128)(2,1)S(1)} %get-tuple-element.88.refs_1_), channel_id=1, source_target_pairs={{8,0},{12,4},{0,8},{4,12},{9,1},{13,5},{1,9},{5,13},{10,2},{14,6},... | collective-permute-start | bytes 393224 | tf_op jit(solution)/shard_map/ppermute | solution.py:59
  16.1 11.3 %collective-permute-start.8 = (f32[512,128]{1,0:T(8,128)S(1)}, f32[512,128]{1,0:T(8,128)S(1)}, u32[]{:S(2)}, u32[]{:S(2)}) collective-permute-start(f32[512,128]{1,0:T(8,128)S(1)} %get-tuple-element.98.refs_2_.refs_4_.refs_0_), channel_id=1, source_target_pairs={{2,0},{0,2},{3,1},{1,3},{6,4},{4,6},{7,5},{5,7},{10,8},{8,10},{11,... | collective-permute-start | bytes 786440 | tf_op jit(solution)/shard_map/ppermute | solution.py:59
  17.6 8.5 %collective-permute-start.1 = (bf16[512,128]{1,0:T(8,128)(2,1)S(1)}, bf16[512,128]{1,0:T(8,128)(2,1)S(1)}, u32[]{:S(2)}, u32[]{:S(2)}) collective-permute-start(bf16[512,128]{1,0:T(8,128)(2,1)S(1)} %get-tuple-element.88.refs_1_), channel_id=1, source_target_pairs={{12,0},{8,4},{4,8},{0,12},{13,1},{9,5},{5,9},{1,13},{14,2},{10,6},... | collective-permute-start | bytes 393224 | tf_op jit(solution)/shard_map/ppermute | solution.py:59
  31.2 8.5 %collective-permute-start.11 = (f32[512,128]{1,0:T(8,128)S(1)}, f32[512,128]{1,0:T(8,128)S(1)}, u32[]{:S(2)}, u32[]{:S(2)}) collective-permute-start(f32[512,128]{1,0:T(8,128)S(1)} %get-tuple-element.102.refs_1_), channel_id=1, source_target_pairs={{2,0},{0,2},{3,1},{1,3},{6,4},{4,6},{7,5},{5,7},{10,8},{8,10},{11,... | collective-permute-start | bytes 786440 | tf_op jit(solution)/shard_map/ppermute | solution.py:59
  36.9 6.2 %collective-permute-start.10 = (f32[104,128]{1,0:T(8,128)S(1)}, f32[104,128]{1,0:T(8,128)S(1)}, u32[]{:S(2)}, u32[]{:S(2)}) collective-permute-start(f32[104,128]{1,0:T(8,128)S(1)} %add.51), channel_id=1, source_target_pairs={{8,0},{10,2},{12,4},{14,6},{0,8},{2,10},{4,12},{6,14},{9,1},{11,3}... | collective-permute-start | bytes 159752 | tf_op jit(solution)/shard_map/ppermute | solution.py:59
  43.8 5.3 %collective-permute-start.14 = (f32[176,128]{1,0:T(8,128)S(1)}, f32[176,128]{1,0:T(8,128)S(1)}, u32[]{:S(2)}, u32[]{:S(2)}) collective-permute-start(f32[176,128]{1,0:T(8,128)S(1)} %pad_maximum_fusion), channel_id=1, source_target_pairs={{4,0},{6,2},{0,4},{2,6},{12,8},{14,10},{8,12},{10,14},{5,1},{7,3},... | collective-permute-start | bytes 270344 | tf_op jit(solution)/shard_map/ppermute | solution.py:59
  45.4 5.7 %collective-permute-start.15 = (f32[176,128]{1,0:T(8,128)S(1)}, f32[176,128]{1,0:T(8,128)S(1)}, u32[]{:S(2)}, u32[]{:S(2)}) collective-permute-start(f32[176,128]{1,0:T(8,128)S(1)} %pad_maximum_fusion), channel_id=1, source_target_pairs={{6,0},{4,2},{2,4},{0,6},{14,8},{12,10},{10,12},{8,14},{7,1},{5,3},... | collective-permute-start | bytes 270344 | tf_op jit(solution)/shard_map/ppermute | solution.py:59
  51.2 7.7 %collective-permute-start.16 = (f32[72,128]{1,0:T(8,128)S(1)}, f32[72,128]{1,0:T(8,128)S(1)}, u32[]{:S(2)}, u32[]{:S(2)}) collective-permute-start(f32[72,128]{1,0:T(8,128)S(1)} %slice.16.refs_5_), channel_id=1, source_target_pairs={{8,0},{10,2},{12,4},{14,6},{0,8},{2,10},{4,12},{6,14},{9,1},{11,3}... | collective-permute-start | bytes 110600 | tf_op jit(solution)/shard_map/ppermute | solution.py:59
  60.7 5.9 %collective-permute-start.19 = (bf16[512,128]{1,0:T(8,128)(2,1)S(1)}, bf16[512,128]{1,0:T(8,128)(2,1)S(1)}, u32[]{:S(2)}, u32[]{:S(2)}) collective-permute-start(bf16[512,128]{1,0:T(8,128)(2,1)S(1)} %get-tuple-element.114.refs_1_), channel_id=1, source_target_pairs={{1,0},{0,1},{3,2},{2,3},{5,4},{4,5},{7,6},{6,7},{9,8},{8,9},{11,10... | collective-permute-start | bytes 393224 | tf_op jit(solution)/shard_map/ppermute | solution.py:59
  60.9 8.4 %collective-permute-start.23 = (bf16[512,128]{1,0:T(8,128)(2,1)S(1)}, bf16[512,128]{1,0:T(8,128)(2,1)S(1)}, u32[]{:S(2)}, u32[]{:S(2)}) collective-permute-start(bf16[512,128]{1,0:T(8,128)(2,1)S(1)} %get-tuple-element.114.refs_1_), channel_id=1, source_target_pairs={{4,0},{0,4},{12,8},{8,12},{5,1},{1,5},{13,9},{9,13},{6,2},{2,6},{1... | collective-permute-start | bytes 393224 | tf_op jit(solution)/shard_map/ppermute | solution.py:59
  62.2 12.9 %collective-permute-start.21 = (bf16[512,128]{1,0:T(8,128)(2,1)S(1)}, bf16[512,128]{1,0:T(8,128)(2,1)S(1)}, u32[]{:S(2)}, u32[]{:S(2)}) collective-permute-start(bf16[512,128]{1,0:T(8,128)(2,1)S(1)} %get-tuple-element.114.refs_1_), channel_id=1, source_target_pairs={{8,0},{12,4},{0,8},{4,12},{9,1},{13,5},{1,9},{5,13},{10,2},{14,6},... | collective-permute-start | bytes 393224 | tf_op jit(solution)/shard_map/ppermute | solution.py:59
  63.3 11.7 %collective-permute-start.18 = (bf16[512,128]{1,0:T(8,128)(2,1)S(1)}, bf16[512,128]{1,0:T(8,128)(2,1)S(1)}, u32[]{:S(2)}, u32[]{:S(2)}) collective-permute-start(bf16[512,128]{1,0:T(8,128)(2,1)S(1)} %get-tuple-element.114.refs_1_), channel_id=1, source_target_pairs={{12,0},{8,4},{4,8},{0,12},{13,1},{9,5},{5,9},{1,13},{14,2},{10,6},... | collective-permute-start | bytes 393224 | tf_op jit(solution)/shard_map/ppermute | solution.py:59
  65.3 11.1 %collective-permute-start.25 = (f32[512,128]{1,0:T(8,128)S(1)}, f32[512,128]{1,0:T(8,128)S(1)}, u32[]{:S(2)}, u32[]{:S(2)}) collective-permute-start(f32[512,128]{1,0:T(8,128)S(1)} %get-tuple-element.122.refs_2_.refs_4_.refs_0_), channel_id=1, source_target_pairs={{2,0},{0,2},{3,1},{1,3},{6,4},{4,6},{7,5},{5,7},{10,8},{8,10},{11,... | collective-permute-start | bytes 786440 | tf_op jit(solution)/shard_map/ppermute | solution.py:59
  69.2 6.3 %collective-permute-start.24 = (bf16[512,128]{1,0:T(8,128)(2,1)S(1)}, bf16[512,128]{1,0:T(8,128)(2,1)S(1)}, u32[]{:S(2)}, u32[]{:S(2)}) collective-permute-start(bf16[512,128]{1,0:T(8,128)(2,1)S(1)} %collective-permute-done.23.refs_4_), channel_id=1, source_target_pairs={{1,0},{0,1},{3,2},{2,3},{5,4},{4,5},{7,6},{6,7},{9,8},{8,9},{11,10... | collective-permute-start | bytes 393224 | tf_op jit(solution)/shard_map/ppermute | solution.py:59
  80.2 8.4 %collective-permute-start.28 = (f32[512,128]{1,0:T(8,128)S(1)}, f32[512,128]{1,0:T(8,128)S(1)}, u32[]{:S(2)}, u32[]{:S(2)}) collective-permute-start(f32[512,128]{1,0:T(8,128)S(1)} %get-tuple-element.126.refs_1_), channel_id=1, source_target_pairs={{2,0},{0,2},{3,1},{1,3},{6,4},{4,6},{7,5},{5,7},{10,8},{8,10},{11,... | collective-permute-start | bytes 786440 | tf_op jit(solution)/shard_map/ppermute | solution.py:59
  84.8 6.1 %collective-permute-start.27 = (f32[104,128]{1,0:T(8,128)S(1)}, f32[104,128]{1,0:T(8,128)S(1)}, u32[]{:S(2)}, u32[]{:S(2)}) collective-permute-start(f32[104,128]{1,0:T(8,128)S(1)} %add.57), channel_id=1, source_target_pairs={{8,0},{10,2},{12,4},{14,6},{0,8},{2,10},{4,12},{6,14},{9,1},{11,3}... | collective-permute-start | bytes 159752 | tf_op jit(solution)/shard_map/ppermute | solution.py:59
  90.9 4.7 %collective-permute-start.30 = (f32[176,128]{1,0:T(8,128)S(1)}, f32[176,128]{1,0:T(8,128)S(1)}, u32[]{:S(2)}, u32[]{:S(2)}) collective-permute-start(f32[176,128]{1,0:T(8,128)S(1)} %pad_maximum_fusion.1), channel_id=1, source_target_pairs={{2,0},{0,2},{6,4},{4,6},{10,8},{8,10},{14,12},{12,14},{3,1},{1,3},... | collective-permute-start | bytes 270344 | tf_op jit(solution)/shard_map/ppermute | solution.py:59
  92.3 5.2 %collective-permute-start.31 = (f32[176,128]{1,0:T(8,128)S(1)}, f32[176,128]{1,0:T(8,128)S(1)}, u32[]{:S(2)}, u32[]{:S(2)}) collective-permute-start(f32[176,128]{1,0:T(8,128)S(1)} %pad_maximum_fusion.1), channel_id=1, source_target_pairs={{4,0},{6,2},{0,4},{2,6},{12,8},{14,10},{8,12},{10,14},{5,1},{7,3},... | collective-permute-start | bytes 270344 | tf_op jit(solution)/shard_map/ppermute | solution.py:59
  93.2 5.7 %collective-permute-start.32 = (f32[176,128]{1,0:T(8,128)S(1)}, f32[176,128]{1,0:T(8,128)S(1)}, u32[]{:S(2)}, u32[]{:S(2)}) collective-permute-start(f32[176,128]{1,0:T(8,128)S(1)} %pad_maximum_fusion.1), channel_id=1, source_target_pairs={{6,0},{4,2},{2,4},{0,6},{14,8},{12,10},{10,12},{8,14},{7,1},{5,3},... | collective-permute-start | bytes 270344 | tf_op jit(solution)/shard_map/ppermute | solution.py:59
  99.0 7.3 %collective-permute-start.33 = (f32[72,128]{1,0:T(8,128)S(1)}, f32[72,128]{1,0:T(8,128)S(1)}, u32[]{:S(2)}, u32[]{:S(2)}) collective-permute-start(f32[72,128]{1,0:T(8,128)S(1)} %slice.18.refs_5_), channel_id=1, source_target_pairs={{8,0},{10,2},{12,4},{14,6},{0,8},{2,10},{4,12},{6,14},{9,1},{11,3}... | collective-permute-start | bytes 110600 | tf_op jit(solution)/shard_map/ppermute | solution.py:59
  108.0 5.8 %collective-permute-start.36 = (bf16[512,128]{1,0:T(8,128)(2,1)S(1)}, bf16[512,128]{1,0:T(8,128)(2,1)S(1)}, u32[]{:S(2)}, u32[]{:S(2)}) collective-permute-start(bf16[512,128]{1,0:T(8,128)(2,1)S(1)} %get-tuple-element.140.refs_1_), channel_id=1, source_target_pairs={{1,0},{0,1},{3,2},{2,3},{5,4},{4,5},{7,6},{6,7},{9,8},{8,9},{11,10... | collective-permute-start | bytes 393224 | tf_op jit(solution)/shard_map/ppermute | solution.py:59
  108.1 9.0 %collective-permute-start.40 = (bf16[512,128]{1,0:T(8,128)(2,1)S(1)}, bf16[512,128]{1,0:T(8,128)(2,1)S(1)}, u32[]{:S(2)}, u32[]{:S(2)}) collective-permute-start(bf16[512,128]{1,0:T(8,128)(2,1)S(1)} %get-tuple-element.140.refs_1_), channel_id=1, source_target_pairs={{4,0},{0,4},{12,8},{8,12},{5,1},{1,5},{13,9},{9,13},{6,2},{2,6},{1... | collective-permute-start | bytes 393224 | tf_op jit(solution)/shard_map/ppermute | solution.py:59
  109.4 12.9 %collective-permute-start.38 = (bf16[512,128]{1,0:T(8,128)(2,1)S(1)}, bf16[512,128]{1,0:T(8,128)(2,1)S(1)}, u32[]{:S(2)}, u32[]{:S(2)}) collective-permute-start(bf16[512,128]{1,0:T(8,128)(2,1)S(1)} %get-tuple-element.140.refs_1_), channel_id=1, source_target_pairs={{8,0},{12,4},{0,8},{4,12},{9,1},{13,5},{1,9},{5,13},{10,2},{14,6},... | collective-permute-start | bytes 393224 | tf_op jit(solution)/shard_map/ppermute | solution.py:59
  111.1 11.7 %collective-permute-start.42 = (f32[512,128]{1,0:T(8,128)S(1)}, f32[512,128]{1,0:T(8,128)S(1)}, u32[]{:S(2)}, u32[]{:S(2)}) collective-permute-start(f32[512,128]{1,0:T(8,128)S(1)} %get-tuple-element.149.refs_2_.refs_3_), channel_id=1, source_target_pairs={{2,0},{0,2},{3,1},{1,3},{6,4},{4,6},{7,5},{5,7},{10,8},{8,10},{11,... | collective-permute-start | bytes 786440 | tf_op jit(solution)/shard_map/ppermute | solution.py:59
  111.8 10.5 %collective-permute-start.35 = (bf16[512,128]{1,0:T(8,128)(2,1)S(1)}, bf16[512,128]{1,0:T(8,128)(2,1)S(1)}, u32[]{:S(2)}, u32[]{:S(2)}) collective-permute-start(bf16[512,128]{1,0:T(8,128)(2,1)S(1)} %get-tuple-element.140.refs_1_), channel_id=1, source_target_pairs={{12,0},{8,4},{4,8},{0,12},{13,1},{9,5},{5,9},{1,13},{14,2},{10,6},... | collective-permute-start | bytes 393224 | tf_op jit(solution)/shard_map/ppermute | solution.py:59
  117.1 5.7 %collective-permute-start.41 = (bf16[512,128]{1,0:T(8,128)(2,1)S(1)}, bf16[512,128]{1,0:T(8,128)(2,1)S(1)}, u32[]{:S(2)}, u32[]{:S(2)}) collective-permute-start(bf16[512,128]{1,0:T(8,128)(2,1)S(1)} %collective-permute-done.40.refs_4_), channel_id=1, source_target_pairs={{1,0},{0,1},{3,2},{2,3},{5,4},{4,5},{7,6},{6,7},{9,8},{8,9},{11,10... | collective-permute-start | bytes 393224 | tf_op jit(solution)/shard_map/ppermute | solution.py:59
  133.0 5.0 %collective-permute-start.46 = (f32[72,128]{1,0:T(8,128)S(1)}, f32[72,128]{1,0:T(8,128)S(1)}, u32[]{:S(2)}, u32[]{:S(2)}) collective-permute-start(f32[72,128]{1,0:T(8,128)S(1)} %add.63), channel_id=1, source_target_pairs={{6,0},{4,2},{2,4},{0,6},{14,8},{12,10},{10,12},{8,14},{7,1},{5,3},... | collective-permute-start | bytes 110600 | tf_op jit(solution)/shard_map/ppermute | solution.py:59
  134.5 8.8 %collective-permute-start.48 = (f32[512,128]{1,0:T(8,128)S(1)}, f32[512,128]{1,0:T(8,128)S(1)}, u32[]{:S(2)}, u32[]{:S(2)}) collective-permute-start(f32[512,128]{1,0:T(8,128)S(1)} %get-tuple-element.152.refs_1_), channel_id=1, source_target_pairs={{2,0},{0,2},{3,1},{1,3},{6,4},{4,6},{7,5},{5,7},{10,8},{8,10},{11,... | collective-permute-start | bytes 786440 | tf_op jit(solution)/shard_map/ppermute | solution.py:59
  137.9 5.3 %collective-permute-start.47 = (f32[72,128]{1,0:T(8,128)S(1)}, f32[72,128]{1,0:T(8,128)S(1)}, u32[]{:S(2)}, u32[]{:S(2)}) collective-permute-start(f32[72,128]{1,0:T(8,128)S(1)} %add_add_fusion.2), channel_id=1, source_target_pairs={{8,0},{10,2},{12,4},{14,6},{0,8},{2,10},{4,12},{6,14},{9,1},{11,3}... | collective-permute-start | bytes 110600 | tf_op jit(solution)/shard_map/ppermute | solution.py:59
  (17 other events, 42.8 us)

commit v5 on v4

--- a/solution.py
+++ b/solution.py
@@ -270,7 +270,7 @@
     panels = lax.axis_size("panel")
     groups = []
     if links == 2 * panels + 1 and panels & (panels - 1) == 0:
-        for s in sorted(range(panels), key=lambda s: (s > 0, s % 2)):
+        for s in range(panels):
 
             def numbers(s=s):
                 me = lax.axis_index("panel")
@@ -291,7 +291,10 @@
 
 def operate(packed, groups, low, direction, between, final):
     n = lax.axis_size("rhs")
-    arrived = [low] + [bring(low) for bring, _, _ in groups[:0:-1]][::-1]
+    arrived = [low] + [bring(low) for bring, _, _ in groups[1:]]
+    if len(groups) == lax.axis_size("panel") == 4:
+        inner = permute(low, "panel", [(1, 2), (2, 1)])
+        arrived[3] = inner + permute(arrived[2], "panel", [(2, 3), (1, 0)])
     directions = [direction] + [swapped(direction, "rhs", s, n) for s in range(1, n)]
     pairs = [[low, swapped(low, "coef", 1, 2)]]
     (acc,), token = link_products(packed[:1], pairs, None, n, None)

time: 149 us -> 158 us (1.060)
  starting transfers between devices: 46.1 us -> 53.2 us
  waiting for transfers between devices: 41.3 us -> 43.8 us
    ppermute x49 -> x52, starting transfers between devices: 46.1 us -> 53.2 us  [permute(): return lax.ppermute(value, axis, pairs)]
    ppermute x49 -> x52, waiting for transfers between devices: 41.3 us -> 43.8 us  [permute(): return lax.ppermute(value, axis, pairs)]
  transfers between devices with their start and end apart: 49 -> 52, of which waited for: 23 -> 24; matrix products, arithmetic and copies ran while one was open for 0% -> 0% of each run, Pallas kernels for 30% -> 28%
where the time goes in v5:
time: 158 us
  Pallas kernels  59.9 us (38%)
  starting transfers between devices  53.2 us (34%)
  waiting for transfers between devices  43.8 us (28%)
    pallas_call x29, Pallas kernels, call(): pl.pallas_call(ordered, out_shape=list(outs) + [shape(SUB)], in_specs=[HB...  59.9 us
    ppermute x52, starting transfers between devices, permute(): return lax.ppermute(value, axis, pairs)  53.2 us
    ppermute x52, waiting for transfers between devices, permute(): return lax.ppermute(value, axis, pairs)  43.8 us
  transfers between devices with their start and end apart: 52, of which 24 were waited for; matrix products, arithmetic and copies ran while one was open for 0% of the time, Pallas kernels for 28%

profile of v5, /device:TPU:0, one launch (start us, length us, event | category | flops | bytes accessed | tf_op | source)
XLA Modules:
  0.0 158.1 jit_solution(2000790727570564830)
XLA Ops:
  2.1 3.0 %collective-permute-start = (f32[512,128]{1,0:T(8,128)S(1)}, f32[512,128]{1,0:T(8,128)S(1)}, u32[]{:S(2)}, u32[]{:S(2)}) collective-permute-start(f32[512,128]{1,0:T(8,128)S(1)} %get-tuple-element.81), channel_id=1, source_target_pairs={{2,0},{0,2},{3,1},{1,3},{6,4},{4,6},{7,5},{5,7},{10,8},{8,10},{11,... | collective-permute-start | bytes 786440 | tf_op jit(solution)/shard_map/ppermute | solution.py:59
  5.1 2.9 %shard_map.51 = (bf16[3,4,1024,2,128]{4,3,2,1,0:T(2,128)(2,1)S(1)}, f32[8,128]{1,0:T(8,128)S(1)}) custom-call(bf16[9,1024,2,512]{3,2,1,0:T(2,128)(2,1)} %bitcast.22, f32[8,128]{1,0:T(8,128)S(1)} %get-tuple-element.82.refs_1_), custom_call_target="tpu_custom_call" | custom-call | flops 1 | bytes 1 | tf_op jit(solution)/shard_map/pallas_call | solution.py:43
  8.0 2.2 %shard_map.52 = (bf16[2,4,1024,2,128]{4,3,2,1,0:T(2,128)(2,1)S(1)}, f32[8,128]{1,0:T(8,128)S(1)}) custom-call(bf16[9,1024,2,512]{3,2,1,0:T(2,128)(2,1)} %bitcast.23, f32[8,128]{1,0:T(8,128)S(1)} %get-tuple-element.83.refs_1_), custom_call_target="tpu_custom_call" | custom-call | flops 1 | bytes 1 | tf_op jit(solution)/shard_map/pallas_call | solution.py:43
  11.5 2.9 %collective-permute-start.2 = (bf16[512,128]{1,0:T(8,128)(2,1)S(1)}, bf16[512,128]{1,0:T(8,128)(2,1)S(1)}, u32[]{:S(2)}, u32[]{:S(2)}) collective-permute-start(bf16[512,128]{1,0:T(8,128)(2,1)S(1)} %get-tuple-element.88.refs_1_), channel_id=1, source_target_pairs={{8,0},{12,4},{0,8},{4,12},{9,1},{13,5},{1,9},{5,13},{10,2},{14,6},... | collective-permute-start | bytes 393224 | tf_op jit(solution)/shard_map/ppermute | solution.py:59
  18.2 1.7 %collective-permute-done.2.refs_4_ = bf16[512,128]{1,0:T(8,128)(2,1)S(1)} collective-permute-done((bf16[512,128]{1,0:T(8,128)(2,1)S(1)}, bf16[512,128]{1,0:T(8,128)(2,1)S(1)}, u32[]{:S(2)}, u32[]{:S(2)}) %collective-permute-start.2) | collective-permute-done | bytes 131104 | tf_op jit(solution)/shard_map/ppermute | solution.py:59
  21.2 2.2 %shard_map.54 = (bf16[2,4,1024,2,128]{4,3,2,1,0:T(2,128)(2,1)S(1)}, f32[8,128]{1,0:T(8,128)S(1)}) custom-call(bf16[9,1024,2,512]{3,2,1,0:T(2,128)(2,1)} %bitcast.24, f32[8,128]{1,0:T(8,128)S(1)} %get-tuple-element.85.refs_1_), custom_call_target="tpu_custom_call" | custom-call | flops 1 | bytes 1 | tf_op jit(solution)/shard_map/pallas_call | solution.py:43
  23.4 2.2 %shard_map.55 = (bf16[2,4,1024,2,128]{4,3,2,1,0:T(2,128)(2,1)S(1)}, f32[8,128]{1,0:T(8,128)S(1)}) custom-call(bf16[9,1024,2,512]{3,2,1,0:T(2,128)(2,1)} %bitcast.25, f32[8,128]{1,0:T(8,128)S(1)} %get-tuple-element.86.refs_1_), custom_call_target="tpu_custom_call" | custom-call | flops 1 | bytes 1 | tf_op jit(solution)/shard_map/pallas_call | solution.py:43
  25.7 2.0 %shard_map.56 = (f32[1024,128]{1,0:T(8,128)S(1)}, f32[8,128]{1,0:T(8,128)S(1)}) custom-call(bf16[3,4,2048,128]{3,2,1,0:T(8,128)(2,1)S(1)} %bitcast.13, bf16[512,128]{1,0:T(8,128)(2,1)S(1)} %get-tuple-element.88.refs_1_, bf16[512,128]{1,0:T(8,128)(2,1)S(1)} %collective-permute-done.4.refs_2_), custom_call_target="tpu_custom_call" | custom-call | flops 1 | bytes 1 | tf_op jit(solution)/shard_map/pallas_call | solution.py:43
  29.2 3.0 %shard_map.57 = (f32[1024,128]{1,0:T(8,128)S(1)}, f32[8,128]{1,0:T(8,128)}) custom-call(bf16[2,4,2048,128]{3,2,1,0:T(8,128)(2,1)S(1)} %bitcast.16, bf16[2,4,2048,128]{3,2,1,0:T(8,128)(2,1)S(1)} %bitcast.19, bf16[512,128]{1,0:T(8,128)(2,1)S(1)} %collective-permute-done.6.refs_2_, bf16[512,128]{1,0:T(8,128)(2,1)S(1)} %collective-permute-done.7.refs_3_, ...), custom_call_target="tpu_custom_call" | custom-call | flops 1 | bytes 1 | tf_op jit(solution)/shard_map/pallas_call | solution.py:43
  38.2 5.8 %collective-permute-start.11 = (f32[104,128]{1,0:T(8,128)S(1)}, f32[104,128]{1,0:T(8,128)S(1)}, u32[]{:S(2)}, u32[]{:S(2)}) collective-permute-start(f32[104,128]{1,0:T(8,128)S(1)} %add.61), channel_id=1, source_target_pairs={{8,0},{10,2},{12,4},{14,6},{0,8},{2,10},{4,12},{6,14},{9,1},{11,3}... | collective-permute-start | bytes 159752 | tf_op jit(solution)/shard_map/ppermute | solution.py:59
  47.9 2.1 %collective-permute-start.16 = (f32[176,128]{1,0:T(8,128)S(1)}, f32[176,128]{1,0:T(8,128)S(1)}, u32[]{:S(2)}, u32[]{:S(2)}) collective-permute-start(f32[176,128]{1,0:T(8,128)S(1)} %pad_maximum_fusion), channel_id=1, source_target_pairs={{6,0},{4,2},{2,4},{0,6},{14,8},{12,10},{10,12},{8,14},{7,1},{5,3},... | collective-permute-start | bytes 270344 | tf_op jit(solution)/shard_map/ppermute | solution.py:59
  52.4 1.8 %collective-permute-done.16 = f32[176,128]{1,0:T(8,128)S(1)} collective-permute-done((f32[176,128]{1,0:T(8,128)S(1)}, f32[176,128]{1,0:T(8,128)S(1)}, u32[]{:S(2)}, u32[]{:S(2)}) %collective-permute-start.16) | collective-permute-done | bytes 90144 | tf_op jit(solution)/shard_map/ppermute | solution.py:59
  54.4 3.1 %collective-permute-start.17 = (f32[72,128]{1,0:T(8,128)S(1)}, f32[72,128]{1,0:T(8,128)S(1)}, u32[]{:S(2)}, u32[]{:S(2)}) collective-permute-start(f32[72,128]{1,0:T(8,128)S(1)} %slice.16.refs_5_), channel_id=1, source_target_pairs={{8,0},{10,2},{12,4},{14,6},{0,8},{2,10},{4,12},{6,14},{9,1},{11,3}... | collective-permute-start | bytes 110600 | tf_op jit(solution)/shard_map/ppermute | solution.py:59
  57.5 5.8 %shard_map.62 = (f32[512,128]{1,0:T(8,128)S(1)}, f32[128,128]{1,0:T(8,128)S(1)}, f32[128,128]{1,0:T(8,128)S(1)}, f32[128,128]{1,0:T(8,128)S(1)}, f32[8,128]{1,0:T(8,128)}) custom-call(f32[104,128]{1,0:T(8,128)S(1)} %slice.17.refs_0_, f32[104,128]{1,0:T(8,128)S(1)} %collective-permute-done.18.refs_1_, ...), custom_call_target="tpu_custom_call" | custom-call | flops 1 | bytes 1 | tf_op jit(solution)/shard_map/pallas_call | solution.py:43
  63.3 1.7 %shard_map.63 = (f32[512,128]{1,0:T(8,128)S(1)}, bf16[512,128]{1,0:T(8,128)(2,1)S(1)}, f32[128,128]{1,0:T(8,128)S(1)}, f32[128,128]{1,0:T(8,128)S(1)}, f32[8,128]{1,0:T(8,128)}) custom-call(f32[128,128]{1,0:T(8,128)S(1)} %get-tuple-element.109.refs_0_.refs_2_, f32[128,128]{1,0:T(8,128)S(1)} %get-tuple-element.110.refs_1_, ...), custom_call_target="tpu_custom_call" | custom-call | flops 1 | bytes 1 | tf_op jit(solution)/shard_map/pallas_call | solution.py:43
  67.9 7.0 %collective-permute-done.20.refs_4_ = bf16[512,128]{1,0:T(8,128)(2,1)S(1)} collective-permute-done((bf16[512,128]{1,0:T(8,128)(2,1)S(1)}, bf16[512,128]{1,0:T(8,128)(2,1)S(1)}, u32[]{:S(2)}, u32[]{:S(2)}) %collective-permute-start.20) | collective-permute-done | bytes 131104 | tf_op jit(solution)/shard_map/ppermute | solution.py:59
  77.1 2.0 %shard_map.64 = (f32[1024,128]{1,0:T(8,128)S(1)}, f32[8,128]{1,0:T(8,128)S(1)}) custom-call(bf16[3,4,2048,128]{3,2,1,0:T(8,128)(2,1)S(1)} %bitcast.14, bf16[512,128]{1,0:T(8,128)(2,1)S(1)} %get-tuple-element.114.refs_1_, bf16[512,128]{1,0:T(8,128)(2,1)S(1)} %collective-permute-done.22.refs_2_), custom_call_target="tpu_custom_call" | custom-call | flops 1 | bytes 1 | tf_op jit(solution)/shard_map/pallas_call | solution.py:43
  83.6 3.0 %shard_map.66 = (f32[1024,128]{1,0:T(8,128)S(1)}, f32[8,128]{1,0:T(8,128)}) custom-call(bf16[2,4,2048,128]{3,2,1,0:T(8,128)(2,1)S(1)} %bitcast.17, bf16[2,4,2048,128]{3,2,1,0:T(8,128)(2,1)S(1)} %bitcast.20, bf16[512,128]{1,0:T(8,128)(2,1)S(1)} %collective-permute-done.24.refs_2_, bf16[512,128]{1,0:T(8,128)(2,1)S(1)} %collective-permute-done.25.refs_3_, ...), custom_call_target="tpu_custom_call" | custom-call | flops 1 | bytes 1 | tf_op jit(solution)/shard_map/pallas_call | solution.py:43
  87.4 1.8 %collective-permute-start.30 = (f32[512,128]{1,0:T(8,128)S(1)}, f32[512,128]{1,0:T(8,128)S(1)}, u32[]{:S(2)}, u32[]{:S(2)}) collective-permute-start(f32[512,128]{1,0:T(8,128)S(1)} %get-tuple-element.126.refs_1_), channel_id=1, source_target_pairs={{2,0},{0,2},{3,1},{1,3},{6,4},{4,6},{7,5},{5,7},{10,8},{8,10},{11,... | collective-permute-start | bytes 786440 | tf_op jit(solution)/shard_map/ppermute | solution.py:59
  95.8 2.3 %collective-permute-done.29 = f32[104,128]{1,0:T(8,128)S(1)} collective-permute-done((f32[104,128]{1,0:T(8,128)S(1)}, f32[104,128]{1,0:T(8,128)S(1)}, u32[]{:S(2)}, u32[]{:S(2)}) %collective-permute-start.29) | collective-permute-done | bytes 53280 | tf_op jit(solution)/shard_map/ppermute | solution.py:59
  98.8 2.0 %collective-permute-start.33 = (f32[176,128]{1,0:T(8,128)S(1)}, f32[176,128]{1,0:T(8,128)S(1)}, u32[]{:S(2)}, u32[]{:S(2)}) collective-permute-start(f32[176,128]{1,0:T(8,128)S(1)} %pad_maximum_fusion.1), channel_id=1, source_target_pairs={{4,0},{6,2},{0,4},{2,6},{12,8},{14,10},{8,12},{10,14},{5,1},{7,3},... | collective-permute-start | bytes 270344 | tf_op jit(solution)/shard_map/ppermute | solution.py:59
  104.1 2.4 %collective-permute-done.34 = f32[176,128]{1,0:T(8,128)S(1)} collective-permute-done((f32[176,128]{1,0:T(8,128)S(1)}, f32[176,128]{1,0:T(8,128)S(1)}, u32[]{:S(2)}, u32[]{:S(2)}) %collective-permute-start.34) | collective-permute-done | bytes 90144 | tf_op jit(solution)/shard_map/ppermute | solution.py:59
  107.8 5.8 %shard_map.71 = (f32[512,128]{1,0:T(8,128)S(1)}, f32[128,128]{1,0:T(8,128)S(1)}, f32[128,128]{1,0:T(8,128)S(1)}, f32[128,128]{1,0:T(8,128)S(1)}, f32[8,128]{1,0:T(8,128)}) custom-call(f32[104,128]{1,0:T(8,128)S(1)} %slice.19.refs_0_, f32[104,128]{1,0:T(8,128)S(1)} %collective-permute-done.36.refs_1_, ...), custom_call_target="tpu_custom_call" | custom-call | flops 1 | bytes 1 | tf_op jit(solution)/shard_map/pallas_call | solution.py:43
  113.6 1.7 %shard_map.72 = (f32[512,128]{1,0:T(8,128)S(1)}, bf16[512,128]{1,0:T(8,128)(2,1)S(1)}, f32[128,128]{1,0:T(8,128)S(1)}, f32[128,128]{1,0:T(8,128)S(1)}, f32[8,128]{1,0:T(8,128)}) custom-call(f32[128,128]{1,0:T(8,128)S(1)} %get-tuple-element.135.refs_0_.refs_2_, f32[128,128]{1,0:T(8,128)S(1)} %get-tuple-element.136.refs_1_, ...), custom_call_target="tpu_custom_call" | custom-call | flops 1 | bytes 1 | tf_op jit(solution)/shard_map/pallas_call | solution.py:43
  115.3 1.8 %collective-permute-start.38 = (bf16[512,128]{1,0:T(8,128)(2,1)S(1)}, bf16[512,128]{1,0:T(8,128)(2,1)S(1)}, u32[]{:S(2)}, u32[]{:S(2)}) collective-permute-start(bf16[512,128]{1,0:T(8,128)(2,1)S(1)} %get-tuple-element.140.refs_1_), channel_id=1, source_target_pairs={{8,0},{12,4},{0,8},{4,12},{9,1},{13,5},{1,9},{5,13},{10,2},{14,6},... | collective-permute-start | bytes 393224 | tf_op jit(solution)/shard_map/ppermute | solution.py:59
  120.0 5.3 %collective-permute-done.38.refs_4_ = bf16[512,128]{1,0:T(8,128)(2,1)S(1)} collective-permute-done((bf16[512,128]{1,0:T(8,128)(2,1)S(1)}, bf16[512,128]{1,0:T(8,128)(2,1)S(1)}, u32[]{:S(2)}, u32[]{:S(2)}) %collective-permute-start.38) | collective-permute-done | bytes 131104 | tf_op jit(solution)/shard_map/ppermute | solution.py:59
  126.8 2.0 %shard_map.73 = (f32[1024,128]{1,0:T(8,128)S(1)}, f32[8,128]{1,0:T(8,128)S(1)}) custom-call(bf16[3,4,2048,128]{3,2,1,0:T(8,128)(2,1)S(1)} %bitcast.15, bf16[512,128]{1,0:T(8,128)(2,1)S(1)} %get-tuple-element.140.refs_1_, bf16[512,128]{1,0:T(8,128)(2,1)S(1)} %collective-permute-done.40.refs_2_), custom_call_target="tpu_custom_call" | custom-call | flops 1 | bytes 1 | tf_op jit(solution)/shard_map/pallas_call | solution.py:43
  132.3 3.0 %shard_map.75 = (f32[1024,128]{1,0:T(8,128)S(1)}, f32[8,128]{1,0:T(8,128)}) custom-call(bf16[2,4,2048,128]{3,2,1,0:T(8,128)(2,1)S(1)} %bitcast.18, bf16[2,4,2048,128]{3,2,1,0:T(8,128)(2,1)S(1)} %bitcast.21, bf16[512,128]{1,0:T(8,128)(2,1)S(1)} %collective-permute-done.42.refs_2_, bf16[512,128]{1,0:T(8,128)(2,1)S(1)} %collective-permute-done.43.refs_3_, ...), custom_call_target="tpu_custom_call" | custom-call | flops 1 | bytes 1 | tf_op jit(solution)/shard_map/pallas_call | solution.py:43
  135.4 1.9 %shard_map.76 = (f32[512,128]{1,0:T(8,128)S(1)}, f32[512,128]{1,0:T(8,128)S(1)}, f32[8,128]{1,0:T(8,128)}) custom-call(bf16[2,4,2048,128]{3,2,1,0:T(8,128)(2,1)S(1)} %bitcast.12, bf16[512,128]{1,0:T(8,128)(2,1)S(1)} %add.74.refs_1_, bf16[512,128]{1,0:T(8,128)(2,1)S(1)} %collective-permute-done.41.refs_2_, f32[1024,128]{1,0:T(8,128)S(1)} %get-tuple-element.150.refs_3_, ...), custom_call_target="tpu_custom_call" | custom-call | flops 1 | bytes 1 | tf_op jit(solution)/shard_map/pallas_call | solution.py:43
  145.2 2.4 %collective-permute-done.49 = f32[72,128]{1,0:T(8,128)S(1)} collective-permute-done((f32[72,128]{1,0:T(8,128)S(1)}, f32[72,128]{1,0:T(8,128)S(1)}, u32[]{:S(2)}, u32[]{:S(2)}) %collective-permute-start.49) | collective-permute-done | bytes 36896 | tf_op jit(solution)/shard_map/ppermute | solution.py:59
  148.9 4.1 %collective-permute-done.50 = f32[72,128]{1,0:T(8,128)S(1)} collective-permute-done((f32[72,128]{1,0:T(8,128)S(1)}, f32[72,128]{1,0:T(8,128)S(1)}, u32[]{:S(2)}, u32[]{:S(2)}) %collective-permute-start.50) | collective-permute-done | bytes 36896 | tf_op jit(solution)/shard_map/ppermute | solution.py:59
  152.9 5.2 %shard_map.78 = (f32[512,128]{1,0:T(8,128)}, f32[512,128]{1,0:T(8,128)}, f32[8,128]{1,0:T(8,128)}) custom-call(f32[72,128]{1,0:T(8,128)S(1)} %add.79.refs_0_, f32[128,128]{1,0:T(8,128)S(1)} %get-tuple-element.154.refs_1_, f32[512,128]{1,0:T(8,128)S(1)} %get-tuple-element.138.refs_3_.refs_2_, f32[512,128]{1,0:T(8,128)S(1)} %get-tuple-element.149.refs_2_.refs_3_, ...), custom_call_target="tpu_custom_call" | custom-call | flops 1 | bytes 1 | tf_op jit(solution)/shard_map/pallas_call | solution.py:43
  (121 shorter events, 61.0 us)
Async XLA Ops:
  2.1 9.3 %collective-permute-start = (f32[512,128]{1,0:T(8,128)S(1)}, f32[512,128]{1,0:T(8,128)S(1)}, u32[]{:S(2)}, u32[]{:S(2)}) collective-permute-start(f32[512,128]{1,0:T(8,128)S(1)} %get-tuple-element.81), channel_id=1, source_target_pairs={{2,0},{0,2},{3,1},{1,3},{6,4},{4,6},{7,5},{5,7},{10,8},{8,10},{11,... | collective-permute-start | bytes 786440 | tf_op jit(solution)/shard_map/ppermute | solution.py:59
  11.5 8.4 %collective-permute-start.2 = (bf16[512,128]{1,0:T(8,128)(2,1)S(1)}, bf16[512,128]{1,0:T(8,128)(2,1)S(1)}, u32[]{:S(2)}, u32[]{:S(2)}) collective-permute-start(bf16[512,128]{1,0:T(8,128)(2,1)S(1)} %get-tuple-element.88.refs_1_), channel_id=1, source_target_pairs={{8,0},{12,4},{0,8},{4,12},{9,1},{13,5},{1,9},{5,13},{10,2},{14,6},... | collective-permute-start | bytes 393224 | tf_op jit(solution)/shard_map/ppermute | solution.py:59
  14.4 11.3 %collective-permute-start.4 = (bf16[512,128]{1,0:T(8,128)(2,1)S(1)}, bf16[512,128]{1,0:T(8,128)(2,1)S(1)}, u32[]{:S(2)}, u32[]{:S(2)}) collective-permute-start(bf16[512,128]{1,0:T(8,128)(2,1)S(1)} %get-tuple-element.88.refs_1_), channel_id=1, source_target_pairs={{1,0},{0,1},{3,2},{2,3},{5,4},{4,5},{7,6},{6,7},{9,8},{8,9},{11,10... | collective-permute-start | bytes 393224 | tf_op jit(solution)/shard_map/ppermute | solution.py:59
  14.4 13.3 %collective-permute-start.6 = (bf16[512,128]{1,0:T(8,128)(2,1)S(1)}, bf16[512,128]{1,0:T(8,128)(2,1)S(1)}, u32[]{:S(2)}, u32[]{:S(2)}) collective-permute-start(bf16[512,128]{1,0:T(8,128)(2,1)S(1)} %get-tuple-element.88.refs_1_), channel_id=1, source_target_pairs={{4,0},{0,4},{12,8},{8,12},{5,1},{1,5},{13,9},{9,13},{6,2},{2,6},{1... | collective-permute-start | bytes 393224 | tf_op jit(solution)/shard_map/ppermute | solution.py:59
  16.0 12.2 %collective-permute-start.1 = (bf16[512,128]{1,0:T(8,128)(2,1)S(1)}, bf16[512,128]{1,0:T(8,128)(2,1)S(1)}, u32[]{:S(2)}, u32[]{:S(2)}) collective-permute-start(bf16[512,128]{1,0:T(8,128)(2,1)S(1)} %get-tuple-element.88.refs_1_), channel_id=1, source_target_pairs={{4,8},{8,4},{5,9},{9,5},{6,10},{10,6},{7,11},{11,7},{20,24},{24,20... | collective-permute-start | bytes 393224 | tf_op jit(solution)/shard_map/ppermute | solution.py:59
  16.7 12.6 %collective-permute-start.9 = (f32[512,128]{1,0:T(8,128)S(1)}, f32[512,128]{1,0:T(8,128)S(1)}, u32[]{:S(2)}, u32[]{:S(2)}) collective-permute-start(f32[512,128]{1,0:T(8,128)S(1)} %get-tuple-element.98.refs_2_.refs_4_.refs_0_), channel_id=1, source_target_pairs={{2,0},{0,2},{3,1},{1,3},{6,4},{4,6},{7,5},{5,7},{10,8},{8,10},{11,... | collective-permute-start | bytes 786440 | tf_op jit(solution)/shard_map/ppermute | solution.py:59
  19.9 8.3 %collective-permute-start.3 = (bf16[512,128]{1,0:T(8,128)(2,1)S(1)}, bf16[512,128]{1,0:T(8,128)(2,1)S(1)}, u32[]{:S(2)}, u32[]{:S(2)}) collective-permute-start(bf16[512,128]{1,0:T(8,128)(2,1)S(1)} %collective-permute-done.2.refs_4_), channel_id=1, source_target_pairs={{8,12},{4,0},{9,13},{5,1},{10,14},{6,2},{11,15},{7,3},{24,28},{20,... | collective-permute-start | bytes 393224 | tf_op jit(solution)/shard_map/ppermute | solution.py:59
  33.1 10.8 %collective-permute-start.12 = (f32[512,128]{1,0:T(8,128)S(1)}, f32[512,128]{1,0:T(8,128)S(1)}, u32[]{:S(2)}, u32[]{:S(2)}) collective-permute-start(f32[512,128]{1,0:T(8,128)S(1)} %get-tuple-element.102.refs_1_), channel_id=1, source_target_pairs={{2,0},{0,2},{3,1},{1,3},{6,4},{4,6},{7,5},{5,7},{10,8},{8,10},{11,... | collective-permute-start | bytes 786440 | tf_op jit(solution)/shard_map/ppermute | solution.py:59
  38.2 8.3 %collective-permute-start.11 = (f32[104,128]{1,0:T(8,128)S(1)}, f32[104,128]{1,0:T(8,128)S(1)}, u32[]{:S(2)}, u32[]{:S(2)}) collective-permute-start(f32[104,128]{1,0:T(8,128)S(1)} %add.61), channel_id=1, source_target_pairs={{8,0},{10,2},{12,4},{14,6},{0,8},{2,10},{4,12},{6,14},{9,1},{11,3}... | collective-permute-start | bytes 159752 | tf_op jit(solution)/shard_map/ppermute | solution.py:59
  47.3 5.1 %collective-permute-start.15 = (f32[176,128]{1,0:T(8,128)S(1)}, f32[176,128]{1,0:T(8,128)S(1)}, u32[]{:S(2)}, u32[]{:S(2)}) collective-permute-start(f32[176,128]{1,0:T(8,128)S(1)} %pad_maximum_fusion), channel_id=1, source_target_pairs={{4,0},{6,2},{0,4},{2,6},{12,8},{14,10},{8,12},{10,14},{5,1},{7,3},... | collective-permute-start | bytes 270344 | tf_op jit(solution)/shard_map/ppermute | solution.py:59
  47.9 6.3 %collective-permute-start.16 = (f32[176,128]{1,0:T(8,128)S(1)}, f32[176,128]{1,0:T(8,128)S(1)}, u32[]{:S(2)}, u32[]{:S(2)}) collective-permute-start(f32[176,128]{1,0:T(8,128)S(1)} %pad_maximum_fusion), channel_id=1, source_target_pairs={{6,0},{4,2},{2,4},{0,6},{14,8},{12,10},{10,12},{8,14},{7,1},{5,3},... | collective-permute-start | bytes 270344 | tf_op jit(solution)/shard_map/ppermute | solution.py:59
  54.4 9.0 %collective-permute-start.17 = (f32[72,128]{1,0:T(8,128)S(1)}, f32[72,128]{1,0:T(8,128)S(1)}, u32[]{:S(2)}, u32[]{:S(2)}) collective-permute-start(f32[72,128]{1,0:T(8,128)S(1)} %slice.16.refs_5_), channel_id=1, source_target_pairs={{8,0},{10,2},{12,4},{14,6},{0,8},{2,10},{4,12},{6,14},{9,1},{11,3}... | collective-permute-start | bytes 110600 | tf_op jit(solution)/shard_map/ppermute | solution.py:59
  65.0 9.9 %collective-permute-start.20 = (bf16[512,128]{1,0:T(8,128)(2,1)S(1)}, bf16[512,128]{1,0:T(8,128)(2,1)S(1)}, u32[]{:S(2)}, u32[]{:S(2)}) collective-permute-start(bf16[512,128]{1,0:T(8,128)(2,1)S(1)} %get-tuple-element.114.refs_1_), channel_id=1, source_target_pairs={{8,0},{12,4},{0,8},{4,12},{9,1},{13,5},{1,9},{5,13},{10,2},{14,6},... | collective-permute-start | bytes 393224 | tf_op jit(solution)/shard_map/ppermute | solution.py:59
  66.1 11.0 %collective-permute-start.22 = (bf16[512,128]{1,0:T(8,128)(2,1)S(1)}, bf16[512,128]{1,0:T(8,128)(2,1)S(1)}, u32[]{:S(2)}, u32[]{:S(2)}) collective-permute-start(bf16[512,128]{1,0:T(8,128)(2,1)S(1)} %get-tuple-element.114.refs_1_), channel_id=1, source_target_pairs={{1,0},{0,1},{3,2},{2,3},{5,4},{4,5},{7,6},{6,7},{9,8},{8,9},{11,10... | collective-permute-start | bytes 393224 | tf_op jit(solution)/shard_map/ppermute | solution.py:59
  66.1 13.6 %collective-permute-start.24 = (bf16[512,128]{1,0:T(8,128)(2,1)S(1)}, bf16[512,128]{1,0:T(8,128)(2,1)S(1)}, u32[]{:S(2)}, u32[]{:S(2)}) collective-permute-start(bf16[512,128]{1,0:T(8,128)(2,1)S(1)} %get-tuple-element.114.refs_1_), channel_id=1, source_target_pairs={{4,0},{0,4},{12,8},{8,12},{5,1},{1,5},{13,9},{9,13},{6,2},{2,6},{1... | collective-permute-start | bytes 393224 | tf_op jit(solution)/shard_map/ppermute | solution.py:59
  67.3 13.0 %collective-permute-start.19 = (bf16[512,128]{1,0:T(8,128)(2,1)S(1)}, bf16[512,128]{1,0:T(8,128)(2,1)S(1)}, u32[]{:S(2)}, u32[]{:S(2)}) collective-permute-start(bf16[512,128]{1,0:T(8,128)(2,1)S(1)} %get-tuple-element.114.refs_1_), channel_id=1, source_target_pairs={{4,8},{8,4},{5,9},{9,5},{6,10},{10,6},{7,11},{11,7},{20,24},{24,20... | collective-permute-start | bytes 393224 | tf_op jit(solution)/shard_map/ppermute | solution.py:59
  74.9 6.8 %collective-permute-start.21 = (bf16[512,128]{1,0:T(8,128)(2,1)S(1)}, bf16[512,128]{1,0:T(8,128)(2,1)S(1)}, u32[]{:S(2)}, u32[]{:S(2)}) collective-permute-start(bf16[512,128]{1,0:T(8,128)(2,1)S(1)} %collective-permute-done.20.refs_4_), channel_id=1, source_target_pairs={{8,12},{4,0},{9,13},{5,1},{10,14},{6,2},{11,15},{7,3},{24,28},{20,... | collective-permute-start | bytes 393224 | tf_op jit(solution)/shard_map/ppermute | solution.py:59
  76.4 7.2 %collective-permute-start.27 = (f32[512,128]{1,0:T(8,128)S(1)}, f32[512,128]{1,0:T(8,128)S(1)}, u32[]{:S(2)}, u32[]{:S(2)}) collective-permute-start(f32[512,128]{1,0:T(8,128)S(1)} %get-tuple-element.122.refs_2_.refs_4_.refs_0_), channel_id=1, source_target_pairs={{2,0},{0,2},{3,1},{1,3},{6,4},{4,6},{7,5},{5,7},{10,8},{8,10},{11,... | collective-permute-start | bytes 786440 | tf_op jit(solution)/shard_map/ppermute | solution.py:59
  87.4 7.4 %collective-permute-start.30 = (f32[512,128]{1,0:T(8,128)S(1)}, f32[512,128]{1,0:T(8,128)S(1)}, u32[]{:S(2)}, u32[]{:S(2)}) collective-permute-start(f32[512,128]{1,0:T(8,128)S(1)} %get-tuple-element.126.refs_1_), channel_id=1, source_target_pairs={{2,0},{0,2},{3,1},{1,3},{6,4},{4,6},{7,5},{5,7},{10,8},{8,10},{11,... | collective-permute-start | bytes 786440 | tf_op jit(solution)/shard_map/ppermute | solution.py:59
  93.0 5.1 %collective-permute-start.29 = (f32[104,128]{1,0:T(8,128)S(1)}, f32[104,128]{1,0:T(8,128)S(1)}, u32[]{:S(2)}, u32[]{:S(2)}) collective-permute-start(f32[104,128]{1,0:T(8,128)S(1)} %add.68), channel_id=1, source_target_pairs={{8,0},{10,2},{12,4},{14,6},{0,8},{2,10},{4,12},{6,14},{9,1},{11,3}... | collective-permute-start | bytes 159752 | tf_op jit(solution)/shard_map/ppermute | solution.py:59
  98.8 5.3 %collective-permute-start.33 = (f32[176,128]{1,0:T(8,128)S(1)}, f32[176,128]{1,0:T(8,128)S(1)}, u32[]{:S(2)}, u32[]{:S(2)}) collective-permute-start(f32[176,128]{1,0:T(8,128)S(1)} %pad_maximum_fusion.1), channel_id=1, source_target_pairs={{4,0},{6,2},{0,4},{2,6},{12,8},{14,10},{8,12},{10,14},{5,1},{7,3},... | collective-permute-start | bytes 270344 | tf_op jit(solution)/shard_map/ppermute | solution.py:59
  100.9 5.6 %collective-permute-start.34 = (f32[176,128]{1,0:T(8,128)S(1)}, f32[176,128]{1,0:T(8,128)S(1)}, u32[]{:S(2)}, u32[]{:S(2)}) collective-permute-start(f32[176,128]{1,0:T(8,128)S(1)} %pad_maximum_fusion.1), channel_id=1, source_target_pairs={{6,0},{4,2},{2,4},{0,6},{14,8},{12,10},{10,12},{8,14},{7,1},{5,3},... | collective-permute-start | bytes 270344 | tf_op jit(solution)/shard_map/ppermute | solution.py:59
  106.6 7.0 %collective-permute-start.35 = (f32[72,128]{1,0:T(8,128)S(1)}, f32[72,128]{1,0:T(8,128)S(1)}, u32[]{:S(2)}, u32[]{:S(2)}) collective-permute-start(f32[72,128]{1,0:T(8,128)S(1)} %slice.18.refs_5_), channel_id=1, source_target_pairs={{8,0},{10,2},{12,4},{14,6},{0,8},{2,10},{4,12},{6,14},{9,1},{11,3}... | collective-permute-start | bytes 110600 | tf_op jit(solution)/shard_map/ppermute | solution.py:59
  115.3 10.1 %collective-permute-start.38 = (bf16[512,128]{1,0:T(8,128)(2,1)S(1)}, bf16[512,128]{1,0:T(8,128)(2,1)S(1)}, u32[]{:S(2)}, u32[]{:S(2)}) collective-permute-start(bf16[512,128]{1,0:T(8,128)(2,1)S(1)} %get-tuple-element.140.refs_1_), channel_id=1, source_target_pairs={{8,0},{12,4},{0,8},{4,12},{9,1},{13,5},{1,9},{5,13},{10,2},{14,6},... | collective-permute-start | bytes 393224 | tf_op jit(solution)/shard_map/ppermute | solution.py:59
  117.1 9.8 %collective-permute-start.40 = (bf16[512,128]{1,0:T(8,128)(2,1)S(1)}, bf16[512,128]{1,0:T(8,128)(2,1)S(1)}, u32[]{:S(2)}, u32[]{:S(2)}) collective-permute-start(bf16[512,128]{1,0:T(8,128)(2,1)S(1)} %get-tuple-element.140.refs_1_), channel_id=1, source_target_pairs={{1,0},{0,1},{3,2},{2,3},{5,4},{4,5},{7,6},{6,7},{9,8},{8,9},{11,10... | collective-permute-start | bytes 393224 | tf_op jit(solution)/shard_map/ppermute | solution.py:59
  117.1 13.0 %collective-permute-start.42 = (bf16[512,128]{1,0:T(8,128)(2,1)S(1)}, bf16[512,128]{1,0:T(8,128)(2,1)S(1)}, u32[]{:S(2)}, u32[]{:S(2)}) collective-permute-start(bf16[512,128]{1,0:T(8,128)(2,1)S(1)} %get-tuple-element.140.refs_1_), channel_id=1, source_target_pairs={{4,0},{0,4},{12,8},{8,12},{5,1},{1,5},{13,9},{9,13},{6,2},{2,6},{1... | collective-permute-start | bytes 393224 | tf_op jit(solution)/shard_map/ppermute | solution.py:59
  118.1 12.5 %collective-permute-start.37 = (bf16[512,128]{1,0:T(8,128)(2,1)S(1)}, bf16[512,128]{1,0:T(8,128)(2,1)S(1)}, u32[]{:S(2)}, u32[]{:S(2)}) collective-permute-start(bf16[512,128]{1,0:T(8,128)(2,1)S(1)} %get-tuple-element.140.refs_1_), channel_id=1, source_target_pairs={{4,8},{8,4},{5,9},{9,5},{6,10},{10,6},{7,11},{11,7},{20,24},{24,20... | collective-permute-start | bytes 393224 | tf_op jit(solution)/shard_map/ppermute | solution.py:59
  118.8 13.5 %collective-permute-start.45 = (f32[512,128]{1,0:T(8,128)S(1)}, f32[512,128]{1,0:T(8,128)S(1)}, u32[]{:S(2)}, u32[]{:S(2)}) collective-permute-start(f32[512,128]{1,0:T(8,128)S(1)} %get-tuple-element.149.refs_2_.refs_3_), channel_id=1, source_target_pairs={{2,0},{0,2},{3,1},{1,3},{6,4},{4,6},{7,5},{5,7},{10,8},{8,10},{11,... | collective-permute-start | bytes 786440 | tf_op jit(solution)/shard_map/ppermute | solution.py:59
  125.3 6.8 %collective-permute-start.39 = (bf16[512,128]{1,0:T(8,128)(2,1)S(1)}, bf16[512,128]{1,0:T(8,128)(2,1)S(1)}, u32[]{:S(2)}, u32[]{:S(2)}) collective-permute-start(bf16[512,128]{1,0:T(8,128)(2,1)S(1)} %collective-permute-done.38.refs_4_), channel_id=1, source_target_pairs={{8,12},{4,0},{9,13},{5,1},{10,14},{6,2},{11,15},{7,3},{24,28},{20,... | collective-permute-start | bytes 393224 | tf_op jit(solution)/shard_map/ppermute | solution.py:59
  142.6 5.0 %collective-permute-start.49 = (f32[72,128]{1,0:T(8,128)S(1)}, f32[72,128]{1,0:T(8,128)S(1)}, u32[]{:S(2)}, u32[]{:S(2)}) collective-permute-start(f32[72,128]{1,0:T(8,128)S(1)} %add.75), channel_id=1, source_target_pairs={{6,0},{4,2},{2,4},{0,6},{14,8},{12,10},{10,12},{8,14},{7,1},{5,3},... | collective-permute-start | bytes 110600 | tf_op jit(solution)/shard_map/ppermute | solution.py:59
  143.3 9.6 %collective-permute-start.51 = (f32[512,128]{1,0:T(8,128)S(1)}, f32[512,128]{1,0:T(8,128)S(1)}, u32[]{:S(2)}, u32[]{:S(2)}) collective-permute-start(f32[512,128]{1,0:T(8,128)S(1)} %get-tuple-element.152.refs_1_), channel_id=1, source_target_pairs={{2,0},{0,2},{3,1},{1,3},{6,4},{4,6},{7,5},{5,7},{10,8},{8,10},{11,... | collective-permute-start | bytes 786440 | tf_op jit(solution)/shard_map/ppermute | solution.py:59
  147.6 5.3 %collective-permute-start.50 = (f32[72,128]{1,0:T(8,128)S(1)}, f32[72,128]{1,0:T(8,128)S(1)}, u32[]{:S(2)}, u32[]{:S(2)}) collective-permute-start(f32[72,128]{1,0:T(8,128)S(1)} %add_add_fusion.2), channel_id=1, source_target_pairs={{8,0},{10,2},{12,4},{14,6},{0,8},{2,10},{4,12},{6,14},{9,1},{11,3}... | collective-permute-start | bytes 110600 | tf_op jit(solution)/shard_map/ppermute | solution.py:59
  (20 other events, 53.8 us)

commit v6 on v5

--- a/solution.py
+++ b/solution.py
@@ -75,7 +75,7 @@
 def sum_near(value):
     axes = ("panel", "rhs")
     count = lax.axis_size(axes)
-    one, two, three = (swapped(value, axes, s, count) for s in (1, 2, 3))
+    three, two, one = (swapped(value, axes, s, count) for s in (3, 2, 1))
     return (value + one) + (two + three)
 
 
@@ -292,9 +292,6 @@
 def operate(packed, groups, low, direction, between, final):
     n = lax.axis_size("rhs")
     arrived = [low] + [bring(low) for bring, _, _ in groups[1:]]
-    if len(groups) == lax.axis_size("panel") == 4:
-        inner = permute(low, "panel", [(1, 2), (2, 1)])
-        arrived[3] = inner + permute(arrived[2], "panel", [(2, 3), (1, 0)])
     directions = [direction] + [swapped(direction, "rhs", s, n) for s in range(1, n)]
     pairs = [[low, swapped(low, "coef", 1, 2)]]
     (acc,), token = link_products(packed[:1], pairs, None, n, None)
@@ -351,10 +348,11 @@
 JOINT = PACKED + SUB + LANES
 
 
-def linear_grams(parts, directions, residual, turns, first, final):
+def linear_grams(parts, directions, residual, turns, gram, final):
     strip = parts[0].shape[0]
     n = len(parts)
-    extra = [] if first or final else [residual, *turns]
+    first = gram is not None
+    extra = [gram] if first else [] if final else [residual, *turns]
     rows = PACKED if final else JOINT // 2
 
     def body(*refs):
@@ -364,7 +362,7 @@
         found = None
         for s in range(n):
             image, right = images[s][...], ds[s][...]
-            if extra:
+            if extra and not first:
                 r = rest[0][...] if s == 0 else right - rest[s][...]
                 right = jnp.concatenate([right, r], axis=1)
             term = mm(image, right, (0, 0))
@@ -374,11 +372,10 @@
             return
         mine, mates, stacked = outs
         if first:
-            r = ds[0][...]
-            sym, whole = mm(r, r, (0, 0)), found
+            stacked[:PACKED], whole = rest[0][...], found
         else:
-            sym, whole = symmetric(found[:, :LANES]), found[:, LANES:]
-        stacked[:PACKED] = packed_symmetric(sym)
+            stacked[:PACKED] = packed_symmetric(symmetric(found[:, :LANES]))
+            whole = found[:, LANES:]
         stacked[PACKED : PACKED + SUB] = jnp.zeros((SUB, LANES), F32)
         stacked[PACKED + SUB :] = whole
         half = lax.axis_index("coef")
@@ -394,6 +391,14 @@
         scratch=[] if final else [pltpu.VMEM((2 * rows, LANES), F32)],
     )
     return pieces
+
+
+def gram_of(field, *tokens):
+    def body(field, out):
+        value = field[...]
+        out[...] = packed_symmetric(mm(value, value, (0, 0)))
+
+    return call(body, [shape(PACKED)], field, after=tokens)
 
 
 def square_gram(image_parts):
@@ -618,48 +623,47 @@
     )[:-1]
 
 
-def advance(pieces, gram, residual, image):
-    strip = residual.shape[0]
+def step_sizes(pieces, gram):
     rows = pieces[0].shape[0]
     first = gram is None
-    fields = [*pieces, residual, image] + ([] if first else [gram])
-
-    def body(*refs):
-        mine, mates, r, image, *refs = refs
-        *refs, raw = refs
+    fields = [*pieces] + ([] if first else [gram])
+
+    def body(mine, mates, *refs):
+        *refs, alpha_out, whole_out, inverse_out, gram_out, raw = refs
         half = lax.axis_index("coef")
         raw[pl.ds(pl.multiple_of(half * rows, SUB), rows), :] = mine[...]
         raw[pl.ds(pl.multiple_of((1 - half) * rows, SUB), rows), :] = mates[...]
         sym, whole = unpacked_symmetric(raw[:PACKED, :]), raw[PACKED + SUB :, :]
-        *refs, new_r, alpha_out, partial, inverse_out = refs
         g = sym if first else refs[0][...]
         curvature = symmetric(whole) if first else sym
-        alpha, inverse_out[...] = eliminated((curvature, g), (g, identity()))
-        new_r[...] = r[...] - mm(image[...], alpha)
-        shared = mm(whole, alpha, (0, 0))
-        alpha_out[...] = alpha
-        partial[...] = g - (shared + shared.T)
+        alpha_out[...], inverse_out[...] = eliminated((curvature, g), (g, identity()))
+        whole_out[...] = whole
+        gram_out[...] = g
 
     return call(
         body,
-        [shape(strip)] + [shape(LANES)] * 3,
+        [shape(LANES)] * 4,
         *fields,
         scratch=[pltpu.VMEM((2 * rows, LANES), F32)],
     )[:-1]
 
 
-def turn(square, alpha, partial, inverse, residual, direction):
+def turn(square, alpha, whole, inverse, gram, residual, direction, image):
     strip = residual.shape[0]
 
-    def body(alpha, partial, inverse, r, d, *refs):
-        *terms, new_d, low, beta_out, gram_out = refs
+    def body(alpha, whole, inverse, gram, r, d, image, *refs):
+        *terms, r_out, new_d, low, beta_out, gram_out = refs
         square = terms[0][...]
         for ref in terms[1:]:
             square = square + ref[...]
         a = alpha[...]
-        following = partial[...] + mm(a, mm(unpacked_symmetric(square), a), (0, 0))
+        shared = mm(whole[...], a, (0, 0))
+        quadratic = mm(a, mm(unpacked_symmetric(square), a), (0, 0))
+        following = gram[...] - (shared + shared.T) + quadratic
         beta = mm(inverse[...], following)
-        value = r[...] + mm(d[...], beta)
+        new_r = r[...] - mm(image[...], a)
+        value = new_r + mm(d[...], beta)
+        r_out[...] = new_r
         low[...] = value.astype(BF16)
         new_d[...] = value
         beta_out[...] = beta
@@ -667,12 +671,14 @@
 
     return call(
         body,
-        [shape(strip), shape(strip, dtype=BF16), shape(LANES), shape(LANES)],
+        [shape(strip), shape(strip), shape(strip, dtype=BF16), shape(LANES), shape(LANES)],
         alpha,
-        partial,
+        whole,
         inverse,
+        gram,
         residual,
         direction,
+        image,
         *square,
     )[:-1]
 
@@ -700,18 +706,19 @@
     solution = gram = beta = before = alpha = None
     for step in range(ITERS):
         first, final = step == 0, step + 1 == ITERS
-        state = [solution, None]
+        state = [solution, None, None]
 
         def between(token):
             if first:
-                return retile_token
-            *state[:], token = stepped(solution, before, alpha, beta, token)
+                state[2], token = gram_of(residual, token, retile_token)
+                return token
+            *state[:2], token = stepped(solution, before, alpha, beta, token)
             return token
 
         parts, directions = operate(packed, groups, low, direction, between, final)
-        solution, turns = state
+        solution, turns, own_gram = state
         image_parts = [parts[0]] + [swapped(parts[s], "rhs", s, n) for s in range(1, n)]
-        linear = linear_grams(parts, directions, residual, turns, first, final)
+        linear = linear_grams(parts, directions, residual, turns, own_gram, final)
         if final:
             small = reduce_one(*linear)
             solution, residual = finish(
@@ -720,11 +727,11 @@
             break
         image, square = square_gram(image_parts)
         linear, square = reduce_both(*linear, square)
-        residual, alpha, partial, inverse = advance(linear, gram, residual, image)
+        alpha, whole, inverse, gram = step_sizes(linear, gram)
         square[1:], alpha = lax.optimization_barrier((square[1:], alpha))
         before = directions
-        direction, low, beta, gram = turn(
-            square, alpha, partial, inverse, residual, direction
+        residual, direction, low, beta, gram = turn(
+            square, alpha, whole, inverse, gram, residual, direction, image
         )
     shape_out = (1, 1, strip, LANES)
     return (solution.reshape(shape_out), residual.reshape(shape_out))

time: 158 us -> 146 us (0.924)
  waiting for transfers between devices: 43.8 us -> 34.7 us
  starting transfers between devices: 53.2 us -> 49.7 us
    ppermute x52 -> x49, waiting for transfers between devices: 43.8 us -> 34.7 us  [permute(): return lax.ppermute(value, axis, pairs)]
    ppermute x52 -> x49, starting transfers between devices: 53.2 us -> 49.7 us  [permute(): return lax.ppermute(value, axis, pairs)]
    pallas_call x29 -> x30, Pallas kernels: 59.9 us -> 59.9 us  [call(): pl.pallas_call(ordered, out_shape=list(outs) + [shape(SUB)], in_specs=[HB...]
  transfers between devices with their start and end apart: 52 -> 49, of which waited for: 24 -> 23; matrix products, arithmetic and copies ran while one was open for 0% -> 0% of each run, Pallas kernels for 28% -> 31%
where the time goes in v6:
time: 146 us; the launch traced here: 145 us
  Pallas kernels  59.9 us (41%)
  starting transfers between devices  49.7 us (34%)
  waiting for transfers between devices  34.7 us (24%)
    pallas_call x30, Pallas kernels, call(): pl.pallas_call(ordered, out_shape=list(outs) + [shape(SUB)], in_specs=[HB...  59.9 us
    ppermute x49, starting transfers between devices, permute(): return lax.ppermute(value, axis, pairs)  49.7 us
    ppermute x49, waiting for transfers between devices, permute(): return lax.ppermute(value, axis, pairs)  34.7 us
  transfers between devices with their start and end apart: 49, of which 23 were waited for; matrix products, arithmetic and copies ran while one was open for 0% of the time, Pallas kernels for 31%

profile of v6, /device:TPU:0, one launch (start us, length us, event | category | flops | bytes accessed | tf_op | source)
XLA Modules:
  0.0 145.4 jit_solution(15197803007247362234)
XLA Ops:
  2.1 3.0 %collective-permute-start = (f32[512,128]{1,0:T(8,128)S(1)}, f32[512,128]{1,0:T(8,128)S(1)}, u32[]{:S(2)}, u32[]{:S(2)}) collective-permute-start(f32[512,128]{1,0:T(8,128)S(1)} %get-tuple-element.85), channel_id=1, source_target_pairs={{2,0},{0,2},{3,1},{1,3},{6,4},{4,6},{7,5},{5,7},{10,8},{8,10},{11,... | collective-permute-start | bytes 786440 | tf_op jit(solution)/shard_map/ppermute | solution.py:59
  5.1 2.9 %shard_map.51 = (bf16[3,4,1024,2,128]{4,3,2,1,0:T(2,128)(2,1)S(1)}, f32[8,128]{1,0:T(8,128)S(1)}) custom-call(bf16[9,1024,2,512]{3,2,1,0:T(2,128)(2,1)} %bitcast.22, f32[8,128]{1,0:T(8,128)S(1)} %get-tuple-element.86.refs_1_), custom_call_target="tpu_custom_call" | custom-call | flops 1 | bytes 1 | tf_op jit(solution)/shard_map/pallas_call | solution.py:43
  8.0 2.2 %shard_map.52 = (bf16[2,4,1024,2,128]{4,3,2,1,0:T(2,128)(2,1)S(1)}, f32[8,128]{1,0:T(8,128)S(1)}) custom-call(bf16[9,1024,2,512]{3,2,1,0:T(2,128)(2,1)} %bitcast.23, f32[8,128]{1,0:T(8,128)S(1)} %get-tuple-element.87.refs_1_), custom_call_target="tpu_custom_call" | custom-call | flops 1 | bytes 1 | tf_op jit(solution)/shard_map/pallas_call | solution.py:43
  11.6 2.9 %collective-permute-start.6 = (bf16[512,128]{1,0:T(8,128)(2,1)S(1)}, bf16[512,128]{1,0:T(8,128)(2,1)S(1)}, u32[]{:S(2)}, u32[]{:S(2)}) collective-permute-start(bf16[512,128]{1,0:T(8,128)(2,1)S(1)} %get-tuple-element.92.refs_1_), channel_id=1, source_target_pairs={{8,0},{12,4},{0,8},{4,12},{9,1},{13,5},{1,9},{5,13},{10,2},{14,6},... | collective-permute-start | bytes 393224 | tf_op jit(solution)/shard_map/ppermute | solution.py:59
  17.8 2.2 %shard_map.54 = (bf16[2,4,1024,2,128]{4,3,2,1,0:T(2,128)(2,1)S(1)}, f32[8,128]{1,0:T(8,128)S(1)}) custom-call(bf16[9,1024,2,512]{3,2,1,0:T(2,128)(2,1)} %bitcast.24, f32[8,128]{1,0:T(8,128)S(1)} %get-tuple-element.89.refs_1_), custom_call_target="tpu_custom_call" | custom-call | flops 1 | bytes 1 | tf_op jit(solution)/shard_map/pallas_call | solution.py:43
  20.0 2.2 %shard_map.55 = (bf16[2,4,1024,2,128]{4,3,2,1,0:T(2,128)(2,1)S(1)}, f32[8,128]{1,0:T(8,128)S(1)}) custom-call(bf16[9,1024,2,512]{3,2,1,0:T(2,128)(2,1)} %bitcast.25, f32[8,128]{1,0:T(8,128)S(1)} %get-tuple-element.90.refs_1_), custom_call_target="tpu_custom_call" | custom-call | flops 1 | bytes 1 | tf_op jit(solution)/shard_map/pallas_call | solution.py:43
  22.2 2.0 %shard_map.56 = (f32[1024,128]{1,0:T(8,128)S(1)}, f32[8,128]{1,0:T(8,128)S(1)}) custom-call(bf16[3,4,2048,128]{3,2,1,0:T(8,128)(2,1)S(1)} %bitcast.13, bf16[512,128]{1,0:T(8,128)(2,1)S(1)} %get-tuple-element.92.refs_1_, bf16[512,128]{1,0:T(8,128)(2,1)S(1)} %collective-permute-done.2.refs_2_), custom_call_target="tpu_custom_call" | custom-call | flops 1 | bytes 1 | tf_op jit(solution)/shard_map/pallas_call | solution.py:43
  26.3 3.0 %shard_map.58 = (f32[1024,128]{1,0:T(8,128)S(1)}, f32[8,128]{1,0:T(8,128)}) custom-call(bf16[2,4,2048,128]{3,2,1,0:T(8,128)(2,1)S(1)} %bitcast.16, bf16[2,4,2048,128]{3,2,1,0:T(8,128)(2,1)S(1)} %bitcast.19, bf16[512,128]{1,0:T(8,128)(2,1)S(1)} %collective-permute-done.4.refs_2_, bf16[512,128]{1,0:T(8,128)(2,1)S(1)} %collective-permute-done.5.refs_3_, ...), custom_call_target="tpu_custom_call" | custom-call | flops 1 | bytes 1 | tf_op jit(solution)/shard_map/pallas_call | solution.py:43
  34.6 4.4 %collective-permute-start.10 = (f32[104,128]{1,0:T(8,128)S(1)}, f32[104,128]{1,0:T(8,128)S(1)}, u32[]{:S(2)}, u32[]{:S(2)}) collective-permute-start(f32[104,128]{1,0:T(8,128)S(1)} %add.51), channel_id=1, source_target_pairs={{8,0},{10,2},{12,4},{14,6},{0,8},{2,10},{4,12},{6,14},{9,1},{11,3}... | collective-permute-start | bytes 159752 | tf_op jit(solution)/shard_map/ppermute | solution.py:59
  39.9 2.3 %collective-permute-done.10 = f32[104,128]{1,0:T(8,128)S(1)} collective-permute-done((f32[104,128]{1,0:T(8,128)S(1)}, f32[104,128]{1,0:T(8,128)S(1)}, u32[]{:S(2)}, u32[]{:S(2)}) %collective-permute-start.10) | collective-permute-done | bytes 53280 | tf_op jit(solution)/shard_map/ppermute | solution.py:59
  48.3 1.9 %collective-permute-done.15 = f32[176,128]{1,0:T(8,128)S(1)} collective-permute-done((f32[176,128]{1,0:T(8,128)S(1)}, f32[176,128]{1,0:T(8,128)S(1)}, u32[]{:S(2)}, u32[]{:S(2)}) %collective-permute-start.15) | collective-permute-done | bytes 90144 | tf_op jit(solution)/shard_map/ppermute | solution.py:59
  50.3 2.3 %collective-permute-start.16 = (f32[72,128]{1,0:T(8,128)S(1)}, f32[72,128]{1,0:T(8,128)S(1)}, u32[]{:S(2)}, u32[]{:S(2)}) collective-permute-start(f32[72,128]{1,0:T(8,128)S(1)} %slice.16.refs_7_), channel_id=1, source_target_pairs={{8,0},{10,2},{12,4},{14,6},{0,8},{2,10},{4,12},{6,14},{9,1},{11,3}... | collective-permute-start | bytes 110600 | tf_op jit(solution)/shard_map/ppermute | solution.py:59
  52.6 5.6 %shard_map.63 = (f32[128,128]{1,0:T(8,128)S(1)}, f32[128,128]{1,0:T(8,128)S(1)}, f32[128,128]{1,0:T(8,128)S(1)}, f32[128,128]{1,0:T(8,128)S(1)}, f32[8,128]{1,0:T(8,128)}) custom-call(f32[104,128]{1,0:T(8,128)S(1)} %slice.17.refs_0_, f32[104,128]{1,0:T(8,128)S(1)} %collective-permute-done.17.refs_1_), custom_call_target="tpu_custom_call" | custom-call | flops 1 | bytes 1 | tf_op jit(solution)/shard_map/pallas_call | solution.py:43
  58.2 1.9 %shard_map.64 = (f32[512,128]{1,0:T(8,128)S(1)}, f32[512,128]{1,0:T(8,128)S(1)}, bf16[512,128]{1,0:T(8,128)(2,1)S(1)}, f32[128,128]{1,0:T(8,128)S(1)}, f32[128,128]{1,0:T(8,128)S(1)}, /*index=5*/f32[8,128]{1,0:T(8,128)}) custom-call(f32[128,128]{1,0:T(8,128)S(1)} %get-tuple-element.114.refs_0_.refs_2_, f32[128,128]{1,0:T(8,128)S(1)} %get-tuple-element.115.refs_1_, ...), custom_call_target="tpu_custom_call" | custom-call | flops 1 | bytes 1 | tf_op jit(solution)/shard_map/pallas_call | solution.py:43
  62.6 2.1 %collective-permute-start.18 = (bf16[512,128]{1,0:T(8,128)(2,1)S(1)}, bf16[512,128]{1,0:T(8,128)(2,1)S(1)}, u32[]{:S(2)}, u32[]{:S(2)}) collective-permute-start(bf16[512,128]{1,0:T(8,128)(2,1)S(1)} %get-tuple-element.120.refs_1_), channel_id=1, source_target_pairs={{12,0},{8,4},{4,8},{0,12},{13,1},{9,5},{5,9},{1,13},{14,2},{10,6},... | collective-permute-start | bytes 393224 | tf_op jit(solution)/shard_map/ppermute | solution.py:59
  66.2 2.0 %shard_map.65 = (f32[1024,128]{1,0:T(8,128)S(1)}, f32[8,128]{1,0:T(8,128)S(1)}) custom-call(bf16[3,4,2048,128]{3,2,1,0:T(8,128)(2,1)S(1)} %bitcast.14, bf16[512,128]{1,0:T(8,128)(2,1)S(1)} %get-tuple-element.120.refs_1_, bf16[512,128]{1,0:T(8,128)(2,1)S(1)} %collective-permute-done.19.refs_2_), custom_call_target="tpu_custom_call" | custom-call | flops 1 | bytes 1 | tf_op jit(solution)/shard_map/pallas_call | solution.py:43
  68.8 2.0 %collective-permute-done.23.refs_4_ = bf16[512,128]{1,0:T(8,128)(2,1)S(1)} collective-permute-done((bf16[512,128]{1,0:T(8,128)(2,1)S(1)}, bf16[512,128]{1,0:T(8,128)(2,1)S(1)}, u32[]{:S(2)}, u32[]{:S(2)}) %collective-permute-start.23) | collective-permute-done | bytes 131104 | tf_op jit(solution)/shard_map/ppermute | solution.py:59
  71.3 2.0 %collective-permute-done.18.refs_1_ = bf16[512,128]{1,0:T(8,128)(2,1)S(1)} collective-permute-done((bf16[512,128]{1,0:T(8,128)(2,1)S(1)}, bf16[512,128]{1,0:T(8,128)(2,1)S(1)}, u32[]{:S(2)}, u32[]{:S(2)}) %collective-permute-start.18) | collective-permute-done | bytes 131104 | tf_op jit(solution)/shard_map/ppermute | solution.py:59
  73.3 3.0 %shard_map.67 = (f32[1024,128]{1,0:T(8,128)S(1)}, f32[8,128]{1,0:T(8,128)}) custom-call(bf16[2,4,2048,128]{3,2,1,0:T(8,128)(2,1)S(1)} %bitcast.17, bf16[2,4,2048,128]{3,2,1,0:T(8,128)(2,1)S(1)} %bitcast.20, bf16[512,128]{1,0:T(8,128)(2,1)S(1)} %collective-permute-done.21.refs_2_, bf16[512,128]{1,0:T(8,128)(2,1)S(1)} %collective-permute-done.22.refs_3_, ...), custom_call_target="tpu_custom_call" | custom-call | flops 1 | bytes 1 | tf_op jit(solution)/shard_map/pallas_call | solution.py:43
  81.8 3.0 %collective-permute-start.27 = (f32[104,128]{1,0:T(8,128)S(1)}, f32[104,128]{1,0:T(8,128)S(1)}, u32[]{:S(2)}, u32[]{:S(2)}) collective-permute-start(f32[104,128]{1,0:T(8,128)S(1)} %add.57), channel_id=1, source_target_pairs={{8,0},{10,2},{12,4},{14,6},{0,8},{2,10},{4,12},{6,14},{9,1},{11,3}... | collective-permute-start | bytes 159752 | tf_op jit(solution)/shard_map/ppermute | solution.py:59
  89.0 3.3 %collective-permute-start.31 = (f32[176,128]{1,0:T(8,128)S(1)}, f32[176,128]{1,0:T(8,128)S(1)}, u32[]{:S(2)}, u32[]{:S(2)}) collective-permute-start(f32[176,128]{1,0:T(8,128)S(1)} %pad_maximum_fusion.1), channel_id=1, source_target_pairs={{4,0},{6,2},{0,4},{2,6},{12,8},{14,10},{8,12},{10,14},{5,1},{7,3},... | collective-permute-start | bytes 270344 | tf_op jit(solution)/shard_map/ppermute | solution.py:59
  92.9 2.5 %collective-permute-done.31 = f32[176,128]{1,0:T(8,128)S(1)} collective-permute-done((f32[176,128]{1,0:T(8,128)S(1)}, f32[176,128]{1,0:T(8,128)S(1)}, u32[]{:S(2)}, u32[]{:S(2)}) %collective-permute-start.31) | collective-permute-done | bytes 90144 | tf_op jit(solution)/shard_map/ppermute | solution.py:59
  95.4 2.3 %collective-permute-done.32 = f32[176,128]{1,0:T(8,128)S(1)} collective-permute-done((f32[176,128]{1,0:T(8,128)S(1)}, f32[176,128]{1,0:T(8,128)S(1)}, u32[]{:S(2)}, u32[]{:S(2)}) %collective-permute-start.32) | collective-permute-done | bytes 90144 | tf_op jit(solution)/shard_map/ppermute | solution.py:59
  99.2 5.3 %shard_map.72 = (f32[128,128]{1,0:T(8,128)S(1)}, f32[128,128]{1,0:T(8,128)S(1)}, f32[128,128]{1,0:T(8,128)S(1)}, f32[128,128]{1,0:T(8,128)S(1)}, f32[8,128]{1,0:T(8,128)}) custom-call(f32[104,128]{1,0:T(8,128)S(1)} %slice.19.refs_0_, f32[104,128]{1,0:T(8,128)S(1)} %collective-permute-done.34.refs_1_, f32[128,128]{1,0:T(8,128)S(1)} %get-tuple-element.139.refs_2_), custom_call_target="tpu_custom_call" | custom-call | flops 1 | bytes 1 | tf_op jit(solution)/shard_map/pallas_call | solution.py:43
  111.5 2.0 %shard_map.74 = (f32[1024,128]{1,0:T(8,128)S(1)}, f32[8,128]{1,0:T(8,128)S(1)}) custom-call(bf16[3,4,2048,128]{3,2,1,0:T(8,128)(2,1)S(1)} %bitcast.15, bf16[512,128]{1,0:T(8,128)(2,1)S(1)} %get-tuple-element.147.refs_1_, bf16[512,128]{1,0:T(8,128)(2,1)S(1)} %collective-permute-done.36.refs_2_), custom_call_target="tpu_custom_call" | custom-call | flops 1 | bytes 1 | tf_op jit(solution)/shard_map/pallas_call | solution.py:43
  114.8 2.0 %collective-permute-done.40.refs_4_ = bf16[512,128]{1,0:T(8,128)(2,1)S(1)} collective-permute-done((bf16[512,128]{1,0:T(8,128)(2,1)S(1)}, bf16[512,128]{1,0:T(8,128)(2,1)S(1)}, u32[]{:S(2)}, u32[]{:S(2)}) %collective-permute-start.40) | collective-permute-done | bytes 131104 | tf_op jit(solution)/shard_map/ppermute | solution.py:59
  119.1 3.0 %shard_map.76 = (f32[1024,128]{1,0:T(8,128)S(1)}, f32[8,128]{1,0:T(8,128)}) custom-call(bf16[2,4,2048,128]{3,2,1,0:T(8,128)(2,1)S(1)} %bitcast.18, bf16[2,4,2048,128]{3,2,1,0:T(8,128)(2,1)S(1)} %bitcast.21, bf16[512,128]{1,0:T(8,128)(2,1)S(1)} %collective-permute-done.38.refs_2_, bf16[512,128]{1,0:T(8,128)(2,1)S(1)} %collective-permute-done.39.refs_3_, ...), custom_call_target="tpu_custom_call" | custom-call | flops 1 | bytes 1 | tf_op jit(solution)/shard_map/pallas_call | solution.py:43
  122.2 1.9 %shard_map.77 = (f32[512,128]{1,0:T(8,128)S(1)}, f32[512,128]{1,0:T(8,128)S(1)}, f32[8,128]{1,0:T(8,128)}) custom-call(bf16[2,4,2048,128]{3,2,1,0:T(8,128)(2,1)S(1)} %bitcast.12, bf16[512,128]{1,0:T(8,128)(2,1)S(1)} %collective-permute-done.35.refs_1_, bf16[512,128]{1,0:T(8,128)(2,1)S(1)} %collective-permute-done.37.refs_2_, ...), custom_call_target="tpu_custom_call" | custom-call | flops 1 | bytes 1 | tf_op jit(solution)/shard_map/pallas_call | solution.py:43
  128.0 2.3 %collective-permute-start.45 = (f32[72,128]{1,0:T(8,128)S(1)}, f32[72,128]{1,0:T(8,128)S(1)}, u32[]{:S(2)}, u32[]{:S(2)}) collective-permute-start(f32[72,128]{1,0:T(8,128)S(1)} %add.63), channel_id=1, source_target_pairs={{4,0},{6,2},{0,4},{2,6},{12,8},{14,10},{8,12},{10,14},{5,1},{7,3},... | collective-permute-start | bytes 110600 | tf_op jit(solution)/shard_map/ppermute | solution.py:59
  132.2 3.0 %collective-permute-done.46 = f32[72,128]{1,0:T(8,128)S(1)} collective-permute-done((f32[72,128]{1,0:T(8,128)S(1)}, f32[72,128]{1,0:T(8,128)S(1)}, u32[]{:S(2)}, u32[]{:S(2)}) %collective-permute-start.46) | collective-permute-done | bytes 36896 | tf_op jit(solution)/shard_map/ppermute | solution.py:59
  136.4 3.8 %collective-permute-done.47 = f32[72,128]{1,0:T(8,128)S(1)} collective-permute-done((f32[72,128]{1,0:T(8,128)S(1)}, f32[72,128]{1,0:T(8,128)S(1)}, u32[]{:S(2)}, u32[]{:S(2)}) %collective-permute-start.47) | collective-permute-done | bytes 36896 | tf_op jit(solution)/shard_map/ppermute | solution.py:59
  140.2 5.2 %shard_map.79 = (f32[512,128]{1,0:T(8,128)}, f32[512,128]{1,0:T(8,128)}, f32[8,128]{1,0:T(8,128)}) custom-call(f32[72,128]{1,0:T(8,128)S(1)} %add.67.refs_0_, f32[128,128]{1,0:T(8,128)S(1)} %get-tuple-element.161.refs_1_, f32[512,128]{1,0:T(8,128)S(1)} %get-tuple-element.162.refs_2_, f32[512,128]{1,0:T(8,128)S(1)} %get-tuple-element.156.refs_2_.refs_3_, ...), custom_call_target="tpu_custom_call" | custom-call | flops 1 | bytes 1 | tf_op jit(solution)/shard_map/pallas_call | solution.py:43
  (113 shorter events, 55.1 us)
Async XLA Ops:
  2.1 9.3 %collective-permute-start = (f32[512,128]{1,0:T(8,128)S(1)}, f32[512,128]{1,0:T(8,128)S(1)}, u32[]{:S(2)}, u32[]{:S(2)}) collective-permute-start(f32[512,128]{1,0:T(8,128)S(1)} %get-tuple-element.85), channel_id=1, source_target_pairs={{2,0},{0,2},{3,1},{1,3},{6,4},{4,6},{7,5},{5,7},{10,8},{8,10},{11,... | collective-permute-start | bytes 786440 | tf_op jit(solution)/shard_map/ppermute | solution.py:59
  11.5 10.7 %collective-permute-start.2 = (bf16[512,128]{1,0:T(8,128)(2,1)S(1)}, bf16[512,128]{1,0:T(8,128)(2,1)S(1)}, u32[]{:S(2)}, u32[]{:S(2)}) collective-permute-start(bf16[512,128]{1,0:T(8,128)(2,1)S(1)} %get-tuple-element.92.refs_1_), channel_id=1, source_target_pairs={{1,0},{0,1},{3,2},{2,3},{5,4},{4,5},{7,6},{6,7},{9,8},{8,9},{11,10... | collective-permute-start | bytes 393224 | tf_op jit(solution)/shard_map/ppermute | solution.py:59
  11.6 13.1 %collective-permute-start.6 = (bf16[512,128]{1,0:T(8,128)(2,1)S(1)}, bf16[512,128]{1,0:T(8,128)(2,1)S(1)}, u32[]{:S(2)}, u32[]{:S(2)}) collective-permute-start(bf16[512,128]{1,0:T(8,128)(2,1)S(1)} %get-tuple-element.92.refs_1_), channel_id=1, source_target_pairs={{8,0},{12,4},{0,8},{4,12},{9,1},{13,5},{1,9},{5,13},{10,2},{14,6},... | collective-permute-start | bytes 393224 | tf_op jit(solution)/shard_map/ppermute | solution.py:59
  14.5 10.3 %collective-permute-start.4 = (bf16[512,128]{1,0:T(8,128)(2,1)S(1)}, bf16[512,128]{1,0:T(8,128)(2,1)S(1)}, u32[]{:S(2)}, u32[]{:S(2)}) collective-permute-start(bf16[512,128]{1,0:T(8,128)(2,1)S(1)} %get-tuple-element.92.refs_1_), channel_id=1, source_target_pairs={{4,0},{0,4},{12,8},{8,12},{5,1},{1,5},{13,9},{9,13},{6,2},{2,6},{1... | collective-permute-start | bytes 393224 | tf_op jit(solution)/shard_map/ppermute | solution.py:59
  16.1 10.3 %collective-permute-start.8 = (f32[512,128]{1,0:T(8,128)S(1)}, f32[512,128]{1,0:T(8,128)S(1)}, u32[]{:S(2)}, u32[]{:S(2)}) collective-permute-start(f32[512,128]{1,0:T(8,128)S(1)} %get-tuple-element.95.refs_0_.refs_2_.refs_4_.refs_5_), channel_id=1, source_target_pairs={{2,0},{0,2},{3,1},{1,3},{6,4},{4,6},{7,5},{5,7},{10,8},{8,10},{11,... | collective-permute-start | bytes 786440 | tf_op jit(solution)/shard_map/ppermute | solution.py:59
  17.5 7.9 %collective-permute-start.1 = (bf16[512,128]{1,0:T(8,128)(2,1)S(1)}, bf16[512,128]{1,0:T(8,128)(2,1)S(1)}, u32[]{:S(2)}, u32[]{:S(2)}) collective-permute-start(bf16[512,128]{1,0:T(8,128)(2,1)S(1)} %get-tuple-element.92.refs_1_), channel_id=1, source_target_pairs={{12,0},{8,4},{4,8},{0,12},{13,1},{9,5},{5,9},{1,13},{14,2},{10,6},... | collective-permute-start | bytes 393224 | tf_op jit(solution)/shard_map/ppermute | solution.py:59
  30.2 8.7 %collective-permute-start.11 = (f32[512,128]{1,0:T(8,128)S(1)}, f32[512,128]{1,0:T(8,128)S(1)}, u32[]{:S(2)}, u32[]{:S(2)}) collective-permute-start(f32[512,128]{1,0:T(8,128)S(1)} %get-tuple-element.107.refs_1_), channel_id=1, source_target_pairs={{2,0},{0,2},{3,1},{1,3},{6,4},{4,6},{7,5},{5,7},{10,8},{8,10},{11,... | collective-permute-start | bytes 786440 | tf_op jit(solution)/shard_map/ppermute | solution.py:59
  34.6 7.7 %collective-permute-start.10 = (f32[104,128]{1,0:T(8,128)S(1)}, f32[104,128]{1,0:T(8,128)S(1)}, u32[]{:S(2)}, u32[]{:S(2)}) collective-permute-start(f32[104,128]{1,0:T(8,128)S(1)} %add.51), channel_id=1, source_target_pairs={{8,0},{10,2},{12,4},{14,6},{0,8},{2,10},{4,12},{6,14},{9,1},{11,3}... | collective-permute-start | bytes 159752 | tf_op jit(solution)/shard_map/ppermute | solution.py:59
  42.3 4.6 %collective-permute-start.13 = (f32[176,128]{1,0:T(8,128)S(1)}, f32[176,128]{1,0:T(8,128)S(1)}, u32[]{:S(2)}, u32[]{:S(2)}) collective-permute-start(f32[176,128]{1,0:T(8,128)S(1)} %pad_maximum_fusion), channel_id=1, source_target_pairs={{2,0},{0,2},{6,4},{4,6},{10,8},{8,10},{14,12},{12,14},{3,1},{1,3},... | collective-permute-start | bytes 270344 | tf_op jit(solution)/shard_map/ppermute | solution.py:59
  42.9 5.4 %collective-permute-start.14 = (f32[176,128]{1,0:T(8,128)S(1)}, f32[176,128]{1,0:T(8,128)S(1)}, u32[]{:S(2)}, u32[]{:S(2)}) collective-permute-start(f32[176,128]{1,0:T(8,128)S(1)} %pad_maximum_fusion), channel_id=1, source_target_pairs={{4,0},{6,2},{0,4},{2,6},{12,8},{14,10},{8,12},{10,14},{5,1},{7,3},... | collective-permute-start | bytes 270344 | tf_op jit(solution)/shard_map/ppermute | solution.py:59
  44.2 6.0 %collective-permute-start.15 = (f32[176,128]{1,0:T(8,128)S(1)}, f32[176,128]{1,0:T(8,128)S(1)}, u32[]{:S(2)}, u32[]{:S(2)}) collective-permute-start(f32[176,128]{1,0:T(8,128)S(1)} %pad_maximum_fusion), channel_id=1, source_target_pairs={{6,0},{4,2},{2,4},{0,6},{14,8},{12,10},{10,12},{8,14},{7,1},{5,3},... | collective-permute-start | bytes 270344 | tf_op jit(solution)/shard_map/ppermute | solution.py:59
  50.3 7.9 %collective-permute-start.16 = (f32[72,128]{1,0:T(8,128)S(1)}, f32[72,128]{1,0:T(8,128)S(1)}, u32[]{:S(2)}, u32[]{:S(2)}) collective-permute-start(f32[72,128]{1,0:T(8,128)S(1)} %slice.16.refs_7_), channel_id=1, source_target_pairs={{8,0},{10,2},{12,4},{14,6},{0,8},{2,10},{4,12},{6,14},{9,1},{11,3}... | collective-permute-start | bytes 110600 | tf_op jit(solution)/shard_map/ppermute | solution.py:59
  60.2 6.0 %collective-permute-start.19 = (bf16[512,128]{1,0:T(8,128)(2,1)S(1)}, bf16[512,128]{1,0:T(8,128)(2,1)S(1)}, u32[]{:S(2)}, u32[]{:S(2)}) collective-permute-start(bf16[512,128]{1,0:T(8,128)(2,1)S(1)} %get-tuple-element.120.refs_1_), channel_id=1, source_target_pairs={{1,0},{0,1},{3,2},{2,3},{5,4},{4,5},{7,6},{6,7},{9,8},{8,9},{11,10... | collective-permute-start | bytes 393224 | tf_op jit(solution)/shard_map/ppermute | solution.py:59
  60.3 10.5 %collective-permute-start.23 = (bf16[512,128]{1,0:T(8,128)(2,1)S(1)}, bf16[512,128]{1,0:T(8,128)(2,1)S(1)}, u32[]{:S(2)}, u32[]{:S(2)}) collective-permute-start(bf16[512,128]{1,0:T(8,128)(2,1)S(1)} %get-tuple-element.120.refs_1_), channel_id=1, source_target_pairs={{8,0},{12,4},{0,8},{4,12},{9,1},{13,5},{1,9},{5,13},{10,2},{14,6},... | collective-permute-start | bytes 393224 | tf_op jit(solution)/shard_map/ppermute | solution.py:59
  61.5 9.4 %collective-permute-start.21 = (bf16[512,128]{1,0:T(8,128)(2,1)S(1)}, bf16[512,128]{1,0:T(8,128)(2,1)S(1)}, u32[]{:S(2)}, u32[]{:S(2)}) collective-permute-start(bf16[512,128]{1,0:T(8,128)(2,1)S(1)} %get-tuple-element.120.refs_1_), channel_id=1, source_target_pairs={{4,0},{0,4},{12,8},{8,12},{5,1},{1,5},{13,9},{9,13},{6,2},{2,6},{1... | collective-permute-start | bytes 393224 | tf_op jit(solution)/shard_map/ppermute | solution.py:59
  62.6 10.7 %collective-permute-start.18 = (bf16[512,128]{1,0:T(8,128)(2,1)S(1)}, bf16[512,128]{1,0:T(8,128)(2,1)S(1)}, u32[]{:S(2)}, u32[]{:S(2)}) collective-permute-start(bf16[512,128]{1,0:T(8,128)(2,1)S(1)} %get-tuple-element.120.refs_1_), channel_id=1, source_target_pairs={{12,0},{8,4},{4,8},{0,12},{13,1},{9,5},{5,9},{1,13},{14,2},{10,6},... | collective-permute-start | bytes 393224 | tf_op jit(solution)/shard_map/ppermute | solution.py:59
  64.7 8.6 %collective-permute-start.25 = (f32[512,128]{1,0:T(8,128)S(1)}, f32[512,128]{1,0:T(8,128)S(1)}, u32[]{:S(2)}, u32[]{:S(2)}) collective-permute-start(f32[512,128]{1,0:T(8,128)S(1)} %get-tuple-element.128.refs_2_.refs_5_.refs_0_), channel_id=1, source_target_pairs={{2,0},{0,2},{3,1},{1,3},{6,4},{4,6},{7,5},{5,7},{10,8},{8,10},{11,... | collective-permute-start | bytes 786440 | tf_op jit(solution)/shard_map/ppermute | solution.py:59
  77.2 8.8 %collective-permute-start.28 = (f32[512,128]{1,0:T(8,128)S(1)}, f32[512,128]{1,0:T(8,128)S(1)}, u32[]{:S(2)}, u32[]{:S(2)}) collective-permute-start(f32[512,128]{1,0:T(8,128)S(1)} %get-tuple-element.132.refs_1_), channel_id=1, source_target_pairs={{2,0},{0,2},{3,1},{1,3},{6,4},{4,6},{7,5},{5,7},{10,8},{8,10},{11,... | collective-permute-start | bytes 786440 | tf_op jit(solution)/shard_map/ppermute | solution.py:59
  81.8 5.2 %collective-permute-start.27 = (f32[104,128]{1,0:T(8,128)S(1)}, f32[104,128]{1,0:T(8,128)S(1)}, u32[]{:S(2)}, u32[]{:S(2)}) collective-permute-start(f32[104,128]{1,0:T(8,128)S(1)} %add.57), channel_id=1, source_target_pairs={{8,0},{10,2},{12,4},{14,6},{0,8},{2,10},{4,12},{6,14},{9,1},{11,3}... | collective-permute-start | bytes 159752 | tf_op jit(solution)/shard_map/ppermute | solution.py:59
  88.2 4.8 %collective-permute-start.30 = (f32[176,128]{1,0:T(8,128)S(1)}, f32[176,128]{1,0:T(8,128)S(1)}, u32[]{:S(2)}, u32[]{:S(2)}) collective-permute-start(f32[176,128]{1,0:T(8,128)S(1)} %pad_maximum_fusion.1), channel_id=1, source_target_pairs={{2,0},{0,2},{6,4},{4,6},{10,8},{8,10},{14,12},{12,14},{3,1},{1,3},... | collective-permute-start | bytes 270344 | tf_op jit(solution)/shard_map/ppermute | solution.py:59
  89.0 6.4 %collective-permute-start.31 = (f32[176,128]{1,0:T(8,128)S(1)}, f32[176,128]{1,0:T(8,128)S(1)}, u32[]{:S(2)}, u32[]{:S(2)}) collective-permute-start(f32[176,128]{1,0:T(8,128)S(1)} %pad_maximum_fusion.1), channel_id=1, source_target_pairs={{4,0},{6,2},{0,4},{2,6},{12,8},{14,10},{8,12},{10,14},{5,1},{7,3},... | collective-permute-start | bytes 270344 | tf_op jit(solution)/shard_map/ppermute | solution.py:59
  92.3 5.4 %collective-permute-start.32 = (f32[176,128]{1,0:T(8,128)S(1)}, f32[176,128]{1,0:T(8,128)S(1)}, u32[]{:S(2)}, u32[]{:S(2)}) collective-permute-start(f32[176,128]{1,0:T(8,128)S(1)} %pad_maximum_fusion.1), channel_id=1, source_target_pairs={{6,0},{4,2},{2,4},{0,6},{14,8},{12,10},{10,12},{8,14},{7,1},{5,3},... | collective-permute-start | bytes 270344 | tf_op jit(solution)/shard_map/ppermute | solution.py:59
  97.9 6.6 %collective-permute-start.33 = (f32[72,128]{1,0:T(8,128)S(1)}, f32[72,128]{1,0:T(8,128)S(1)}, u32[]{:S(2)}, u32[]{:S(2)}) collective-permute-start(f32[72,128]{1,0:T(8,128)S(1)} %slice.18.refs_7_), channel_id=1, source_target_pairs={{8,0},{10,2},{12,4},{14,6},{0,8},{2,10},{4,12},{6,14},{9,1},{11,3}... | collective-permute-start | bytes 110600 | tf_op jit(solution)/shard_map/ppermute | solution.py:59
  106.3 5.3 %collective-permute-start.36 = (bf16[512,128]{1,0:T(8,128)(2,1)S(1)}, bf16[512,128]{1,0:T(8,128)(2,1)S(1)}, u32[]{:S(2)}, u32[]{:S(2)}) collective-permute-start(bf16[512,128]{1,0:T(8,128)(2,1)S(1)} %get-tuple-element.147.refs_1_), channel_id=1, source_target_pairs={{1,0},{0,1},{3,2},{2,3},{5,4},{4,5},{7,6},{6,7},{9,8},{8,9},{11,10... | collective-permute-start | bytes 393224 | tf_op jit(solution)/shard_map/ppermute | solution.py:59
  106.4 10.4 %collective-permute-start.40 = (bf16[512,128]{1,0:T(8,128)(2,1)S(1)}, bf16[512,128]{1,0:T(8,128)(2,1)S(1)}, u32[]{:S(2)}, u32[]{:S(2)}) collective-permute-start(bf16[512,128]{1,0:T(8,128)(2,1)S(1)} %get-tuple-element.147.refs_1_), channel_id=1, source_target_pairs={{8,0},{12,4},{0,8},{4,12},{9,1},{13,5},{1,9},{5,13},{10,2},{14,6},... | collective-permute-start | bytes 393224 | tf_op jit(solution)/shard_map/ppermute | solution.py:59
  108.1 8.7 %collective-permute-start.38 = (bf16[512,128]{1,0:T(8,128)(2,1)S(1)}, bf16[512,128]{1,0:T(8,128)(2,1)S(1)}, u32[]{:S(2)}, u32[]{:S(2)}) collective-permute-start(bf16[512,128]{1,0:T(8,128)(2,1)S(1)} %get-tuple-element.147.refs_1_), channel_id=1, source_target_pairs={{4,0},{0,4},{12,8},{8,12},{5,1},{1,5},{13,9},{9,13},{6,2},{2,6},{1... | collective-permute-start | bytes 393224 | tf_op jit(solution)/shard_map/ppermute | solution.py:59
  109.0 10.1 %collective-permute-start.42 = (f32[512,128]{1,0:T(8,128)S(1)}, f32[512,128]{1,0:T(8,128)S(1)}, u32[]{:S(2)}, u32[]{:S(2)}) collective-permute-start(f32[512,128]{1,0:T(8,128)S(1)} %get-tuple-element.156.refs_2_.refs_3_), channel_id=1, source_target_pairs={{2,0},{0,2},{3,1},{1,3},{6,4},{4,6},{7,5},{5,7},{10,8},{8,10},{11,... | collective-permute-start | bytes 786440 | tf_op jit(solution)/shard_map/ppermute | solution.py:59
  110.4 8.7 %collective-permute-start.35 = (bf16[512,128]{1,0:T(8,128)(2,1)S(1)}, bf16[512,128]{1,0:T(8,128)(2,1)S(1)}, u32[]{:S(2)}, u32[]{:S(2)}) collective-permute-start(bf16[512,128]{1,0:T(8,128)(2,1)S(1)} %get-tuple-element.147.refs_1_), channel_id=1, source_target_pairs={{12,0},{8,4},{4,8},{0,12},{13,1},{9,5},{5,9},{1,13},{14,2},{10,6},... | collective-permute-start | bytes 393224 | tf_op jit(solution)/shard_map/ppermute | solution.py:59
  126.6 5.1 %collective-permute-start.44 = (f32[72,128]{1,0:T(8,128)S(1)}, f32[72,128]{1,0:T(8,128)S(1)}, u32[]{:S(2)}, u32[]{:S(2)}) collective-permute-start(f32[72,128]{1,0:T(8,128)S(1)} %add.63), channel_id=1, source_target_pairs={{2,0},{0,2},{6,4},{4,6},{10,8},{8,10},{14,12},{12,14},{3,1},{1,3},... | collective-permute-start | bytes 110600 | tf_op jit(solution)/shard_map/ppermute | solution.py:59
  130.3 5.0 %collective-permute-start.46 = (f32[72,128]{1,0:T(8,128)S(1)}, f32[72,128]{1,0:T(8,128)S(1)}, u32[]{:S(2)}, u32[]{:S(2)}) collective-permute-start(f32[72,128]{1,0:T(8,128)S(1)} %add.63), channel_id=1, source_target_pairs={{6,0},{4,2},{2,4},{0,6},{14,8},{12,10},{10,12},{8,14},{7,1},{5,3},... | collective-permute-start | bytes 110600 | tf_op jit(solution)/shard_map/ppermute | solution.py:59
  131.1 9.1 %collective-permute-start.48 = (f32[512,128]{1,0:T(8,128)S(1)}, f32[512,128]{1,0:T(8,128)S(1)}, u32[]{:S(2)}, u32[]{:S(2)}) collective-permute-start(f32[512,128]{1,0:T(8,128)S(1)} %get-tuple-element.159.refs_1_), channel_id=1, source_target_pairs={{2,0},{0,2},{3,1},{1,3},{6,4},{4,6},{7,5},{5,7},{10,8},{8,10},{11,... | collective-permute-start | bytes 786440 | tf_op jit(solution)/shard_map/ppermute | solution.py:59
  135.3 4.9 %collective-permute-start.47 = (f32[72,128]{1,0:T(8,128)S(1)}, f32[72,128]{1,0:T(8,128)S(1)}, u32[]{:S(2)}, u32[]{:S(2)}) collective-permute-start(f32[72,128]{1,0:T(8,128)S(1)} %add_add_fusion.2), channel_id=1, source_target_pairs={{8,0},{10,2},{12,4},{14,6},{0,8},{2,10},{4,12},{6,14},{9,1},{11,3}... | collective-permute-start | bytes 110600 | tf_op jit(solution)/shard_map/ppermute | solution.py:59
  (17 other events, 38.0 us)

commit v7 on v6

--- a/solution.py
+++ b/solution.py
@@ -26,6 +26,33 @@
         precision=lax.Precision.HIGHEST,
         preferred_element_type=F32,
     )
+
+
+def halves(value):
+    high = value.astype(BF16)
+    return high, (value - high.astype(F32)).astype(BF16)
+
+
+def mm_field(a, b, dims=(1, 0)):
+    def part(left, right):
+        return lax.dot_general(
+            left, right, (((dims[0],), (dims[1],)), ((), ())), preferred_element_type=F32
+        )
+
+    (a, a_low), (b, b_low) = halves(a), halves(b)
+    return part(a, b) + (part(a, b_low) + part(a_low, b))
+
+
+def square_of(field):
+    high, low = halves(field)
+    both = lax.dot_general(
+        high,
+        jnp.concatenate([high, low], axis=1),
+        (((0,), (0,)), ((), ())),
+        preferred_element_type=F32,
+    )
+    cross = both[:, LANES:]
+    return both[:, :LANES] + (cross + cross.T)
 
 
 def call(body, outs, *args, scratch=(), after=(), any_args=0, any_outs=False):
@@ -214,8 +241,8 @@
 
     def body(*refs):
         k_refs, piece_refs = refs[:many], refs[many : 3 * many]
-        acc_ref = refs[3 * many] if acc is not None else None
-        outs = refs[3 * many + (acc is not None) : -3]
+        acc_refs = refs[3 * many : 3 * many + len(acc)]
+        outs = refs[3 * many + len(acc) : -3]
         weights, even_acc, odd_acc = refs[-3:]
         half = lax.axis_index("coef")
         own = pl.ds(pl.multiple_of(half * LANES, LANES), LANES)
@@ -224,7 +251,7 @@
             weights[g, :, own] = piece_refs[2 * g][...]
             weights[g, :, other] = piece_refs[2 * g + 1][...]
         me = lax.axis_index("rhs")
-        for out, s in zip(outs, [None] if slots is None else slots):
+        for place, (out, s) in enumerate(zip(outs, [None] if slots is None else slots)):
             first = 0 if s is None else pl.multiple_of(mate(me, s, n) * size, size)
             for start in range(0, 2 * size, block):
                 here = slice(start, start + block)
@@ -245,12 +272,14 @@
             even = even_acc[pl.ds(0, size, stride=2), :]
             odd = odd_acc[pl.ds(1, size, stride=2), :]
             total = even + odd
-            if acc_ref is not None:
-                total = total + acc_ref[pl.ds(first, size), :]
+            if acc and acc[0].shape[0] == rows:
+                total = total + acc_refs[0][pl.ds(first, size), :]
+            elif acc:
+                total = total + acc_refs[place][...]
             out[...] = total
 
     args = [*packed, *(value for pair in pieces for value in pair)]
-    args += [acc] if acc is not None else []
+    args += acc
     *result, token = call(
         body,
         [shape(size)] * (1 if slots is None else len(slots)),
@@ -270,7 +299,7 @@
     panels = lax.axis_size("panel")
     groups = []
     if links == 2 * panels + 1 and panels & (panels - 1) == 0:
-        for s in range(panels):
+        for s in sorted(range(panels), key=lambda s: (s > 0, s % 2)):
 
             def numbers(s=s):
                 me = lax.axis_index("panel")
@@ -294,19 +323,19 @@
     arrived = [low] + [bring(low) for bring, _, _ in groups[1:]]
     directions = [direction] + [swapped(direction, "rhs", s, n) for s in range(1, n)]
     pairs = [[low, swapped(low, "coef", 1, 2)]]
-    (acc,), token = link_products(packed[:1], pairs, None, n, None)
+    acc, token = link_products(packed[:1], pairs, [], n, None)
     after = (token, between(token))
     for piece in arrived[1:]:
         piece, _ = lax.optimization_barrier((piece, after))
         pairs.append([piece, swapped(piece, "coef", 1, 2)])
     after = (*after, *directions[1:])
-    if len(groups) > 2:
-        (acc,), _ = link_products(packed[1:-1], pairs[1:-1], acc, n, None, after)
     if final:
+        acc, _ = link_products(packed[1:-1], pairs[1:-1], acc, n, None, after)
         parts, _ = link_products(packed[-1:], pairs[-1:], acc, n, range(n), after)
         return parts, directions
-    mates, token = link_products(packed[-1:], pairs[-1:], acc, n, range(1, n), after)
-    own, _ = link_products(packed[-1:], pairs[-1:], acc, n, [0], (token,))
+    mates, _ = link_products(packed[1:-1], pairs[1:-1], acc, n, range(1, n), after)
+    mates, token = link_products(packed[-1:], pairs[-1:], mates, n, range(1, n), after)
+    own, _ = link_products(packed[1:], pairs[1:], acc, n, [0], (token,))
     return own + mates, directions
 
 
@@ -365,7 +394,7 @@
             if extra and not first:
                 r = rest[0][...] if s == 0 else right - rest[s][...]
                 right = jnp.concatenate([right, r], axis=1)
-            term = mm(image, right, (0, 0))
+            term = mm_field(image, right, (0, 0))
             found = term if s == 0 else found + term
         if final:
             outs[0][...] = packed_symmetric(symmetric(found))
@@ -396,7 +425,7 @@
 def gram_of(field, *tokens):
     def body(field, out):
         value = field[...]
-        out[...] = packed_symmetric(mm(value, value, (0, 0)))
+        out[...] = packed_symmetric(square_of(value))
 
     return call(body, [shape(PACKED)], field, after=tokens)
 
@@ -411,7 +440,7 @@
         for ref in ins[1:]:
             image = image + ref[...]
         image_out[...] = image
-        out[...] = packed_symmetric(mm(image, image, (0, 0)))
+        out[...] = packed_symmetric(square_of(image))
 
     image, square, _ = call(
         body,
@@ -588,10 +617,10 @@
 
     def body(*refs):
         ds, a, b, refs = refs[:n], refs[n], refs[n + 1], refs[n + 2 :]
-        change = mm(ds[0][...], a[...])
+        change = mm_field(ds[0][...], a[...])
         refs[-n][...] = change if solution is None else refs[0][...] + change
         for s in range(1, n):
-            refs[s - n][...] = mm(ds[s][...], b[...])
+            refs[s - n][...] = mm_field(ds[s][...], b[...])
 
     solution, *turns, token = call(
         body, [shape(before[0].shape[0])] * n, *fields, after=[token]
@@ -608,8 +637,8 @@
         image = images[0][...]
         for ref in images[1:]:
             image = image + ref[...]
-        out[...] = s[...] + mm(d[...], alpha)
-        new_r[...] = r[...] - mm(image, alpha)
+        out[...] = s[...] + mm_field(d[...], alpha)
+        new_r[...] = r[...] - mm_field(image, alpha)
 
     return call(
         body,
@@ -661,8 +690,8 @@
         quadratic = mm(a, mm(unpacked_symmetric(square), a), (0, 0))
         following = gram[...] - (shared + shared.T) + quadratic
         beta = mm(inverse[...], following)
-        new_r = r[...] - mm(image[...], a)
-        value = new_r + mm(d[...], beta)
+        new_r = r[...] - mm_field(image[...], a)
+        value = new_r + mm_field(d[...], beta)
         r_out[...] = new_r
         low[...] = value.astype(BF16)
         new_d[...] = value

time: 146 us -> 145 us (level)
  waiting for transfers between devices: 34.7 us -> 39.6 us
  starting transfers between devices: 49.7 us -> 46.5 us
  Pallas kernels: 59.9 us -> 58 us
    ppermute x49, waiting for transfers between devices: 34.7 us -> 39.6 us  [permute(): return lax.ppermute(value, axis, pairs)]
    ppermute x49, starting transfers between devices: 49.7 us -> 46.5 us  [permute(): return lax.ppermute(value, axis, pairs)]
    pallas_call x30, Pallas kernels: 59.9 us -> 58 us  [call(): pl.pallas_call(ordered, out_shape=list(outs) + [shape(SUB)], in_specs=[HB...]
  transfers between devices with their start and end apart: 49 -> 49, of which waited for: 23 -> 28; matrix products, arithmetic and copies ran while one was open for 0% -> 0% of each run, Pallas kernels for 31% -> 30%
where the time goes in v7:
time: 145 us
  Pallas kernels  58 us (40%)
  starting transfers between devices  46.5 us (32%)
  waiting for transfers between devices  39.6 us (27%)
    pallas_call x30, Pallas kernels, call(): pl.pallas_call(ordered, out_shape=list(outs) + [shape(SUB)], in_specs=[HB...  58 us
    ppermute x49, starting transfers between devices, permute(): return lax.ppermute(value, axis, pairs)  46.5 us
    ppermute x49, waiting for transfers between devices, permute(): return lax.ppermute(value, axis, pairs)  39.6 us
  transfers between devices with their start and end apart: 49, of which 28 were waited for; matrix products, arithmetic and copies ran while one was open for 0% of the time, Pallas kernels for 30%

profile of v7, /device:TPU:0, one launch (start us, length us, event | category | flops | bytes accessed | tf_op | source)
XLA Modules:
  0.0 145.2 jit_solution(18230629388872121390)
XLA Ops:
  2.1 3.0 %collective-permute-start = (f32[512,128]{1,0:T(8,128)S(1)}, f32[512,128]{1,0:T(8,128)S(1)}, u32[]{:S(2)}, u32[]{:S(2)}) collective-permute-start(f32[512,128]{1,0:T(8,128)S(1)} %get-tuple-element.85), channel_id=1, source_target_pairs={{2,0},{0,2},{3,1},{1,3},{6,4},{4,6},{7,5},{5,7},{10,8},{8,10},{11,... | collective-permute-start | bytes 786440 | tf_op jit(solution)/shard_map/ppermute | solution.py:86
  5.1 2.9 %shard_map.51 = (bf16[3,4,1024,2,128]{4,3,2,1,0:T(2,128)(2,1)S(1)}, f32[8,128]{1,0:T(8,128)S(1)}) custom-call(bf16[9,1024,2,512]{3,2,1,0:T(2,128)(2,1)} %bitcast.26, f32[8,128]{1,0:T(8,128)S(1)} %get-tuple-element.86.refs_1_), custom_call_target="tpu_custom_call" | custom-call | flops 1 | bytes 1 | tf_op jit(solution)/shard_map/pallas_call | solution.py:70
  8.0 2.2 %shard_map.52 = (bf16[2,4,1024,2,128]{4,3,2,1,0:T(2,128)(2,1)S(1)}, f32[8,128]{1,0:T(8,128)S(1)}) custom-call(bf16[9,1024,2,512]{3,2,1,0:T(2,128)(2,1)} %bitcast.27, f32[8,128]{1,0:T(8,128)S(1)} %get-tuple-element.87.refs_1_), custom_call_target="tpu_custom_call" | custom-call | flops 1 | bytes 1 | tf_op jit(solution)/shard_map/pallas_call | solution.py:70
  11.6 1.9 %collective-permute-start.4 = (bf16[512,128]{1,0:T(8,128)(2,1)S(1)}, bf16[512,128]{1,0:T(8,128)(2,1)S(1)}, u32[]{:S(2)}, u32[]{:S(2)}) collective-permute-start(bf16[512,128]{1,0:T(8,128)(2,1)S(1)} %get-tuple-element.94.refs_1_), channel_id=1, source_target_pairs={{4,0},{0,4},{12,8},{8,12},{5,1},{1,5},{13,9},{9,13},{6,2},{2,6},{1... | collective-permute-start | bytes 393224 | tf_op jit(solution)/shard_map/ppermute | solution.py:86
  13.5 2.6 %collective-permute-start.1 = (bf16[512,128]{1,0:T(8,128)(2,1)S(1)}, bf16[512,128]{1,0:T(8,128)(2,1)S(1)}, u32[]{:S(2)}, u32[]{:S(2)}) collective-permute-start(bf16[512,128]{1,0:T(8,128)(2,1)S(1)} %get-tuple-element.94.refs_1_), channel_id=1, source_target_pairs={{8,0},{12,4},{0,8},{4,12},{9,1},{13,5},{1,9},{5,13},{10,2},{14,6},... | collective-permute-start | bytes 393224 | tf_op jit(solution)/shard_map/ppermute | solution.py:86
  17.8 2.2 %shard_map.54 = (bf16[2,4,1024,2,128]{4,3,2,1,0:T(2,128)(2,1)S(1)}, f32[8,128]{1,0:T(8,128)S(1)}) custom-call(bf16[9,1024,2,512]{3,2,1,0:T(2,128)(2,1)} %bitcast.28, f32[8,128]{1,0:T(8,128)S(1)} %get-tuple-element.89.refs_1_), custom_call_target="tpu_custom_call" | custom-call | flops 1 | bytes 1 | tf_op jit(solution)/shard_map/pallas_call | solution.py:70
  20.0 2.2 %shard_map.55 = (bf16[2,4,1024,2,128]{4,3,2,1,0:T(2,128)(2,1)S(1)}, f32[8,128]{1,0:T(8,128)S(1)}) custom-call(bf16[9,1024,2,512]{3,2,1,0:T(2,128)(2,1)} %bitcast.29, f32[8,128]{1,0:T(8,128)S(1)} %get-tuple-element.90.refs_1_), custom_call_target="tpu_custom_call" | custom-call | flops 1 | bytes 1 | tf_op jit(solution)/shard_map/pallas_call | solution.py:70
  22.2 2.0 %shard_map.56 = (f32[1024,128]{1,0:T(8,128)S(1)}, f32[8,128]{1,0:T(8,128)S(1)}) custom-call(bf16[3,4,2048,128]{3,2,1,0:T(8,128)(2,1)S(1)} %bitcast.23, bf16[512,128]{1,0:T(8,128)(2,1)S(1)} %get-tuple-element.94.refs_1_, bf16[512,128]{1,0:T(8,128)(2,1)S(1)} %collective-permute-done.2.refs_2_), custom_call_target="tpu_custom_call" | custom-call | flops 1 | bytes 1 | tf_op jit(solution)/shard_map/pallas_call | solution.py:70
  27.6 1.9 %shard_map.58 = (f32[512,128]{1,0:T(8,128)S(1)}, f32[8,128]{1,0:T(8,128)}) custom-call(bf16[2,4,2048,128]{3,2,1,0:T(8,128)(2,1)S(1)} %bitcast.8, bf16[2,4,2048,128]{3,2,1,0:T(8,128)(2,1)S(1)} %bitcast.18, bf16[512,128]{1,0:T(8,128)(2,1)S(1)} %collective-permute-done.1.refs_2_.refs_3_, bf16[512,128]{1,0:T(8,128)(2,1)S(1)} %collective-permute-done.3.refs_3_.refs_4_, ...), custom_call_target="tpu_custom_call" | custom-call | flops 1 | bytes 1 | tf_op jit(solution)/shard_map/pallas_call | solution.py:70
  30.3 1.9 %collective-permute-start.11 = (f32[512,128]{1,0:T(8,128)S(1)}, f32[512,128]{1,0:T(8,128)S(1)}, u32[]{:S(2)}, u32[]{:S(2)}) collective-permute-start(f32[512,128]{1,0:T(8,128)S(1)} %get-tuple-element.107.refs_1_), channel_id=1, source_target_pairs={{2,0},{0,2},{3,1},{1,3},{6,4},{4,6},{7,5},{5,7},{10,8},{8,10},{11,... | collective-permute-start | bytes 786440 | tf_op jit(solution)/shard_map/ppermute | solution.py:86
  32.2 2.4 %shard_map.60 = (f32[512,128]{1,0:T(8,128)S(1)}, f32[8,128]{1,0:T(8,128)}) custom-call(bf16[2,4,2048,128]{3,2,1,0:T(8,128)(2,1)S(1)} %bitcast.9, bf16[2,4,2048,128]{3,2,1,0:T(8,128)(2,1)S(1)} %bitcast.19, bf16[2,4,2048,128]{3,2,1,0:T(8,128)(2,1)S(1)} %bitcast.14, bf16[512,128]{1,0:T(8,128)(2,1)S(1)} %collective-permute-done.1.refs_2_.refs_3_, ...), custom_call_target="tpu_custom_call" | custom-call | flops 1 | bytes 1 | tf_op jit(solution)/shard_map/pallas_call | solution.py:70
  36.7 2.2 %collective-permute-start.10 = (f32[104,128]{1,0:T(8,128)S(1)}, f32[104,128]{1,0:T(8,128)S(1)}, u32[]{:S(2)}, u32[]{:S(2)}) collective-permute-start(f32[104,128]{1,0:T(8,128)S(1)} %add.51), channel_id=1, source_target_pairs={{8,0},{10,2},{12,4},{14,6},{0,8},{2,10},{4,12},{6,14},{9,1},{11,3}... | collective-permute-start | bytes 159752 | tf_op jit(solution)/shard_map/ppermute | solution.py:86
  39.9 2.9 %collective-permute-done.10 = f32[104,128]{1,0:T(8,128)S(1)} collective-permute-done((f32[104,128]{1,0:T(8,128)S(1)}, f32[104,128]{1,0:T(8,128)S(1)}, u32[]{:S(2)}, u32[]{:S(2)}) %collective-permute-start.10) | collective-permute-done | bytes 53280 | tf_op jit(solution)/shard_map/ppermute | solution.py:86
  50.1 2.6 %collective-permute-start.16 = (f32[72,128]{1,0:T(8,128)S(1)}, f32[72,128]{1,0:T(8,128)S(1)}, u32[]{:S(2)}, u32[]{:S(2)}) collective-permute-start(f32[72,128]{1,0:T(8,128)S(1)} %slice.16.refs_7_), channel_id=1, source_target_pairs={{8,0},{10,2},{12,4},{14,6},{0,8},{2,10},{4,12},{6,14},{9,1},{11,3}... | collective-permute-start | bytes 110600 | tf_op jit(solution)/shard_map/ppermute | solution.py:86
  52.7 5.6 %shard_map.63 = (f32[128,128]{1,0:T(8,128)S(1)}, f32[128,128]{1,0:T(8,128)S(1)}, f32[128,128]{1,0:T(8,128)S(1)}, f32[128,128]{1,0:T(8,128)S(1)}, f32[8,128]{1,0:T(8,128)}) custom-call(f32[104,128]{1,0:T(8,128)S(1)} %slice.17.refs_0_, f32[104,128]{1,0:T(8,128)S(1)} %collective-permute-done.17.refs_1_), custom_call_target="tpu_custom_call" | custom-call | flops 1 | bytes 1 | tf_op jit(solution)/shard_map/pallas_call | solution.py:70
  62.0 2.5 %collective-permute-start.23 = (bf16[512,128]{1,0:T(8,128)(2,1)S(1)}, bf16[512,128]{1,0:T(8,128)(2,1)S(1)}, u32[]{:S(2)}, u32[]{:S(2)}) collective-permute-start(bf16[512,128]{1,0:T(8,128)(2,1)S(1)} %get-tuple-element.120.refs_1_), channel_id=1, source_target_pairs={{12,0},{8,4},{4,8},{0,12},{13,1},{9,5},{5,9},{1,13},{14,2},{10,6},... | collective-permute-start | bytes 393224 | tf_op jit(solution)/shard_map/ppermute | solution.py:86
  65.1 2.1 %shard_map.65 = (f32[1024,128]{1,0:T(8,128)S(1)}, f32[8,128]{1,0:T(8,128)S(1)}) custom-call(bf16[3,4,2048,128]{3,2,1,0:T(8,128)(2,1)S(1)} %bitcast.24, bf16[512,128]{1,0:T(8,128)(2,1)S(1)} %get-tuple-element.120.refs_1_, bf16[512,128]{1,0:T(8,128)(2,1)S(1)} %collective-permute-done.19.refs_2_), custom_call_target="tpu_custom_call" | custom-call | flops 1 | bytes 1 | tf_op jit(solution)/shard_map/pallas_call | solution.py:70
  67.9 5.5 %collective-permute-done.18.refs_2_.refs_3_ = bf16[512,128]{1,0:T(8,128)(2,1)S(1)} collective-permute-done((bf16[512,128]{1,0:T(8,128)(2,1)S(1)}, bf16[512,128]{1,0:T(8,128)(2,1)S(1)}, u32[]{:S(2)}, u32[]{:S(2)}) %collective-permute-start.18) | collective-permute-done | bytes 131104 | tf_op jit(solution)/shard_map/ppermute | solution.py:86
  75.0 1.9 %shard_map.67 = (f32[512,128]{1,0:T(8,128)S(1)}, f32[8,128]{1,0:T(8,128)}) custom-call(bf16[2,4,2048,128]{3,2,1,0:T(8,128)(2,1)S(1)} %bitcast.10, bf16[2,4,2048,128]{3,2,1,0:T(8,128)(2,1)S(1)} %bitcast.20, bf16[512,128]{1,0:T(8,128)(2,1)S(1)} %collective-permute-done.18.refs_2_.refs_3_, bf16[512,128]{1,0:T(8,128)(2,1)S(1)} %collective-permute-done.20.refs_3_.refs_4_, ...), custom_call_target="tpu_custom_call" | custom-call | flops 1 | bytes 1 | tf_op jit(solution)/shard_map/pallas_call | solution.py:70
  79.1 2.4 %shard_map.69 = (f32[512,128]{1,0:T(8,128)S(1)}, f32[8,128]{1,0:T(8,128)}) custom-call(bf16[2,4,2048,128]{3,2,1,0:T(8,128)(2,1)S(1)} %bitcast.11, bf16[2,4,2048,128]{3,2,1,0:T(8,128)(2,1)S(1)} %bitcast.21, bf16[2,4,2048,128]{3,2,1,0:T(8,128)(2,1)S(1)} %bitcast.16, bf16[512,128]{1,0:T(8,128)(2,1)S(1)} %collective-permute-done.18.refs_2_.refs_3_, ...), custom_call_target="tpu_custom_call" | custom-call | flops 1 | bytes 1 | tf_op jit(solution)/shard_map/pallas_call | solution.py:70
  87.1 2.6 %collective-permute-done.27 = f32[104,128]{1,0:T(8,128)S(1)} collective-permute-done((f32[104,128]{1,0:T(8,128)S(1)}, f32[104,128]{1,0:T(8,128)S(1)}, u32[]{:S(2)}, u32[]{:S(2)}) %collective-permute-start.27) | collective-permute-done | bytes 53280 | tf_op jit(solution)/shard_map/ppermute | solution.py:86
  90.0 2.0 %collective-permute-start.32 = (f32[176,128]{1,0:T(8,128)S(1)}, f32[176,128]{1,0:T(8,128)S(1)}, u32[]{:S(2)}, u32[]{:S(2)}) collective-permute-start(f32[176,128]{1,0:T(8,128)S(1)} %pad_maximum_fusion.1), channel_id=1, source_target_pairs={{6,0},{4,2},{2,4},{0,6},{14,8},{12,10},{10,12},{8,14},{7,1},{5,3},... | collective-permute-start | bytes 270344 | tf_op jit(solution)/shard_map/ppermute | solution.py:86
  98.6 5.3 %shard_map.72 = (f32[128,128]{1,0:T(8,128)S(1)}, f32[128,128]{1,0:T(8,128)S(1)}, f32[128,128]{1,0:T(8,128)S(1)}, f32[128,128]{1,0:T(8,128)S(1)}, f32[8,128]{1,0:T(8,128)}) custom-call(f32[104,128]{1,0:T(8,128)S(1)} %slice.19.refs_0_, f32[104,128]{1,0:T(8,128)S(1)} %collective-permute-done.34.refs_1_, f32[128,128]{1,0:T(8,128)S(1)} %get-tuple-element.139.refs_2_), custom_call_target="tpu_custom_call" | custom-call | flops 1 | bytes 1 | tf_op jit(solution)/shard_map/pallas_call | solution.py:70
  106.8 1.8 %collective-permute-start.38 = (bf16[512,128]{1,0:T(8,128)(2,1)S(1)}, bf16[512,128]{1,0:T(8,128)(2,1)S(1)}, u32[]{:S(2)}, u32[]{:S(2)}) collective-permute-start(bf16[512,128]{1,0:T(8,128)(2,1)S(1)} %get-tuple-element.147.refs_1_), channel_id=1, source_target_pairs={{8,0},{12,4},{0,8},{4,12},{9,1},{13,5},{1,9},{5,13},{10,2},{14,6},... | collective-permute-start | bytes 393224 | tf_op jit(solution)/shard_map/ppermute | solution.py:86
  109.3 2.0 %collective-permute-start.35 = (bf16[512,128]{1,0:T(8,128)(2,1)S(1)}, bf16[512,128]{1,0:T(8,128)(2,1)S(1)}, u32[]{:S(2)}, u32[]{:S(2)}) collective-permute-start(bf16[512,128]{1,0:T(8,128)(2,1)S(1)} %get-tuple-element.147.refs_1_), channel_id=1, source_target_pairs={{12,0},{8,4},{4,8},{0,12},{13,1},{9,5},{5,9},{1,13},{14,2},{10,6},... | collective-permute-start | bytes 393224 | tf_op jit(solution)/shard_map/ppermute | solution.py:86
  111.3 2.0 %shard_map.74 = (f32[1024,128]{1,0:T(8,128)S(1)}, f32[8,128]{1,0:T(8,128)S(1)}) custom-call(bf16[3,4,2048,128]{3,2,1,0:T(8,128)(2,1)S(1)} %bitcast.25, bf16[512,128]{1,0:T(8,128)(2,1)S(1)} %get-tuple-element.147.refs_1_, bf16[512,128]{1,0:T(8,128)(2,1)S(1)} %collective-permute-done.36.refs_2_), custom_call_target="tpu_custom_call" | custom-call | flops 1 | bytes 1 | tf_op jit(solution)/shard_map/pallas_call | solution.py:70
  114.3 5.4 %collective-permute-done.38.refs_2_ = bf16[512,128]{1,0:T(8,128)(2,1)S(1)} collective-permute-done((bf16[512,128]{1,0:T(8,128)(2,1)S(1)}, bf16[512,128]{1,0:T(8,128)(2,1)S(1)}, u32[]{:S(2)}, u32[]{:S(2)}) %collective-permute-start.38) | collective-permute-done | bytes 131104 | tf_op jit(solution)/shard_map/ppermute | solution.py:86
  121.2 3.2 %shard_map.76 = (f32[1024,128]{1,0:T(8,128)S(1)}, f32[8,128]{1,0:T(8,128)}) custom-call(bf16[2,4,2048,128]{3,2,1,0:T(8,128)(2,1)S(1)} %bitcast.12, bf16[2,4,2048,128]{3,2,1,0:T(8,128)(2,1)S(1)} %bitcast.22, bf16[512,128]{1,0:T(8,128)(2,1)S(1)} %collective-permute-done.38.refs_2_, bf16[512,128]{1,0:T(8,128)(2,1)S(1)} %collective-permute-done.39.refs_3_, ...), custom_call_target="tpu_custom_call" | custom-call | flops 1 | bytes 1 | tf_op jit(solution)/shard_map/pallas_call | solution.py:70
  124.4 1.9 %shard_map.77 = (f32[512,128]{1,0:T(8,128)S(1)}, f32[512,128]{1,0:T(8,128)S(1)}, f32[8,128]{1,0:T(8,128)}) custom-call(bf16[2,4,2048,128]{3,2,1,0:T(8,128)(2,1)S(1)} %bitcast.17, bf16[512,128]{1,0:T(8,128)(2,1)S(1)} %collective-permute-done.35.refs_1_, bf16[512,128]{1,0:T(8,128)(2,1)S(1)} %collective-permute-done.37.refs_2_, ...), custom_call_target="tpu_custom_call" | custom-call | flops 1 | bytes 1 | tf_op jit(solution)/shard_map/pallas_call | solution.py:70
  135.1 2.1 %collective-permute-start.47 = (f32[72,128]{1,0:T(8,128)S(1)}, f32[72,128]{1,0:T(8,128)S(1)}, u32[]{:S(2)}, u32[]{:S(2)}) collective-permute-start(f32[72,128]{1,0:T(8,128)S(1)} %add_add_fusion.2), channel_id=1, source_target_pairs={{8,0},{10,2},{12,4},{14,6},{0,8},{2,10},{4,12},{6,14},{9,1},{11,3}... | collective-permute-start | bytes 110600 | tf_op jit(solution)/shard_map/ppermute | solution.py:86
  137.2 2.8 %collective-permute-done.47 = f32[72,128]{1,0:T(8,128)S(1)} collective-permute-done((f32[72,128]{1,0:T(8,128)S(1)}, f32[72,128]{1,0:T(8,128)S(1)}, u32[]{:S(2)}, u32[]{:S(2)}) %collective-permute-start.47) | collective-permute-done | bytes 36896 | tf_op jit(solution)/shard_map/ppermute | solution.py:86
  140.1 5.0 %shard_map.79 = (f32[512,128]{1,0:T(8,128)}, f32[512,128]{1,0:T(8,128)}, f32[8,128]{1,0:T(8,128)}) custom-call(f32[72,128]{1,0:T(8,128)S(1)} %add.67.refs_0_, f32[128,128]{1,0:T(8,128)S(1)} %get-tuple-element.161.refs_1_, f32[512,128]{1,0:T(8,128)S(1)} %get-tuple-element.162.refs_2_, f32[512,128]{1,0:T(8,128)S(1)} %get-tuple-element.156.refs_2_.refs_3_, ...), custom_call_target="tpu_custom_call" | custom-call | flops 1 | bytes 1 | tf_op jit(solution)/shard_map/pallas_call | solution.py:70
  (113 shorter events, 55.5 us)
Async XLA Ops:
  2.1 9.3 %collective-permute-start = (f32[512,128]{1,0:T(8,128)S(1)}, f32[512,128]{1,0:T(8,128)S(1)}, u32[]{:S(2)}, u32[]{:S(2)}) collective-permute-start(f32[512,128]{1,0:T(8,128)S(1)} %get-tuple-element.85), channel_id=1, source_target_pairs={{2,0},{0,2},{3,1},{1,3},{6,4},{4,6},{7,5},{5,7},{10,8},{8,10},{11,... | collective-permute-start | bytes 786440 | tf_op jit(solution)/shard_map/ppermute | solution.py:86
  11.5 10.7 %collective-permute-start.2 = (bf16[512,128]{1,0:T(8,128)(2,1)S(1)}, bf16[512,128]{1,0:T(8,128)(2,1)S(1)}, u32[]{:S(2)}, u32[]{:S(2)}) collective-permute-start(bf16[512,128]{1,0:T(8,128)(2,1)S(1)} %get-tuple-element.94.refs_1_), channel_id=1, source_target_pairs={{1,0},{0,1},{3,2},{2,3},{5,4},{4,5},{7,6},{6,7},{9,8},{8,9},{11,10... | collective-permute-start | bytes 393224 | tf_op jit(solution)/shard_map/ppermute | solution.py:86
  11.6 13.0 %collective-permute-start.4 = (bf16[512,128]{1,0:T(8,128)(2,1)S(1)}, bf16[512,128]{1,0:T(8,128)(2,1)S(1)}, u32[]{:S(2)}, u32[]{:S(2)}) collective-permute-start(bf16[512,128]{1,0:T(8,128)(2,1)S(1)} %get-tuple-element.94.refs_1_), channel_id=1, source_target_pairs={{4,0},{0,4},{12,8},{8,12},{5,1},{1,5},{13,9},{9,13},{6,2},{2,6},{1... | collective-permute-start | bytes 393224 | tf_op jit(solution)/shard_map/ppermute | solution.py:86
  13.5 12.6 %collective-permute-start.1 = (bf16[512,128]{1,0:T(8,128)(2,1)S(1)}, bf16[512,128]{1,0:T(8,128)(2,1)S(1)}, u32[]{:S(2)}, u32[]{:S(2)}) collective-permute-start(bf16[512,128]{1,0:T(8,128)(2,1)S(1)} %get-tuple-element.94.refs_1_), channel_id=1, source_target_pairs={{8,0},{12,4},{0,8},{4,12},{9,1},{13,5},{1,9},{5,13},{10,2},{14,6},... | collective-permute-start | bytes 393224 | tf_op jit(solution)/shard_map/ppermute | solution.py:86
  16.1 10.5 %collective-permute-start.8 = (f32[512,128]{1,0:T(8,128)S(1)}, f32[512,128]{1,0:T(8,128)S(1)}, u32[]{:S(2)}, u32[]{:S(2)}) collective-permute-start(f32[512,128]{1,0:T(8,128)S(1)} %get-tuple-element.97.refs_0_.refs_2_.refs_4_.refs_5_), channel_id=1, source_target_pairs={{2,0},{0,2},{3,1},{1,3},{6,4},{4,6},{7,5},{5,7},{10,8},{8,10},{11,... | collective-permute-start | bytes 786440 | tf_op jit(solution)/shard_map/ppermute | solution.py:86
  17.5 9.0 %collective-permute-start.6 = (bf16[512,128]{1,0:T(8,128)(2,1)S(1)}, bf16[512,128]{1,0:T(8,128)(2,1)S(1)}, u32[]{:S(2)}, u32[]{:S(2)}) collective-permute-start(bf16[512,128]{1,0:T(8,128)(2,1)S(1)} %get-tuple-element.94.refs_1_), channel_id=1, source_target_pairs={{12,0},{8,4},{4,8},{0,12},{13,1},{9,5},{5,9},{1,13},{14,2},{10,6},... | collective-permute-start | bytes 393224 | tf_op jit(solution)/shard_map/ppermute | solution.py:86
  30.3 8.7 %collective-permute-start.11 = (f32[512,128]{1,0:T(8,128)S(1)}, f32[512,128]{1,0:T(8,128)S(1)}, u32[]{:S(2)}, u32[]{:S(2)}) collective-permute-start(f32[512,128]{1,0:T(8,128)S(1)} %get-tuple-element.107.refs_1_), channel_id=1, source_target_pairs={{2,0},{0,2},{3,1},{1,3},{6,4},{4,6},{7,5},{5,7},{10,8},{8,10},{11,... | collective-permute-start | bytes 786440 | tf_op jit(solution)/shard_map/ppermute | solution.py:86
  36.7 6.0 %collective-permute-start.10 = (f32[104,128]{1,0:T(8,128)S(1)}, f32[104,128]{1,0:T(8,128)S(1)}, u32[]{:S(2)}, u32[]{:S(2)}) collective-permute-start(f32[104,128]{1,0:T(8,128)S(1)} %add.51), channel_id=1, source_target_pairs={{8,0},{10,2},{12,4},{14,6},{0,8},{2,10},{4,12},{6,14},{9,1},{11,3}... | collective-permute-start | bytes 159752 | tf_op jit(solution)/shard_map/ppermute | solution.py:86
  42.8 5.2 %collective-permute-start.14 = (f32[176,128]{1,0:T(8,128)S(1)}, f32[176,128]{1,0:T(8,128)S(1)}, u32[]{:S(2)}, u32[]{:S(2)}) collective-permute-start(f32[176,128]{1,0:T(8,128)S(1)} %pad_maximum_fusion), channel_id=1, source_target_pairs={{4,0},{6,2},{0,4},{2,6},{12,8},{14,10},{8,12},{10,14},{5,1},{7,3},... | collective-permute-start | bytes 270344 | tf_op jit(solution)/shard_map/ppermute | solution.py:86
  43.1 6.0 %collective-permute-start.15 = (f32[176,128]{1,0:T(8,128)S(1)}, f32[176,128]{1,0:T(8,128)S(1)}, u32[]{:S(2)}, u32[]{:S(2)}) collective-permute-start(f32[176,128]{1,0:T(8,128)S(1)} %pad_maximum_fusion), channel_id=1, source_target_pairs={{6,0},{4,2},{2,4},{0,6},{14,8},{12,10},{10,12},{8,14},{7,1},{5,3},... | collective-permute-start | bytes 270344 | tf_op jit(solution)/shard_map/ppermute | solution.py:86
  44.8 5.3 %collective-permute-start.13 = (f32[176,128]{1,0:T(8,128)S(1)}, f32[176,128]{1,0:T(8,128)S(1)}, u32[]{:S(2)}, u32[]{:S(2)}) collective-permute-start(f32[176,128]{1,0:T(8,128)S(1)} %pad_maximum_fusion), channel_id=1, source_target_pairs={{2,0},{0,2},{6,4},{4,6},{10,8},{8,10},{14,12},{12,14},{3,1},{1,3},... | collective-permute-start | bytes 270344 | tf_op jit(solution)/shard_map/ppermute | solution.py:86
  50.1 8.2 %collective-permute-start.16 = (f32[72,128]{1,0:T(8,128)S(1)}, f32[72,128]{1,0:T(8,128)S(1)}, u32[]{:S(2)}, u32[]{:S(2)}) collective-permute-start(f32[72,128]{1,0:T(8,128)S(1)} %slice.16.refs_7_), channel_id=1, source_target_pairs={{8,0},{10,2},{12,4},{14,6},{0,8},{2,10},{4,12},{6,14},{9,1},{11,3}... | collective-permute-start | bytes 110600 | tf_op jit(solution)/shard_map/ppermute | solution.py:86
  59.9 5.2 %collective-permute-start.19 = (bf16[512,128]{1,0:T(8,128)(2,1)S(1)}, bf16[512,128]{1,0:T(8,128)(2,1)S(1)}, u32[]{:S(2)}, u32[]{:S(2)}) collective-permute-start(bf16[512,128]{1,0:T(8,128)(2,1)S(1)} %get-tuple-element.120.refs_1_), channel_id=1, source_target_pairs={{1,0},{0,1},{3,2},{2,3},{5,4},{4,5},{7,6},{6,7},{9,8},{8,9},{11,10... | collective-permute-start | bytes 393224 | tf_op jit(solution)/shard_map/ppermute | solution.py:86
  60.0 7.9 %collective-permute-start.21 = (bf16[512,128]{1,0:T(8,128)(2,1)S(1)}, bf16[512,128]{1,0:T(8,128)(2,1)S(1)}, u32[]{:S(2)}, u32[]{:S(2)}) collective-permute-start(bf16[512,128]{1,0:T(8,128)(2,1)S(1)} %get-tuple-element.120.refs_1_), channel_id=1, source_target_pairs={{4,0},{0,4},{12,8},{8,12},{5,1},{1,5},{13,9},{9,13},{6,2},{2,6},{1... | collective-permute-start | bytes 393224 | tf_op jit(solution)/shard_map/ppermute | solution.py:86
  60.5 12.9 %collective-permute-start.18 = (bf16[512,128]{1,0:T(8,128)(2,1)S(1)}, bf16[512,128]{1,0:T(8,128)(2,1)S(1)}, u32[]{:S(2)}, u32[]{:S(2)}) collective-permute-start(bf16[512,128]{1,0:T(8,128)(2,1)S(1)} %get-tuple-element.120.refs_1_), channel_id=1, source_target_pairs={{8,0},{12,4},{0,8},{4,12},{9,1},{13,5},{1,9},{5,13},{10,2},{14,6},... | collective-permute-start | bytes 393224 | tf_op jit(solution)/shard_map/ppermute | solution.py:86
  62.0 12.0 %collective-permute-start.23 = (bf16[512,128]{1,0:T(8,128)(2,1)S(1)}, bf16[512,128]{1,0:T(8,128)(2,1)S(1)}, u32[]{:S(2)}, u32[]{:S(2)}) collective-permute-start(bf16[512,128]{1,0:T(8,128)(2,1)S(1)} %get-tuple-element.120.refs_1_), channel_id=1, source_target_pairs={{12,0},{8,4},{4,8},{0,12},{13,1},{9,5},{5,9},{1,13},{14,2},{10,6},... | collective-permute-start | bytes 393224 | tf_op jit(solution)/shard_map/ppermute | solution.py:86
  64.4 10.5 %collective-permute-start.25 = (f32[512,128]{1,0:T(8,128)S(1)}, f32[512,128]{1,0:T(8,128)S(1)}, u32[]{:S(2)}, u32[]{:S(2)}) collective-permute-start(f32[512,128]{1,0:T(8,128)S(1)} %get-tuple-element.128.refs_2_.refs_5_.refs_0_), channel_id=1, source_target_pairs={{2,0},{0,2},{3,1},{1,3},{6,4},{4,6},{7,5},{5,7},{10,8},{8,10},{11,... | collective-permute-start | bytes 786440 | tf_op jit(solution)/shard_map/ppermute | solution.py:86
  77.7 8.6 %collective-permute-start.28 = (f32[512,128]{1,0:T(8,128)S(1)}, f32[512,128]{1,0:T(8,128)S(1)}, u32[]{:S(2)}, u32[]{:S(2)}) collective-permute-start(f32[512,128]{1,0:T(8,128)S(1)} %get-tuple-element.132.refs_1_), channel_id=1, source_target_pairs={{2,0},{0,2},{3,1},{1,3},{6,4},{4,6},{7,5},{5,7},{10,8},{8,10},{11,... | collective-permute-start | bytes 786440 | tf_op jit(solution)/shard_map/ppermute | solution.py:86
  83.8 6.0 %collective-permute-start.27 = (f32[104,128]{1,0:T(8,128)S(1)}, f32[104,128]{1,0:T(8,128)S(1)}, u32[]{:S(2)}, u32[]{:S(2)}) collective-permute-start(f32[104,128]{1,0:T(8,128)S(1)} %add.57), channel_id=1, source_target_pairs={{8,0},{10,2},{12,4},{14,6},{0,8},{2,10},{4,12},{6,14},{9,1},{11,3}... | collective-permute-start | bytes 159752 | tf_op jit(solution)/shard_map/ppermute | solution.py:86
  89.8 5.1 %collective-permute-start.31 = (f32[176,128]{1,0:T(8,128)S(1)}, f32[176,128]{1,0:T(8,128)S(1)}, u32[]{:S(2)}, u32[]{:S(2)}) collective-permute-start(f32[176,128]{1,0:T(8,128)S(1)} %pad_maximum_fusion.1), channel_id=1, source_target_pairs={{4,0},{6,2},{0,4},{2,6},{12,8},{14,10},{8,12},{10,14},{5,1},{7,3},... | collective-permute-start | bytes 270344 | tf_op jit(solution)/shard_map/ppermute | solution.py:86
  90.0 6.0 %collective-permute-start.32 = (f32[176,128]{1,0:T(8,128)S(1)}, f32[176,128]{1,0:T(8,128)S(1)}, u32[]{:S(2)}, u32[]{:S(2)}) collective-permute-start(f32[176,128]{1,0:T(8,128)S(1)} %pad_maximum_fusion.1), channel_id=1, source_target_pairs={{6,0},{4,2},{2,4},{0,6},{14,8},{12,10},{10,12},{8,14},{7,1},{5,3},... | collective-permute-start | bytes 270344 | tf_op jit(solution)/shard_map/ppermute | solution.py:86
  91.9 5.0 %collective-permute-start.30 = (f32[176,128]{1,0:T(8,128)S(1)}, f32[176,128]{1,0:T(8,128)S(1)}, u32[]{:S(2)}, u32[]{:S(2)}) collective-permute-start(f32[176,128]{1,0:T(8,128)S(1)} %pad_maximum_fusion.1), channel_id=1, source_target_pairs={{2,0},{0,2},{6,4},{4,6},{10,8},{8,10},{14,12},{12,14},{3,1},{1,3},... | collective-permute-start | bytes 270344 | tf_op jit(solution)/shard_map/ppermute | solution.py:86
  97.0 6.9 %collective-permute-start.33 = (f32[72,128]{1,0:T(8,128)S(1)}, f32[72,128]{1,0:T(8,128)S(1)}, u32[]{:S(2)}, u32[]{:S(2)}) collective-permute-start(f32[72,128]{1,0:T(8,128)S(1)} %slice.18.refs_7_), channel_id=1, source_target_pairs={{8,0},{10,2},{12,4},{14,6},{0,8},{2,10},{4,12},{6,14},{9,1},{11,3}... | collective-permute-start | bytes 110600 | tf_op jit(solution)/shard_map/ppermute | solution.py:86
  105.5 5.8 %collective-permute-start.36 = (bf16[512,128]{1,0:T(8,128)(2,1)S(1)}, bf16[512,128]{1,0:T(8,128)(2,1)S(1)}, u32[]{:S(2)}, u32[]{:S(2)}) collective-permute-start(bf16[512,128]{1,0:T(8,128)(2,1)S(1)} %get-tuple-element.147.refs_1_), channel_id=1, source_target_pairs={{1,0},{0,1},{3,2},{2,3},{5,4},{4,5},{7,6},{6,7},{9,8},{8,9},{11,10... | collective-permute-start | bytes 393224 | tf_op jit(solution)/shard_map/ppermute | solution.py:86
  105.6 8.7 %collective-permute-start.40 = (bf16[512,128]{1,0:T(8,128)(2,1)S(1)}, bf16[512,128]{1,0:T(8,128)(2,1)S(1)}, u32[]{:S(2)}, u32[]{:S(2)}) collective-permute-start(bf16[512,128]{1,0:T(8,128)(2,1)S(1)} %get-tuple-element.147.refs_1_), channel_id=1, source_target_pairs={{4,0},{0,4},{12,8},{8,12},{5,1},{1,5},{13,9},{9,13},{6,2},{2,6},{1... | collective-permute-start | bytes 393224 | tf_op jit(solution)/shard_map/ppermute | solution.py:86
  106.8 12.9 %collective-permute-start.38 = (bf16[512,128]{1,0:T(8,128)(2,1)S(1)}, bf16[512,128]{1,0:T(8,128)(2,1)S(1)}, u32[]{:S(2)}, u32[]{:S(2)}) collective-permute-start(bf16[512,128]{1,0:T(8,128)(2,1)S(1)} %get-tuple-element.147.refs_1_), channel_id=1, source_target_pairs={{8,0},{12,4},{0,8},{4,12},{9,1},{13,5},{1,9},{5,13},{10,2},{14,6},... | collective-permute-start | bytes 393224 | tf_op jit(solution)/shard_map/ppermute | solution.py:86
  108.5 11.7 %collective-permute-start.42 = (f32[512,128]{1,0:T(8,128)S(1)}, f32[512,128]{1,0:T(8,128)S(1)}, u32[]{:S(2)}, u32[]{:S(2)}) collective-permute-start(f32[512,128]{1,0:T(8,128)S(1)} %get-tuple-element.156.refs_2_.refs_3_), channel_id=1, source_target_pairs={{2,0},{0,2},{3,1},{1,3},{6,4},{4,6},{7,5},{5,7},{10,8},{8,10},{11,... | collective-permute-start | bytes 786440 | tf_op jit(solution)/shard_map/ppermute | solution.py:86
  109.3 10.9 %collective-permute-start.35 = (bf16[512,128]{1,0:T(8,128)(2,1)S(1)}, bf16[512,128]{1,0:T(8,128)(2,1)S(1)}, u32[]{:S(2)}, u32[]{:S(2)}) collective-permute-start(bf16[512,128]{1,0:T(8,128)(2,1)S(1)} %get-tuple-element.147.refs_1_), channel_id=1, source_target_pairs={{12,0},{8,4},{4,8},{0,12},{13,1},{9,5},{5,9},{1,13},{14,2},{10,6},... | collective-permute-start | bytes 393224 | tf_op jit(solution)/shard_map/ppermute | solution.py:86
  128.5 5.0 %collective-permute-start.46 = (f32[72,128]{1,0:T(8,128)S(1)}, f32[72,128]{1,0:T(8,128)S(1)}, u32[]{:S(2)}, u32[]{:S(2)}) collective-permute-start(f32[72,128]{1,0:T(8,128)S(1)} %add.63), channel_id=1, source_target_pairs={{6,0},{4,2},{2,4},{0,6},{14,8},{12,10},{10,12},{8,14},{7,1},{5,3},... | collective-permute-start | bytes 110600 | tf_op jit(solution)/shard_map/ppermute | solution.py:86
  130.7 4.3 %collective-permute-start.44 = (f32[72,128]{1,0:T(8,128)S(1)}, f32[72,128]{1,0:T(8,128)S(1)}, u32[]{:S(2)}, u32[]{:S(2)}) collective-permute-start(f32[72,128]{1,0:T(8,128)S(1)} %add.63), channel_id=1, source_target_pairs={{2,0},{0,2},{6,4},{4,6},{10,8},{8,10},{14,12},{12,14},{3,1},{1,3},... | collective-permute-start | bytes 110600 | tf_op jit(solution)/shard_map/ppermute | solution.py:86
  132.0 8.1 %collective-permute-start.48 = (f32[512,128]{1,0:T(8,128)S(1)}, f32[512,128]{1,0:T(8,128)S(1)}, u32[]{:S(2)}, u32[]{:S(2)}) collective-permute-start(f32[512,128]{1,0:T(8,128)S(1)} %get-tuple-element.159.refs_1_), channel_id=1, source_target_pairs={{2,0},{0,2},{3,1},{1,3},{6,4},{4,6},{7,5},{5,7},{10,8},{8,10},{11,... | collective-permute-start | bytes 786440 | tf_op jit(solution)/shard_map/ppermute | solution.py:86
  135.1 4.9 %collective-permute-start.47 = (f32[72,128]{1,0:T(8,128)S(1)}, f32[72,128]{1,0:T(8,128)S(1)}, u32[]{:S(2)}, u32[]{:S(2)}) collective-permute-start(f32[72,128]{1,0:T(8,128)S(1)} %add_add_fusion.2), channel_id=1, source_target_pairs={{8,0},{10,2},{12,4},{14,6},{0,8},{2,10},{4,12},{6,14},{9,1},{11,3}... | collective-permute-start | bytes 110600 | tf_op jit(solution)/shard_map/ppermute | solution.py:86
  (17 other events, 36.2 us)

commit v8 on v6

--- a/solution.py
+++ b/solution.py
@@ -8,6 +8,7 @@
 from jax.sharding import PartitionSpec as P
 
 ITERS = 3
+PARTS = 2
 LANES = 128
 SUB = 8
 VMEM_LIMIT = 14 * 2**20
@@ -213,16 +214,22 @@
     block = min(512, 2 * size)
 
     def body(*refs):
-        k_refs, piece_refs = refs[:many], refs[many : 3 * many]
-        acc_ref = refs[3 * many] if acc is not None else None
-        outs = refs[3 * many + (acc is not None) : -3]
+        k_refs, refs = refs[:many], refs[many:]
+        piece_refs = []
+        for pair in pieces:
+            piece_refs.append(refs[: len(pair)])
+            refs = refs[len(pair) :]
+        acc_ref = refs[0] if acc is not None else None
+        outs = refs[acc is not None : -3]
         weights, even_acc, odd_acc = refs[-3:]
         half = lax.axis_index("coef")
         own = pl.ds(pl.multiple_of(half * LANES, LANES), LANES)
         other = pl.ds(pl.multiple_of((1 - half) * LANES, LANES), LANES)
-        for g in range(many):
-            weights[g, :, own] = piece_refs[2 * g][...]
-            weights[g, :, other] = piece_refs[2 * g + 1][...]
+        for g, (mine, *theirs) in enumerate(piece_refs):
+            weights[g, :, own] = mine[...]
+            size_of = strip // len(theirs)
+            for i, part in enumerate(theirs):
+                weights[g, i * size_of : (i + 1) * size_of, other] = part[...]
         me = lax.axis_index("rhs")
         for out, s in zip(outs, [None] if slots is None else slots):
             first = 0 if s is None else pl.multiple_of(mate(me, s, n) * size, size)
@@ -270,7 +277,7 @@
     panels = lax.axis_size("panel")
     groups = []
     if links == 2 * panels + 1 and panels & (panels - 1) == 0:
-        for s in range(panels):
+        for s in sorted(range(panels), key=lambda s: (s > 0, s % 2)):
 
             def numbers(s=s):
                 me = lax.axis_index("panel")
@@ -296,16 +303,21 @@
     pairs = [[low, swapped(low, "coef", 1, 2)]]
     (acc,), token = link_products(packed[:1], pairs, None, n, None)
     after = (token, between(token))
-    for piece in arrived[1:]:
+    held = (*after, *directions[1:])
+    for piece in arrived[1:-1]:
         piece, _ = lax.optimization_barrier((piece, after))
-        pairs.append([piece, swapped(piece, "coef", 1, 2)])
-    after = (*after, *directions[1:])
+        rows = piece.shape[0] // PARTS
+        cut = [piece[i * rows : (i + 1) * rows] for i in range(PARTS)]
+        pairs.append([piece, *(swapped(part, "coef", 1, 2) for part in cut)])
     if len(groups) > 2:
-        (acc,), _ = link_products(packed[1:-1], pairs[1:-1], acc, n, None, after)
+        (acc,), token = link_products(packed[1:-1], pairs[1:], acc, n, None, held)
+        held = (token,)
+    piece, held = lax.optimization_barrier((arrived[-1], held))
+    pairs.append([piece, swapped(piece, "coef", 1, 2)])
     if final:
-        parts, _ = link_products(packed[-1:], pairs[-1:], acc, n, range(n), after)
+        parts, _ = link_products(packed[-1:], pairs[-1:], acc, n, range(n), held)
         return parts, directions
-    mates, token = link_products(packed[-1:], pairs[-1:], acc, n, range(1, n), after)
+    mates, token = link_products(packed[-1:], pairs[-1:], acc, n, range(1, n), held)
     own, _ = link_products(packed[-1:], pairs[-1:], acc, n, [0], (token,))
     return own + mates, directions
 

time: 146 us -> 153 us (1.048)
  waiting for transfers between devices: 34.7 us -> 50.7 us
  starting transfers between devices: 49.7 us -> 42.2 us
    ppermute x49 -> x55, waiting for transfers between devices: 34.7 us -> 50.7 us  [permute(): return lax.ppermute(value, axis, pairs)]
    ppermute x49 -> x55, starting transfers between devices: 49.7 us -> 42.2 us  [permute(): return lax.ppermute(value, axis, pairs)]
  transfers between devices with their start and end apart: 49 -> 55, of which waited for: 23 -> 34; matrix products, arithmetic and copies ran while one was open for 0% -> 0% of each run, Pallas kernels for 31% -> 28%
where the time goes in v8:
time: 153 us
  Pallas kernels  58.7 us (38%)
  waiting for transfers between devices  50.7 us (33%)
  starting transfers between devices  42.2 us (28%)
    pallas_call x30, Pallas kernels, call(): pl.pallas_call(ordered, out_shape=list(outs) + [shape(SUB)], in_specs=[HB...  58.7 us
    ppermute x55, waiting for transfers between devices, permute(): return lax.ppermute(value, axis, pairs)  50.7 us
    ppermute x55, starting transfers between devices, permute(): return lax.ppermute(value, axis, pairs)  42.2 us
  transfers between devices with their start and end apart: 55, of which 34 were waited for; matrix products, arithmetic and copies ran while one was open for 0% of the time, Pallas kernels for 28%

profile of v8, /device:TPU:0, one launch (start us, length us, event | category | flops | bytes accessed | tf_op | source)
XLA Modules:
  0.0 152.9 jit_solution(6105145425154172423)
XLA Ops:
  2.1 3.0 %collective-permute-start = (f32[512,128]{1,0:T(8,128)S(1)}, f32[512,128]{1,0:T(8,128)S(1)}, u32[]{:S(2)}, u32[]{:S(2)}) collective-permute-start(f32[512,128]{1,0:T(8,128)S(1)} %get-tuple-element.91), channel_id=1, source_target_pairs={{2,0},{0,2},{3,1},{1,3},{6,4},{4,6},{7,5},{5,7},{10,8},{8,10},{11,... | collective-permute-start | bytes 786440 | tf_op jit(solution)/shard_map/ppermute | solution.py:60
  5.1 2.9 %shard_map.51 = (bf16[3,4,1024,2,128]{4,3,2,1,0:T(2,128)(2,1)S(1)}, f32[8,128]{1,0:T(8,128)S(1)}) custom-call(bf16[9,1024,2,512]{3,2,1,0:T(2,128)(2,1)} %bitcast.22, f32[8,128]{1,0:T(8,128)S(1)} %get-tuple-element.92.refs_1_), custom_call_target="tpu_custom_call" | custom-call | flops 1 | bytes 1 | tf_op jit(solution)/shard_map/pallas_call | solution.py:44
  8.0 2.2 %shard_map.52 = (bf16[2,4,1024,2,128]{4,3,2,1,0:T(2,128)(2,1)S(1)}, f32[8,128]{1,0:T(8,128)S(1)}) custom-call(bf16[9,1024,2,512]{3,2,1,0:T(2,128)(2,1)} %bitcast.23, f32[8,128]{1,0:T(8,128)S(1)} %get-tuple-element.93.refs_1_), custom_call_target="tpu_custom_call" | custom-call | flops 1 | bytes 1 | tf_op jit(solution)/shard_map/pallas_call | solution.py:44
  11.6 1.9 %collective-permute-start.6 = (bf16[512,128]{1,0:T(8,128)(2,1)S(1)}, bf16[512,128]{1,0:T(8,128)(2,1)S(1)}, u32[]{:S(2)}, u32[]{:S(2)}) collective-permute-start(bf16[512,128]{1,0:T(8,128)(2,1)S(1)} %get-tuple-element.98.refs_1_), channel_id=1, source_target_pairs={{4,0},{0,4},{12,8},{8,12},{5,1},{1,5},{13,9},{9,13},{6,2},{2,6},{1... | collective-permute-start | bytes 393224 | tf_op jit(solution)/shard_map/ppermute | solution.py:60
  13.5 2.6 %collective-permute-start.2 = (bf16[512,128]{1,0:T(8,128)(2,1)S(1)}, bf16[512,128]{1,0:T(8,128)(2,1)S(1)}, u32[]{:S(2)}, u32[]{:S(2)}) collective-permute-start(bf16[512,128]{1,0:T(8,128)(2,1)S(1)} %get-tuple-element.98.refs_1_), channel_id=1, source_target_pairs={{8,0},{12,4},{0,8},{4,12},{9,1},{13,5},{1,9},{5,13},{10,2},{14,6},... | collective-permute-start | bytes 393224 | tf_op jit(solution)/shard_map/ppermute | solution.py:60
  17.8 2.2 %shard_map.54 = (bf16[2,4,1024,2,128]{4,3,2,1,0:T(2,128)(2,1)S(1)}, f32[8,128]{1,0:T(8,128)S(1)}) custom-call(bf16[9,1024,2,512]{3,2,1,0:T(2,128)(2,1)} %bitcast.24, f32[8,128]{1,0:T(8,128)S(1)} %get-tuple-element.95.refs_1_), custom_call_target="tpu_custom_call" | custom-call | flops 1 | bytes 1 | tf_op jit(solution)/shard_map/pallas_call | solution.py:44
  20.0 2.2 %shard_map.55 = (bf16[2,4,1024,2,128]{4,3,2,1,0:T(2,128)(2,1)S(1)}, f32[8,128]{1,0:T(8,128)S(1)}) custom-call(bf16[9,1024,2,512]{3,2,1,0:T(2,128)(2,1)} %bitcast.25, f32[8,128]{1,0:T(8,128)S(1)} %get-tuple-element.96.refs_1_), custom_call_target="tpu_custom_call" | custom-call | flops 1 | bytes 1 | tf_op jit(solution)/shard_map/pallas_call | solution.py:44
  22.3 2.0 %shard_map.56 = (f32[1024,128]{1,0:T(8,128)S(1)}, f32[8,128]{1,0:T(8,128)S(1)}) custom-call(bf16[3,4,2048,128]{3,2,1,0:T(8,128)(2,1)S(1)} %bitcast.13, bf16[512,128]{1,0:T(8,128)(2,1)S(1)} %get-tuple-element.98.refs_1_, bf16[512,128]{1,0:T(8,128)(2,1)S(1)} %collective-permute-done.3.refs_2_), custom_call_target="tpu_custom_call" | custom-call | flops 1 | bytes 1 | tf_op jit(solution)/shard_map/pallas_call | solution.py:44
  29.0 2.5 %shard_map.58 = (f32[1024,128]{1,0:T(8,128)S(1)}, f32[8,128]{1,0:T(8,128)S(1)}) custom-call(bf16[2,4,2048,128]{3,2,1,0:T(8,128)(2,1)S(1)} %bitcast.16, bf16[2,4,2048,128]{3,2,1,0:T(8,128)(2,1)S(1)} %bitcast.19, bf16[512,128]{1,0:T(8,128)(2,1)S(1)} %collective-permute-done.2.refs_2_, bf16[256,128]{1,0:T(8,128)(2,1)S(1)} %collective-permute-done.4.refs_3_, ...), custom_call_target="tpu_custom_call" | custom-call | flops 1 | bytes 1 | tf_op jit(solution)/shard_map/pallas_call | solution.py:44
  39.1 3.1 %collective-permute-done.13.refs_1_ = f32[512,128]{1,0:T(8,128)S(1)} collective-permute-done((f32[512,128]{1,0:T(8,128)S(1)}, f32[512,128]{1,0:T(8,128)S(1)}, u32[]{:S(2)}, u32[]{:S(2)}) %collective-permute-start.13) | collective-permute-done | bytes 262176 | tf_op jit(solution)/shard_map/ppermute | solution.py:60
  44.9 2.5 %collective-permute-start.17 = (f32[176,128]{1,0:T(8,128)S(1)}, f32[176,128]{1,0:T(8,128)S(1)}, u32[]{:S(2)}, u32[]{:S(2)}) collective-permute-start(f32[176,128]{1,0:T(8,128)S(1)} %pad_maximum_fusion), channel_id=1, source_target_pairs={{6,0},{4,2},{2,4},{0,6},{14,8},{12,10},{10,12},{8,14},{7,1},{5,3},... | collective-permute-start | bytes 270344 | tf_op jit(solution)/shard_map/ppermute | solution.py:60
  48.4 2.0 %collective-permute-done.16 = f32[176,128]{1,0:T(8,128)S(1)} collective-permute-done((f32[176,128]{1,0:T(8,128)S(1)}, f32[176,128]{1,0:T(8,128)S(1)}, u32[]{:S(2)}, u32[]{:S(2)}) %collective-permute-start.16) | collective-permute-done | bytes 90144 | tf_op jit(solution)/shard_map/ppermute | solution.py:60
  50.4 1.7 %collective-permute-done.17 = f32[176,128]{1,0:T(8,128)S(1)} collective-permute-done((f32[176,128]{1,0:T(8,128)S(1)}, f32[176,128]{1,0:T(8,128)S(1)}, u32[]{:S(2)}, u32[]{:S(2)}) %collective-permute-start.17) | collective-permute-done | bytes 90144 | tf_op jit(solution)/shard_map/ppermute | solution.py:60
  55.0 5.6 %shard_map.63 = (f32[128,128]{1,0:T(8,128)S(1)}, f32[128,128]{1,0:T(8,128)S(1)}, f32[128,128]{1,0:T(8,128)S(1)}, f32[128,128]{1,0:T(8,128)S(1)}, f32[8,128]{1,0:T(8,128)}) custom-call(f32[104,128]{1,0:T(8,128)S(1)} %slice.65.refs_0_, f32[104,128]{1,0:T(8,128)S(1)} %collective-permute-done.19.refs_1_), custom_call_target="tpu_custom_call" | custom-call | flops 1 | bytes 1 | tf_op jit(solution)/shard_map/pallas_call | solution.py:44
  60.7 1.9 %shard_map.64 = (f32[512,128]{1,0:T(8,128)S(1)}, f32[512,128]{1,0:T(8,128)S(1)}, bf16[512,128]{1,0:T(8,128)(2,1)S(1)}, f32[128,128]{1,0:T(8,128)S(1)}, f32[128,128]{1,0:T(8,128)S(1)}, /*index=5*/f32[8,128]{1,0:T(8,128)}) custom-call(f32[128,128]{1,0:T(8,128)S(1)} %get-tuple-element.122.refs_0_.refs_2_, f32[128,128]{1,0:T(8,128)S(1)} %get-tuple-element.123.refs_1_, ...), custom_call_target="tpu_custom_call" | custom-call | flops 1 | bytes 1 | tf_op jit(solution)/shard_map/pallas_call | solution.py:44
  67.7 2.0 %shard_map.65 = (f32[1024,128]{1,0:T(8,128)S(1)}, f32[8,128]{1,0:T(8,128)S(1)}) custom-call(bf16[3,4,2048,128]{3,2,1,0:T(8,128)(2,1)S(1)} %bitcast.14, bf16[512,128]{1,0:T(8,128)(2,1)S(1)} %get-tuple-element.128.refs_1_, bf16[512,128]{1,0:T(8,128)(2,1)S(1)} %collective-permute-done.22.refs_2_), custom_call_target="tpu_custom_call" | custom-call | flops 1 | bytes 1 | tf_op jit(solution)/shard_map/pallas_call | solution.py:44
  70.3 6.9 %collective-permute-done.21.refs_2_ = bf16[512,128]{1,0:T(8,128)(2,1)S(1)} collective-permute-done((bf16[512,128]{1,0:T(8,128)(2,1)S(1)}, bf16[512,128]{1,0:T(8,128)(2,1)S(1)}, u32[]{:S(2)}, u32[]{:S(2)}) %collective-permute-start.21) | collective-permute-done | bytes 131104 | tf_op jit(solution)/shard_map/ppermute | solution.py:60
  79.8 2.5 %shard_map.67 = (f32[1024,128]{1,0:T(8,128)S(1)}, f32[8,128]{1,0:T(8,128)S(1)}) custom-call(bf16[2,4,2048,128]{3,2,1,0:T(8,128)(2,1)S(1)} %bitcast.17, bf16[2,4,2048,128]{3,2,1,0:T(8,128)(2,1)S(1)} %bitcast.20, bf16[512,128]{1,0:T(8,128)(2,1)S(1)} %collective-permute-done.21.refs_2_, bf16[256,128]{1,0:T(8,128)(2,1)S(1)} %collective-permute-done.23.refs_3_, ...), custom_call_target="tpu_custom_call" | custom-call | flops 1 | bytes 1 | tf_op jit(solution)/shard_map/pallas_call | solution.py:44
  89.1 3.9 %collective-permute-done.32.refs_1_ = f32[512,128]{1,0:T(8,128)S(1)} collective-permute-done((f32[512,128]{1,0:T(8,128)S(1)}, f32[512,128]{1,0:T(8,128)S(1)}, u32[]{:S(2)}, u32[]{:S(2)}) %collective-permute-start.32) | collective-permute-done | bytes 262176 | tf_op jit(solution)/shard_map/ppermute | solution.py:60
  95.3 2.0 %collective-permute-start.36 = (f32[176,128]{1,0:T(8,128)S(1)}, f32[176,128]{1,0:T(8,128)S(1)}, u32[]{:S(2)}, u32[]{:S(2)}) collective-permute-start(f32[176,128]{1,0:T(8,128)S(1)} %pad_maximum_fusion.1), channel_id=1, source_target_pairs={{6,0},{4,2},{2,4},{0,6},{14,8},{12,10},{10,12},{8,14},{7,1},{5,3},... | collective-permute-start | bytes 270344 | tf_op jit(solution)/shard_map/ppermute | solution.py:60
  98.8 2.0 %collective-permute-done.35 = f32[176,128]{1,0:T(8,128)S(1)} collective-permute-done((f32[176,128]{1,0:T(8,128)S(1)}, f32[176,128]{1,0:T(8,128)S(1)}, u32[]{:S(2)}, u32[]{:S(2)}) %collective-permute-start.35) | collective-permute-done | bytes 90144 | tf_op jit(solution)/shard_map/ppermute | solution.py:60
  104.6 5.3 %shard_map.72 = (f32[128,128]{1,0:T(8,128)S(1)}, f32[128,128]{1,0:T(8,128)S(1)}, f32[128,128]{1,0:T(8,128)S(1)}, f32[128,128]{1,0:T(8,128)S(1)}, f32[8,128]{1,0:T(8,128)}) custom-call(f32[104,128]{1,0:T(8,128)S(1)} %slice.67.refs_0_, f32[104,128]{1,0:T(8,128)S(1)} %collective-permute-done.38.refs_1_, f32[128,128]{1,0:T(8,128)S(1)} %get-tuple-element.149.refs_2_), custom_call_target="tpu_custom_call" | custom-call | flops 1 | bytes 1 | tf_op jit(solution)/shard_map/pallas_call | solution.py:44
  109.9 2.0 %shard_map.73 = (f32[512,128]{1,0:T(8,128)S(1)}, f32[512,128]{1,0:T(8,128)S(1)}, bf16[512,128]{1,0:T(8,128)(2,1)S(1)}, f32[128,128]{1,0:T(8,128)S(1)}, f32[128,128]{1,0:T(8,128)S(1)}, /*index=5*/f32[8,128]{1,0:T(8,128)}) custom-call(f32[128,128]{1,0:T(8,128)S(1)} %get-tuple-element.151.refs_0_.refs_2_, f32[128,128]{1,0:T(8,128)S(1)} %get-tuple-element.152.refs_1_, ...), custom_call_target="tpu_custom_call" | custom-call | flops 1 | bytes 1 | tf_op jit(solution)/shard_map/pallas_call | solution.py:44
  114.3 2.1 %collective-permute-start.39 = (bf16[512,128]{1,0:T(8,128)(2,1)S(1)}, bf16[512,128]{1,0:T(8,128)(2,1)S(1)}, u32[]{:S(2)}, u32[]{:S(2)}) collective-permute-start(bf16[512,128]{1,0:T(8,128)(2,1)S(1)} %get-tuple-element.157.refs_1_), channel_id=1, source_target_pairs={{12,0},{8,4},{4,8},{0,12},{13,1},{9,5},{5,9},{1,13},{14,2},{10,6},... | collective-permute-start | bytes 393224 | tf_op jit(solution)/shard_map/ppermute | solution.py:60
  117.9 2.0 %shard_map.74 = (f32[1024,128]{1,0:T(8,128)S(1)}, f32[8,128]{1,0:T(8,128)S(1)}) custom-call(bf16[3,4,2048,128]{3,2,1,0:T(8,128)(2,1)S(1)} %bitcast.15, bf16[512,128]{1,0:T(8,128)(2,1)S(1)} %get-tuple-element.157.refs_1_, bf16[512,128]{1,0:T(8,128)(2,1)S(1)} %collective-permute-done.41.refs_2_), custom_call_target="tpu_custom_call" | custom-call | flops 1 | bytes 1 | tf_op jit(solution)/shard_map/pallas_call | solution.py:44
  121.7 4.3 %collective-permute-done.40.refs_2_ = bf16[512,128]{1,0:T(8,128)(2,1)S(1)} collective-permute-done((bf16[512,128]{1,0:T(8,128)(2,1)S(1)}, bf16[512,128]{1,0:T(8,128)(2,1)S(1)}, u32[]{:S(2)}, u32[]{:S(2)}) %collective-permute-start.40) | collective-permute-done | bytes 131104 | tf_op jit(solution)/shard_map/ppermute | solution.py:60
  127.5 2.5 %shard_map.76 = (f32[1024,128]{1,0:T(8,128)S(1)}, f32[8,128]{1,0:T(8,128)S(1)}) custom-call(bf16[2,4,2048,128]{3,2,1,0:T(8,128)(2,1)S(1)} %bitcast.18, bf16[2,4,2048,128]{3,2,1,0:T(8,128)(2,1)S(1)} %bitcast.21, bf16[512,128]{1,0:T(8,128)(2,1)S(1)} %collective-permute-done.40.refs_2_, bf16[256,128]{1,0:T(8,128)(2,1)S(1)} %collective-permute-done.42.refs_3_, ...), custom_call_target="tpu_custom_call" | custom-call | flops 1 | bytes 1 | tf_op jit(solution)/shard_map/pallas_call | solution.py:44
  131.4 1.9 %shard_map.77 = (f32[512,128]{1,0:T(8,128)S(1)}, f32[512,128]{1,0:T(8,128)S(1)}, f32[8,128]{1,0:T(8,128)}) custom-call(bf16[2,4,2048,128]{3,2,1,0:T(8,128)(2,1)S(1)} %bitcast.12, bf16[512,128]{1,0:T(8,128)(2,1)S(1)} %collective-permute-done.39.refs_1_, bf16[512,128]{1,0:T(8,128)(2,1)S(1)} %collective-permute-done.48.refs_2_, ...), custom_call_target="tpu_custom_call" | custom-call | flops 1 | bytes 1 | tf_op jit(solution)/shard_map/pallas_call | solution.py:44
  136.0 2.4 %collective-permute-start.51 = (f32[72,128]{1,0:T(8,128)S(1)}, f32[72,128]{1,0:T(8,128)S(1)}, u32[]{:S(2)}, u32[]{:S(2)}) collective-permute-start(f32[72,128]{1,0:T(8,128)S(1)} %add.63), channel_id=1, source_target_pairs={{4,0},{6,2},{0,4},{2,6},{12,8},{14,10},{8,12},{10,14},{5,1},{7,3},... | collective-permute-start | bytes 110600 | tf_op jit(solution)/shard_map/ppermute | solution.py:60
  140.9 1.8 %collective-permute-done.50 = f32[72,128]{1,0:T(8,128)S(1)} collective-permute-done((f32[72,128]{1,0:T(8,128)S(1)}, f32[72,128]{1,0:T(8,128)S(1)}, u32[]{:S(2)}, u32[]{:S(2)}) %collective-permute-start.50) | collective-permute-done | bytes 36896 | tf_op jit(solution)/shard_map/ppermute | solution.py:60
  143.8 3.9 %collective-permute-done.53 = f32[72,128]{1,0:T(8,128)S(1)} collective-permute-done((f32[72,128]{1,0:T(8,128)S(1)}, f32[72,128]{1,0:T(8,128)S(1)}, u32[]{:S(2)}, u32[]{:S(2)}) %collective-permute-start.53) | collective-permute-done | bytes 36896 | tf_op jit(solution)/shard_map/ppermute | solution.py:60
  147.7 5.2 %shard_map.79 = (f32[512,128]{1,0:T(8,128)}, f32[512,128]{1,0:T(8,128)}, f32[8,128]{1,0:T(8,128)}) custom-call(f32[72,128]{1,0:T(8,128)S(1)} %add.67.refs_0_, f32[128,128]{1,0:T(8,128)S(1)} %get-tuple-element.173.refs_1_, f32[512,128]{1,0:T(8,128)S(1)} %get-tuple-element.174.refs_2_, f32[512,128]{1,0:T(8,128)S(1)} %get-tuple-element.165.refs_2_.refs_3_, ...), custom_call_target="tpu_custom_call" | custom-call | flops 1 | bytes 1 | tf_op jit(solution)/shard_map/pallas_call | solution.py:44
  (131 shorter events, 60.9 us)
Async XLA Ops:
  2.1 9.3 %collective-permute-start = (f32[512,128]{1,0:T(8,128)S(1)}, f32[512,128]{1,0:T(8,128)S(1)}, u32[]{:S(2)}, u32[]{:S(2)}) collective-permute-start(f32[512,128]{1,0:T(8,128)S(1)} %get-tuple-element.91), channel_id=1, source_target_pairs={{2,0},{0,2},{3,1},{1,3},{6,4},{4,6},{7,5},{5,7},{10,8},{8,10},{11,... | collective-permute-start | bytes 786440 | tf_op jit(solution)/shard_map/ppermute | solution.py:60
  11.5 10.7 %collective-permute-start.3 = (bf16[512,128]{1,0:T(8,128)(2,1)S(1)}, bf16[512,128]{1,0:T(8,128)(2,1)S(1)}, u32[]{:S(2)}, u32[]{:S(2)}) collective-permute-start(bf16[512,128]{1,0:T(8,128)(2,1)S(1)} %get-tuple-element.98.refs_1_), channel_id=1, source_target_pairs={{1,0},{0,1},{3,2},{2,3},{5,4},{4,5},{7,6},{6,7},{9,8},{8,9},{11,10... | collective-permute-start | bytes 393224 | tf_op jit(solution)/shard_map/ppermute | solution.py:60
  11.6 13.1 %collective-permute-start.6 = (bf16[512,128]{1,0:T(8,128)(2,1)S(1)}, bf16[512,128]{1,0:T(8,128)(2,1)S(1)}, u32[]{:S(2)}, u32[]{:S(2)}) collective-permute-start(bf16[512,128]{1,0:T(8,128)(2,1)S(1)} %get-tuple-element.98.refs_1_), channel_id=1, source_target_pairs={{4,0},{0,4},{12,8},{8,12},{5,1},{1,5},{13,9},{9,13},{6,2},{2,6},{1... | collective-permute-start | bytes 393224 | tf_op jit(solution)/shard_map/ppermute | solution.py:60
  13.5 12.9 %collective-permute-start.2 = (bf16[512,128]{1,0:T(8,128)(2,1)S(1)}, bf16[512,128]{1,0:T(8,128)(2,1)S(1)}, u32[]{:S(2)}, u32[]{:S(2)}) collective-permute-start(bf16[512,128]{1,0:T(8,128)(2,1)S(1)} %get-tuple-element.98.refs_1_), channel_id=1, source_target_pairs={{8,0},{12,4},{0,8},{4,12},{9,1},{13,5},{1,9},{5,13},{10,2},{14,6},... | collective-permute-start | bytes 393224 | tf_op jit(solution)/shard_map/ppermute | solution.py:60
  16.1 15.5 %collective-permute-start.1 = (bf16[512,128]{1,0:T(8,128)(2,1)S(1)}, bf16[512,128]{1,0:T(8,128)(2,1)S(1)}, u32[]{:S(2)}, u32[]{:S(2)}) collective-permute-start(bf16[512,128]{1,0:T(8,128)(2,1)S(1)} %get-tuple-element.98.refs_1_), channel_id=1, source_target_pairs={{12,0},{8,4},{4,8},{0,12},{13,1},{9,5},{5,9},{1,13},{14,2},{10,6},... | collective-permute-start | bytes 393224 | tf_op jit(solution)/shard_map/ppermute | solution.py:60
  16.1 12.9 %collective-permute-start.9 = (f32[512,128]{1,0:T(8,128)S(1)}, f32[512,128]{1,0:T(8,128)S(1)}, u32[]{:S(2)}, u32[]{:S(2)}) collective-permute-start(f32[512,128]{1,0:T(8,128)S(1)} %get-tuple-element.103.refs_0_.refs_2_.refs_4_.refs_5_), channel_id=1, source_target_pairs={{2,0},{0,2},{3,1},{1,3},{6,4},{4,6},{7,5},{5,7},{10,8},{8,10},{11,... | collective-permute-start | bytes 786440 | tf_op jit(solution)/shard_map/ppermute | solution.py:60
  33.8 8.4 %collective-permute-start.13 = (f32[512,128]{1,0:T(8,128)S(1)}, f32[512,128]{1,0:T(8,128)S(1)}, u32[]{:S(2)}, u32[]{:S(2)}) collective-permute-start(f32[512,128]{1,0:T(8,128)S(1)} %get-tuple-element.115.refs_1_), channel_id=1, source_target_pairs={{2,0},{0,2},{3,1},{1,3},{6,4},{4,6},{7,5},{5,7},{10,8},{8,10},{11,... | collective-permute-start | bytes 786440 | tf_op jit(solution)/shard_map/ppermute | solution.py:60
  39.0 5.8 %collective-permute-start.12 = (f32[104,128]{1,0:T(8,128)S(1)}, f32[104,128]{1,0:T(8,128)S(1)}, u32[]{:S(2)}, u32[]{:S(2)}) collective-permute-start(f32[104,128]{1,0:T(8,128)S(1)} %add.51), channel_id=1, source_target_pairs={{8,0},{10,2},{12,4},{14,6},{0,8},{2,10},{4,12},{6,14},{9,1},{11,3}... | collective-permute-start | bytes 159752 | tf_op jit(solution)/shard_map/ppermute | solution.py:60
  44.9 5.5 %collective-permute-start.16 = (f32[176,128]{1,0:T(8,128)S(1)}, f32[176,128]{1,0:T(8,128)S(1)}, u32[]{:S(2)}, u32[]{:S(2)}) collective-permute-start(f32[176,128]{1,0:T(8,128)S(1)} %pad_maximum_fusion), channel_id=1, source_target_pairs={{4,0},{6,2},{0,4},{2,6},{12,8},{14,10},{8,12},{10,14},{5,1},{7,3},... | collective-permute-start | bytes 270344 | tf_op jit(solution)/shard_map/ppermute | solution.py:60
  44.9 7.2 %collective-permute-start.17 = (f32[176,128]{1,0:T(8,128)S(1)}, f32[176,128]{1,0:T(8,128)S(1)}, u32[]{:S(2)}, u32[]{:S(2)}) collective-permute-start(f32[176,128]{1,0:T(8,128)S(1)} %pad_maximum_fusion), channel_id=1, source_target_pairs={{6,0},{4,2},{2,4},{0,6},{14,8},{12,10},{10,12},{8,14},{7,1},{5,3},... | collective-permute-start | bytes 270344 | tf_op jit(solution)/shard_map/ppermute | solution.py:60
  47.5 5.9 %collective-permute-start.15 = (f32[176,128]{1,0:T(8,128)S(1)}, f32[176,128]{1,0:T(8,128)S(1)}, u32[]{:S(2)}, u32[]{:S(2)}) collective-permute-start(f32[176,128]{1,0:T(8,128)S(1)} %pad_maximum_fusion), channel_id=1, source_target_pairs={{2,0},{0,2},{6,4},{4,6},{10,8},{8,10},{14,12},{12,14},{3,1},{1,3},... | collective-permute-start | bytes 270344 | tf_op jit(solution)/shard_map/ppermute | solution.py:60
  53.5 7.2 %collective-permute-start.18 = (f32[72,128]{1,0:T(8,128)S(1)}, f32[72,128]{1,0:T(8,128)S(1)}, u32[]{:S(2)}, u32[]{:S(2)}) collective-permute-start(f32[72,128]{1,0:T(8,128)S(1)} %slice.64.refs_7_), channel_id=1, source_target_pairs={{8,0},{10,2},{12,4},{14,6},{0,8},{2,10},{4,12},{6,14},{9,1},{11,3}... | collective-permute-start | bytes 110600 | tf_op jit(solution)/shard_map/ppermute | solution.py:60
  62.6 5.1 %collective-permute-start.22 = (bf16[512,128]{1,0:T(8,128)(2,1)S(1)}, bf16[512,128]{1,0:T(8,128)(2,1)S(1)}, u32[]{:S(2)}, u32[]{:S(2)}) collective-permute-start(bf16[512,128]{1,0:T(8,128)(2,1)S(1)} %get-tuple-element.128.refs_1_), channel_id=1, source_target_pairs={{1,0},{0,1},{3,2},{2,3},{5,4},{4,5},{7,6},{6,7},{9,8},{8,9},{11,10... | collective-permute-start | bytes 393224 | tf_op jit(solution)/shard_map/ppermute | solution.py:60
  62.8 7.5 %collective-permute-start.25 = (bf16[512,128]{1,0:T(8,128)(2,1)S(1)}, bf16[512,128]{1,0:T(8,128)(2,1)S(1)}, u32[]{:S(2)}, u32[]{:S(2)}) collective-permute-start(bf16[512,128]{1,0:T(8,128)(2,1)S(1)} %get-tuple-element.128.refs_1_), channel_id=1, source_target_pairs={{4,0},{0,4},{12,8},{8,12},{5,1},{1,5},{13,9},{9,13},{6,2},{2,6},{1... | collective-permute-start | bytes 393224 | tf_op jit(solution)/shard_map/ppermute | solution.py:60
  64.3 12.9 %collective-permute-start.21 = (bf16[512,128]{1,0:T(8,128)(2,1)S(1)}, bf16[512,128]{1,0:T(8,128)(2,1)S(1)}, u32[]{:S(2)}, u32[]{:S(2)}) collective-permute-start(bf16[512,128]{1,0:T(8,128)(2,1)S(1)} %get-tuple-element.128.refs_1_), channel_id=1, source_target_pairs={{8,0},{12,4},{0,8},{4,12},{9,1},{13,5},{1,9},{5,13},{10,2},{14,6},... | collective-permute-start | bytes 393224 | tf_op jit(solution)/shard_map/ppermute | solution.py:60
  65.4 16.9 %collective-permute-start.20 = (bf16[512,128]{1,0:T(8,128)(2,1)S(1)}, bf16[512,128]{1,0:T(8,128)(2,1)S(1)}, u32[]{:S(2)}, u32[]{:S(2)}) collective-permute-start(bf16[512,128]{1,0:T(8,128)(2,1)S(1)} %get-tuple-element.128.refs_1_), channel_id=1, source_target_pairs={{12,0},{8,4},{4,8},{0,12},{13,1},{9,5},{5,9},{1,13},{14,2},{10,6},... | collective-permute-start | bytes 393224 | tf_op jit(solution)/shard_map/ppermute | solution.py:60
  67.1 12.6 %collective-permute-start.28 = (f32[512,128]{1,0:T(8,128)S(1)}, f32[512,128]{1,0:T(8,128)S(1)}, u32[]{:S(2)}, u32[]{:S(2)}) collective-permute-start(f32[512,128]{1,0:T(8,128)S(1)} %get-tuple-element.135.refs_2_.refs_5_.refs_0_), channel_id=1, source_target_pairs={{2,0},{0,2},{3,1},{1,3},{6,4},{4,6},{7,5},{5,7},{10,8},{8,10},{11,... | collective-permute-start | bytes 786440 | tf_op jit(solution)/shard_map/ppermute | solution.py:60
  84.6 8.4 %collective-permute-start.32 = (f32[512,128]{1,0:T(8,128)S(1)}, f32[512,128]{1,0:T(8,128)S(1)}, u32[]{:S(2)}, u32[]{:S(2)}) collective-permute-start(f32[512,128]{1,0:T(8,128)S(1)} %get-tuple-element.142.refs_1_), channel_id=1, source_target_pairs={{2,0},{0,2},{3,1},{1,3},{6,4},{4,6},{7,5},{5,7},{10,8},{8,10},{11,... | collective-permute-start | bytes 786440 | tf_op jit(solution)/shard_map/ppermute | solution.py:60
  89.0 5.1 %collective-permute-start.31 = (f32[104,128]{1,0:T(8,128)S(1)}, f32[104,128]{1,0:T(8,128)S(1)}, u32[]{:S(2)}, u32[]{:S(2)}) collective-permute-start(f32[104,128]{1,0:T(8,128)S(1)} %add.57), channel_id=1, source_target_pairs={{8,0},{10,2},{12,4},{14,6},{0,8},{2,10},{4,12},{6,14},{9,1},{11,3}... | collective-permute-start | bytes 159752 | tf_op jit(solution)/shard_map/ppermute | solution.py:60
  95.2 5.5 %collective-permute-start.35 = (f32[176,128]{1,0:T(8,128)S(1)}, f32[176,128]{1,0:T(8,128)S(1)}, u32[]{:S(2)}, u32[]{:S(2)}) collective-permute-start(f32[176,128]{1,0:T(8,128)S(1)} %pad_maximum_fusion.1), channel_id=1, source_target_pairs={{4,0},{6,2},{0,4},{2,6},{12,8},{14,10},{8,12},{10,14},{5,1},{7,3},... | collective-permute-start | bytes 270344 | tf_op jit(solution)/shard_map/ppermute | solution.py:60
  95.3 6.7 %collective-permute-start.36 = (f32[176,128]{1,0:T(8,128)S(1)}, f32[176,128]{1,0:T(8,128)S(1)}, u32[]{:S(2)}, u32[]{:S(2)}) collective-permute-start(f32[176,128]{1,0:T(8,128)S(1)} %pad_maximum_fusion.1), channel_id=1, source_target_pairs={{6,0},{4,2},{2,4},{0,6},{14,8},{12,10},{10,12},{8,14},{7,1},{5,3},... | collective-permute-start | bytes 270344 | tf_op jit(solution)/shard_map/ppermute | solution.py:60
  97.3 5.9 %collective-permute-start.34 = (f32[176,128]{1,0:T(8,128)S(1)}, f32[176,128]{1,0:T(8,128)S(1)}, u32[]{:S(2)}, u32[]{:S(2)}) collective-permute-start(f32[176,128]{1,0:T(8,128)S(1)} %pad_maximum_fusion.1), channel_id=1, source_target_pairs={{2,0},{0,2},{6,4},{4,6},{10,8},{8,10},{14,12},{12,14},{3,1},{1,3},... | collective-permute-start | bytes 270344 | tf_op jit(solution)/shard_map/ppermute | solution.py:60
  103.4 6.5 %collective-permute-start.37 = (f32[72,128]{1,0:T(8,128)S(1)}, f32[72,128]{1,0:T(8,128)S(1)}, u32[]{:S(2)}, u32[]{:S(2)}) collective-permute-start(f32[72,128]{1,0:T(8,128)S(1)} %slice.66.refs_7_), channel_id=1, source_target_pairs={{8,0},{10,2},{12,4},{14,6},{0,8},{2,10},{4,12},{6,14},{9,1},{11,3}... | collective-permute-start | bytes 110600 | tf_op jit(solution)/shard_map/ppermute | solution.py:60
  111.9 6.0 %collective-permute-start.41 = (bf16[512,128]{1,0:T(8,128)(2,1)S(1)}, bf16[512,128]{1,0:T(8,128)(2,1)S(1)}, u32[]{:S(2)}, u32[]{:S(2)}) collective-permute-start(bf16[512,128]{1,0:T(8,128)(2,1)S(1)} %get-tuple-element.157.refs_1_), channel_id=1, source_target_pairs={{1,0},{0,1},{3,2},{2,3},{5,4},{4,5},{7,6},{6,7},{9,8},{8,9},{11,10... | collective-permute-start | bytes 393224 | tf_op jit(solution)/shard_map/ppermute | solution.py:60
  112.0 9.1 %collective-permute-start.44 = (bf16[512,128]{1,0:T(8,128)(2,1)S(1)}, bf16[512,128]{1,0:T(8,128)(2,1)S(1)}, u32[]{:S(2)}, u32[]{:S(2)}) collective-permute-start(bf16[512,128]{1,0:T(8,128)(2,1)S(1)} %get-tuple-element.157.refs_1_), channel_id=1, source_target_pairs={{4,0},{0,4},{12,8},{8,12},{5,1},{1,5},{13,9},{9,13},{6,2},{2,6},{1... | collective-permute-start | bytes 393224 | tf_op jit(solution)/shard_map/ppermute | solution.py:60
  113.1 12.9 %collective-permute-start.40 = (bf16[512,128]{1,0:T(8,128)(2,1)S(1)}, bf16[512,128]{1,0:T(8,128)(2,1)S(1)}, u32[]{:S(2)}, u32[]{:S(2)}) collective-permute-start(bf16[512,128]{1,0:T(8,128)(2,1)S(1)} %get-tuple-element.157.refs_1_), channel_id=1, source_target_pairs={{8,0},{12,4},{0,8},{4,12},{9,1},{13,5},{1,9},{5,13},{10,2},{14,6},... | collective-permute-start | bytes 393224 | tf_op jit(solution)/shard_map/ppermute | solution.py:60
  114.3 15.7 %collective-permute-start.39 = (bf16[512,128]{1,0:T(8,128)(2,1)S(1)}, bf16[512,128]{1,0:T(8,128)(2,1)S(1)}, u32[]{:S(2)}, u32[]{:S(2)}) collective-permute-start(bf16[512,128]{1,0:T(8,128)(2,1)S(1)} %get-tuple-element.157.refs_1_), channel_id=1, source_target_pairs={{12,0},{8,4},{4,8},{0,12},{13,1},{9,5},{5,9},{1,13},{14,2},{10,6},... | collective-permute-start | bytes 393224 | tf_op jit(solution)/shard_map/ppermute | solution.py:60
  116.4 11.1 %collective-permute-start.47 = (f32[512,128]{1,0:T(8,128)S(1)}, f32[512,128]{1,0:T(8,128)S(1)}, u32[]{:S(2)}, u32[]{:S(2)}) collective-permute-start(f32[512,128]{1,0:T(8,128)S(1)} %get-tuple-element.165.refs_2_.refs_3_), channel_id=1, source_target_pairs={{2,0},{0,2},{3,1},{1,3},{6,4},{4,6},{7,5},{5,7},{10,8},{8,10},{11,... | collective-permute-start | bytes 786440 | tf_op jit(solution)/shard_map/ppermute | solution.py:60
  121.2 4.9 %collective-permute-start.46 = (bf16[256,128]{1,0:T(8,128)(2,1)S(1)}, bf16[256,128]{1,0:T(8,128)(2,1)S(1)}, u32[]{:S(2)}, u32[]{:S(2)}) collective-permute-start(bf16[256,128]{1,0:T(8,128)(2,1)S(1)} %get-tuple-element.178), channel_id=1, source_target_pairs={{1,0},{0,1},{3,2},{2,3},{5,4},{4,5},{7,6},{6,7},{9,8},{8,9},{11,10... | collective-permute-start | bytes 196616 | tf_op jit(solution)/shard_map/ppermute | solution.py:60
  121.2 5.3 %collective-permute-start.45 = (bf16[256,128]{1,0:T(8,128)(2,1)S(1)}, bf16[256,128]{1,0:T(8,128)(2,1)S(1)}, u32[]{:S(2)}, u32[]{:S(2)}) collective-permute-start(bf16[256,128]{1,0:T(8,128)(2,1)S(1)} %get-tuple-element.179), channel_id=1, source_target_pairs={{1,0},{0,1},{3,2},{2,3},{5,4},{4,5},{7,6},{6,7},{9,8},{8,9},{11,10... | collective-permute-start | bytes 196616 | tf_op jit(solution)/shard_map/ppermute | solution.py:60
  135.8 5.0 %collective-permute-start.52 = (f32[72,128]{1,0:T(8,128)S(1)}, f32[72,128]{1,0:T(8,128)S(1)}, u32[]{:S(2)}, u32[]{:S(2)}) collective-permute-start(f32[72,128]{1,0:T(8,128)S(1)} %add.63), channel_id=1, source_target_pairs={{6,0},{4,2},{2,4},{0,6},{14,8},{12,10},{10,12},{8,14},{7,1},{5,3},... | collective-permute-start | bytes 110600 | tf_op jit(solution)/shard_map/ppermute | solution.py:60
  139.3 8.4 %collective-permute-start.54 = (f32[512,128]{1,0:T(8,128)S(1)}, f32[512,128]{1,0:T(8,128)S(1)}, u32[]{:S(2)}, u32[]{:S(2)}) collective-permute-start(f32[512,128]{1,0:T(8,128)S(1)} %get-tuple-element.171.refs_1_), channel_id=1, source_target_pairs={{2,0},{0,2},{3,1},{1,3},{6,4},{4,6},{7,5},{5,7},{10,8},{8,10},{11,... | collective-permute-start | bytes 786440 | tf_op jit(solution)/shard_map/ppermute | solution.py:60
  (23 other events, 41.2 us)

commit v9 on v8

--- a/solution.py
+++ b/solution.py
@@ -277,7 +277,7 @@
     panels = lax.axis_size("panel")
     groups = []
     if links == 2 * panels + 1 and panels & (panels - 1) == 0:
-        for s in sorted(range(panels), key=lambda s: (s > 0, s % 2)):
+        for s in range(panels):
 
             def numbers(s=s):
                 me = lax.axis_index("panel")

time: 153 us -> 148 us (0.967)
  waiting for transfers between devices: 50.7 us -> 36.7 us
  starting transfers between devices: 42.2 us -> 50.9 us
    ppermute x55, waiting for transfers between devices: 50.7 us -> 36.7 us  [permute(): return lax.ppermute(value, axis, pairs)]
    ppermute x55, starting transfers between devices: 42.2 us -> 50.9 us  [permute(): return lax.ppermute(value, axis, pairs)]
  transfers between devices with their start and end apart: 55 -> 55, of which waited for: 34 -> 34; matrix products, arithmetic and copies ran while one was open for 0% -> 0% of each run, Pallas kernels for 28% -> 29%
where the time goes in v9:
time: 148 us
  Pallas kernels  58.7 us (40%)
  starting transfers between devices  50.9 us (34%)
  waiting for transfers between devices  36.7 us (25%)
    pallas_call x30, Pallas kernels, call(): pl.pallas_call(ordered, out_shape=list(outs) + [shape(SUB)], in_specs=[HB...  58.7 us
    ppermute x55, starting transfers between devices, permute(): return lax.ppermute(value, axis, pairs)  50.9 us
    ppermute x55, waiting for transfers between devices, permute(): return lax.ppermute(value, axis, pairs)  36.7 us
  transfers between devices with their start and end apart: 55, of which 34 were waited for; matrix products, arithmetic and copies ran while one was open for 0% of the time, Pallas kernels for 29%

profile of v9, /device:TPU:0, one launch (start us, length us, event | category | flops | bytes accessed | tf_op | source)
XLA Modules:
  0.0 147.5 jit_solution(1320185381337789467)
XLA Ops:
  2.1 3.0 %collective-permute-start = (f32[512,128]{1,0:T(8,128)S(1)}, f32[512,128]{1,0:T(8,128)S(1)}, u32[]{:S(2)}, u32[]{:S(2)}) collective-permute-start(f32[512,128]{1,0:T(8,128)S(1)} %get-tuple-element.91), channel_id=1, source_target_pairs={{2,0},{0,2},{3,1},{1,3},{6,4},{4,6},{7,5},{5,7},{10,8},{8,10},{11,... | collective-permute-start | bytes 786440 | tf_op jit(solution)/shard_map/ppermute | solution.py:60
  5.1 2.9 %shard_map.51 = (bf16[3,4,1024,2,128]{4,3,2,1,0:T(2,128)(2,1)S(1)}, f32[8,128]{1,0:T(8,128)S(1)}) custom-call(bf16[9,1024,2,512]{3,2,1,0:T(2,128)(2,1)} %bitcast.22, f32[8,128]{1,0:T(8,128)S(1)} %get-tuple-element.92.refs_1_), custom_call_target="tpu_custom_call" | custom-call | flops 1 | bytes 1 | tf_op jit(solution)/shard_map/pallas_call | solution.py:44
  8.0 2.2 %shard_map.52 = (bf16[2,4,1024,2,128]{4,3,2,1,0:T(2,128)(2,1)S(1)}, f32[8,128]{1,0:T(8,128)S(1)}) custom-call(bf16[9,1024,2,512]{3,2,1,0:T(2,128)(2,1)} %bitcast.23, f32[8,128]{1,0:T(8,128)S(1)} %get-tuple-element.93.refs_1_), custom_call_target="tpu_custom_call" | custom-call | flops 1 | bytes 1 | tf_op jit(solution)/shard_map/pallas_call | solution.py:44
  11.6 2.9 %collective-permute-start.6 = (bf16[512,128]{1,0:T(8,128)(2,1)S(1)}, bf16[512,128]{1,0:T(8,128)(2,1)S(1)}, u32[]{:S(2)}, u32[]{:S(2)}) collective-permute-start(bf16[512,128]{1,0:T(8,128)(2,1)S(1)} %get-tuple-element.98.refs_1_), channel_id=1, source_target_pairs={{8,0},{12,4},{0,8},{4,12},{9,1},{13,5},{1,9},{5,13},{10,2},{14,6},... | collective-permute-start | bytes 393224 | tf_op jit(solution)/shard_map/ppermute | solution.py:60
  17.8 2.2 %shard_map.54 = (bf16[2,4,1024,2,128]{4,3,2,1,0:T(2,128)(2,1)S(1)}, f32[8,128]{1,0:T(8,128)S(1)}) custom-call(bf16[9,1024,2,512]{3,2,1,0:T(2,128)(2,1)} %bitcast.24, f32[8,128]{1,0:T(8,128)S(1)} %get-tuple-element.95.refs_1_), custom_call_target="tpu_custom_call" | custom-call | flops 1 | bytes 1 | tf_op jit(solution)/shard_map/pallas_call | solution.py:44
  20.0 2.2 %shard_map.55 = (bf16[2,4,1024,2,128]{4,3,2,1,0:T(2,128)(2,1)S(1)}, f32[8,128]{1,0:T(8,128)S(1)}) custom-call(bf16[9,1024,2,512]{3,2,1,0:T(2,128)(2,1)} %bitcast.25, f32[8,128]{1,0:T(8,128)S(1)} %get-tuple-element.96.refs_1_), custom_call_target="tpu_custom_call" | custom-call | flops 1 | bytes 1 | tf_op jit(solution)/shard_map/pallas_call | solution.py:44
  22.3 2.0 %shard_map.56 = (f32[1024,128]{1,0:T(8,128)S(1)}, f32[8,128]{1,0:T(8,128)S(1)}) custom-call(bf16[3,4,2048,128]{3,2,1,0:T(8,128)(2,1)S(1)} %bitcast.13, bf16[512,128]{1,0:T(8,128)(2,1)S(1)} %get-tuple-element.98.refs_1_, bf16[512,128]{1,0:T(8,128)(2,1)S(1)} %collective-permute-done.3.refs_2_), custom_call_target="tpu_custom_call" | custom-call | flops 1 | bytes 1 | tf_op jit(solution)/shard_map/pallas_call | solution.py:44
  27.3 2.5 %shard_map.58 = (f32[1024,128]{1,0:T(8,128)S(1)}, f32[8,128]{1,0:T(8,128)S(1)}) custom-call(bf16[2,4,2048,128]{3,2,1,0:T(8,128)(2,1)S(1)} %bitcast.16, bf16[2,4,2048,128]{3,2,1,0:T(8,128)(2,1)S(1)} %bitcast.19, bf16[512,128]{1,0:T(8,128)(2,1)S(1)} %collective-permute-done.2.refs_2_, bf16[256,128]{1,0:T(8,128)(2,1)S(1)} %collective-permute-done.4.refs_3_, ...), custom_call_target="tpu_custom_call" | custom-call | flops 1 | bytes 1 | tf_op jit(solution)/shard_map/pallas_call | solution.py:44
  36.2 2.0 %collective-permute-start.12 = (f32[104,128]{1,0:T(8,128)S(1)}, f32[104,128]{1,0:T(8,128)S(1)}, u32[]{:S(2)}, u32[]{:S(2)}) collective-permute-start(f32[104,128]{1,0:T(8,128)S(1)} %add.51), channel_id=1, source_target_pairs={{8,0},{10,2},{12,4},{14,6},{0,8},{2,10},{4,12},{6,14},{9,1},{11,3}... | collective-permute-start | bytes 159752 | tf_op jit(solution)/shard_map/ppermute | solution.py:60
  38.2 2.4 %collective-permute-done.13.refs_1_ = f32[512,128]{1,0:T(8,128)S(1)} collective-permute-done((f32[512,128]{1,0:T(8,128)S(1)}, f32[512,128]{1,0:T(8,128)S(1)}, u32[]{:S(2)}, u32[]{:S(2)}) %collective-permute-start.13) | collective-permute-done | bytes 262176 | tf_op jit(solution)/shard_map/ppermute | solution.py:60
  43.6 2.2 %collective-permute-start.17 = (f32[176,128]{1,0:T(8,128)S(1)}, f32[176,128]{1,0:T(8,128)S(1)}, u32[]{:S(2)}, u32[]{:S(2)}) collective-permute-start(f32[176,128]{1,0:T(8,128)S(1)} %pad_maximum_fusion), channel_id=1, source_target_pairs={{6,0},{4,2},{2,4},{0,6},{14,8},{12,10},{10,12},{8,14},{7,1},{5,3},... | collective-permute-start | bytes 270344 | tf_op jit(solution)/shard_map/ppermute | solution.py:60
  46.4 2.0 %collective-permute-done.16 = f32[176,128]{1,0:T(8,128)S(1)} collective-permute-done((f32[176,128]{1,0:T(8,128)S(1)}, f32[176,128]{1,0:T(8,128)S(1)}, u32[]{:S(2)}, u32[]{:S(2)}) %collective-permute-start.16) | collective-permute-done | bytes 90144 | tf_op jit(solution)/shard_map/ppermute | solution.py:60
  50.9 2.7 %collective-permute-start.18 = (f32[72,128]{1,0:T(8,128)S(1)}, f32[72,128]{1,0:T(8,128)S(1)}, u32[]{:S(2)}, u32[]{:S(2)}) collective-permute-start(f32[72,128]{1,0:T(8,128)S(1)} %slice.64.refs_7_), channel_id=1, source_target_pairs={{8,0},{10,2},{12,4},{14,6},{0,8},{2,10},{4,12},{6,14},{9,1},{11,3}... | collective-permute-start | bytes 110600 | tf_op jit(solution)/shard_map/ppermute | solution.py:60
  53.6 5.6 %shard_map.63 = (f32[128,128]{1,0:T(8,128)S(1)}, f32[128,128]{1,0:T(8,128)S(1)}, f32[128,128]{1,0:T(8,128)S(1)}, f32[128,128]{1,0:T(8,128)S(1)}, f32[8,128]{1,0:T(8,128)}) custom-call(f32[104,128]{1,0:T(8,128)S(1)} %slice.65.refs_0_, f32[104,128]{1,0:T(8,128)S(1)} %collective-permute-done.19.refs_1_), custom_call_target="tpu_custom_call" | custom-call | flops 1 | bytes 1 | tf_op jit(solution)/shard_map/pallas_call | solution.py:44
  59.2 1.9 %shard_map.64 = (f32[512,128]{1,0:T(8,128)S(1)}, f32[512,128]{1,0:T(8,128)S(1)}, bf16[512,128]{1,0:T(8,128)(2,1)S(1)}, f32[128,128]{1,0:T(8,128)S(1)}, f32[128,128]{1,0:T(8,128)S(1)}, /*index=5*/f32[8,128]{1,0:T(8,128)}) custom-call(f32[128,128]{1,0:T(8,128)S(1)} %get-tuple-element.122.refs_0_.refs_2_, f32[128,128]{1,0:T(8,128)S(1)} %get-tuple-element.123.refs_1_, ...), custom_call_target="tpu_custom_call" | custom-call | flops 1 | bytes 1 | tf_op jit(solution)/shard_map/pallas_call | solution.py:44
  67.2 2.0 %shard_map.65 = (f32[1024,128]{1,0:T(8,128)S(1)}, f32[8,128]{1,0:T(8,128)S(1)}) custom-call(bf16[3,4,2048,128]{3,2,1,0:T(8,128)(2,1)S(1)} %bitcast.14, bf16[512,128]{1,0:T(8,128)(2,1)S(1)} %get-tuple-element.128.refs_1_, bf16[512,128]{1,0:T(8,128)(2,1)S(1)} %collective-permute-done.22.refs_2_), custom_call_target="tpu_custom_call" | custom-call | flops 1 | bytes 1 | tf_op jit(solution)/shard_map/pallas_call | solution.py:44
  74.1 2.5 %shard_map.67 = (f32[1024,128]{1,0:T(8,128)S(1)}, f32[8,128]{1,0:T(8,128)S(1)}) custom-call(bf16[2,4,2048,128]{3,2,1,0:T(8,128)(2,1)S(1)} %bitcast.17, bf16[2,4,2048,128]{3,2,1,0:T(8,128)(2,1)S(1)} %bitcast.20, bf16[512,128]{1,0:T(8,128)(2,1)S(1)} %collective-permute-done.21.refs_2_, bf16[256,128]{1,0:T(8,128)(2,1)S(1)} %collective-permute-done.23.refs_3_, ...), custom_call_target="tpu_custom_call" | custom-call | flops 1 | bytes 1 | tf_op jit(solution)/shard_map/pallas_call | solution.py:44
  84.2 3.0 %collective-permute-start.31 = (f32[104,128]{1,0:T(8,128)S(1)}, f32[104,128]{1,0:T(8,128)S(1)}, u32[]{:S(2)}, u32[]{:S(2)}) collective-permute-start(f32[104,128]{1,0:T(8,128)S(1)} %add.57), channel_id=1, source_target_pairs={{8,0},{10,2},{12,4},{14,6},{0,8},{2,10},{4,12},{6,14},{9,1},{11,3}... | collective-permute-start | bytes 159752 | tf_op jit(solution)/shard_map/ppermute | solution.py:60
  89.5 2.4 %collective-permute-start.35 = (f32[176,128]{1,0:T(8,128)S(1)}, f32[176,128]{1,0:T(8,128)S(1)}, u32[]{:S(2)}, u32[]{:S(2)}) collective-permute-start(f32[176,128]{1,0:T(8,128)S(1)} %pad_maximum_fusion.1), channel_id=1, source_target_pairs={{4,0},{6,2},{0,4},{2,6},{12,8},{14,10},{8,12},{10,14},{5,1},{7,3},... | collective-permute-start | bytes 270344 | tf_op jit(solution)/shard_map/ppermute | solution.py:60
  93.5 1.9 %collective-permute-done.35 = f32[176,128]{1,0:T(8,128)S(1)} collective-permute-done((f32[176,128]{1,0:T(8,128)S(1)}, f32[176,128]{1,0:T(8,128)S(1)}, u32[]{:S(2)}, u32[]{:S(2)}) %collective-permute-start.35) | collective-permute-done | bytes 90144 | tf_op jit(solution)/shard_map/ppermute | solution.py:60
  95.3 2.1 %collective-permute-done.36 = f32[176,128]{1,0:T(8,128)S(1)} collective-permute-done((f32[176,128]{1,0:T(8,128)S(1)}, f32[176,128]{1,0:T(8,128)S(1)}, u32[]{:S(2)}, u32[]{:S(2)}) %collective-permute-start.36) | collective-permute-done | bytes 90144 | tf_op jit(solution)/shard_map/ppermute | solution.py:60
  98.7 3.7 %collective-permute-start.37 = (f32[72,128]{1,0:T(8,128)S(1)}, f32[72,128]{1,0:T(8,128)S(1)}, u32[]{:S(2)}, u32[]{:S(2)}) collective-permute-start(f32[72,128]{1,0:T(8,128)S(1)} %slice.66.refs_7_), channel_id=1, source_target_pairs={{8,0},{10,2},{12,4},{14,6},{0,8},{2,10},{4,12},{6,14},{9,1},{11,3}... | collective-permute-start | bytes 110600 | tf_op jit(solution)/shard_map/ppermute | solution.py:60
  102.4 5.3 %shard_map.72 = (f32[128,128]{1,0:T(8,128)S(1)}, f32[128,128]{1,0:T(8,128)S(1)}, f32[128,128]{1,0:T(8,128)S(1)}, f32[128,128]{1,0:T(8,128)S(1)}, f32[8,128]{1,0:T(8,128)}) custom-call(f32[104,128]{1,0:T(8,128)S(1)} %slice.67.refs_0_, f32[104,128]{1,0:T(8,128)S(1)} %collective-permute-done.38.refs_1_, f32[128,128]{1,0:T(8,128)S(1)} %get-tuple-element.149.refs_2_), custom_call_target="tpu_custom_call" | custom-call | flops 1 | bytes 1 | tf_op jit(solution)/shard_map/pallas_call | solution.py:44
  107.8 2.0 %shard_map.73 = (f32[512,128]{1,0:T(8,128)S(1)}, f32[512,128]{1,0:T(8,128)S(1)}, bf16[512,128]{1,0:T(8,128)(2,1)S(1)}, f32[128,128]{1,0:T(8,128)S(1)}, f32[128,128]{1,0:T(8,128)S(1)}, /*index=5*/f32[8,128]{1,0:T(8,128)}) custom-call(f32[128,128]{1,0:T(8,128)S(1)} %get-tuple-element.151.refs_0_.refs_2_, f32[128,128]{1,0:T(8,128)S(1)} %get-tuple-element.152.refs_1_, ...), custom_call_target="tpu_custom_call" | custom-call | flops 1 | bytes 1 | tf_op jit(solution)/shard_map/pallas_call | solution.py:44
  114.8 2.0 %shard_map.74 = (f32[1024,128]{1,0:T(8,128)S(1)}, f32[8,128]{1,0:T(8,128)S(1)}) custom-call(bf16[3,4,2048,128]{3,2,1,0:T(8,128)(2,1)S(1)} %bitcast.15, bf16[512,128]{1,0:T(8,128)(2,1)S(1)} %get-tuple-element.157.refs_1_, bf16[512,128]{1,0:T(8,128)(2,1)S(1)} %collective-permute-done.41.refs_2_), custom_call_target="tpu_custom_call" | custom-call | flops 1 | bytes 1 | tf_op jit(solution)/shard_map/pallas_call | solution.py:44
  118.1 1.9 %collective-permute-done.44.refs_5_ = bf16[512,128]{1,0:T(8,128)(2,1)S(1)} collective-permute-done((bf16[512,128]{1,0:T(8,128)(2,1)S(1)}, bf16[512,128]{1,0:T(8,128)(2,1)S(1)}, u32[]{:S(2)}, u32[]{:S(2)}) %collective-permute-start.44) | collective-permute-done | bytes 131104 | tf_op jit(solution)/shard_map/ppermute | solution.py:60
  122.6 2.5 %shard_map.76 = (f32[1024,128]{1,0:T(8,128)S(1)}, f32[8,128]{1,0:T(8,128)S(1)}) custom-call(bf16[2,4,2048,128]{3,2,1,0:T(8,128)(2,1)S(1)} %bitcast.18, bf16[2,4,2048,128]{3,2,1,0:T(8,128)(2,1)S(1)} %bitcast.21, bf16[512,128]{1,0:T(8,128)(2,1)S(1)} %collective-permute-done.40.refs_2_, bf16[256,128]{1,0:T(8,128)(2,1)S(1)} %collective-permute-done.42.refs_3_, ...), custom_call_target="tpu_custom_call" | custom-call | flops 1 | bytes 1 | tf_op jit(solution)/shard_map/pallas_call | solution.py:44
  126.6 1.9 %shard_map.77 = (f32[512,128]{1,0:T(8,128)S(1)}, f32[512,128]{1,0:T(8,128)S(1)}, f32[8,128]{1,0:T(8,128)}) custom-call(bf16[2,4,2048,128]{3,2,1,0:T(8,128)(2,1)S(1)} %bitcast.12, bf16[512,128]{1,0:T(8,128)(2,1)S(1)} %collective-permute-done.39.refs_1_, bf16[512,128]{1,0:T(8,128)(2,1)S(1)} %collective-permute-done.48.refs_2_, ...), custom_call_target="tpu_custom_call" | custom-call | flops 1 | bytes 1 | tf_op jit(solution)/shard_map/pallas_call | solution.py:44
  131.2 1.7 %collective-permute-start.51 = (f32[72,128]{1,0:T(8,128)S(1)}, f32[72,128]{1,0:T(8,128)S(1)}, u32[]{:S(2)}, u32[]{:S(2)}) collective-permute-start(f32[72,128]{1,0:T(8,128)S(1)} %add.63), channel_id=1, source_target_pairs={{4,0},{6,2},{0,4},{2,6},{12,8},{14,10},{8,12},{10,14},{5,1},{7,3},... | collective-permute-start | bytes 110600 | tf_op jit(solution)/shard_map/ppermute | solution.py:60
  137.3 2.2 %collective-permute-start.53 = (f32[72,128]{1,0:T(8,128)S(1)}, f32[72,128]{1,0:T(8,128)S(1)}, u32[]{:S(2)}, u32[]{:S(2)}) collective-permute-start(f32[72,128]{1,0:T(8,128)S(1)} %add_add_fusion.2), channel_id=1, source_target_pairs={{8,0},{10,2},{12,4},{14,6},{0,8},{2,10},{4,12},{6,14},{9,1},{11,3}... | collective-permute-start | bytes 110600 | tf_op jit(solution)/shard_map/ppermute | solution.py:60
  139.5 2.8 %collective-permute-done.53 = f32[72,128]{1,0:T(8,128)S(1)} collective-permute-done((f32[72,128]{1,0:T(8,128)S(1)}, f32[72,128]{1,0:T(8,128)S(1)}, u32[]{:S(2)}, u32[]{:S(2)}) %collective-permute-start.53) | collective-permute-done | bytes 36896 | tf_op jit(solution)/shard_map/ppermute | solution.py:60
  142.3 5.2 %shard_map.79 = (f32[512,128]{1,0:T(8,128)}, f32[512,128]{1,0:T(8,128)}, f32[8,128]{1,0:T(8,128)}) custom-call(f32[72,128]{1,0:T(8,128)S(1)} %add.67.refs_0_, f32[128,128]{1,0:T(8,128)S(1)} %get-tuple-element.173.refs_1_, f32[512,128]{1,0:T(8,128)S(1)} %get-tuple-element.174.refs_2_, f32[512,128]{1,0:T(8,128)S(1)} %get-tuple-element.165.refs_2_.refs_3_, ...), custom_call_target="tpu_custom_call" | custom-call | flops 1 | bytes 1 | tf_op jit(solution)/shard_map/pallas_call | solution.py:44
  (131 shorter events, 62.9 us)
Async XLA Ops:
  2.1 9.3 %collective-permute-start = (f32[512,128]{1,0:T(8,128)S(1)}, f32[512,128]{1,0:T(8,128)S(1)}, u32[]{:S(2)}, u32[]{:S(2)}) collective-permute-start(f32[512,128]{1,0:T(8,128)S(1)} %get-tuple-element.91), channel_id=1, source_target_pairs={{2,0},{0,2},{3,1},{1,3},{6,4},{4,6},{7,5},{5,7},{10,8},{8,10},{11,... | collective-permute-start | bytes 786440 | tf_op jit(solution)/shard_map/ppermute | solution.py:60
  11.5 10.7 %collective-permute-start.3 = (bf16[512,128]{1,0:T(8,128)(2,1)S(1)}, bf16[512,128]{1,0:T(8,128)(2,1)S(1)}, u32[]{:S(2)}, u32[]{:S(2)}) collective-permute-start(bf16[512,128]{1,0:T(8,128)(2,1)S(1)} %get-tuple-element.98.refs_1_), channel_id=1, source_target_pairs={{1,0},{0,1},{3,2},{2,3},{5,4},{4,5},{7,6},{6,7},{9,8},{8,9},{11,10... | collective-permute-start | bytes 393224 | tf_op jit(solution)/shard_map/ppermute | solution.py:60
  11.6 13.1 %collective-permute-start.6 = (bf16[512,128]{1,0:T(8,128)(2,1)S(1)}, bf16[512,128]{1,0:T(8,128)(2,1)S(1)}, u32[]{:S(2)}, u32[]{:S(2)}) collective-permute-start(bf16[512,128]{1,0:T(8,128)(2,1)S(1)} %get-tuple-element.98.refs_1_), channel_id=1, source_target_pairs={{8,0},{12,4},{0,8},{4,12},{9,1},{13,5},{1,9},{5,13},{10,2},{14,6},... | collective-permute-start | bytes 393224 | tf_op jit(solution)/shard_map/ppermute | solution.py:60
  14.5 10.3 %collective-permute-start.2 = (bf16[512,128]{1,0:T(8,128)(2,1)S(1)}, bf16[512,128]{1,0:T(8,128)(2,1)S(1)}, u32[]{:S(2)}, u32[]{:S(2)}) collective-permute-start(bf16[512,128]{1,0:T(8,128)(2,1)S(1)} %get-tuple-element.98.refs_1_), channel_id=1, source_target_pairs={{4,0},{0,4},{12,8},{8,12},{5,1},{1,5},{13,9},{9,13},{6,2},{2,6},{1... | collective-permute-start | bytes 393224 | tf_op jit(solution)/shard_map/ppermute | solution.py:60
  16.1 13.8 %collective-permute-start.1 = (bf16[512,128]{1,0:T(8,128)(2,1)S(1)}, bf16[512,128]{1,0:T(8,128)(2,1)S(1)}, u32[]{:S(2)}, u32[]{:S(2)}) collective-permute-start(bf16[512,128]{1,0:T(8,128)(2,1)S(1)} %get-tuple-element.98.refs_1_), channel_id=1, source_target_pairs={{12,0},{8,4},{4,8},{0,12},{13,1},{9,5},{5,9},{1,13},{14,2},{10,6},... | collective-permute-start | bytes 393224 | tf_op jit(solution)/shard_map/ppermute | solution.py:60
  16.1 11.3 %collective-permute-start.9 = (f32[512,128]{1,0:T(8,128)S(1)}, f32[512,128]{1,0:T(8,128)S(1)}, u32[]{:S(2)}, u32[]{:S(2)}) collective-permute-start(f32[512,128]{1,0:T(8,128)S(1)} %get-tuple-element.103.refs_0_.refs_2_.refs_4_.refs_5_), channel_id=1, source_target_pairs={{2,0},{0,2},{3,1},{1,3},{6,4},{4,6},{7,5},{5,7},{10,8},{8,10},{11,... | collective-permute-start | bytes 786440 | tf_op jit(solution)/shard_map/ppermute | solution.py:60
  32.1 8.4 %collective-permute-start.13 = (f32[512,128]{1,0:T(8,128)S(1)}, f32[512,128]{1,0:T(8,128)S(1)}, u32[]{:S(2)}, u32[]{:S(2)}) collective-permute-start(f32[512,128]{1,0:T(8,128)S(1)} %get-tuple-element.115.refs_1_), channel_id=1, source_target_pairs={{2,0},{0,2},{3,1},{1,3},{6,4},{4,6},{7,5},{5,7},{10,8},{8,10},{11,... | collective-permute-start | bytes 786440 | tf_op jit(solution)/shard_map/ppermute | solution.py:60
  36.2 6.2 %collective-permute-start.12 = (f32[104,128]{1,0:T(8,128)S(1)}, f32[104,128]{1,0:T(8,128)S(1)}, u32[]{:S(2)}, u32[]{:S(2)}) collective-permute-start(f32[104,128]{1,0:T(8,128)S(1)} %add.51), channel_id=1, source_target_pairs={{8,0},{10,2},{12,4},{14,6},{0,8},{2,10},{4,12},{6,14},{9,1},{11,3}... | collective-permute-start | bytes 159752 | tf_op jit(solution)/shard_map/ppermute | solution.py:60
  42.8 5.5 %collective-permute-start.16 = (f32[176,128]{1,0:T(8,128)S(1)}, f32[176,128]{1,0:T(8,128)S(1)}, u32[]{:S(2)}, u32[]{:S(2)}) collective-permute-start(f32[176,128]{1,0:T(8,128)S(1)} %pad_maximum_fusion), channel_id=1, source_target_pairs={{4,0},{6,2},{0,4},{2,6},{12,8},{14,10},{8,12},{10,14},{5,1},{7,3},... | collective-permute-start | bytes 270344 | tf_op jit(solution)/shard_map/ppermute | solution.py:60
  43.6 6.3 %collective-permute-start.17 = (f32[176,128]{1,0:T(8,128)S(1)}, f32[176,128]{1,0:T(8,128)S(1)}, u32[]{:S(2)}, u32[]{:S(2)}) collective-permute-start(f32[176,128]{1,0:T(8,128)S(1)} %pad_maximum_fusion), channel_id=1, source_target_pairs={{6,0},{4,2},{2,4},{0,6},{14,8},{12,10},{10,12},{8,14},{7,1},{5,3},... | collective-permute-start | bytes 270344 | tf_op jit(solution)/shard_map/ppermute | solution.py:60
  45.7 5.0 %collective-permute-start.15 = (f32[176,128]{1,0:T(8,128)S(1)}, f32[176,128]{1,0:T(8,128)S(1)}, u32[]{:S(2)}, u32[]{:S(2)}) collective-permute-start(f32[176,128]{1,0:T(8,128)S(1)} %pad_maximum_fusion), channel_id=1, source_target_pairs={{2,0},{0,2},{6,4},{4,6},{10,8},{8,10},{14,12},{12,14},{3,1},{1,3},... | collective-permute-start | bytes 270344 | tf_op jit(solution)/shard_map/ppermute | solution.py:60
  50.9 8.3 %collective-permute-start.18 = (f32[72,128]{1,0:T(8,128)S(1)}, f32[72,128]{1,0:T(8,128)S(1)}, u32[]{:S(2)}, u32[]{:S(2)}) collective-permute-start(f32[72,128]{1,0:T(8,128)S(1)} %slice.64.refs_7_), channel_id=1, source_target_pairs={{8,0},{10,2},{12,4},{14,6},{0,8},{2,10},{4,12},{6,14},{9,1},{11,3}... | collective-permute-start | bytes 110600 | tf_op jit(solution)/shard_map/ppermute | solution.py:60
  61.2 6.0 %collective-permute-start.22 = (bf16[512,128]{1,0:T(8,128)(2,1)S(1)}, bf16[512,128]{1,0:T(8,128)(2,1)S(1)}, u32[]{:S(2)}, u32[]{:S(2)}) collective-permute-start(bf16[512,128]{1,0:T(8,128)(2,1)S(1)} %get-tuple-element.128.refs_1_), channel_id=1, source_target_pairs={{1,0},{0,1},{3,2},{2,3},{5,4},{4,5},{7,6},{6,7},{9,8},{8,9},{11,10... | collective-permute-start | bytes 393224 | tf_op jit(solution)/shard_map/ppermute | solution.py:60
  61.3 10.2 %collective-permute-start.25 = (bf16[512,128]{1,0:T(8,128)(2,1)S(1)}, bf16[512,128]{1,0:T(8,128)(2,1)S(1)}, u32[]{:S(2)}, u32[]{:S(2)}) collective-permute-start(bf16[512,128]{1,0:T(8,128)(2,1)S(1)} %get-tuple-element.128.refs_1_), channel_id=1, source_target_pairs={{8,0},{12,4},{0,8},{4,12},{9,1},{13,5},{1,9},{5,13},{10,2},{14,6},... | collective-permute-start | bytes 393224 | tf_op jit(solution)/shard_map/ppermute | solution.py:60
  62.5 9.0 %collective-permute-start.21 = (bf16[512,128]{1,0:T(8,128)(2,1)S(1)}, bf16[512,128]{1,0:T(8,128)(2,1)S(1)}, u32[]{:S(2)}, u32[]{:S(2)}) collective-permute-start(bf16[512,128]{1,0:T(8,128)(2,1)S(1)} %get-tuple-element.128.refs_1_), channel_id=1, source_target_pairs={{4,0},{0,4},{12,8},{8,12},{5,1},{1,5},{13,9},{9,13},{6,2},{2,6},{1... | collective-permute-start | bytes 393224 | tf_op jit(solution)/shard_map/ppermute | solution.py:60
  64.0 12.6 %collective-permute-start.20 = (bf16[512,128]{1,0:T(8,128)(2,1)S(1)}, bf16[512,128]{1,0:T(8,128)(2,1)S(1)}, u32[]{:S(2)}, u32[]{:S(2)}) collective-permute-start(bf16[512,128]{1,0:T(8,128)(2,1)S(1)} %get-tuple-element.128.refs_1_), channel_id=1, source_target_pairs={{12,0},{8,4},{4,8},{0,12},{13,1},{9,5},{5,9},{1,13},{14,2},{10,6},... | collective-permute-start | bytes 393224 | tf_op jit(solution)/shard_map/ppermute | solution.py:60
  65.7 8.4 %collective-permute-start.28 = (f32[512,128]{1,0:T(8,128)S(1)}, f32[512,128]{1,0:T(8,128)S(1)}, u32[]{:S(2)}, u32[]{:S(2)}) collective-permute-start(f32[512,128]{1,0:T(8,128)S(1)} %get-tuple-element.135.refs_2_.refs_5_.refs_0_), channel_id=1, source_target_pairs={{2,0},{0,2},{3,1},{1,3},{6,4},{4,6},{7,5},{5,7},{10,8},{8,10},{11,... | collective-permute-start | bytes 786440 | tf_op jit(solution)/shard_map/ppermute | solution.py:60
  78.9 8.4 %collective-permute-start.32 = (f32[512,128]{1,0:T(8,128)S(1)}, f32[512,128]{1,0:T(8,128)S(1)}, u32[]{:S(2)}, u32[]{:S(2)}) collective-permute-start(f32[512,128]{1,0:T(8,128)S(1)} %get-tuple-element.142.refs_1_), channel_id=1, source_target_pairs={{2,0},{0,2},{3,1},{1,3},{6,4},{4,6},{7,5},{5,7},{10,8},{8,10},{11,... | collective-permute-start | bytes 786440 | tf_op jit(solution)/shard_map/ppermute | solution.py:60
  84.2 5.1 %collective-permute-start.31 = (f32[104,128]{1,0:T(8,128)S(1)}, f32[104,128]{1,0:T(8,128)S(1)}, u32[]{:S(2)}, u32[]{:S(2)}) collective-permute-start(f32[104,128]{1,0:T(8,128)S(1)} %add.57), channel_id=1, source_target_pairs={{8,0},{10,2},{12,4},{14,6},{0,8},{2,10},{4,12},{6,14},{9,1},{11,3}... | collective-permute-start | bytes 159752 | tf_op jit(solution)/shard_map/ppermute | solution.py:60
  89.5 5.8 %collective-permute-start.35 = (f32[176,128]{1,0:T(8,128)S(1)}, f32[176,128]{1,0:T(8,128)S(1)}, u32[]{:S(2)}, u32[]{:S(2)}) collective-permute-start(f32[176,128]{1,0:T(8,128)S(1)} %pad_maximum_fusion.1), channel_id=1, source_target_pairs={{4,0},{6,2},{0,4},{2,6},{12,8},{14,10},{8,12},{10,14},{5,1},{7,3},... | collective-permute-start | bytes 270344 | tf_op jit(solution)/shard_map/ppermute | solution.py:60
  91.9 5.5 %collective-permute-start.36 = (f32[176,128]{1,0:T(8,128)S(1)}, f32[176,128]{1,0:T(8,128)S(1)}, u32[]{:S(2)}, u32[]{:S(2)}) collective-permute-start(f32[176,128]{1,0:T(8,128)S(1)} %pad_maximum_fusion.1), channel_id=1, source_target_pairs={{6,0},{4,2},{2,4},{0,6},{14,8},{12,10},{10,12},{8,14},{7,1},{5,3},... | collective-permute-start | bytes 270344 | tf_op jit(solution)/shard_map/ppermute | solution.py:60
  92.5 6.1 %collective-permute-start.34 = (f32[176,128]{1,0:T(8,128)S(1)}, f32[176,128]{1,0:T(8,128)S(1)}, u32[]{:S(2)}, u32[]{:S(2)}) collective-permute-start(f32[176,128]{1,0:T(8,128)S(1)} %pad_maximum_fusion.1), channel_id=1, source_target_pairs={{2,0},{0,2},{6,4},{4,6},{10,8},{8,10},{14,12},{12,14},{3,1},{1,3},... | collective-permute-start | bytes 270344 | tf_op jit(solution)/shard_map/ppermute | solution.py:60
  98.7 9.0 %collective-permute-start.37 = (f32[72,128]{1,0:T(8,128)S(1)}, f32[72,128]{1,0:T(8,128)S(1)}, u32[]{:S(2)}, u32[]{:S(2)}) collective-permute-start(f32[72,128]{1,0:T(8,128)S(1)} %slice.66.refs_7_), channel_id=1, source_target_pairs={{8,0},{10,2},{12,4},{14,6},{0,8},{2,10},{4,12},{6,14},{9,1},{11,3}... | collective-permute-start | bytes 110600 | tf_op jit(solution)/shard_map/ppermute | solution.py:60
  109.7 5.1 %collective-permute-start.41 = (bf16[512,128]{1,0:T(8,128)(2,1)S(1)}, bf16[512,128]{1,0:T(8,128)(2,1)S(1)}, u32[]{:S(2)}, u32[]{:S(2)}) collective-permute-start(bf16[512,128]{1,0:T(8,128)(2,1)S(1)} %get-tuple-element.157.refs_1_), channel_id=1, source_target_pairs={{1,0},{0,1},{3,2},{2,3},{5,4},{4,5},{7,6},{6,7},{9,8},{8,9},{11,10... | collective-permute-start | bytes 393224 | tf_op jit(solution)/shard_map/ppermute | solution.py:60
  109.9 10.1 %collective-permute-start.44 = (bf16[512,128]{1,0:T(8,128)(2,1)S(1)}, bf16[512,128]{1,0:T(8,128)(2,1)S(1)}, u32[]{:S(2)}, u32[]{:S(2)}) collective-permute-start(bf16[512,128]{1,0:T(8,128)(2,1)S(1)} %get-tuple-element.157.refs_1_), channel_id=1, source_target_pairs={{8,0},{12,4},{0,8},{4,12},{9,1},{13,5},{1,9},{5,13},{10,2},{14,6},... | collective-permute-start | bytes 393224 | tf_op jit(solution)/shard_map/ppermute | solution.py:60
  111.0 9.6 %collective-permute-start.40 = (bf16[512,128]{1,0:T(8,128)(2,1)S(1)}, bf16[512,128]{1,0:T(8,128)(2,1)S(1)}, u32[]{:S(2)}, u32[]{:S(2)}) collective-permute-start(bf16[512,128]{1,0:T(8,128)(2,1)S(1)} %get-tuple-element.157.refs_1_), channel_id=1, source_target_pairs={{4,0},{0,4},{12,8},{8,12},{5,1},{1,5},{13,9},{9,13},{6,2},{2,6},{1... | collective-permute-start | bytes 393224 | tf_op jit(solution)/shard_map/ppermute | solution.py:60
  112.6 12.6 %collective-permute-start.39 = (bf16[512,128]{1,0:T(8,128)(2,1)S(1)}, bf16[512,128]{1,0:T(8,128)(2,1)S(1)}, u32[]{:S(2)}, u32[]{:S(2)}) collective-permute-start(bf16[512,128]{1,0:T(8,128)(2,1)S(1)} %get-tuple-element.157.refs_1_), channel_id=1, source_target_pairs={{12,0},{8,4},{4,8},{0,12},{13,1},{9,5},{5,9},{1,13},{14,2},{10,6},... | collective-permute-start | bytes 393224 | tf_op jit(solution)/shard_map/ppermute | solution.py:60
  114.3 8.4 %collective-permute-start.47 = (f32[512,128]{1,0:T(8,128)S(1)}, f32[512,128]{1,0:T(8,128)S(1)}, u32[]{:S(2)}, u32[]{:S(2)}) collective-permute-start(f32[512,128]{1,0:T(8,128)S(1)} %get-tuple-element.165.refs_2_.refs_3_), channel_id=1, source_target_pairs={{2,0},{0,2},{3,1},{1,3},{6,4},{4,6},{7,5},{5,7},{10,8},{8,10},{11,... | collective-permute-start | bytes 786440 | tf_op jit(solution)/shard_map/ppermute | solution.py:60
  130.9 5.0 %collective-permute-start.52 = (f32[72,128]{1,0:T(8,128)S(1)}, f32[72,128]{1,0:T(8,128)S(1)}, u32[]{:S(2)}, u32[]{:S(2)}) collective-permute-start(f32[72,128]{1,0:T(8,128)S(1)} %add.63), channel_id=1, source_target_pairs={{6,0},{4,2},{2,4},{0,6},{14,8},{12,10},{10,12},{8,14},{7,1},{5,3},... | collective-permute-start | bytes 110600 | tf_op jit(solution)/shard_map/ppermute | solution.py:60
  131.2 4.7 %collective-permute-start.51 = (f32[72,128]{1,0:T(8,128)S(1)}, f32[72,128]{1,0:T(8,128)S(1)}, u32[]{:S(2)}, u32[]{:S(2)}) collective-permute-start(f32[72,128]{1,0:T(8,128)S(1)} %add.63), channel_id=1, source_target_pairs={{4,0},{6,2},{0,4},{2,6},{12,8},{14,10},{8,12},{10,14},{5,1},{7,3},... | collective-permute-start | bytes 110600 | tf_op jit(solution)/shard_map/ppermute | solution.py:60
  134.4 7.9 %collective-permute-start.54 = (f32[512,128]{1,0:T(8,128)S(1)}, f32[512,128]{1,0:T(8,128)S(1)}, u32[]{:S(2)}, u32[]{:S(2)}) collective-permute-start(f32[512,128]{1,0:T(8,128)S(1)} %get-tuple-element.171.refs_1_), channel_id=1, source_target_pairs={{2,0},{0,2},{3,1},{1,3},{6,4},{4,6},{7,5},{5,7},{10,8},{8,10},{11,... | collective-permute-start | bytes 786440 | tf_op jit(solution)/shard_map/ppermute | solution.py:60
  137.3 4.9 %collective-permute-start.53 = (f32[72,128]{1,0:T(8,128)S(1)}, f32[72,128]{1,0:T(8,128)S(1)}, u32[]{:S(2)}, u32[]{:S(2)}) collective-permute-start(f32[72,128]{1,0:T(8,128)S(1)} %add_add_fusion.2), channel_id=1, source_target_pairs={{8,0},{10,2},{12,4},{14,6},{0,8},{2,10},{4,12},{6,14},{9,1},{11,3}... | collective-permute-start | bytes 110600 | tf_op jit(solution)/shard_map/ppermute | solution.py:60
  (23 other events, 37.2 us)

commit v10 on v9

--- a/solution.py
+++ b/solution.py
@@ -304,19 +304,22 @@
     (acc,), token = link_products(packed[:1], pairs, None, n, None)
     after = (token, between(token))
     held = (*after, *directions[1:])
-    for piece in arrived[1:-1]:
-        piece, _ = lax.optimization_barrier((piece, after))
+    for place, piece in enumerate(arrived[1:], start=1):
+        if final and place == len(groups) - 1:
+            (acc,), token = link_products(packed[1:-1], pairs[1:], acc, n, None, held)
+            piece, held = lax.optimization_barrier((piece, (token,)))
+        else:
+            piece, _ = lax.optimization_barrier((piece, after))
         rows = piece.shape[0] // PARTS
-        cut = [piece[i * rows : (i + 1) * rows] for i in range(PARTS)]
+        cut = [piece]
+        if final and place < len(groups) - 1:
+            cut = [piece[i * rows : (i + 1) * rows] for i in range(PARTS)]
         pairs.append([piece, *(swapped(part, "coef", 1, 2) for part in cut)])
-    if len(groups) > 2:
-        (acc,), token = link_products(packed[1:-1], pairs[1:], acc, n, None, held)
-        held = (token,)
-    piece, held = lax.optimization_barrier((arrived[-1], held))
-    pairs.append([piece, swapped(piece, "coef", 1, 2)])
     if final:
         parts, _ = link_products(packed[-1:], pairs[-1:], acc, n, range(n), held)
         return parts, directions
+    if len(groups) > 2:
+        (acc,), _ = link_products(packed[1:-1], pairs[1:-1], acc, n, None, held)
     mates, token = link_products(packed[-1:], pairs[-1:], acc, n, range(1, n), held)
     own, _ = link_products(packed[-1:], pairs[-1:], acc, n, [0], (token,))
     return own + mates, directions

time: 148 us -> 145 us (0.980)
  waiting for transfers between devices: 36.7 us -> 32.9 us
    ppermute x55 -> x51, waiting for transfers between devices: 36.7 us -> 32.9 us  [permute(): return lax.ppermute(value, axis, pairs)]
    ppermute x55 -> x51, starting transfers between devices: 50.9 us -> 51.5 us  [permute(): return lax.ppermute(value, axis, pairs)]
  transfers between devices with their start and end apart: 55 -> 51, of which waited for: 34 -> 26; matrix products, arithmetic and copies ran while one was open for 0% -> 0% of each run, Pallas kernels for 29% -> 31%
where the time goes in v10:
time: 145 us
  Pallas kernels  59.4 us (41%)
  starting transfers between devices  51.5 us (36%)
  waiting for transfers between devices  32.9 us (23%)
    pallas_call x30, Pallas kernels, call(): pl.pallas_call(ordered, out_shape=list(outs) + [shape(SUB)], in_specs=[HB...  59.4 us
    ppermute x51, starting transfers between devices, permute(): return lax.ppermute(value, axis, pairs)  51.5 us
    ppermute x51, waiting for transfers between devices, permute(): return lax.ppermute(value, axis, pairs)  32.9 us
  transfers between devices with their start and end apart: 51, of which 26 were waited for; matrix products, arithmetic and copies ran while one was open for 0% of the time, Pallas kernels for 31%

profile of v10, /device:TPU:0, one launch (start us, length us, event | category | flops | bytes accessed | tf_op | source)
XLA Modules:
  0.0 145.0 jit_solution(1353418139726976622)
XLA Ops:
  2.1 3.0 %collective-permute-start = (f32[512,128]{1,0:T(8,128)S(1)}, f32[512,128]{1,0:T(8,128)S(1)}, u32[]{:S(2)}, u32[]{:S(2)}) collective-permute-start(f32[512,128]{1,0:T(8,128)S(1)} %get-tuple-element.87), channel_id=1, source_target_pairs={{2,0},{0,2},{3,1},{1,3},{6,4},{4,6},{7,5},{5,7},{10,8},{8,10},{11,... | collective-permute-start | bytes 786440 | tf_op jit(solution)/shard_map/ppermute | solution.py:60
  5.1 2.9 %shard_map.51 = (bf16[3,4,1024,2,128]{4,3,2,1,0:T(2,128)(2,1)S(1)}, f32[8,128]{1,0:T(8,128)S(1)}) custom-call(bf16[9,1024,2,512]{3,2,1,0:T(2,128)(2,1)} %bitcast.22, f32[8,128]{1,0:T(8,128)S(1)} %get-tuple-element.88.refs_1_), custom_call_target="tpu_custom_call" | custom-call | flops 1 | bytes 1 | tf_op jit(solution)/shard_map/pallas_call | solution.py:44
  8.0 2.2 %shard_map.52 = (bf16[2,4,1024,2,128]{4,3,2,1,0:T(2,128)(2,1)S(1)}, f32[8,128]{1,0:T(8,128)S(1)}) custom-call(bf16[9,1024,2,512]{3,2,1,0:T(2,128)(2,1)} %bitcast.23, f32[8,128]{1,0:T(8,128)S(1)} %get-tuple-element.89.refs_1_), custom_call_target="tpu_custom_call" | custom-call | flops 1 | bytes 1 | tf_op jit(solution)/shard_map/pallas_call | solution.py:44
  11.6 2.9 %collective-permute-start.6 = (bf16[512,128]{1,0:T(8,128)(2,1)S(1)}, bf16[512,128]{1,0:T(8,128)(2,1)S(1)}, u32[]{:S(2)}, u32[]{:S(2)}) collective-permute-start(bf16[512,128]{1,0:T(8,128)(2,1)S(1)} %get-tuple-element.94.refs_1_), channel_id=1, source_target_pairs={{8,0},{12,4},{0,8},{4,12},{9,1},{13,5},{1,9},{5,13},{10,2},{14,6},... | collective-permute-start | bytes 393224 | tf_op jit(solution)/shard_map/ppermute | solution.py:60
  17.8 2.2 %shard_map.54 = (bf16[2,4,1024,2,128]{4,3,2,1,0:T(2,128)(2,1)S(1)}, f32[8,128]{1,0:T(8,128)S(1)}) custom-call(bf16[9,1024,2,512]{3,2,1,0:T(2,128)(2,1)} %bitcast.24, f32[8,128]{1,0:T(8,128)S(1)} %get-tuple-element.91.refs_1_), custom_call_target="tpu_custom_call" | custom-call | flops 1 | bytes 1 | tf_op jit(solution)/shard_map/pallas_call | solution.py:44
  20.0 2.2 %shard_map.55 = (bf16[2,4,1024,2,128]{4,3,2,1,0:T(2,128)(2,1)S(1)}, f32[8,128]{1,0:T(8,128)S(1)}) custom-call(bf16[9,1024,2,512]{3,2,1,0:T(2,128)(2,1)} %bitcast.25, f32[8,128]{1,0:T(8,128)S(1)} %get-tuple-element.92.refs_1_), custom_call_target="tpu_custom_call" | custom-call | flops 1 | bytes 1 | tf_op jit(solution)/shard_map/pallas_call | solution.py:44
  22.2 2.0 %shard_map.56 = (f32[1024,128]{1,0:T(8,128)S(1)}, f32[8,128]{1,0:T(8,128)S(1)}) custom-call(bf16[3,4,2048,128]{3,2,1,0:T(8,128)(2,1)S(1)} %bitcast.13, bf16[512,128]{1,0:T(8,128)(2,1)S(1)} %get-tuple-element.94.refs_1_, bf16[512,128]{1,0:T(8,128)(2,1)S(1)} %collective-permute-done.2.refs_2_), custom_call_target="tpu_custom_call" | custom-call | flops 1 | bytes 1 | tf_op jit(solution)/shard_map/pallas_call | solution.py:44
  26.3 3.0 %shard_map.58 = (f32[1024,128]{1,0:T(8,128)S(1)}, f32[8,128]{1,0:T(8,128)}) custom-call(bf16[2,4,2048,128]{3,2,1,0:T(8,128)(2,1)S(1)} %bitcast.16, bf16[2,4,2048,128]{3,2,1,0:T(8,128)(2,1)S(1)} %bitcast.19, bf16[512,128]{1,0:T(8,128)(2,1)S(1)} %collective-permute-done.4.refs_2_, bf16[512,128]{1,0:T(8,128)(2,1)S(1)} %collective-permute-done.5.refs_3_, ...), custom_call_target="tpu_custom_call" | custom-call | flops 1 | bytes 1 | tf_op jit(solution)/shard_map/pallas_call | solution.py:44
  34.6 4.4 %collective-permute-start.10 = (f32[104,128]{1,0:T(8,128)S(1)}, f32[104,128]{1,0:T(8,128)S(1)}, u32[]{:S(2)}, u32[]{:S(2)}) collective-permute-start(f32[104,128]{1,0:T(8,128)S(1)} %add.51), channel_id=1, source_target_pairs={{8,0},{10,2},{12,4},{14,6},{0,8},{2,10},{4,12},{6,14},{9,1},{11,3}... | collective-permute-start | bytes 159752 | tf_op jit(solution)/shard_map/ppermute | solution.py:60
  39.9 2.3 %collective-permute-done.10 = f32[104,128]{1,0:T(8,128)S(1)} collective-permute-done((f32[104,128]{1,0:T(8,128)S(1)}, f32[104,128]{1,0:T(8,128)S(1)}, u32[]{:S(2)}, u32[]{:S(2)}) %collective-permute-start.10) | collective-permute-done | bytes 53280 | tf_op jit(solution)/shard_map/ppermute | solution.py:60
  48.3 1.9 %collective-permute-done.15 = f32[176,128]{1,0:T(8,128)S(1)} collective-permute-done((f32[176,128]{1,0:T(8,128)S(1)}, f32[176,128]{1,0:T(8,128)S(1)}, u32[]{:S(2)}, u32[]{:S(2)}) %collective-permute-start.15) | collective-permute-done | bytes 90144 | tf_op jit(solution)/shard_map/ppermute | solution.py:60
  50.3 2.3 %collective-permute-start.16 = (f32[72,128]{1,0:T(8,128)S(1)}, f32[72,128]{1,0:T(8,128)S(1)}, u32[]{:S(2)}, u32[]{:S(2)}) collective-permute-start(f32[72,128]{1,0:T(8,128)S(1)} %slice.32.refs_7_), channel_id=1, source_target_pairs={{8,0},{10,2},{12,4},{14,6},{0,8},{2,10},{4,12},{6,14},{9,1},{11,3}... | collective-permute-start | bytes 110600 | tf_op jit(solution)/shard_map/ppermute | solution.py:60
  52.6 5.6 %shard_map.63 = (f32[128,128]{1,0:T(8,128)S(1)}, f32[128,128]{1,0:T(8,128)S(1)}, f32[128,128]{1,0:T(8,128)S(1)}, f32[128,128]{1,0:T(8,128)S(1)}, f32[8,128]{1,0:T(8,128)}) custom-call(f32[104,128]{1,0:T(8,128)S(1)} %slice.33.refs_0_, f32[104,128]{1,0:T(8,128)S(1)} %collective-permute-done.17.refs_1_), custom_call_target="tpu_custom_call" | custom-call | flops 1 | bytes 1 | tf_op jit(solution)/shard_map/pallas_call | solution.py:44
  58.2 1.9 %shard_map.64 = (f32[512,128]{1,0:T(8,128)S(1)}, f32[512,128]{1,0:T(8,128)S(1)}, bf16[512,128]{1,0:T(8,128)(2,1)S(1)}, f32[128,128]{1,0:T(8,128)S(1)}, f32[128,128]{1,0:T(8,128)S(1)}, /*index=5*/f32[8,128]{1,0:T(8,128)}) custom-call(f32[128,128]{1,0:T(8,128)S(1)} %get-tuple-element.116.refs_0_.refs_2_, f32[128,128]{1,0:T(8,128)S(1)} %get-tuple-element.117.refs_1_, ...), custom_call_target="tpu_custom_call" | custom-call | flops 1 | bytes 1 | tf_op jit(solution)/shard_map/pallas_call | solution.py:44
  62.6 2.1 %collective-permute-start.18 = (bf16[512,128]{1,0:T(8,128)(2,1)S(1)}, bf16[512,128]{1,0:T(8,128)(2,1)S(1)}, u32[]{:S(2)}, u32[]{:S(2)}) collective-permute-start(bf16[512,128]{1,0:T(8,128)(2,1)S(1)} %get-tuple-element.122.refs_1_), channel_id=1, source_target_pairs={{12,0},{8,4},{4,8},{0,12},{13,1},{9,5},{5,9},{1,13},{14,2},{10,6},... | collective-permute-start | bytes 393224 | tf_op jit(solution)/shard_map/ppermute | solution.py:60
  66.2 2.0 %shard_map.65 = (f32[1024,128]{1,0:T(8,128)S(1)}, f32[8,128]{1,0:T(8,128)S(1)}) custom-call(bf16[3,4,2048,128]{3,2,1,0:T(8,128)(2,1)S(1)} %bitcast.14, bf16[512,128]{1,0:T(8,128)(2,1)S(1)} %get-tuple-element.122.refs_1_, bf16[512,128]{1,0:T(8,128)(2,1)S(1)} %collective-permute-done.19.refs_2_), custom_call_target="tpu_custom_call" | custom-call | flops 1 | bytes 1 | tf_op jit(solution)/shard_map/pallas_call | solution.py:44
  68.8 2.0 %collective-permute-done.23.refs_4_ = bf16[512,128]{1,0:T(8,128)(2,1)S(1)} collective-permute-done((bf16[512,128]{1,0:T(8,128)(2,1)S(1)}, bf16[512,128]{1,0:T(8,128)(2,1)S(1)}, u32[]{:S(2)}, u32[]{:S(2)}) %collective-permute-start.23) | collective-permute-done | bytes 131104 | tf_op jit(solution)/shard_map/ppermute | solution.py:60
  71.3 2.0 %collective-permute-done.18.refs_1_ = bf16[512,128]{1,0:T(8,128)(2,1)S(1)} collective-permute-done((bf16[512,128]{1,0:T(8,128)(2,1)S(1)}, bf16[512,128]{1,0:T(8,128)(2,1)S(1)}, u32[]{:S(2)}, u32[]{:S(2)}) %collective-permute-start.18) | collective-permute-done | bytes 131104 | tf_op jit(solution)/shard_map/ppermute | solution.py:60
  73.3 3.0 %shard_map.67 = (f32[1024,128]{1,0:T(8,128)S(1)}, f32[8,128]{1,0:T(8,128)}) custom-call(bf16[2,4,2048,128]{3,2,1,0:T(8,128)(2,1)S(1)} %bitcast.17, bf16[2,4,2048,128]{3,2,1,0:T(8,128)(2,1)S(1)} %bitcast.20, bf16[512,128]{1,0:T(8,128)(2,1)S(1)} %collective-permute-done.21.refs_2_, bf16[512,128]{1,0:T(8,128)(2,1)S(1)} %collective-permute-done.22.refs_3_, ...), custom_call_target="tpu_custom_call" | custom-call | flops 1 | bytes 1 | tf_op jit(solution)/shard_map/pallas_call | solution.py:44
  81.8 3.0 %collective-permute-start.27 = (f32[104,128]{1,0:T(8,128)S(1)}, f32[104,128]{1,0:T(8,128)S(1)}, u32[]{:S(2)}, u32[]{:S(2)}) collective-permute-start(f32[104,128]{1,0:T(8,128)S(1)} %add.57), channel_id=1, source_target_pairs={{8,0},{10,2},{12,4},{14,6},{0,8},{2,10},{4,12},{6,14},{9,1},{11,3}... | collective-permute-start | bytes 159752 | tf_op jit(solution)/shard_map/ppermute | solution.py:60
  89.0 3.3 %collective-permute-start.31 = (f32[176,128]{1,0:T(8,128)S(1)}, f32[176,128]{1,0:T(8,128)S(1)}, u32[]{:S(2)}, u32[]{:S(2)}) collective-permute-start(f32[176,128]{1,0:T(8,128)S(1)} %pad_maximum_fusion.1), channel_id=1, source_target_pairs={{4,0},{6,2},{0,4},{2,6},{12,8},{14,10},{8,12},{10,14},{5,1},{7,3},... | collective-permute-start | bytes 270344 | tf_op jit(solution)/shard_map/ppermute | solution.py:60
  92.9 2.5 %collective-permute-done.31 = f32[176,128]{1,0:T(8,128)S(1)} collective-permute-done((f32[176,128]{1,0:T(8,128)S(1)}, f32[176,128]{1,0:T(8,128)S(1)}, u32[]{:S(2)}, u32[]{:S(2)}) %collective-permute-start.31) | collective-permute-done | bytes 90144 | tf_op jit(solution)/shard_map/ppermute | solution.py:60
  95.4 2.3 %collective-permute-done.32 = f32[176,128]{1,0:T(8,128)S(1)} collective-permute-done((f32[176,128]{1,0:T(8,128)S(1)}, f32[176,128]{1,0:T(8,128)S(1)}, u32[]{:S(2)}, u32[]{:S(2)}) %collective-permute-start.32) | collective-permute-done | bytes 90144 | tf_op jit(solution)/shard_map/ppermute | solution.py:60
  99.2 5.3 %shard_map.72 = (f32[128,128]{1,0:T(8,128)S(1)}, f32[128,128]{1,0:T(8,128)S(1)}, f32[128,128]{1,0:T(8,128)S(1)}, f32[128,128]{1,0:T(8,128)S(1)}, f32[8,128]{1,0:T(8,128)}) custom-call(f32[104,128]{1,0:T(8,128)S(1)} %slice.35.refs_0_, f32[104,128]{1,0:T(8,128)S(1)} %collective-permute-done.34.refs_1_, f32[128,128]{1,0:T(8,128)S(1)} %get-tuple-element.141.refs_2_), custom_call_target="tpu_custom_call" | custom-call | flops 1 | bytes 1 | tf_op jit(solution)/shard_map/pallas_call | solution.py:44
  111.5 2.0 %shard_map.74 = (f32[1024,128]{1,0:T(8,128)S(1)}, f32[8,128]{1,0:T(8,128)S(1)}) custom-call(bf16[3,4,2048,128]{3,2,1,0:T(8,128)(2,1)S(1)} %bitcast.15, bf16[512,128]{1,0:T(8,128)(2,1)S(1)} %get-tuple-element.149.refs_1_, bf16[512,128]{1,0:T(8,128)(2,1)S(1)} %collective-permute-done.37.refs_2_), custom_call_target="tpu_custom_call" | custom-call | flops 1 | bytes 1 | tf_op jit(solution)/shard_map/pallas_call | solution.py:44
  114.8 2.0 %collective-permute-done.40.refs_5_ = bf16[512,128]{1,0:T(8,128)(2,1)S(1)} collective-permute-done((bf16[512,128]{1,0:T(8,128)(2,1)S(1)}, bf16[512,128]{1,0:T(8,128)(2,1)S(1)}, u32[]{:S(2)}, u32[]{:S(2)}) %collective-permute-start.40) | collective-permute-done | bytes 131104 | tf_op jit(solution)/shard_map/ppermute | solution.py:60
  119.4 2.5 %shard_map.76 = (f32[1024,128]{1,0:T(8,128)S(1)}, f32[8,128]{1,0:T(8,128)S(1)}) custom-call(bf16[2,4,2048,128]{3,2,1,0:T(8,128)(2,1)S(1)} %bitcast.18, bf16[2,4,2048,128]{3,2,1,0:T(8,128)(2,1)S(1)} %bitcast.21, bf16[512,128]{1,0:T(8,128)(2,1)S(1)} %collective-permute-done.36.refs_2_, bf16[256,128]{1,0:T(8,128)(2,1)S(1)} %collective-permute-done.38.refs_3_, ...), custom_call_target="tpu_custom_call" | custom-call | flops 1 | bytes 1 | tf_op jit(solution)/shard_map/pallas_call | solution.py:44
  123.4 1.9 %shard_map.77 = (f32[512,128]{1,0:T(8,128)S(1)}, f32[512,128]{1,0:T(8,128)S(1)}, f32[8,128]{1,0:T(8,128)}) custom-call(bf16[2,4,2048,128]{3,2,1,0:T(8,128)(2,1)S(1)} %bitcast.12, bf16[512,128]{1,0:T(8,128)(2,1)S(1)} %collective-permute-done.35.refs_1_, bf16[512,128]{1,0:T(8,128)(2,1)S(1)} %collective-permute-done.44.refs_2_, ...), custom_call_target="tpu_custom_call" | custom-call | flops 1 | bytes 1 | tf_op jit(solution)/shard_map/pallas_call | solution.py:44
  128.5 2.7 %collective-permute-start.48 = (f32[72,128]{1,0:T(8,128)S(1)}, f32[72,128]{1,0:T(8,128)S(1)}, u32[]{:S(2)}, u32[]{:S(2)}) collective-permute-start(f32[72,128]{1,0:T(8,128)S(1)} %add.63), channel_id=1, source_target_pairs={{6,0},{4,2},{2,4},{0,6},{14,8},{12,10},{10,12},{8,14},{7,1},{5,3},... | collective-permute-start | bytes 110600 | tf_op jit(solution)/shard_map/ppermute | solution.py:60
  133.6 3.9 %collective-permute-start.49 = (f32[72,128]{1,0:T(8,128)S(1)}, f32[72,128]{1,0:T(8,128)S(1)}, u32[]{:S(2)}, u32[]{:S(2)}) collective-permute-start(f32[72,128]{1,0:T(8,128)S(1)} %add_add_fusion.2), channel_id=1, source_target_pairs={{8,0},{10,2},{12,4},{14,6},{0,8},{2,10},{4,12},{6,14},{9,1},{11,3}... | collective-permute-start | bytes 110600 | tf_op jit(solution)/shard_map/ppermute | solution.py:60
  137.5 2.3 %collective-permute-done.49 = f32[72,128]{1,0:T(8,128)S(1)} collective-permute-done((f32[72,128]{1,0:T(8,128)S(1)}, f32[72,128]{1,0:T(8,128)S(1)}, u32[]{:S(2)}, u32[]{:S(2)}) %collective-permute-start.49) | collective-permute-done | bytes 36896 | tf_op jit(solution)/shard_map/ppermute | solution.py:60
  139.8 5.2 %shard_map.79 = (f32[512,128]{1,0:T(8,128)}, f32[512,128]{1,0:T(8,128)}, f32[8,128]{1,0:T(8,128)}) custom-call(f32[72,128]{1,0:T(8,128)S(1)} %add.67.refs_0_, f32[128,128]{1,0:T(8,128)S(1)} %get-tuple-element.165.refs_1_, f32[512,128]{1,0:T(8,128)S(1)} %get-tuple-element.166.refs_2_, f32[512,128]{1,0:T(8,128)S(1)} %get-tuple-element.157.refs_2_.refs_3_, ...), custom_call_target="tpu_custom_call" | custom-call | flops 1 | bytes 1 | tf_op jit(solution)/shard_map/pallas_call | solution.py:44
  (119 shorter events, 55.4 us)
Async XLA Ops:
  2.1 9.3 %collective-permute-start = (f32[512,128]{1,0:T(8,128)S(1)}, f32[512,128]{1,0:T(8,128)S(1)}, u32[]{:S(2)}, u32[]{:S(2)}) collective-permute-start(f32[512,128]{1,0:T(8,128)S(1)} %get-tuple-element.87), channel_id=1, source_target_pairs={{2,0},{0,2},{3,1},{1,3},{6,4},{4,6},{7,5},{5,7},{10,8},{8,10},{11,... | collective-permute-start | bytes 786440 | tf_op jit(solution)/shard_map/ppermute | solution.py:60
  11.5 10.7 %collective-permute-start.2 = (bf16[512,128]{1,0:T(8,128)(2,1)S(1)}, bf16[512,128]{1,0:T(8,128)(2,1)S(1)}, u32[]{:S(2)}, u32[]{:S(2)}) collective-permute-start(bf16[512,128]{1,0:T(8,128)(2,1)S(1)} %get-tuple-element.94.refs_1_), channel_id=1, source_target_pairs={{1,0},{0,1},{3,2},{2,3},{5,4},{4,5},{7,6},{6,7},{9,8},{8,9},{11,10... | collective-permute-start | bytes 393224 | tf_op jit(solution)/shard_map/ppermute | solution.py:60
  11.6 13.1 %collective-permute-start.6 = (bf16[512,128]{1,0:T(8,128)(2,1)S(1)}, bf16[512,128]{1,0:T(8,128)(2,1)S(1)}, u32[]{:S(2)}, u32[]{:S(2)}) collective-permute-start(bf16[512,128]{1,0:T(8,128)(2,1)S(1)} %get-tuple-element.94.refs_1_), channel_id=1, source_target_pairs={{8,0},{12,4},{0,8},{4,12},{9,1},{13,5},{1,9},{5,13},{10,2},{14,6},... | collective-permute-start | bytes 393224 | tf_op jit(solution)/shard_map/ppermute | solution.py:60
  14.5 10.3 %collective-permute-start.4 = (bf16[512,128]{1,0:T(8,128)(2,1)S(1)}, bf16[512,128]{1,0:T(8,128)(2,1)S(1)}, u32[]{:S(2)}, u32[]{:S(2)}) collective-permute-start(bf16[512,128]{1,0:T(8,128)(2,1)S(1)} %get-tuple-element.94.refs_1_), channel_id=1, source_target_pairs={{4,0},{0,4},{12,8},{8,12},{5,1},{1,5},{13,9},{9,13},{6,2},{2,6},{1... | collective-permute-start | bytes 393224 | tf_op jit(solution)/shard_map/ppermute | solution.py:60
  16.1 10.3 %collective-permute-start.8 = (f32[512,128]{1,0:T(8,128)S(1)}, f32[512,128]{1,0:T(8,128)S(1)}, u32[]{:S(2)}, u32[]{:S(2)}) collective-permute-start(f32[512,128]{1,0:T(8,128)S(1)} %get-tuple-element.97.refs_0_.refs_2_.refs_4_.refs_5_), channel_id=1, source_target_pairs={{2,0},{0,2},{3,1},{1,3},{6,4},{4,6},{7,5},{5,7},{10,8},{8,10},{11,... | collective-permute-start | bytes 786440 | tf_op jit(solution)/shard_map/ppermute | solution.py:60
  17.5 7.9 %collective-permute-start.1 = (bf16[512,128]{1,0:T(8,128)(2,1)S(1)}, bf16[512,128]{1,0:T(8,128)(2,1)S(1)}, u32[]{:S(2)}, u32[]{:S(2)}) collective-permute-start(bf16[512,128]{1,0:T(8,128)(2,1)S(1)} %get-tuple-element.94.refs_1_), channel_id=1, source_target_pairs={{12,0},{8,4},{4,8},{0,12},{13,1},{9,5},{5,9},{1,13},{14,2},{10,6},... | collective-permute-start | bytes 393224 | tf_op jit(solution)/shard_map/ppermute | solution.py:60
  30.2 8.7 %collective-permute-start.11 = (f32[512,128]{1,0:T(8,128)S(1)}, f32[512,128]{1,0:T(8,128)S(1)}, u32[]{:S(2)}, u32[]{:S(2)}) collective-permute-start(f32[512,128]{1,0:T(8,128)S(1)} %get-tuple-element.109.refs_1_), channel_id=1, source_target_pairs={{2,0},{0,2},{3,1},{1,3},{6,4},{4,6},{7,5},{5,7},{10,8},{8,10},{11,... | collective-permute-start | bytes 786440 | tf_op jit(solution)/shard_map/ppermute | solution.py:60
  34.6 7.7 %collective-permute-start.10 = (f32[104,128]{1,0:T(8,128)S(1)}, f32[104,128]{1,0:T(8,128)S(1)}, u32[]{:S(2)}, u32[]{:S(2)}) collective-permute-start(f32[104,128]{1,0:T(8,128)S(1)} %add.51), channel_id=1, source_target_pairs={{8,0},{10,2},{12,4},{14,6},{0,8},{2,10},{4,12},{6,14},{9,1},{11,3}... | collective-permute-start | bytes 159752 | tf_op jit(solution)/shard_map/ppermute | solution.py:60
  42.3 4.6 %collective-permute-start.13 = (f32[176,128]{1,0:T(8,128)S(1)}, f32[176,128]{1,0:T(8,128)S(1)}, u32[]{:S(2)}, u32[]{:S(2)}) collective-permute-start(f32[176,128]{1,0:T(8,128)S(1)} %pad_maximum_fusion), channel_id=1, source_target_pairs={{2,0},{0,2},{6,4},{4,6},{10,8},{8,10},{14,12},{12,14},{3,1},{1,3},... | collective-permute-start | bytes 270344 | tf_op jit(solution)/shard_map/ppermute | solution.py:60
  42.9 5.4 %collective-permute-start.14 = (f32[176,128]{1,0:T(8,128)S(1)}, f32[176,128]{1,0:T(8,128)S(1)}, u32[]{:S(2)}, u32[]{:S(2)}) collective-permute-start(f32[176,128]{1,0:T(8,128)S(1)} %pad_maximum_fusion), channel_id=1, source_target_pairs={{4,0},{6,2},{0,4},{2,6},{12,8},{14,10},{8,12},{10,14},{5,1},{7,3},... | collective-permute-start | bytes 270344 | tf_op jit(solution)/shard_map/ppermute | solution.py:60
  44.2 6.0 %collective-permute-start.15 = (f32[176,128]{1,0:T(8,128)S(1)}, f32[176,128]{1,0:T(8,128)S(1)}, u32[]{:S(2)}, u32[]{:S(2)}) collective-permute-start(f32[176,128]{1,0:T(8,128)S(1)} %pad_maximum_fusion), channel_id=1, source_target_pairs={{6,0},{4,2},{2,4},{0,6},{14,8},{12,10},{10,12},{8,14},{7,1},{5,3},... | collective-permute-start | bytes 270344 | tf_op jit(solution)/shard_map/ppermute | solution.py:60
  50.3 7.9 %collective-permute-start.16 = (f32[72,128]{1,0:T(8,128)S(1)}, f32[72,128]{1,0:T(8,128)S(1)}, u32[]{:S(2)}, u32[]{:S(2)}) collective-permute-start(f32[72,128]{1,0:T(8,128)S(1)} %slice.32.refs_7_), channel_id=1, source_target_pairs={{8,0},{10,2},{12,4},{14,6},{0,8},{2,10},{4,12},{6,14},{9,1},{11,3}... | collective-permute-start | bytes 110600 | tf_op jit(solution)/shard_map/ppermute | solution.py:60
  60.2 6.0 %collective-permute-start.19 = (bf16[512,128]{1,0:T(8,128)(2,1)S(1)}, bf16[512,128]{1,0:T(8,128)(2,1)S(1)}, u32[]{:S(2)}, u32[]{:S(2)}) collective-permute-start(bf16[512,128]{1,0:T(8,128)(2,1)S(1)} %get-tuple-element.122.refs_1_), channel_id=1, source_target_pairs={{1,0},{0,1},{3,2},{2,3},{5,4},{4,5},{7,6},{6,7},{9,8},{8,9},{11,10... | collective-permute-start | bytes 393224 | tf_op jit(solution)/shard_map/ppermute | solution.py:60
  60.3 10.5 %collective-permute-start.23 = (bf16[512,128]{1,0:T(8,128)(2,1)S(1)}, bf16[512,128]{1,0:T(8,128)(2,1)S(1)}, u32[]{:S(2)}, u32[]{:S(2)}) collective-permute-start(bf16[512,128]{1,0:T(8,128)(2,1)S(1)} %get-tuple-element.122.refs_1_), channel_id=1, source_target_pairs={{8,0},{12,4},{0,8},{4,12},{9,1},{13,5},{1,9},{5,13},{10,2},{14,6},... | collective-permute-start | bytes 393224 | tf_op jit(solution)/shard_map/ppermute | solution.py:60
  61.5 9.4 %collective-permute-start.21 = (bf16[512,128]{1,0:T(8,128)(2,1)S(1)}, bf16[512,128]{1,0:T(8,128)(2,1)S(1)}, u32[]{:S(2)}, u32[]{:S(2)}) collective-permute-start(bf16[512,128]{1,0:T(8,128)(2,1)S(1)} %get-tuple-element.122.refs_1_), channel_id=1, source_target_pairs={{4,0},{0,4},{12,8},{8,12},{5,1},{1,5},{13,9},{9,13},{6,2},{2,6},{1... | collective-permute-start | bytes 393224 | tf_op jit(solution)/shard_map/ppermute | solution.py:60
  62.6 10.7 %collective-permute-start.18 = (bf16[512,128]{1,0:T(8,128)(2,1)S(1)}, bf16[512,128]{1,0:T(8,128)(2,1)S(1)}, u32[]{:S(2)}, u32[]{:S(2)}) collective-permute-start(bf16[512,128]{1,0:T(8,128)(2,1)S(1)} %get-tuple-element.122.refs_1_), channel_id=1, source_target_pairs={{12,0},{8,4},{4,8},{0,12},{13,1},{9,5},{5,9},{1,13},{14,2},{10,6},... | collective-permute-start | bytes 393224 | tf_op jit(solution)/shard_map/ppermute | solution.py:60
  64.7 8.6 %collective-permute-start.25 = (f32[512,128]{1,0:T(8,128)S(1)}, f32[512,128]{1,0:T(8,128)S(1)}, u32[]{:S(2)}, u32[]{:S(2)}) collective-permute-start(f32[512,128]{1,0:T(8,128)S(1)} %get-tuple-element.130.refs_2_.refs_5_.refs_0_), channel_id=1, source_target_pairs={{2,0},{0,2},{3,1},{1,3},{6,4},{4,6},{7,5},{5,7},{10,8},{8,10},{11,... | collective-permute-start | bytes 786440 | tf_op jit(solution)/shard_map/ppermute | solution.py:60
  77.2 8.8 %collective-permute-start.28 = (f32[512,128]{1,0:T(8,128)S(1)}, f32[512,128]{1,0:T(8,128)S(1)}, u32[]{:S(2)}, u32[]{:S(2)}) collective-permute-start(f32[512,128]{1,0:T(8,128)S(1)} %get-tuple-element.134.refs_1_), channel_id=1, source_target_pairs={{2,0},{0,2},{3,1},{1,3},{6,4},{4,6},{7,5},{5,7},{10,8},{8,10},{11,... | collective-permute-start | bytes 786440 | tf_op jit(solution)/shard_map/ppermute | solution.py:60
  81.8 5.2 %collective-permute-start.27 = (f32[104,128]{1,0:T(8,128)S(1)}, f32[104,128]{1,0:T(8,128)S(1)}, u32[]{:S(2)}, u32[]{:S(2)}) collective-permute-start(f32[104,128]{1,0:T(8,128)S(1)} %add.57), channel_id=1, source_target_pairs={{8,0},{10,2},{12,4},{14,6},{0,8},{2,10},{4,12},{6,14},{9,1},{11,3}... | collective-permute-start | bytes 159752 | tf_op jit(solution)/shard_map/ppermute | solution.py:60
  88.2 4.8 %collective-permute-start.30 = (f32[176,128]{1,0:T(8,128)S(1)}, f32[176,128]{1,0:T(8,128)S(1)}, u32[]{:S(2)}, u32[]{:S(2)}) collective-permute-start(f32[176,128]{1,0:T(8,128)S(1)} %pad_maximum_fusion.1), channel_id=1, source_target_pairs={{2,0},{0,2},{6,4},{4,6},{10,8},{8,10},{14,12},{12,14},{3,1},{1,3},... | collective-permute-start | bytes 270344 | tf_op jit(solution)/shard_map/ppermute | solution.py:60
  89.0 6.4 %collective-permute-start.31 = (f32[176,128]{1,0:T(8,128)S(1)}, f32[176,128]{1,0:T(8,128)S(1)}, u32[]{:S(2)}, u32[]{:S(2)}) collective-permute-start(f32[176,128]{1,0:T(8,128)S(1)} %pad_maximum_fusion.1), channel_id=1, source_target_pairs={{4,0},{6,2},{0,4},{2,6},{12,8},{14,10},{8,12},{10,14},{5,1},{7,3},... | collective-permute-start | bytes 270344 | tf_op jit(solution)/shard_map/ppermute | solution.py:60
  92.3 5.4 %collective-permute-start.32 = (f32[176,128]{1,0:T(8,128)S(1)}, f32[176,128]{1,0:T(8,128)S(1)}, u32[]{:S(2)}, u32[]{:S(2)}) collective-permute-start(f32[176,128]{1,0:T(8,128)S(1)} %pad_maximum_fusion.1), channel_id=1, source_target_pairs={{6,0},{4,2},{2,4},{0,6},{14,8},{12,10},{10,12},{8,14},{7,1},{5,3},... | collective-permute-start | bytes 270344 | tf_op jit(solution)/shard_map/ppermute | solution.py:60
  97.9 6.6 %collective-permute-start.33 = (f32[72,128]{1,0:T(8,128)S(1)}, f32[72,128]{1,0:T(8,128)S(1)}, u32[]{:S(2)}, u32[]{:S(2)}) collective-permute-start(f32[72,128]{1,0:T(8,128)S(1)} %slice.34.refs_7_), channel_id=1, source_target_pairs={{8,0},{10,2},{12,4},{14,6},{0,8},{2,10},{4,12},{6,14},{9,1},{11,3}... | collective-permute-start | bytes 110600 | tf_op jit(solution)/shard_map/ppermute | solution.py:60
  106.3 5.3 %collective-permute-start.37 = (bf16[512,128]{1,0:T(8,128)(2,1)S(1)}, bf16[512,128]{1,0:T(8,128)(2,1)S(1)}, u32[]{:S(2)}, u32[]{:S(2)}) collective-permute-start(bf16[512,128]{1,0:T(8,128)(2,1)S(1)} %get-tuple-element.149.refs_1_), channel_id=1, source_target_pairs={{1,0},{0,1},{3,2},{2,3},{5,4},{4,5},{7,6},{6,7},{9,8},{8,9},{11,10... | collective-permute-start | bytes 393224 | tf_op jit(solution)/shard_map/ppermute | solution.py:60
  106.4 10.4 %collective-permute-start.40 = (bf16[512,128]{1,0:T(8,128)(2,1)S(1)}, bf16[512,128]{1,0:T(8,128)(2,1)S(1)}, u32[]{:S(2)}, u32[]{:S(2)}) collective-permute-start(bf16[512,128]{1,0:T(8,128)(2,1)S(1)} %get-tuple-element.149.refs_1_), channel_id=1, source_target_pairs={{8,0},{12,4},{0,8},{4,12},{9,1},{13,5},{1,9},{5,13},{10,2},{14,6},... | collective-permute-start | bytes 393224 | tf_op jit(solution)/shard_map/ppermute | solution.py:60
  108.1 9.3 %collective-permute-start.36 = (bf16[512,128]{1,0:T(8,128)(2,1)S(1)}, bf16[512,128]{1,0:T(8,128)(2,1)S(1)}, u32[]{:S(2)}, u32[]{:S(2)}) collective-permute-start(bf16[512,128]{1,0:T(8,128)(2,1)S(1)} %get-tuple-element.149.refs_1_), channel_id=1, source_target_pairs={{4,0},{0,4},{12,8},{8,12},{5,1},{1,5},{13,9},{9,13},{6,2},{2,6},{1... | collective-permute-start | bytes 393224 | tf_op jit(solution)/shard_map/ppermute | solution.py:60
  109.0 12.9 %collective-permute-start.35 = (bf16[512,128]{1,0:T(8,128)(2,1)S(1)}, bf16[512,128]{1,0:T(8,128)(2,1)S(1)}, u32[]{:S(2)}, u32[]{:S(2)}) collective-permute-start(bf16[512,128]{1,0:T(8,128)(2,1)S(1)} %get-tuple-element.149.refs_1_), channel_id=1, source_target_pairs={{12,0},{8,4},{4,8},{0,12},{13,1},{9,5},{5,9},{1,13},{14,2},{10,6},... | collective-permute-start | bytes 393224 | tf_op jit(solution)/shard_map/ppermute | solution.py:60
  110.8 8.6 %collective-permute-start.43 = (f32[512,128]{1,0:T(8,128)S(1)}, f32[512,128]{1,0:T(8,128)S(1)}, u32[]{:S(2)}, u32[]{:S(2)}) collective-permute-start(f32[512,128]{1,0:T(8,128)S(1)} %get-tuple-element.157.refs_2_.refs_3_), channel_id=1, source_target_pairs={{2,0},{0,2},{3,1},{1,3},{6,4},{4,6},{7,5},{5,7},{10,8},{8,10},{11,... | collective-permute-start | bytes 786440 | tf_op jit(solution)/shard_map/ppermute | solution.py:60
  128.2 4.2 %collective-permute-start.47 = (f32[72,128]{1,0:T(8,128)S(1)}, f32[72,128]{1,0:T(8,128)S(1)}, u32[]{:S(2)}, u32[]{:S(2)}) collective-permute-start(f32[72,128]{1,0:T(8,128)S(1)} %add.63), channel_id=1, source_target_pairs={{4,0},{6,2},{0,4},{2,6},{12,8},{14,10},{8,12},{10,14},{5,1},{7,3},... | collective-permute-start | bytes 110600 | tf_op jit(solution)/shard_map/ppermute | solution.py:60
  128.5 5.1 %collective-permute-start.48 = (f32[72,128]{1,0:T(8,128)S(1)}, f32[72,128]{1,0:T(8,128)S(1)}, u32[]{:S(2)}, u32[]{:S(2)}) collective-permute-start(f32[72,128]{1,0:T(8,128)S(1)} %add.63), channel_id=1, source_target_pairs={{6,0},{4,2},{2,4},{0,6},{14,8},{12,10},{10,12},{8,14},{7,1},{5,3},... | collective-permute-start | bytes 110600 | tf_op jit(solution)/shard_map/ppermute | solution.py:60
  131.2 8.7 %collective-permute-start.50 = (f32[512,128]{1,0:T(8,128)S(1)}, f32[512,128]{1,0:T(8,128)S(1)}, u32[]{:S(2)}, u32[]{:S(2)}) collective-permute-start(f32[512,128]{1,0:T(8,128)S(1)} %get-tuple-element.163.refs_1_), channel_id=1, source_target_pairs={{2,0},{0,2},{3,1},{1,3},{6,4},{4,6},{7,5},{5,7},{10,8},{8,10},{11,... | collective-permute-start | bytes 786440 | tf_op jit(solution)/shard_map/ppermute | solution.py:60
  133.6 6.2 %collective-permute-start.49 = (f32[72,128]{1,0:T(8,128)S(1)}, f32[72,128]{1,0:T(8,128)S(1)}, u32[]{:S(2)}, u32[]{:S(2)}) collective-permute-start(f32[72,128]{1,0:T(8,128)S(1)} %add_add_fusion.2), channel_id=1, source_target_pairs={{8,0},{10,2},{12,4},{14,6},{0,8},{2,10},{4,12},{6,14},{9,1},{11,3}... | collective-permute-start | bytes 110600 | tf_op jit(solution)/shard_map/ppermute | solution.py:60
  (19 other events, 36.6 us)

commit v11 on v10

--- a/solution.py
+++ b/solution.py
@@ -27,6 +27,20 @@
         precision=lax.Precision.HIGHEST,
         preferred_element_type=F32,
     )
+
+
+def halves(value):
+    high = value.astype(BF16)
+    return high, (value - high.astype(F32)).astype(BF16)
+
+
+def mm_field(a, b):
+    (a, a_low), (b, b_low) = halves(a), halves(b)
+
+    def part(left, right):
+        return jnp.dot(left, right, preferred_element_type=F32)
+
+    return part(a, b) + (part(a, b_low) + part(a_low, b))
 
 
 def call(body, outs, *args, scratch=(), after=(), any_args=0, any_outs=False):
@@ -623,8 +637,8 @@
         image = images[0][...]
         for ref in images[1:]:
             image = image + ref[...]
-        out[...] = s[...] + mm(d[...], alpha)
-        new_r[...] = r[...] - mm(image, alpha)
+        out[...] = s[...] + mm_field(d[...], alpha)
+        new_r[...] = r[...] - mm_field(image, alpha)
 
     return call(
         body,
@@ -676,8 +690,8 @@
         quadratic = mm(a, mm(unpacked_symmetric(square), a), (0, 0))
         following = gram[...] - (shared + shared.T) + quadratic
         beta = mm(inverse[...], following)
-        new_r = r[...] - mm(image[...], a)
-        value = new_r + mm(d[...], beta)
+        new_r = r[...] - mm_field(image[...], a)
+        value = new_r + mm_field(d[...], beta)
         r_out[...] = new_r
         low[...] = value.astype(BF16)
         new_d[...] = value

time: 145 us -> 145 us (level)
  no operation moved by 1% of the time
where the time goes in v11:
time: 145 us
  Pallas kernels  59.1 us (41%)
  starting transfers between devices  51.5 us (36%)
  waiting for transfers between devices  32.8 us (23%)
    pallas_call x30, Pallas kernels, call(): pl.pallas_call(ordered, out_shape=list(outs) + [shape(SUB)], in_specs=[HB...  59.1 us
    ppermute x51, starting transfers between devices, permute(): return lax.ppermute(value, axis, pairs)  51.5 us
    ppermute x51, waiting for transfers between devices, permute(): return lax.ppermute(value, axis, pairs)  32.8 us
  transfers between devices with their start and end apart: 51, of which 26 were waited for; matrix products, arithmetic and copies ran while one was open for 0% of the time, Pallas kernels for 31%

profile of v11, /device:TPU:0, one launch (start us, length us, event | category | flops | bytes accessed | tf_op | source)
XLA Modules:
  0.0 144.5 jit_solution(5211212503899244907)
XLA Ops:
  2.1 3.0 %collective-permute-start = (f32[512,128]{1,0:T(8,128)S(1)}, f32[512,128]{1,0:T(8,128)S(1)}, u32[]{:S(2)}, u32[]{:S(2)}) collective-permute-start(f32[512,128]{1,0:T(8,128)S(1)} %get-tuple-element.87), channel_id=1, source_target_pairs={{2,0},{0,2},{3,1},{1,3},{6,4},{4,6},{7,5},{5,7},{10,8},{8,10},{11,... | collective-permute-start | bytes 786440 | tf_op jit(solution)/shard_map/ppermute | solution.py:74
  5.1 2.9 %shard_map.51 = (bf16[3,4,1024,2,128]{4,3,2,1,0:T(2,128)(2,1)S(1)}, f32[8,128]{1,0:T(8,128)S(1)}) custom-call(bf16[9,1024,2,512]{3,2,1,0:T(2,128)(2,1)} %bitcast.22, f32[8,128]{1,0:T(8,128)S(1)} %get-tuple-element.88.refs_1_), custom_call_target="tpu_custom_call" | custom-call | flops 1 | bytes 1 | tf_op jit(solution)/shard_map/pallas_call | solution.py:58
  8.0 2.2 %shard_map.52 = (bf16[2,4,1024,2,128]{4,3,2,1,0:T(2,128)(2,1)S(1)}, f32[8,128]{1,0:T(8,128)S(1)}) custom-call(bf16[9,1024,2,512]{3,2,1,0:T(2,128)(2,1)} %bitcast.23, f32[8,128]{1,0:T(8,128)S(1)} %get-tuple-element.89.refs_1_), custom_call_target="tpu_custom_call" | custom-call | flops 1 | bytes 1 | tf_op jit(solution)/shard_map/pallas_call | solution.py:58
  11.6 2.9 %collective-permute-start.6 = (bf16[512,128]{1,0:T(8,128)(2,1)S(1)}, bf16[512,128]{1,0:T(8,128)(2,1)S(1)}, u32[]{:S(2)}, u32[]{:S(2)}) collective-permute-start(bf16[512,128]{1,0:T(8,128)(2,1)S(1)} %get-tuple-element.94.refs_1_), channel_id=1, source_target_pairs={{8,0},{12,4},{0,8},{4,12},{9,1},{13,5},{1,9},{5,13},{10,2},{14,6},... | collective-permute-start | bytes 393224 | tf_op jit(solution)/shard_map/ppermute | solution.py:74
  17.8 2.2 %shard_map.54 = (bf16[2,4,1024,2,128]{4,3,2,1,0:T(2,128)(2,1)S(1)}, f32[8,128]{1,0:T(8,128)S(1)}) custom-call(bf16[9,1024,2,512]{3,2,1,0:T(2,128)(2,1)} %bitcast.24, f32[8,128]{1,0:T(8,128)S(1)} %get-tuple-element.91.refs_1_), custom_call_target="tpu_custom_call" | custom-call | flops 1 | bytes 1 | tf_op jit(solution)/shard_map/pallas_call | solution.py:58
  20.0 2.2 %shard_map.55 = (bf16[2,4,1024,2,128]{4,3,2,1,0:T(2,128)(2,1)S(1)}, f32[8,128]{1,0:T(8,128)S(1)}) custom-call(bf16[9,1024,2,512]{3,2,1,0:T(2,128)(2,1)} %bitcast.25, f32[8,128]{1,0:T(8,128)S(1)} %get-tuple-element.92.refs_1_), custom_call_target="tpu_custom_call" | custom-call | flops 1 | bytes 1 | tf_op jit(solution)/shard_map/pallas_call | solution.py:58
  22.2 2.0 %shard_map.56 = (f32[1024,128]{1,0:T(8,128)S(1)}, f32[8,128]{1,0:T(8,128)S(1)}) custom-call(bf16[3,4,2048,128]{3,2,1,0:T(8,128)(2,1)S(1)} %bitcast.13, bf16[512,128]{1,0:T(8,128)(2,1)S(1)} %get-tuple-element.94.refs_1_, bf16[512,128]{1,0:T(8,128)(2,1)S(1)} %collective-permute-done.2.refs_2_), custom_call_target="tpu_custom_call" | custom-call | flops 1 | bytes 1 | tf_op jit(solution)/shard_map/pallas_call | solution.py:58
  26.3 3.0 %shard_map.58 = (f32[1024,128]{1,0:T(8,128)S(1)}, f32[8,128]{1,0:T(8,128)}) custom-call(bf16[2,4,2048,128]{3,2,1,0:T(8,128)(2,1)S(1)} %bitcast.16, bf16[2,4,2048,128]{3,2,1,0:T(8,128)(2,1)S(1)} %bitcast.19, bf16[512,128]{1,0:T(8,128)(2,1)S(1)} %collective-permute-done.4.refs_2_, bf16[512,128]{1,0:T(8,128)(2,1)S(1)} %collective-permute-done.5.refs_3_, ...), custom_call_target="tpu_custom_call" | custom-call | flops 1 | bytes 1 | tf_op jit(solution)/shard_map/pallas_call | solution.py:58
  34.6 4.4 %collective-permute-start.10 = (f32[104,128]{1,0:T(8,128)S(1)}, f32[104,128]{1,0:T(8,128)S(1)}, u32[]{:S(2)}, u32[]{:S(2)}) collective-permute-start(f32[104,128]{1,0:T(8,128)S(1)} %add.51), channel_id=1, source_target_pairs={{8,0},{10,2},{12,4},{14,6},{0,8},{2,10},{4,12},{6,14},{9,1},{11,3}... | collective-permute-start | bytes 159752 | tf_op jit(solution)/shard_map/ppermute | solution.py:74
  39.9 2.3 %collective-permute-done.10 = f32[104,128]{1,0:T(8,128)S(1)} collective-permute-done((f32[104,128]{1,0:T(8,128)S(1)}, f32[104,128]{1,0:T(8,128)S(1)}, u32[]{:S(2)}, u32[]{:S(2)}) %collective-permute-start.10) | collective-permute-done | bytes 53280 | tf_op jit(solution)/shard_map/ppermute | solution.py:74
  48.3 1.9 %collective-permute-done.15 = f32[176,128]{1,0:T(8,128)S(1)} collective-permute-done((f32[176,128]{1,0:T(8,128)S(1)}, f32[176,128]{1,0:T(8,128)S(1)}, u32[]{:S(2)}, u32[]{:S(2)}) %collective-permute-start.15) | collective-permute-done | bytes 90144 | tf_op jit(solution)/shard_map/ppermute | solution.py:74
  50.3 2.3 %collective-permute-start.16 = (f32[72,128]{1,0:T(8,128)S(1)}, f32[72,128]{1,0:T(8,128)S(1)}, u32[]{:S(2)}, u32[]{:S(2)}) collective-permute-start(f32[72,128]{1,0:T(8,128)S(1)} %slice.32.refs_7_), channel_id=1, source_target_pairs={{8,0},{10,2},{12,4},{14,6},{0,8},{2,10},{4,12},{6,14},{9,1},{11,3}... | collective-permute-start | bytes 110600 | tf_op jit(solution)/shard_map/ppermute | solution.py:74
  52.6 5.6 %shard_map.63 = (f32[128,128]{1,0:T(8,128)S(1)}, f32[128,128]{1,0:T(8,128)S(1)}, f32[128,128]{1,0:T(8,128)S(1)}, f32[128,128]{1,0:T(8,128)S(1)}, f32[8,128]{1,0:T(8,128)}) custom-call(f32[104,128]{1,0:T(8,128)S(1)} %slice.33.refs_0_, f32[104,128]{1,0:T(8,128)S(1)} %collective-permute-done.17.refs_1_), custom_call_target="tpu_custom_call" | custom-call | flops 1 | bytes 1 | tf_op jit(solution)/shard_map/pallas_call | solution.py:58
  62.4 2.1 %collective-permute-start.18 = (bf16[512,128]{1,0:T(8,128)(2,1)S(1)}, bf16[512,128]{1,0:T(8,128)(2,1)S(1)}, u32[]{:S(2)}, u32[]{:S(2)}) collective-permute-start(bf16[512,128]{1,0:T(8,128)(2,1)S(1)} %get-tuple-element.122.refs_1_), channel_id=1, source_target_pairs={{12,0},{8,4},{4,8},{0,12},{13,1},{9,5},{5,9},{1,13},{14,2},{10,6},... | collective-permute-start | bytes 393224 | tf_op jit(solution)/shard_map/ppermute | solution.py:74
  66.0 2.0 %shard_map.65 = (f32[1024,128]{1,0:T(8,128)S(1)}, f32[8,128]{1,0:T(8,128)S(1)}) custom-call(bf16[3,4,2048,128]{3,2,1,0:T(8,128)(2,1)S(1)} %bitcast.14, bf16[512,128]{1,0:T(8,128)(2,1)S(1)} %get-tuple-element.122.refs_1_, bf16[512,128]{1,0:T(8,128)(2,1)S(1)} %collective-permute-done.19.refs_2_), custom_call_target="tpu_custom_call" | custom-call | flops 1 | bytes 1 | tf_op jit(solution)/shard_map/pallas_call | solution.py:58
  68.5 2.0 %collective-permute-done.23.refs_4_ = bf16[512,128]{1,0:T(8,128)(2,1)S(1)} collective-permute-done((bf16[512,128]{1,0:T(8,128)(2,1)S(1)}, bf16[512,128]{1,0:T(8,128)(2,1)S(1)}, u32[]{:S(2)}, u32[]{:S(2)}) %collective-permute-start.23) | collective-permute-done | bytes 131104 | tf_op jit(solution)/shard_map/ppermute | solution.py:74
  71.1 2.0 %collective-permute-done.18.refs_1_ = bf16[512,128]{1,0:T(8,128)(2,1)S(1)} collective-permute-done((bf16[512,128]{1,0:T(8,128)(2,1)S(1)}, bf16[512,128]{1,0:T(8,128)(2,1)S(1)}, u32[]{:S(2)}, u32[]{:S(2)}) %collective-permute-start.18) | collective-permute-done | bytes 131104 | tf_op jit(solution)/shard_map/ppermute | solution.py:74
  73.1 3.0 %shard_map.67 = (f32[1024,128]{1,0:T(8,128)S(1)}, f32[8,128]{1,0:T(8,128)}) custom-call(bf16[2,4,2048,128]{3,2,1,0:T(8,128)(2,1)S(1)} %bitcast.17, bf16[2,4,2048,128]{3,2,1,0:T(8,128)(2,1)S(1)} %bitcast.20, bf16[512,128]{1,0:T(8,128)(2,1)S(1)} %collective-permute-done.21.refs_2_, bf16[512,128]{1,0:T(8,128)(2,1)S(1)} %collective-permute-done.22.refs_3_, ...), custom_call_target="tpu_custom_call" | custom-call | flops 1 | bytes 1 | tf_op jit(solution)/shard_map/pallas_call | solution.py:58
  81.6 3.0 %collective-permute-start.27 = (f32[104,128]{1,0:T(8,128)S(1)}, f32[104,128]{1,0:T(8,128)S(1)}, u32[]{:S(2)}, u32[]{:S(2)}) collective-permute-start(f32[104,128]{1,0:T(8,128)S(1)} %add.57), channel_id=1, source_target_pairs={{8,0},{10,2},{12,4},{14,6},{0,8},{2,10},{4,12},{6,14},{9,1},{11,3}... | collective-permute-start | bytes 159752 | tf_op jit(solution)/shard_map/ppermute | solution.py:74
  88.8 3.3 %collective-permute-start.31 = (f32[176,128]{1,0:T(8,128)S(1)}, f32[176,128]{1,0:T(8,128)S(1)}, u32[]{:S(2)}, u32[]{:S(2)}) collective-permute-start(f32[176,128]{1,0:T(8,128)S(1)} %pad_maximum_fusion.1), channel_id=1, source_target_pairs={{4,0},{6,2},{0,4},{2,6},{12,8},{14,10},{8,12},{10,14},{5,1},{7,3},... | collective-permute-start | bytes 270344 | tf_op jit(solution)/shard_map/ppermute | solution.py:74
  92.7 2.5 %collective-permute-done.31 = f32[176,128]{1,0:T(8,128)S(1)} collective-permute-done((f32[176,128]{1,0:T(8,128)S(1)}, f32[176,128]{1,0:T(8,128)S(1)}, u32[]{:S(2)}, u32[]{:S(2)}) %collective-permute-start.31) | collective-permute-done | bytes 90144 | tf_op jit(solution)/shard_map/ppermute | solution.py:74
  95.2 2.3 %collective-permute-done.32 = f32[176,128]{1,0:T(8,128)S(1)} collective-permute-done((f32[176,128]{1,0:T(8,128)S(1)}, f32[176,128]{1,0:T(8,128)S(1)}, u32[]{:S(2)}, u32[]{:S(2)}) %collective-permute-start.32) | collective-permute-done | bytes 90144 | tf_op jit(solution)/shard_map/ppermute | solution.py:74
  99.0 5.3 %shard_map.72 = (f32[128,128]{1,0:T(8,128)S(1)}, f32[128,128]{1,0:T(8,128)S(1)}, f32[128,128]{1,0:T(8,128)S(1)}, f32[128,128]{1,0:T(8,128)S(1)}, f32[8,128]{1,0:T(8,128)}) custom-call(f32[104,128]{1,0:T(8,128)S(1)} %slice.35.refs_0_, f32[104,128]{1,0:T(8,128)S(1)} %collective-permute-done.34.refs_1_, f32[128,128]{1,0:T(8,128)S(1)} %get-tuple-element.141.refs_2_), custom_call_target="tpu_custom_call" | custom-call | flops 1 | bytes 1 | tf_op jit(solution)/shard_map/pallas_call | solution.py:58
  108.6 1.8 %collective-permute-start.35 = (bf16[512,128]{1,0:T(8,128)(2,1)S(1)}, bf16[512,128]{1,0:T(8,128)(2,1)S(1)}, u32[]{:S(2)}, u32[]{:S(2)}) collective-permute-start(bf16[512,128]{1,0:T(8,128)(2,1)S(1)} %get-tuple-element.149.refs_1_), channel_id=1, source_target_pairs={{12,0},{8,4},{4,8},{0,12},{13,1},{9,5},{5,9},{1,13},{14,2},{10,6},... | collective-permute-start | bytes 393224 | tf_op jit(solution)/shard_map/ppermute | solution.py:74
  111.1 2.2 %shard_map.74 = (f32[1024,128]{1,0:T(8,128)S(1)}, f32[8,128]{1,0:T(8,128)S(1)}) custom-call(bf16[3,4,2048,128]{3,2,1,0:T(8,128)(2,1)S(1)} %bitcast.15, bf16[512,128]{1,0:T(8,128)(2,1)S(1)} %get-tuple-element.149.refs_1_, bf16[512,128]{1,0:T(8,128)(2,1)S(1)} %collective-permute-done.37.refs_2_), custom_call_target="tpu_custom_call" | custom-call | flops 1 | bytes 1 | tf_op jit(solution)/shard_map/pallas_call | solution.py:58
  114.6 1.8 %collective-permute-done.40.refs_5_ = bf16[512,128]{1,0:T(8,128)(2,1)S(1)} collective-permute-done((bf16[512,128]{1,0:T(8,128)(2,1)S(1)}, bf16[512,128]{1,0:T(8,128)(2,1)S(1)}, u32[]{:S(2)}, u32[]{:S(2)}) %collective-permute-start.40) | collective-permute-done | bytes 131104 | tf_op jit(solution)/shard_map/ppermute | solution.py:74
  119.0 2.5 %shard_map.76 = (f32[1024,128]{1,0:T(8,128)S(1)}, f32[8,128]{1,0:T(8,128)S(1)}) custom-call(bf16[2,4,2048,128]{3,2,1,0:T(8,128)(2,1)S(1)} %bitcast.18, bf16[2,4,2048,128]{3,2,1,0:T(8,128)(2,1)S(1)} %bitcast.21, bf16[512,128]{1,0:T(8,128)(2,1)S(1)} %collective-permute-done.36.refs_2_, bf16[256,128]{1,0:T(8,128)(2,1)S(1)} %collective-permute-done.38.refs_3_, ...), custom_call_target="tpu_custom_call" | custom-call | flops 1 | bytes 1 | tf_op jit(solution)/shard_map/pallas_call | solution.py:58
  123.0 1.9 %shard_map.77 = (f32[512,128]{1,0:T(8,128)S(1)}, f32[512,128]{1,0:T(8,128)S(1)}, f32[8,128]{1,0:T(8,128)}) custom-call(bf16[2,4,2048,128]{3,2,1,0:T(8,128)(2,1)S(1)} %bitcast.12, bf16[512,128]{1,0:T(8,128)(2,1)S(1)} %collective-permute-done.35.refs_1_, bf16[512,128]{1,0:T(8,128)(2,1)S(1)} %collective-permute-done.44.refs_2_, ...), custom_call_target="tpu_custom_call" | custom-call | flops 1 | bytes 1 | tf_op jit(solution)/shard_map/pallas_call | solution.py:58
  128.0 2.7 %collective-permute-start.48 = (f32[72,128]{1,0:T(8,128)S(1)}, f32[72,128]{1,0:T(8,128)S(1)}, u32[]{:S(2)}, u32[]{:S(2)}) collective-permute-start(f32[72,128]{1,0:T(8,128)S(1)} %add.63), channel_id=1, source_target_pairs={{6,0},{4,2},{2,4},{0,6},{14,8},{12,10},{10,12},{8,14},{7,1},{5,3},... | collective-permute-start | bytes 110600 | tf_op jit(solution)/shard_map/ppermute | solution.py:74
  133.2 3.9 %collective-permute-start.49 = (f32[72,128]{1,0:T(8,128)S(1)}, f32[72,128]{1,0:T(8,128)S(1)}, u32[]{:S(2)}, u32[]{:S(2)}) collective-permute-start(f32[72,128]{1,0:T(8,128)S(1)} %add_add_fusion.2), channel_id=1, source_target_pairs={{8,0},{10,2},{12,4},{14,6},{0,8},{2,10},{4,12},{6,14},{9,1},{11,3}... | collective-permute-start | bytes 110600 | tf_op jit(solution)/shard_map/ppermute | solution.py:74
  137.1 2.3 %collective-permute-done.49 = f32[72,128]{1,0:T(8,128)S(1)} collective-permute-done((f32[72,128]{1,0:T(8,128)S(1)}, f32[72,128]{1,0:T(8,128)S(1)}, u32[]{:S(2)}, u32[]{:S(2)}) %collective-permute-start.49) | collective-permute-done | bytes 36896 | tf_op jit(solution)/shard_map/ppermute | solution.py:74
  139.4 5.1 %shard_map.79 = (f32[512,128]{1,0:T(8,128)}, f32[512,128]{1,0:T(8,128)}, f32[8,128]{1,0:T(8,128)}) custom-call(f32[72,128]{1,0:T(8,128)S(1)} %add.67.refs_0_, f32[128,128]{1,0:T(8,128)S(1)} %get-tuple-element.165.refs_1_, f32[512,128]{1,0:T(8,128)S(1)} %get-tuple-element.166.refs_2_, f32[512,128]{1,0:T(8,128)S(1)} %get-tuple-element.157.refs_2_.refs_3_, ...), custom_call_target="tpu_custom_call" | custom-call | flops 1 | bytes 1 | tf_op jit(solution)/shard_map/pallas_call | solution.py:58
  (119 shorter events, 55.1 us)
Async XLA Ops:
  2.1 9.3 %collective-permute-start = (f32[512,128]{1,0:T(8,128)S(1)}, f32[512,128]{1,0:T(8,128)S(1)}, u32[]{:S(2)}, u32[]{:S(2)}) collective-permute-start(f32[512,128]{1,0:T(8,128)S(1)} %get-tuple-element.87), channel_id=1, source_target_pairs={{2,0},{0,2},{3,1},{1,3},{6,4},{4,6},{7,5},{5,7},{10,8},{8,10},{11,... | collective-permute-start | bytes 786440 | tf_op jit(solution)/shard_map/ppermute | solution.py:74
  11.5 10.7 %collective-permute-start.2 = (bf16[512,128]{1,0:T(8,128)(2,1)S(1)}, bf16[512,128]{1,0:T(8,128)(2,1)S(1)}, u32[]{:S(2)}, u32[]{:S(2)}) collective-permute-start(bf16[512,128]{1,0:T(8,128)(2,1)S(1)} %get-tuple-element.94.refs_1_), channel_id=1, source_target_pairs={{1,0},{0,1},{3,2},{2,3},{5,4},{4,5},{7,6},{6,7},{9,8},{8,9},{11,10... | collective-permute-start | bytes 393224 | tf_op jit(solution)/shard_map/ppermute | solution.py:74
  11.6 13.1 %collective-permute-start.6 = (bf16[512,128]{1,0:T(8,128)(2,1)S(1)}, bf16[512,128]{1,0:T(8,128)(2,1)S(1)}, u32[]{:S(2)}, u32[]{:S(2)}) collective-permute-start(bf16[512,128]{1,0:T(8,128)(2,1)S(1)} %get-tuple-element.94.refs_1_), channel_id=1, source_target_pairs={{8,0},{12,4},{0,8},{4,12},{9,1},{13,5},{1,9},{5,13},{10,2},{14,6},... | collective-permute-start | bytes 393224 | tf_op jit(solution)/shard_map/ppermute | solution.py:74
  14.5 10.3 %collective-permute-start.4 = (bf16[512,128]{1,0:T(8,128)(2,1)S(1)}, bf16[512,128]{1,0:T(8,128)(2,1)S(1)}, u32[]{:S(2)}, u32[]{:S(2)}) collective-permute-start(bf16[512,128]{1,0:T(8,128)(2,1)S(1)} %get-tuple-element.94.refs_1_), channel_id=1, source_target_pairs={{4,0},{0,4},{12,8},{8,12},{5,1},{1,5},{13,9},{9,13},{6,2},{2,6},{1... | collective-permute-start | bytes 393224 | tf_op jit(solution)/shard_map/ppermute | solution.py:74
  16.1 10.3 %collective-permute-start.8 = (f32[512,128]{1,0:T(8,128)S(1)}, f32[512,128]{1,0:T(8,128)S(1)}, u32[]{:S(2)}, u32[]{:S(2)}) collective-permute-start(f32[512,128]{1,0:T(8,128)S(1)} %get-tuple-element.97.refs_0_.refs_2_.refs_4_.refs_5_), channel_id=1, source_target_pairs={{2,0},{0,2},{3,1},{1,3},{6,4},{4,6},{7,5},{5,7},{10,8},{8,10},{11,... | collective-permute-start | bytes 786440 | tf_op jit(solution)/shard_map/ppermute | solution.py:74
  17.5 7.9 %collective-permute-start.1 = (bf16[512,128]{1,0:T(8,128)(2,1)S(1)}, bf16[512,128]{1,0:T(8,128)(2,1)S(1)}, u32[]{:S(2)}, u32[]{:S(2)}) collective-permute-start(bf16[512,128]{1,0:T(8,128)(2,1)S(1)} %get-tuple-element.94.refs_1_), channel_id=1, source_target_pairs={{12,0},{8,4},{4,8},{0,12},{13,1},{9,5},{5,9},{1,13},{14,2},{10,6},... | collective-permute-start | bytes 393224 | tf_op jit(solution)/shard_map/ppermute | solution.py:74
  30.2 8.7 %collective-permute-start.11 = (f32[512,128]{1,0:T(8,128)S(1)}, f32[512,128]{1,0:T(8,128)S(1)}, u32[]{:S(2)}, u32[]{:S(2)}) collective-permute-start(f32[512,128]{1,0:T(8,128)S(1)} %get-tuple-element.109.refs_1_), channel_id=1, source_target_pairs={{2,0},{0,2},{3,1},{1,3},{6,4},{4,6},{7,5},{5,7},{10,8},{8,10},{11,... | collective-permute-start | bytes 786440 | tf_op jit(solution)/shard_map/ppermute | solution.py:74
  34.6 7.7 %collective-permute-start.10 = (f32[104,128]{1,0:T(8,128)S(1)}, f32[104,128]{1,0:T(8,128)S(1)}, u32[]{:S(2)}, u32[]{:S(2)}) collective-permute-start(f32[104,128]{1,0:T(8,128)S(1)} %add.51), channel_id=1, source_target_pairs={{8,0},{10,2},{12,4},{14,6},{0,8},{2,10},{4,12},{6,14},{9,1},{11,3}... | collective-permute-start | bytes 159752 | tf_op jit(solution)/shard_map/ppermute | solution.py:74
  42.3 4.6 %collective-permute-start.13 = (f32[176,128]{1,0:T(8,128)S(1)}, f32[176,128]{1,0:T(8,128)S(1)}, u32[]{:S(2)}, u32[]{:S(2)}) collective-permute-start(f32[176,128]{1,0:T(8,128)S(1)} %pad_maximum_fusion), channel_id=1, source_target_pairs={{2,0},{0,2},{6,4},{4,6},{10,8},{8,10},{14,12},{12,14},{3,1},{1,3},... | collective-permute-start | bytes 270344 | tf_op jit(solution)/shard_map/ppermute | solution.py:74
  42.9 5.4 %collective-permute-start.14 = (f32[176,128]{1,0:T(8,128)S(1)}, f32[176,128]{1,0:T(8,128)S(1)}, u32[]{:S(2)}, u32[]{:S(2)}) collective-permute-start(f32[176,128]{1,0:T(8,128)S(1)} %pad_maximum_fusion), channel_id=1, source_target_pairs={{4,0},{6,2},{0,4},{2,6},{12,8},{14,10},{8,12},{10,14},{5,1},{7,3},... | collective-permute-start | bytes 270344 | tf_op jit(solution)/shard_map/ppermute | solution.py:74
  44.2 6.0 %collective-permute-start.15 = (f32[176,128]{1,0:T(8,128)S(1)}, f32[176,128]{1,0:T(8,128)S(1)}, u32[]{:S(2)}, u32[]{:S(2)}) collective-permute-start(f32[176,128]{1,0:T(8,128)S(1)} %pad_maximum_fusion), channel_id=1, source_target_pairs={{6,0},{4,2},{2,4},{0,6},{14,8},{12,10},{10,12},{8,14},{7,1},{5,3},... | collective-permute-start | bytes 270344 | tf_op jit(solution)/shard_map/ppermute | solution.py:74
  50.3 7.9 %collective-permute-start.16 = (f32[72,128]{1,0:T(8,128)S(1)}, f32[72,128]{1,0:T(8,128)S(1)}, u32[]{:S(2)}, u32[]{:S(2)}) collective-permute-start(f32[72,128]{1,0:T(8,128)S(1)} %slice.32.refs_7_), channel_id=1, source_target_pairs={{8,0},{10,2},{12,4},{14,6},{0,8},{2,10},{4,12},{6,14},{9,1},{11,3}... | collective-permute-start | bytes 110600 | tf_op jit(solution)/shard_map/ppermute | solution.py:74
  59.9 6.0 %collective-permute-start.19 = (bf16[512,128]{1,0:T(8,128)(2,1)S(1)}, bf16[512,128]{1,0:T(8,128)(2,1)S(1)}, u32[]{:S(2)}, u32[]{:S(2)}) collective-permute-start(bf16[512,128]{1,0:T(8,128)(2,1)S(1)} %get-tuple-element.122.refs_1_), channel_id=1, source_target_pairs={{1,0},{0,1},{3,2},{2,3},{5,4},{4,5},{7,6},{6,7},{9,8},{8,9},{11,10... | collective-permute-start | bytes 393224 | tf_op jit(solution)/shard_map/ppermute | solution.py:74
  60.1 10.5 %collective-permute-start.23 = (bf16[512,128]{1,0:T(8,128)(2,1)S(1)}, bf16[512,128]{1,0:T(8,128)(2,1)S(1)}, u32[]{:S(2)}, u32[]{:S(2)}) collective-permute-start(bf16[512,128]{1,0:T(8,128)(2,1)S(1)} %get-tuple-element.122.refs_1_), channel_id=1, source_target_pairs={{8,0},{12,4},{0,8},{4,12},{9,1},{13,5},{1,9},{5,13},{10,2},{14,6},... | collective-permute-start | bytes 393224 | tf_op jit(solution)/shard_map/ppermute | solution.py:74
  61.2 9.4 %collective-permute-start.21 = (bf16[512,128]{1,0:T(8,128)(2,1)S(1)}, bf16[512,128]{1,0:T(8,128)(2,1)S(1)}, u32[]{:S(2)}, u32[]{:S(2)}) collective-permute-start(bf16[512,128]{1,0:T(8,128)(2,1)S(1)} %get-tuple-element.122.refs_1_), channel_id=1, source_target_pairs={{4,0},{0,4},{12,8},{8,12},{5,1},{1,5},{13,9},{9,13},{6,2},{2,6},{1... | collective-permute-start | bytes 393224 | tf_op jit(solution)/shard_map/ppermute | solution.py:74
  62.4 10.7 %collective-permute-start.18 = (bf16[512,128]{1,0:T(8,128)(2,1)S(1)}, bf16[512,128]{1,0:T(8,128)(2,1)S(1)}, u32[]{:S(2)}, u32[]{:S(2)}) collective-permute-start(bf16[512,128]{1,0:T(8,128)(2,1)S(1)} %get-tuple-element.122.refs_1_), channel_id=1, source_target_pairs={{12,0},{8,4},{4,8},{0,12},{13,1},{9,5},{5,9},{1,13},{14,2},{10,6},... | collective-permute-start | bytes 393224 | tf_op jit(solution)/shard_map/ppermute | solution.py:74
  64.5 8.6 %collective-permute-start.25 = (f32[512,128]{1,0:T(8,128)S(1)}, f32[512,128]{1,0:T(8,128)S(1)}, u32[]{:S(2)}, u32[]{:S(2)}) collective-permute-start(f32[512,128]{1,0:T(8,128)S(1)} %get-tuple-element.130.refs_2_.refs_5_.refs_0_), channel_id=1, source_target_pairs={{2,0},{0,2},{3,1},{1,3},{6,4},{4,6},{7,5},{5,7},{10,8},{8,10},{11,... | collective-permute-start | bytes 786440 | tf_op jit(solution)/shard_map/ppermute | solution.py:74
  77.0 8.8 %collective-permute-start.28 = (f32[512,128]{1,0:T(8,128)S(1)}, f32[512,128]{1,0:T(8,128)S(1)}, u32[]{:S(2)}, u32[]{:S(2)}) collective-permute-start(f32[512,128]{1,0:T(8,128)S(1)} %get-tuple-element.134.refs_1_), channel_id=1, source_target_pairs={{2,0},{0,2},{3,1},{1,3},{6,4},{4,6},{7,5},{5,7},{10,8},{8,10},{11,... | collective-permute-start | bytes 786440 | tf_op jit(solution)/shard_map/ppermute | solution.py:74
  81.6 5.2 %collective-permute-start.27 = (f32[104,128]{1,0:T(8,128)S(1)}, f32[104,128]{1,0:T(8,128)S(1)}, u32[]{:S(2)}, u32[]{:S(2)}) collective-permute-start(f32[104,128]{1,0:T(8,128)S(1)} %add.57), channel_id=1, source_target_pairs={{8,0},{10,2},{12,4},{14,6},{0,8},{2,10},{4,12},{6,14},{9,1},{11,3}... | collective-permute-start | bytes 159752 | tf_op jit(solution)/shard_map/ppermute | solution.py:74
  88.0 4.8 %collective-permute-start.30 = (f32[176,128]{1,0:T(8,128)S(1)}, f32[176,128]{1,0:T(8,128)S(1)}, u32[]{:S(2)}, u32[]{:S(2)}) collective-permute-start(f32[176,128]{1,0:T(8,128)S(1)} %pad_maximum_fusion.1), channel_id=1, source_target_pairs={{2,0},{0,2},{6,4},{4,6},{10,8},{8,10},{14,12},{12,14},{3,1},{1,3},... | collective-permute-start | bytes 270344 | tf_op jit(solution)/shard_map/ppermute | solution.py:74
  88.8 6.4 %collective-permute-start.31 = (f32[176,128]{1,0:T(8,128)S(1)}, f32[176,128]{1,0:T(8,128)S(1)}, u32[]{:S(2)}, u32[]{:S(2)}) collective-permute-start(f32[176,128]{1,0:T(8,128)S(1)} %pad_maximum_fusion.1), channel_id=1, source_target_pairs={{4,0},{6,2},{0,4},{2,6},{12,8},{14,10},{8,12},{10,14},{5,1},{7,3},... | collective-permute-start | bytes 270344 | tf_op jit(solution)/shard_map/ppermute | solution.py:74
  92.1 5.4 %collective-permute-start.32 = (f32[176,128]{1,0:T(8,128)S(1)}, f32[176,128]{1,0:T(8,128)S(1)}, u32[]{:S(2)}, u32[]{:S(2)}) collective-permute-start(f32[176,128]{1,0:T(8,128)S(1)} %pad_maximum_fusion.1), channel_id=1, source_target_pairs={{6,0},{4,2},{2,4},{0,6},{14,8},{12,10},{10,12},{8,14},{7,1},{5,3},... | collective-permute-start | bytes 270344 | tf_op jit(solution)/shard_map/ppermute | solution.py:74
  97.7 6.6 %collective-permute-start.33 = (f32[72,128]{1,0:T(8,128)S(1)}, f32[72,128]{1,0:T(8,128)S(1)}, u32[]{:S(2)}, u32[]{:S(2)}) collective-permute-start(f32[72,128]{1,0:T(8,128)S(1)} %slice.34.refs_7_), channel_id=1, source_target_pairs={{8,0},{10,2},{12,4},{14,6},{0,8},{2,10},{4,12},{6,14},{9,1},{11,3}... | collective-permute-start | bytes 110600 | tf_op jit(solution)/shard_map/ppermute | solution.py:74
  105.9 5.3 %collective-permute-start.37 = (bf16[512,128]{1,0:T(8,128)(2,1)S(1)}, bf16[512,128]{1,0:T(8,128)(2,1)S(1)}, u32[]{:S(2)}, u32[]{:S(2)}) collective-permute-start(bf16[512,128]{1,0:T(8,128)(2,1)S(1)} %get-tuple-element.149.refs_1_), channel_id=1, source_target_pairs={{1,0},{0,1},{3,2},{2,3},{5,4},{4,5},{7,6},{6,7},{9,8},{8,9},{11,10... | collective-permute-start | bytes 393224 | tf_op jit(solution)/shard_map/ppermute | solution.py:74
  106.0 10.4 %collective-permute-start.40 = (bf16[512,128]{1,0:T(8,128)(2,1)S(1)}, bf16[512,128]{1,0:T(8,128)(2,1)S(1)}, u32[]{:S(2)}, u32[]{:S(2)}) collective-permute-start(bf16[512,128]{1,0:T(8,128)(2,1)S(1)} %get-tuple-element.149.refs_1_), channel_id=1, source_target_pairs={{8,0},{12,4},{0,8},{4,12},{9,1},{13,5},{1,9},{5,13},{10,2},{14,6},... | collective-permute-start | bytes 393224 | tf_op jit(solution)/shard_map/ppermute | solution.py:74
  107.7 9.3 %collective-permute-start.36 = (bf16[512,128]{1,0:T(8,128)(2,1)S(1)}, bf16[512,128]{1,0:T(8,128)(2,1)S(1)}, u32[]{:S(2)}, u32[]{:S(2)}) collective-permute-start(bf16[512,128]{1,0:T(8,128)(2,1)S(1)} %get-tuple-element.149.refs_1_), channel_id=1, source_target_pairs={{4,0},{0,4},{12,8},{8,12},{5,1},{1,5},{13,9},{9,13},{6,2},{2,6},{1... | collective-permute-start | bytes 393224 | tf_op jit(solution)/shard_map/ppermute | solution.py:74
  108.6 12.9 %collective-permute-start.35 = (bf16[512,128]{1,0:T(8,128)(2,1)S(1)}, bf16[512,128]{1,0:T(8,128)(2,1)S(1)}, u32[]{:S(2)}, u32[]{:S(2)}) collective-permute-start(bf16[512,128]{1,0:T(8,128)(2,1)S(1)} %get-tuple-element.149.refs_1_), channel_id=1, source_target_pairs={{12,0},{8,4},{4,8},{0,12},{13,1},{9,5},{5,9},{1,13},{14,2},{10,6},... | collective-permute-start | bytes 393224 | tf_op jit(solution)/shard_map/ppermute | solution.py:74
  110.4 8.6 %collective-permute-start.43 = (f32[512,128]{1,0:T(8,128)S(1)}, f32[512,128]{1,0:T(8,128)S(1)}, u32[]{:S(2)}, u32[]{:S(2)}) collective-permute-start(f32[512,128]{1,0:T(8,128)S(1)} %get-tuple-element.157.refs_2_.refs_3_), channel_id=1, source_target_pairs={{2,0},{0,2},{3,1},{1,3},{6,4},{4,6},{7,5},{5,7},{10,8},{8,10},{11,... | collective-permute-start | bytes 786440 | tf_op jit(solution)/shard_map/ppermute | solution.py:74
  127.8 4.3 %collective-permute-start.47 = (f32[72,128]{1,0:T(8,128)S(1)}, f32[72,128]{1,0:T(8,128)S(1)}, u32[]{:S(2)}, u32[]{:S(2)}) collective-permute-start(f32[72,128]{1,0:T(8,128)S(1)} %add.63), channel_id=1, source_target_pairs={{4,0},{6,2},{0,4},{2,6},{12,8},{14,10},{8,12},{10,14},{5,1},{7,3},... | collective-permute-start | bytes 110600 | tf_op jit(solution)/shard_map/ppermute | solution.py:74
  128.0 5.2 %collective-permute-start.48 = (f32[72,128]{1,0:T(8,128)S(1)}, f32[72,128]{1,0:T(8,128)S(1)}, u32[]{:S(2)}, u32[]{:S(2)}) collective-permute-start(f32[72,128]{1,0:T(8,128)S(1)} %add.63), channel_id=1, source_target_pairs={{6,0},{4,2},{2,4},{0,6},{14,8},{12,10},{10,12},{8,14},{7,1},{5,3},... | collective-permute-start | bytes 110600 | tf_op jit(solution)/shard_map/ppermute | solution.py:74
  130.8 8.7 %collective-permute-start.50 = (f32[512,128]{1,0:T(8,128)S(1)}, f32[512,128]{1,0:T(8,128)S(1)}, u32[]{:S(2)}, u32[]{:S(2)}) collective-permute-start(f32[512,128]{1,0:T(8,128)S(1)} %get-tuple-element.163.refs_1_), channel_id=1, source_target_pairs={{2,0},{0,2},{3,1},{1,3},{6,4},{4,6},{7,5},{5,7},{10,8},{8,10},{11,... | collective-permute-start | bytes 786440 | tf_op jit(solution)/shard_map/ppermute | solution.py:74
  133.2 6.2 %collective-permute-start.49 = (f32[72,128]{1,0:T(8,128)S(1)}, f32[72,128]{1,0:T(8,128)S(1)}, u32[]{:S(2)}, u32[]{:S(2)}) collective-permute-start(f32[72,128]{1,0:T(8,128)S(1)} %add_add_fusion.2), channel_id=1, source_target_pairs={{8,0},{10,2},{12,4},{14,6},{0,8},{2,10},{4,12},{6,14},{9,1},{11,3}... | collective-permute-start | bytes 110600 | tf_op jit(solution)/shard_map/ppermute | solution.py:74
  (19 other events, 36.6 us)
